TPU v7x, 32 devices: a whole 2x2x4 slice. The times are simulated.
32 devices in a mesh: dp: 8 (over y, x, core), expert: 4 (over z).
Axes of the slice: x: 2, y: 2, z: 4, core: 2. Of those that a mesh axis runs over, the one named last changes fastest.
Arguments:
- tokens: bfloat16 [4096, 2048], P(('dp', 'expert')), may hold values from -6 to 6
- expert_ids: int32 [4096, 2], P(('dp', 'expert')), may hold values from 0 to 3, all different within a row; in each aligned block of 128 rows (0 to 127, 128 to 255, ...) at most 64 rows name the same one
- gate_probs: float32 [4096, 2], P(('dp', 'expert')), may hold values from 0.25 to 1
- w_gate: bfloat16 [4, 2048, 768], P('expert'), may hold values from -0.125 to 0.125
- w_up: bfloat16 [4, 2048, 768], P('expert'), may hold values from -0.125 to 0.125
- w_down: bfloat16 [4, 768, 2048], P('expert'), may hold values from -0.21875 to 0.21875
- out_grad: bfloat16 [4096, 2048], P(('dp', 'expert')), may hold values from -6 to 6
Outputs:
- layer_out: bfloat16 [4096, 2048], P(('dp', 'expert'))
- prob_grad: float32 [4096, 2], P(('dp', 'expert'))
- token_grad: bfloat16 [4096, 2048], P(('dp', 'expert'))
- grad_gate: bfloat16 [4, 2048, 768], P('expert', 'dp')
- grad_up: bfloat16 [4, 2048, 768], P('expert', 'dp')
- grad_down: bfloat16 [4, 768, 2048], P('expert', 'dp')
Inputs may be any that keep to these rules, and one draw needn't show every extreme that they name: `expert_ids`: the 2 experts of one token differ. Among the 128 tokens of one device (aligned blocks of rows), no expert is chosen by more than 64 tokens, and in every draw some expert is chosen by exactly 64 of some device's tokens.
All inputs are finite; a program needn't handle non-finite values.
Results may differ from a plain program's by a relative error of at most 0.015.
Values may be sent and summed in bfloat16 or wider, within the bound.
No kernel may reach another device: no remote copies, remote signals or barrier semaphores. Data moves between devices by JAX's collectives and lax.ppermute only.
A program may use at most 128 MiB of HBM per device.

v0:
```python
import jax
import jax.numpy as jnp
from jax import lax
from jax.sharding import PartitionSpec as P

CAP = 64


def silu_parts(gate_val):
    sig_val = jax.nn.sigmoid(gate_val)
    return (gate_val * sig_val, sig_val * (1.0 + gate_val * (1.0 - sig_val)))


def contract_rows(left, right):
    return lax.dot_general(
        left, right, (((0,), (0,)), ((), ())), preferred_element_type=jnp.float32
    )


def contract_cols(left, right):
    return lax.dot_general(
        left, right, (((1,), (1,)), ((), ())), preferred_element_type=jnp.float32
    )


def local(tokens, expert_ids, gate_probs, w_gate, w_up, w_down, out_grad):
    tok_count, model_width = tokens.shape
    top_count = expert_ids.shape[1]
    peer_count = lax.axis_size("expert")
    slot_count = tok_count * top_count
    flat_ids = expert_ids.reshape(slot_count)
    onehot = (flat_ids[:, None] == jnp.arange(peer_count, dtype=jnp.int32)[None, :]).astype(
        jnp.int32
    )
    slot_rank = jnp.sum((jnp.cumsum(onehot, axis=0) - 1) * onehot, axis=1)
    slot_index = flat_ids * CAP + slot_rank
    row_of_place = (
        jnp.full((peer_count * CAP,), slot_count, jnp.int32)
        .at[slot_index]
        .set(jnp.arange(slot_count, dtype=jnp.int32))
    )
    token_of_place = jnp.where(row_of_place < slot_count, row_of_place // top_count, tok_count)
    zero_row = jnp.zeros((1, model_width), jnp.bfloat16)
    send_x = jnp.concatenate([tokens, zero_row], 0)[token_of_place].reshape(
        peer_count, CAP, model_width
    )
    scaled_grad = (gate_probs[:, :, None] * out_grad.astype(jnp.float32)[:, None, :]).astype(
        jnp.bfloat16
    )
    scaled_grad = scaled_grad.reshape(slot_count, model_width)
    send_grad = jnp.concatenate([scaled_grad, zero_row], 0)[row_of_place].reshape(
        peer_count, CAP, model_width
    )
    gate_w = w_gate[0]
    up_w = w_up[0]
    down_w = w_down[0]
    recv_x = lax.all_to_all(send_x, "expert", split_axis=0, concat_axis=0, tiled=True)
    x_rows = recv_x.reshape(peer_count * CAP, model_width)
    gate_val = jnp.dot(x_rows, gate_w, preferred_element_type=jnp.float32)
    up_val = jnp.dot(x_rows, up_w, preferred_element_type=jnp.float32)
    act_val, act_slope = silu_parts(gate_val)
    hidden = (act_val * up_val).astype(jnp.bfloat16)
    out_rows = jnp.dot(hidden, down_w, preferred_element_type=jnp.float32).astype(jnp.bfloat16)
    out_rows = out_rows.reshape(peer_count, CAP, model_width)
    back_out = lax.all_to_all(out_rows, "expert", split_axis=0, concat_axis=0, tiled=True)
    recv_grad = lax.all_to_all(send_grad, "expert", split_axis=0, concat_axis=0, tiled=True)
    d_rows = recv_grad.reshape(peer_count * CAP, model_width)
    hid_grad = contract_cols(d_rows, down_w)
    gate_grad = (hid_grad * up_val * act_slope).astype(jnp.bfloat16)
    up_grad = (hid_grad * act_val).astype(jnp.bfloat16)
    in_rows = (contract_cols(gate_grad, gate_w) + contract_cols(up_grad, up_w)).astype(jnp.bfloat16)
    in_rows = in_rows.reshape(peer_count, CAP, model_width)
    back_in = lax.all_to_all(in_rows, "expert", split_axis=0, concat_axis=0, tiled=True)
    out_slots = (
        back_out.reshape(peer_count * CAP, model_width)[slot_index]
        .reshape(tok_count, top_count, model_width)
        .astype(jnp.float32)
    )
    in_slots = (
        back_in.reshape(peer_count * CAP, model_width)[slot_index]
        .reshape(tok_count, top_count, model_width)
        .astype(jnp.float32)
    )
    layer_out = jnp.sum(gate_probs[:, :, None] * out_slots, axis=1).astype(jnp.bfloat16)
    prob_grad = jnp.sum(out_grad.astype(jnp.float32)[:, None, :] * out_slots, axis=2)
    token_grad = jnp.sum(in_slots, axis=1).astype(jnp.bfloat16)
    part_gate = contract_rows(x_rows, gate_grad)
    part_up = contract_rows(x_rows, up_grad)
    part_down = contract_rows(hidden, d_rows)
    sum_gate, sum_up, sum_down = (
        lax.psum_scatter(
            part_gate.astype(jnp.bfloat16), "dp", scatter_dimension=0, tiled=True
        ).astype(jnp.float32),
        lax.psum_scatter(
            part_up.astype(jnp.bfloat16), "dp", scatter_dimension=0, tiled=True
        ).astype(jnp.float32),
        lax.psum_scatter(
            part_down.astype(jnp.bfloat16), "dp", scatter_dimension=0, tiled=True
        ).astype(jnp.float32),
    )
    return (
        layer_out,
        prob_grad,
        token_grad,
        sum_gate.astype(jnp.bfloat16)[None],
        sum_up.astype(jnp.bfloat16)[None],
        sum_down.astype(jnp.bfloat16)[None],
    )


def solution(mesh):
    return jax.shard_map(
        local,
        mesh=mesh,
        in_specs=(
            P(("dp", "expert"), None),
            P(("dp", "expert"), None),
            P(("dp", "expert"), None),
            P("expert", None, None),
            P("expert", None, None),
            P("expert", None, None),
            P(("dp", "expert"), None),
        ),
        out_specs=(
            P(("dp", "expert"), None),
            P(("dp", "expert"), None),
            P(("dp", "expert"), None),
            P("expert", "dp", None),
            P("expert", "dp", None),
            P("expert", "dp", None),
        ),
        check_vma=False,
    )
```

profile of v0, /device:TPU:0, one launch (start us, length us, event | category | flops | bytes accessed | tf_op | source)
XLA Modules:
  0.0 244.0 jit_solution(4180590473970144971)
XLA Ops:
  12.4 1.9 concatenate.6
  14.3 4.5 %gather_fusion = bf16[256,2048]{1,0:T(8,128)(2,1)} fusion(bf16[129,2048]{1,0:T(8,128)(2,1)} %concatenate.6, s32[1024]{0:T(1024)S(1)} %get-tuple-element.20), kind=kCustom, calls=%fused_computation | custom fusion | bytes 2098176 | tf_op jit(solution)/shard_map/gather | solution.py:44
  18.8 6.3 %all-to-all-start = ((bf16[4,64,2048]{2,1,0:T(8,128)(2,1)}), bf16[4,64,2048]{2,1,0:T(8,128)(2,1)}, u32[]{:S(2)}, u32[]{:S(2)}) async-start(bf16[4,64,2048]{2,1,0:T(8,128)(2,1)} %bitcast.63), calls=%async_computation | async-start | bytes 2097152 | tf_op jit(solution)/shard_map/all_to_all | solution.py:57
  25.4 3.5 %mul.84 = f32[128,2,2048]{2,1,0:T(2,128)} broadcast(bf16[128,2048]{1,0:T(8,128)(2,1)} %param.13), dimensions={0,2} | broadcast | bytes 2621440 | tf_op jit(solution)/shard_map/mul | solution.py:85
  28.8 3.7 %mul.88 = f32[256,2048]{1,0:T(8,128)} reshape(f32[128,2,2048]{2,1,0:T(2,128)} %mul.84) | data formatting | bytes 4194304 | tf_op jit(solution)/shard_map/mul | solution.py:85
  32.5 1.8 multiply_convert_fusion
  35.3 4.8 %gather_fusion.2 = bf16[256,2048]{1,0:T(8,128)(2,1)} fusion(bf16[257,2048]{1,0:T(8,128)(2,1)} %concatenate.7, s32[1024]{0:T(1024)S(1)} %get-tuple-element.19), kind=kCustom, calls=%fused_computation.2 | custom fusion | bytes 2098176 | tf_op jit(solution)/shard_map/gather | solution.py:51
  40.1 10.9 %all-to-all-done = bf16[4,64,2048]{2,1,0:T(8,128)(2,1)} async-done(((bf16[4,64,2048]{2,1,0:T(8,128)(2,1)}), bf16[4,64,2048]{2,1,0:T(8,128)(2,1)}, u32[]{:S(2)}, u32[]{:S(2)}) %all-to-all-start) | async-done | bytes 1048608 | tf_op jit(solution)/shard_map/all_to_all | solution.py:57
  50.9 4.2 %all-to-all-start.2 = ((bf16[4,64,2048]{2,1,0:T(8,128)(2,1)}), bf16[4,64,2048]{2,1,0:T(8,128)(2,1)}, u32[]{:S(2)}, u32[]{:S(2)}) async-start(bf16[4,64,2048]{2,1,0:T(8,128)(2,1)} %bitcast.64), calls=%async_computation.2 | async-start | bytes 2097152 | tf_op jit(solution)/shard_map/all_to_all | solution.py:66
  55.2 4.1 %fusion.6 = f32[256,768]{1,0:T(8,128)} fusion(bf16[256,2048]{1,0:T(8,128)(2,1)} %bitcast.5, bf16[1,2048,768]{2,1,0:T(8,128)(2,1)} %param.11), kind=kOutput, calls=%fused_computation.14 | convolution fusion | flops 805306368 | bytes 4980736 | tf_op jit(solution)/shard_map/dot_general | solution.py:60
  59.3 21.2 %all-to-all-done.2 = bf16[4,64,2048]{2,1,0:T(8,128)(2,1)} async-done(((bf16[4,64,2048]{2,1,0:T(8,128)(2,1)}), bf16[4,64,2048]{2,1,0:T(8,128)(2,1)}, u32[]{:S(2)}, u32[]{:S(2)}) %all-to-all-start.2) | async-done | bytes 1048608 | tf_op jit(solution)/shard_map/all_to_all | solution.py:66
  80.5 3.3 %fusion = f32[256,768]{1,0:T(8,128)S(1)} fusion(bf16[256,2048]{1,0:T(8,128)(2,1)} %bitcast.12, bf16[1,768,2048]{2,1,0:T(8,128)(2,1)} %param.12), kind=kOutput, calls=%fused_computation.8 | convolution fusion | flops 805306368 | bytes 4980736 | tf_op jit(solution)/shard_map/dot_general | solution.py:21
  83.8 3.3 %multiply_convert_fusion.2 = (bf16[256,768]{1,0:T(8,128)(2,1)S(1)}, bf16[256,768]{1,0:T(8,128)(2,1)}, bf16[256,768]{1,0:T(8,128)(2,1)}) fusion(f32[256,768]{1,0:T(8,128)S(1)} %fusion, f32[256,768]{1,0:T(8,128)S(1)} %copy-done.4, bf16[256,2048]{1,0:T(8,128)(2,1)} %bitcast.5, bf16[1,2048,768]{2,1,0:T(8,128)(2,1)S(1)} %copy-done), kind=kOutput, calls=%fused_computation.27 | convolution fusion | flops 808255488 | bytes 6946816 | tf_op jit(solution)/shard_map/dot_general | solution.py:59
  87.2 3.9 %convolution_convert_fusion.2 = bf16[2048,768]{1,0:T(8,128)(2,1)} fusion(bf16[256,2048]{1,0:T(8,128)(2,1)} %bitcast.5, bf16[256,768]{1,0:T(8,128)(2,1)S(1)} %get-tuple-element.14), kind=kOutput, calls=%fused_computation.7 | convolution fusion | flops 806879232 | bytes 4587520 | tf_op jit(solution)/shard_map/dot_general | solution.py:15
  91.3 4.0 %convolution_convert_fusion.1 = bf16[2048,768]{1,0:T(8,128)(2,1)} fusion(bf16[256,2048]{1,0:T(8,128)(2,1)} %bitcast.5, bf16[256,768]{1,0:T(8,128)(2,1)} %get-tuple-element.15), kind=kOutput, calls=%fused_computation.6 | convolution fusion | flops 806879232 | bytes 4587520 | tf_op jit(solution)/shard_map/dot_general | solution.py:15
  95.5 4.1 %convolution_convert_fusion = bf16[768,2048]{1,0:T(8,128)(2,1)} fusion(bf16[256,768]{1,0:T(8,128)(2,1)} %get-tuple-element.16, bf16[256,2048]{1,0:T(8,128)(2,1)} %bitcast.12), kind=kOutput, calls=%fused_computation.5 | convolution fusion | flops 806879232 | bytes 4587520 | tf_op jit(solution)/shard_map/dot_general | solution.py:15
  99.6 3.3 %fusion.4 = f32[256,2048]{1,0:T(8,128)S(1)} fusion(bf16[256,768]{1,0:T(8,128)(2,1)} %get-tuple-element.15, bf16[1,2048,768]{2,1,0:T(8,128)(2,1)} %param.11), kind=kOutput, calls=%fused_computation.12 | convolution fusion | flops 805306368 | bytes 5636096 | tf_op jit(solution)/shard_map/dot_general | solution.py:21
  102.9 2.0 fusion.15
  104.9 4.2 %all-to-all-start.3 = ((bf16[4,64,2048]{2,1,0:T(8,128)(2,1)}), bf16[4,64,2048]{2,1,0:T(8,128)(2,1)}, u32[]{:S(2)}, u32[]{:S(2)}) async-start(bf16[4,64,2048]{2,1,0:T(8,128)(2,1)} %bitcast.65), calls=%async_computation.3 | async-start | bytes 2097152 | tf_op jit(solution)/shard_map/all_to_all | solution.py:73
  109.2 4.0 %fusion.18 = bf16[256,2048]{1,0:T(8,128)(2,1)} fusion(bf16[256,768]{1,0:T(8,128)(2,1)} %get-tuple-element.16, bf16[1,768,2048]{2,1,0:T(8,128)(2,1)} %param.12), kind=kOutput, calls=%fused_computation.22 | convolution fusion | flops 805830656 | bytes 4587520 | tf_op jit(solution)/shard_map/dot_general | solution.py:63
  113.1 21.2 %all-to-all-done.3 = bf16[4,64,2048]{2,1,0:T(8,128)(2,1)} async-done(((bf16[4,64,2048]{2,1,0:T(8,128)(2,1)}), bf16[4,64,2048]{2,1,0:T(8,128)(2,1)}, u32[]{:S(2)}, u32[]{:S(2)}) %all-to-all-start.3) | async-done | bytes 1048608 | tf_op jit(solution)/shard_map/all_to_all | solution.py:73
  134.4 4.3 %all-to-all-start.1 = ((bf16[4,64,2048]{2,1,0:T(8,128)(2,1)}), bf16[4,64,2048]{2,1,0:T(8,128)(2,1)}, u32[]{:S(2)}, u32[]{:S(2)}) async-start(bf16[4,64,2048]{2,1,0:T(8,128)(2,1)} %bitcast.66), calls=%async_computation.1 | async-start | bytes 2097152 | tf_op jit(solution)/shard_map/all_to_all | solution.py:65
  138.6 2.1 convert_element_type.64
  140.8 4.7 %gather_fusion.3 = bf16[256,2048]{1,0:T(8,128)(2,1)} fusion(bf16[256,2048]{1,0:T(8,128)(2,1)} %bitcast.14, s32[1024]{0:T(1024)S(1)} %pad_clamp_fusion.1), kind=kCustom, calls=%fused_computation.3 | custom fusion | bytes 2098176 | tf_op jit(solution)/shard_map/gather | solution.py:80
  145.4 2.7 %reshape.114 = bf16[128,2,2048]{2,1,0:T(2,128)(2,1)} reshape(bf16[256,2048]{1,0:T(8,128)(2,1)} %gather_fusion.3) | data formatting | bytes 2097152 | tf_op jit(solution)/shard_map/reshape | solution.py:81
  148.2 4.7 %reduce_sum.45 = bf16[128,2048]{1,0:T(8,128)(2,1)} reduce(bf16[128,2,2048]{2,1,0:T(2,128)(2,1)} %reshape.114, bf16[]{:T(256)} %constant.14.clone.1), dimensions={1}, to_apply=%region_6.7 | reduce | flops 262144 | bytes 1572866 | tf_op jit(solution)/shard_map/reduce_sum | solution.py:86
  152.8 11.1 %all-to-all-done.1 = bf16[4,64,2048]{2,1,0:T(8,128)(2,1)} async-done(((bf16[4,64,2048]{2,1,0:T(8,128)(2,1)}), bf16[4,64,2048]{2,1,0:T(8,128)(2,1)}, u32[]{:S(2)}, u32[]{:S(2)}) %all-to-all-start.1) | async-done | bytes 1048608 | tf_op jit(solution)/shard_map/all_to_all | solution.py:65
  163.9 4.8 %gather_fusion.1 = bf16[256,2048]{1,0:T(8,128)(2,1)} fusion(bf16[256,2048]{1,0:T(8,128)(2,1)} %bitcast.10, s32[1024]{0:T(1024)S(1)} %pad_clamp_fusion.1), kind=kCustom, calls=%fused_computation.1 | custom fusion | bytes 2098176 | tf_op jit(solution)/shard_map/gather | solution.py:75
  168.7 3.4 %reshape.115 = f32[128,2,2048]{2,1,0:T(2,128)} reshape(bf16[256,2048]{1,0:T(8,128)(2,1)} %gather_fusion.1) | data formatting | bytes 3145728 | tf_op jit(solution)/shard_map/convert_element_type | solution.py:77
  172.0 6.3 %multiply_reduce_fusion = (f32[128,2]{1,0:T(8,128)S(1)}, bf16[128,2048]{1,0:T(8,128)(2,1)}) fusion(f32[128,2,2048]{2,1,0:T(2,128)} %reshape.115, f32[128,2048]{1,0:T(8,128)} %convert_element_type.64, f32[128,2]{1,0:T(8,128)S(1)} %copy-done.2), kind=kLoop, calls=%fused_computation.24 | loop fusion | flops 1834752 | bytes 3672064 | tf_op jit(solution)/shard_map/reduce_sum | solution.py:85
  179.0 8.2 %reduce-scatter.6.cloned.1.call-done = bf16[256,768]{1,0:T(8,128)(2,1)} async-done(((bf16[2048,768]{1,0:T(8,128)(2,1)}), bf16[256,768]{1,0:T(8,128)(2,1)}) %reduce-scatter.6.cloned.1.call-update) | async-done | bytes 393232 | tf_op jit(solution)/shard_map/reduce_scatter | solution.py:94
  187.2 50.3 %reduce-scatter.8.cloned.1.call-done = bf16[96,2048]{1,0:T(8,128)(2,1)} async-done(((bf16[768,2048]{1,0:T(8,128)(2,1)}), bf16[96,2048]{1,0:T(8,128)(2,1)}) %reduce-scatter.8.cloned.1.call-update) | async-done | bytes 393232 | tf_op jit(solution)/shard_map/reduce_scatter | solution.py:97
  (42 shorter events, 7.5 us)
Async XLA Ops:
  7.2 76.6 %copy-start = (bf16[1,2048,768]{2,1,0:T(8,128)(2,1)S(1)}, bf16[1,2048,768]{2,1,0:T(8,128)(2,1)}, u32[]{:S(2)}) copy-start(bf16[1,2048,768]{2,1,0:T(8,128)(2,1)} %param.10) | copy-start | bytes 9437188
  14.3 10.8 %copy-start.3 = (f32[128,2]{0,1:T(2,128)S(1)}, f32[128,2]{0,1:T(2,128)}, u32[]{:S(2)}) copy-start(f32[128,2]{0,1:T(2,128)} %param.9) | copy-start | bytes 3076
  18.8 32.1 %all-to-all-start = ((bf16[4,64,2048]{2,1,0:T(8,128)(2,1)}), bf16[4,64,2048]{2,1,0:T(8,128)(2,1)}, u32[]{:S(2)}, u32[]{:S(2)}) async-start(bf16[4,64,2048]{2,1,0:T(8,128)(2,1)} %bitcast.63), calls=%async_computation | async-start | bytes 2097152 | tf_op jit(solution)/shard_map/all_to_all | solution.py:57
  25.2 7.3 %copy-start.1 = (f32[128,2]{1,0:T(8,128)}, f32[128,2]{1,0:T(8,128)S(1)}, u32[]{:S(2)}) copy-start(f32[128,2]{1,0:T(8,128)S(1)} %copy.23) | copy-start | bytes 3076
  50.9 29.5 %all-to-all-start.2 = ((bf16[4,64,2048]{2,1,0:T(8,128)(2,1)}), bf16[4,64,2048]{2,1,0:T(8,128)(2,1)}, u32[]{:S(2)}, u32[]{:S(2)}) async-start(bf16[4,64,2048]{2,1,0:T(8,128)(2,1)} %bitcast.64), calls=%async_computation.2 | async-start | bytes 2097152 | tf_op jit(solution)/shard_map/all_to_all | solution.py:66
  55.2 123.8 %reduce-scatter.4.cloned.1.call-start = ((), (), s32[]{:S(2)}) async-start(), calls=%async_computation.7 | async-start | bytes 3538944 | tf_op jit(solution)/shard_map/reduce_scatter | solution.py:91
  80.5 3.3 %copy-start.4 = (f32[256,768]{1,0:T(8,128)S(1)}, f32[256,768]{1,0:T(8,128)}, u32[]{:S(2)}) copy-start(f32[256,768]{1,0:T(8,128)} %fusion.6) | copy-start | bytes 2359300
  91.1 96.1 %reduce-scatter.6.cloned.1.call-start = ((), (), s32[]{:S(2)}) async-start(), calls=%async_computation.8 | async-start | bytes 3538944 | tf_op jit(solution)/shard_map/reduce_scatter | solution.py:94
  95.4 142.0 %reduce-scatter.8.cloned.1.call-start = ((), (), s32[]{:S(2)}) async-start(), calls=%async_computation.9 | async-start | bytes 3538944 | tf_op jit(solution)/shard_map/reduce_scatter | solution.py:97
  104.9 29.5 %all-to-all-start.3 = ((bf16[4,64,2048]{2,1,0:T(8,128)(2,1)}), bf16[4,64,2048]{2,1,0:T(8,128)(2,1)}, u32[]{:S(2)}, u32[]{:S(2)}) async-start(bf16[4,64,2048]{2,1,0:T(8,128)(2,1)} %bitcast.65), calls=%async_computation.3 | async-start | bytes 2097152 | tf_op jit(solution)/shard_map/all_to_all | solution.py:73
  134.4 29.5 %all-to-all-start.1 = ((bf16[4,64,2048]{2,1,0:T(8,128)(2,1)}), bf16[4,64,2048]{2,1,0:T(8,128)(2,1)}, u32[]{:S(2)}, u32[]{:S(2)}) async-start(bf16[4,64,2048]{2,1,0:T(8,128)(2,1)} %bitcast.66), calls=%async_computation.1 | async-start | bytes 2097152 | tf_op jit(solution)/shard_map/all_to_all | solution.py:65
  168.7 3.4 %copy-start.2 = (f32[128,2]{1,0:T(8,128)S(1)}, f32[128,2]{1,0:T(8,128)}, u32[]{:S(2)}) copy-start(f32[128,2]{1,0:T(8,128)} %copy-done.1) | copy-start | bytes 3076
Sparse Core Ops, SparseCore 0:
  91.2 45.3 reduce-scatter.3
  141.0 46.2 reduce-scatter.5
  191.2 46.2 reduce-scatter.7
where the time goes:
time: 245 us; the launch traced here: 244 us
  waiting for transfers between devices  123 us (50%)
  local copies, waits for them, and re-layouts  38.9 us (16%)
  matrix products  32.1 us (13%)
  starting transfers between devices  19.4 us (8%)
  other arithmetic  16.9 us (7%)
  between operations  13.9 us (6%)
    reduce_scatter x1, waiting for transfers between devices, local(): lax.psum_scatter(part_down.astype(jnp.bfloat16), 'dp', scatter_dimension=...  50.3 us
    all_to_all x1, waiting for transfers between devices, local(): lax.all_to_all(in_rows, 'expert', split_axis=0, concat_axis=0, tiled=True)  21.2 us
    all_to_all x1, waiting for transfers between devices, local(): lax.all_to_all(send_grad, 'expert', split_axis=0, concat_axis=0, tiled=True)  21.2 us
    dot_general x3, matrix products, contract_rows(): lax.dot_general(left, right, (((0,), (0,)), ((), ())), preferred_element_...  12.1 us
    all_to_all x1, waiting for transfers between devices, local(): lax.all_to_all(out_rows, 'expert', split_axis=0, concat_axis=0, tiled=True)  11.1 us
    all_to_all x1, waiting for transfers between devices, local(): lax.all_to_all(send_x, 'expert', split_axis=0, concat_axis=0, tiled=True)  10.9 us
    dot_general x3, matrix products, contract_cols(): lax.dot_general(left, right, (((1,), (1,)), ((), ())), preferred_element_...  8.62 us
    reduce_scatter x1, waiting for transfers between devices, local(): lax.psum_scatter(part_up.astype(jnp.bfloat16), 'dp', scatter_dimension=0,...  8.21 us
  transfers between devices with their start and end apart: 7, of which 6 were waited for; matrix products, arithmetic and copies ran while one was open for 27% of the time, Pallas kernels for 0%

commit v1 on v0

v1 whole, which is shorter than its diff:
```python
import functools
import jax
import jax.numpy as jnp
from jax import lax
from jax.experimental import pallas as pl
from jax.experimental.pallas import tpu as pltpu
from jax.sharding import PartitionSpec as P

CAP = 64
BF = jnp.bfloat16
F32 = jnp.float32
MIB = 1 << 20


def mm(left, right):
    return jnp.dot(left, right, preferred_element_type=F32)


def mm_rows(left, right):
    return lax.dot_general(left, right, (((0,), (0,)), ((), ())), preferred_element_type=F32)


def mm_cols(left, right):
    return lax.dot_general(left, right, (((1,), (1,)), ((), ())), preferred_element_type=F32)


def shape_of(shape, dtype=BF):
    return jax.ShapeDtypeStruct(tuple(shape), dtype)


def whole(shape):
    return pl.BlockSpec(tuple(shape), lambda *_: (0,) * len(shape))


def in_smem():
    return pl.BlockSpec(memory_space=pltpu.SMEM)


def params(limit=48):
    return pltpu.CompilerParams(vmem_limit_bytes=limit * MIB)


def cost(flops, moved):
    return pl.CostEstimate(flops=int(flops), bytes_accessed=int(moved), transcendentals=0)


def chosen(ids, expert):
    first = ids[0:1, :] == expert
    second = ids[1:2, :] == expert
    return first, second


def ranks(ids, experts):
    tok_count = ids.shape[1]
    masks = [jnp.where(jnp.logical_or(*chosen(ids, e)), 1.0, 0.0) for e in experts]
    mask = jnp.concatenate(masks + [jnp.zeros((-len(masks) % 16, tok_count), F32)], axis=0)
    before = lax.broadcasted_iota(jnp.int32, (tok_count, tok_count), 0)
    after = lax.broadcasted_iota(jnp.int32, (tok_count, tok_count), 1)
    upper = jnp.where(before < after, 1.0, 0.0).astype(BF)
    return mm(mask.astype(BF), upper).astype(jnp.int32)


def places(rank_row):
    tok_count = rank_row.shape[1]
    return lax.broadcasted_iota(jnp.int32, (CAP, tok_count), 0) == rank_row


def pick_kernel(n, z_ref, ids_ref, prob_ref, tok_ref, grad_ref, *outs):
    ids = ids_ref[...]
    prob = prob_ref[...]
    experts = [lax.rem(z_ref[0] + k, n) for k in range(n)]
    rank = ranks(ids, experts)
    for k in range(n):
        first, second = chosen(ids, experts[k])
        at = places(rank[k : k + 1, :])
        here = jnp.logical_and(at, jnp.logical_or(first, second))
        pick = jnp.where(here, 1.0, 0.0)
        outs[k][...] = mm(pick.astype(BF), tok_ref[...]).astype(BF)
        weight = jnp.where(first, prob[0:1, :], prob[1:2, :])
        scale = jnp.sum(jnp.where(here, weight, 0.0), axis=1, keepdims=True)
        outs[n + k][...] = (scale * mm(pick.astype(BF), grad_ref[...])).astype(BF)


def pick_rows(n, z, ids_t, prob_t, tokens, out_grad):
    tok_count, width = tokens.shape
    return pl.pallas_call(
        functools.partial(pick_kernel, n),
        out_shape=[shape_of((CAP, width))] * (2 * n),
        in_specs=[in_smem(), whole(ids_t.shape), whole(prob_t.shape)] + [whole(tokens.shape)] * 2,
        out_specs=[whole((CAP, width))] * (2 * n),
        grid=(1,),
        compiler_params=params(),
        cost_estimate=cost(4 * n * CAP * tok_count * width, 4 * tok_count * width * 3),
        name="pick_rows",
    )(z, ids_t, prob_t, tokens, out_grad)


def forward_kernel(n, steps, *refs):
    x_refs = refs[:n]
    wg_ref, wu_ref, wd_ref = refs[n : n + 3]
    slope_ref, act_ref, hid_ref = refs[n + 3 : n + 6]
    out_refs = refs[n + 6 : 2 * n + 6]
    rows, total = refs[2 * n + 6 :]
    step = pl.program_id(0)

    @pl.when(step == 0)
    def _():
        for k in range(n):
            rows[k * CAP : (k + 1) * CAP, :] = x_refs[k][...]

    x = rows[...]
    gate = mm(x, wg_ref[0])
    up = mm(x, wu_ref[0])
    sig = jax.nn.sigmoid(gate)
    act = gate * sig
    act_ref[...] = act
    slope_ref[...] = up * (sig * (1.0 + gate * (1.0 - sig)))
    hidden = (act * up).astype(BF)
    hid_ref[...] = hidden
    part = mm(hidden, wd_ref[0])

    @pl.when(step == 0)
    def _():
        total[...] = part

    @pl.when(step > 0)
    def _():
        total[...] += part

    @pl.when(step == steps - 1)
    def _():
        for k in range(n):
            out_refs[k][...] = total[k * CAP : (k + 1) * CAP, :].astype(BF)


def forward(xs, w_gate, w_up, w_down):
    n = len(xs)
    width, ff = w_gate.shape[1:]
    tile = 256
    steps = ff // tile
    rows = n * CAP
    by_col = pl.BlockSpec((1, width, tile), lambda j: (0, 0, j))
    by_row = pl.BlockSpec((1, tile, width), lambda j: (0, j, 0))
    part = pl.BlockSpec((rows, tile), lambda j: (0, j))
    return pl.pallas_call(
        functools.partial(forward_kernel, n, steps),
        grid=(steps,),
        out_shape=[shape_of((rows, ff), F32)] * 2 + [shape_of((rows, ff))] + [shape_of((CAP, width))] * n,
        in_specs=[whole((CAP, width))] * n + [by_col, by_col, by_row],
        out_specs=[part, part, part] + [whole((CAP, width))] * n,
        scratch_shapes=[pltpu.VMEM((rows, width), BF), pltpu.VMEM((rows, width), F32)],
        compiler_params=params(),
        cost_estimate=cost(6 * rows * width * ff, 6 * width * ff + 4 * rows * width + 10 * rows * ff),
        name="forward",
    )(*xs, w_gate, w_up, w_down)


def down_kernel(n, parts, me_ref, *refs):
    g_refs = refs[:n]
    hid_ref, keep_ref, send_ref, rows, total = refs[n:]
    for k in range(n):
        rows[k * CAP : (k + 1) * CAP, :] = g_refs[k][...]
    total[...] = mm_rows(hid_ref[...], rows[...])
    size = keep_ref.shape[1]
    half = parts // 2
    for rel in range(parts):
        owner = me_ref[rel]
        block = total[pl.ds(pl.multiple_of(owner * size, 16), size), :].astype(BF)
        if rel < half:
            keep_ref[rel] = block
        else:
            send_ref[rel - half] = block


def down_part(parts, owners, gs, hidden):
    n = len(gs)
    rows, width = n * CAP, gs[0].shape[1]
    ff = hidden.shape[1]
    size = ff // parts
    tile = 512
    part = pl.BlockSpec((parts // 2, size, tile), lambda j: (0, 0, j))
    return pl.pallas_call(
        functools.partial(down_kernel, n, parts),
        grid=(width // tile,),
        out_shape=[shape_of((parts // 2, size, width))] * 2,
        in_specs=[in_smem()] + [pl.BlockSpec((CAP, tile), lambda j: (0, j))] * n + [whole((rows, ff))],
        out_specs=[part, part],
        scratch_shapes=[pltpu.VMEM((rows, tile), BF), pltpu.VMEM((ff, tile), F32)],
        compiler_params=params(),
        cost_estimate=cost(2 * rows * width * ff, 2 * width * ff + 2 * rows * (width + ff)),
        name="down_part",
    )(owners, *gs, hidden)


def hidden_grad_kernel(n, *refs):
    g_refs = refs[:n]
    wd_ref, slope_ref, act_ref, dgate_ref, dup_ref, rows = refs[n:]

    @pl.when(pl.program_id(0) == 0)
    def _():
        for k in range(n):
            rows[k * CAP : (k + 1) * CAP, :] = g_refs[k][...]

    grad = mm_cols(rows[...], wd_ref[0])
    dgate_ref[...] = (grad * slope_ref[...]).astype(BF)
    dup_ref[...] = (grad * act_ref[...]).astype(BF)


def hidden_grad(gs, w_down, slope, act):
    n = len(gs)
    ff, width = w_down.shape[1:]
    rows = n * CAP
    tile = 256
    part = pl.BlockSpec((rows, tile), lambda j: (0, j))
    return pl.pallas_call(
        functools.partial(hidden_grad_kernel, n),
        grid=(ff // tile,),
        out_shape=[shape_of((rows, ff))] * 2,
        in_specs=[whole((CAP, width))] * n + [pl.BlockSpec((1, tile, width), lambda j: (0, j, 0)), part, part],
        out_specs=[part, part],
        scratch_shapes=[pltpu.VMEM((rows, width), BF)],
        compiler_params=params(),
        cost_estimate=cost(2 * rows * width * ff, 2 * width * ff + 2 * rows * width + 12 * rows * ff),
        name="hidden_grad",
    )(*gs, w_down, slope, act)


def weight_kernel(n, parts, me_ref, *refs):
    x_refs = refs[:n]
    d_ref, keep_ref, send_ref, rows = refs[n:]
    half = parts // 2
    size = keep_ref.shape[1]

    @pl.when(pl.program_id(0) == 0)
    def _():
        for k in range(n):
            rows[k * CAP : (k + 1) * CAP, :] = x_refs[k][...]

    d = d_ref[...]
    for rel in range(parts):
        at = pl.multiple_of(me_ref[rel] * size, size)
        block = mm_rows(rows[:, pl.ds(at, size)], d).astype(BF)
        if rel < half:
            keep_ref[rel] = block
        else:
            send_ref[rel - half] = block


def weight_part(parts, owners, xs, d):
    n = len(xs)
    rows, width = n * CAP, xs[0].shape[1]
    ff = d.shape[1]
    size = width // parts
    tile = 256
    part = pl.BlockSpec((parts // 2, size, tile), lambda j: (0, 0, j))
    return pl.pallas_call(
        functools.partial(weight_kernel, n, parts),
        grid=(ff // tile,),
        out_shape=[shape_of((parts // 2, size, ff))] * 2,
        in_specs=[in_smem()] + [whole((CAP, width))] * n + [pl.BlockSpec((rows, tile), lambda j: (0, j))],
        out_specs=[part, part],
        scratch_shapes=[pltpu.VMEM((rows, width), BF)],
        compiler_params=params(),
        cost_estimate=cost(2 * rows * width * ff, 2 * width * ff + 2 * rows * (width + ff)),
        name="weight_part",
    )(owners, *xs, d)


def input_grad_kernel(n, dgate_ref, dup_ref, wg_ref, wu_ref, *out_refs):
    total = mm_cols(dgate_ref[...], wg_ref[0]) + mm_cols(dup_ref[...], wu_ref[0])
    for k in range(n):
        out_refs[k][...] = total[k * CAP : (k + 1) * CAP, :].astype(BF)


def input_grad(n, dgate, dup, w_gate, w_up):
    rows, ff = dgate.shape
    width = w_gate.shape[1]
    tile = 512
    by_row = pl.BlockSpec((1, tile, ff), lambda j: (0, j, 0))
    return pl.pallas_call(
        functools.partial(input_grad_kernel, n),
        grid=(width // tile,),
        out_shape=[shape_of((CAP, width))] * n,
        in_specs=[whole((rows, ff))] * 2 + [by_row, by_row],
        out_specs=[pl.BlockSpec((CAP, tile), lambda j: (0, j))] * n,
        compiler_params=params(),
        cost_estimate=cost(4 * rows * width * ff, 4 * width * ff + 2 * rows * (width + 2 * ff)),
        name="input_grad",
    )(dgate, dup, w_gate, w_up)


def fold_kernel(keep_ref, recv_ref, a_send, a_keep, b_send, b_keep):
    half = a_send.shape[1]
    total = [keep_ref[i].astype(F32) + recv_ref[i].astype(F32) for i in range(4)]
    for i in range(2):
        a_keep[i] = total[2 * i][:half].astype(BF)
        a_send[i] = total[2 * i + 1][:half].astype(BF)
        b_keep[i] = total[i][half:].astype(BF)
        b_send[i] = total[2 + i][half:].astype(BF)


def fold(keep, recv):
    _, size, width = keep.shape
    tile = 256 if width < 1024 else 512
    full = pl.BlockSpec((4, size, tile), lambda j: (0, 0, j))
    half = pl.BlockSpec((2, size // 2, tile), lambda j: (0, 0, j))
    return pl.pallas_call(
        fold_kernel,
        grid=(width // tile,),
        out_shape=[shape_of((2, size // 2, width))] * 4,
        in_specs=[full, full],
        out_specs=[half] * 4,
        compiler_params=params(),
        cost_estimate=cost(4 * size * width, 24 * size * width),
        name="fold",
    )(keep, recv)


def fold_two_kernel(a_keep, a_recv, b_keep, b_recv, a_next, a_mine, b_next, b_mine):
    for keep, recv, away, mine in ((a_keep, a_recv, a_next, a_mine), (b_keep, b_recv, b_next, b_mine)):
        mine[...] = (keep[0].astype(F32) + recv[0].astype(F32)).astype(BF)
        away[...] = (keep[1].astype(F32) + recv[1].astype(F32)).astype(BF)


def fold_two(a_keep, a_recv, b_keep, b_recv):
    _, half, width = a_keep.shape
    return pl.pallas_call(
        fold_two_kernel,
        grid=(1,),
        out_shape=[shape_of((half, width))] * 4,
        in_specs=[whole((2, half, width))] * 4,
        out_specs=[whole((half, width))] * 4,
        compiler_params=params(),
        cost_estimate=cost(4 * half * width, 24 * half * width),
        name="fold_two",
    )(a_keep, a_recv, b_keep, b_recv)


def fold_last_kernel(a_mine, a_recv, b_mine, b_recv, out_ref):
    half = a_mine.shape[0]
    out_ref[0, :half] = (a_mine[...].astype(F32) + a_recv[...].astype(F32)).astype(BF)
    out_ref[0, half:] = (b_mine[...].astype(F32) + b_recv[...].astype(F32)).astype(BF)


def fold_last(a_mine, a_recv, b_mine, b_recv):
    half, width = a_mine.shape
    return pl.pallas_call(
        fold_last_kernel,
        grid=(1,),
        out_shape=shape_of((1, 2 * half, width)),
        in_specs=[whole((half, width))] * 4,
        out_specs=whole((1, 2 * half, width)),
        compiler_params=params(),
        cost_estimate=cost(2 * half * width, 12 * half * width),
        name="fold_last",
    )(a_mine, a_recv, b_mine, b_recv)


def swap(value, bit, count=8):
    return lax.ppermute(value, "dp", [(i, i ^ bit) for i in range(count)])


def sum_over_dp(keep, send):
    a_send, a_keep, b_send, b_keep = fold(keep, swap(send, 1))
    a_recv, b_recv = swap(a_send, 2), swap(b_send, 4)
    a_next, a_mine, b_next, b_mine = fold_two(a_keep, a_recv, b_keep, b_recv)
    return fold_last(a_mine, swap(a_next, 4), b_mine, swap(b_next, 2))


def combine_out_kernel(n, z_ref, ids_ref, prob_ref, grad_ref, *refs):
    back_refs = refs[:n]
    out_ref, prob_grad_ref, rows, sums = refs[n:]
    ids = ids_ref[...]
    experts = [lax.rem(z_ref[0] + k, n) for k in range(n)]
    rank = ranks(ids, experts)
    firsts, seconds = [], []
    for k in range(n):
        rows[k * CAP : (k + 1) * CAP, :] = back_refs[k][...]
        first, second = chosen(ids, experts[k])
        at = places(rank[k : k + 1, :])
        firsts.append(jnp.where(jnp.logical_and(at, first), 1.0, 0.0))
        seconds.append(jnp.where(jnp.logical_and(at, second), 1.0, 0.0))
    tok_count = ids.shape[1]
    prob = jnp.concatenate([prob_ref[...], jnp.zeros((6, tok_count), F32)], axis=0).T
    grad = grad_ref[...].astype(F32)
    total = 0.0
    part = []
    for choice, at in enumerate((firsts, seconds)):
        out = mm_rows(jnp.concatenate(at, axis=0).astype(BF), rows[...])
        total = total + prob[:, choice : choice + 1] * out
        part.append(jnp.sum(grad * out, axis=1, keepdims=True))
    out_ref[...] = total.astype(BF)
    step = pl.program_id(0)
    both = jnp.concatenate(part + [jnp.zeros((tok_count, 6), F32)], axis=1)

    @pl.when(step == 0)
    def _():
        sums[...] = both

    @pl.when(step > 0)
    def _():
        sums[...] += both

    @pl.when(step == pl.num_programs(0) - 1)
    def _():
        prob_grad_ref[...] = sums[...].T[0:2, :]


def combine_out(z, ids_t, prob_t, out_grad, backs):
    n = len(backs)
    tok_count, width = out_grad.shape
    tile = 512
    by_tile = pl.BlockSpec((tok_count, tile), lambda j: (0, j))
    return pl.pallas_call(
        functools.partial(combine_out_kernel, n),
        grid=(width // tile,),
        out_shape=[shape_of((tok_count, width)), shape_of((2, tok_count), F32)],
        in_specs=[in_smem(), whole(ids_t.shape), whole(prob_t.shape), by_tile]
        + [pl.BlockSpec((CAP, tile), lambda j: (0, j))] * n,
        out_specs=[by_tile, whole((2, tok_count))],
        scratch_shapes=[pltpu.VMEM((n * CAP, tile), BF), pltpu.VMEM((tok_count, 8), F32)],
        compiler_params=params(),
        cost_estimate=cost(4 * n * CAP * tok_count * width, 2 * width * (n * CAP + 2 * tok_count)),
        name="combine_out",
    )(z, ids_t, prob_t, out_grad, *backs)


def combine_in_kernel(n, z_ref, ids_ref, *refs):
    back_refs = refs[:n]
    out_ref, rows = refs[n:]
    ids = ids_ref[...]
    experts = [lax.rem(z_ref[0] + k, n) for k in range(n)]
    rank = ranks(ids, experts)
    picks = []
    for k in range(n):
        rows[k * CAP : (k + 1) * CAP, :] = back_refs[k][...]
        here = jnp.logical_and(places(rank[k : k + 1, :]), jnp.logical_or(*chosen(ids, experts[k])))
        picks.append(jnp.where(here, 1.0, 0.0))
    out_ref[...] = mm_rows(jnp.concatenate(picks, axis=0).astype(BF), rows[...]).astype(BF)


def combine_in(z, ids_t, backs):
    n = len(backs)
    width = backs[0].shape[1]
    tok_count = ids_t.shape[1]
    tile = 1024
    return pl.pallas_call(
        functools.partial(combine_in_kernel, n),
        grid=(width // tile,),
        out_shape=shape_of((tok_count, width)),
        in_specs=[in_smem(), whole(ids_t.shape)] + [pl.BlockSpec((CAP, tile), lambda j: (0, j))] * n,
        out_specs=pl.BlockSpec((tok_count, tile), lambda j: (0, j)),
        scratch_shapes=[pltpu.VMEM((n * CAP, tile), BF)],
        compiler_params=params(),
        cost_estimate=cost(2 * n * CAP * tok_count * width, 2 * width * (n * CAP + tok_count)),
        name="combine_in",
    )(z, ids_t, *backs)


def shift(values, sign):
    n = len(values)
    order = sorted(range(1, n), key=lambda k: -min(k, n - k))
    moved = list(values)
    for k in order:
        moved[k] = lax.ppermute(values[k], "expert", [(i, (i + sign * k) % n) for i in range(n)])
    return moved


def local(tokens, expert_ids, gate_probs, w_gate, w_up, w_down, out_grad):
    n = lax.axis_size("expert")
    parts = lax.axis_size("dp")
    z = lax.axis_index("expert").astype(jnp.int32).reshape(1)
    ids_t, prob_t = expert_ids.T, gate_probs.T
    sent = pick_rows(n, z, ids_t, prob_t, tokens, out_grad)
    xs = shift(sent[:n], 1)
    gs = shift(sent[n:], 1)
    made = forward(xs, w_gate, w_up, w_down)
    slope, act, hidden = made[:3]
    back_out = shift(made[3:], -1)
    dgate, dup = hidden_grad(gs, w_down, slope, act)
    if parts == 8:
        me = lax.axis_index("dp").astype(jnp.int32)
        flips = [(r >> 2 & 1) | (r & 1) << 1 | (r >> 1 & 1) << 2 for r in range(8)]
        owners = jnp.stack([me ^ f for f in flips])
        sum_down = sum_over_dp(*down_part(parts, owners, gs, hidden))
        sum_gate = sum_over_dp(*weight_part(parts, owners, xs, dgate))
        sum_up = sum_over_dp(*weight_part(parts, owners, xs, dup))
    else:
        x_rows, d_rows = jnp.concatenate(xs, 0), jnp.concatenate(gs, 0)
        sum_gate, sum_up, sum_down = (
            lax.psum_scatter(mm_rows(a, b).astype(BF), "dp", scatter_dimension=0, tiled=True)[None]
            for a, b in ((x_rows, dgate), (x_rows, dup), (hidden, d_rows))
        )
    back_in = shift(input_grad(n, dgate, dup, w_gate, w_up), -1)
    layer_out, prob_grad_t = combine_out(z, ids_t, prob_t, out_grad, back_out)
    token_grad = combine_in(z, ids_t, back_in)
    return layer_out, prob_grad_t.T, token_grad, sum_gate, sum_up, sum_down


def solution(mesh):
    rows = P(("dp", "expert"), None)
    weights = P("expert", None, None)
    summed = P("expert", "dp", None)
    return jax.shard_map(
        local,
        mesh=mesh,
        in_specs=(rows, rows, rows, weights, weights, weights, rows),
        out_specs=(rows, rows, rows, summed, summed, summed),
        check_vma=False,
    )
```

time: 245 us -> 141 us (0.58)
  waiting for transfers between devices: 123 us -> 62.4 us
  Pallas kernels: 0 us -> 37.2 us
  local copies, waits for them, and re-layouts: 38.9 us -> 4.25 us
  matrix products: 32.1 us -> 0 us
  other arithmetic: 16.9 us -> 0 us
  starting transfers between devices: 19.4 us -> 35.8 us
  between operations: 13.9 us -> 0.8 us
    all_to_all x4 -> x0, waiting for transfers between devices: 64.3 us -> none  [the longest x1 21.2 us: local(): lax.all_to_all(in_rows, 'expert', split_axis=0, concat_axis=0, tiled=True)]
    ppermute x0 -> x27, waiting for transfers between devices: none -> 62.4 us  [the longest x12 61.3 us: shift(): lax.ppermute(values[k], 'expert', [(i, (i + sign * k) % n) for i in range...]
    reduce_scatter x3 -> x0, waiting for transfers between devices: 58.5 us -> none  [the longest x1 50.3 us: local(): lax.psum_scatter(part_down.astype(jnp.bfloat16), 'dp', scatter_dimension=...]
    pallas_call x0 -> x18, Pallas kernels: none -> 37.2 us  [the longest x1 7.41 us: forward(): pl.pallas_call(functools.partial(forward_kernel, n, steps), grid=(steps,)...]
    ppermute x0 -> x27, starting transfers between devices: none -> 35.8 us  [the longest x12 22.7 us: shift(): lax.ppermute(values[k], 'expert', [(i, (i + sign * k) % n) for i in range...]
    dot_general x9 -> x0, matrix products: 32.1 us -> none  [the longest x3 12.1 us: contract_rows(): lax.dot_general(left, right, (((0,), (0,)), ((), ())), preferred_element_...]
    all_to_all x4 -> x0, starting transfers between devices: 19.1 us -> none  [the longest x1 6.32 us: local(): lax.all_to_all(send_x, 'expert', split_axis=0, concat_axis=0, tiled=True)]
    gather x4 -> x0, local copies, waits for them, and re-layouts: 18.7 us -> none  [the longest x1 4.77 us: local(): back_out.reshape(peer_count * CAP, model_width)[slot_index]]
  transfers between devices with their start and end apart: 7 -> 27, of which waited for: 6 -> 10; matrix products, arithmetic and copies ran while one was open for 27% -> 0% of each run, Pallas kernels for 0% -> 22%
where the time goes in v1:
time: 141 us; the launch traced here: 140 us
  waiting for transfers between devices  62.4 us (44%)
  Pallas kernels  37.2 us (26%)
  starting transfers between devices  35.8 us (25%)
  local copies, waits for them, and re-layouts  4.25 us (3%)
    ppermute x12, waiting for transfers between devices, shift(): lax.ppermute(values[k], 'expert', [(i, (i + sign * k) % n) for i in range...  61.3 us
    ppermute x12, starting transfers between devices, shift(): lax.ppermute(values[k], 'expert', [(i, (i + sign * k) % n) for i in range...  22.7 us
    ppermute x15, starting transfers between devices, swap(): return lax.ppermute(value, 'dp', [(i, i ^ bit) for i in range(count)])  13.1 us
    pallas_call x1, Pallas kernels, forward(): pl.pallas_call(functools.partial(forward_kernel, n, steps), grid=(steps,)...  7.41 us
    pallas_call x2, Pallas kernels, weight_part(): pl.pallas_call(functools.partial(weight_kernel, n, parts), grid=(ff // ti...  6.93 us
    pallas_call x1, Pallas kernels, input_grad(): pl.pallas_call(functools.partial(input_grad_kernel, n), grid=(width // ti...  4.22 us
    unnamed x20, local copies, waits for them, and re-layouts  4.16 us
    pallas_call x1, Pallas kernels, down_part(): pl.pallas_call(functools.partial(down_kernel, n, parts), grid=(width // t...  3.71 us
  transfers between devices with their start and end apart: 27, of which 10 were waited for; matrix products, arithmetic and copies ran while one was open for 0% of the time, Pallas kernels for 22%

profile of v1, /device:TPU:0, one launch (start us, length us, event | category | flops | bytes accessed | tf_op | source)
XLA Modules:
  0.0 140.4 jit_solution(18057366563074718420)
XLA Ops:
  0.6 1.0 copy-done.1
  1.7 1.0 copy-done.3
  4.1 1.3 pick_rows.1
  5.4 3.0 %collective-permute-start = (bf16[64,2048]{1,0:T(8,128)(2,1)S(1)}, bf16[64,2048]{1,0:T(8,128)(2,1)S(1)}, u32[]{:S(2)}, u32[]{:S(2)}) collective-permute-start(bf16[64,2048]{1,0:T(8,128)(2,1)S(1)} %get-tuple-element.60), channel_id=1, source_target_pairs={{0,1},{1,2},{2,3},{3,0},{4,5},{5,6},{6,7},{7,4},{8,9},{9,10},{10,1... | collective-permute-start | bytes 786440 | tf_op jit(solution)/shard_map/ppermute | solution.py:465
  8.4 2.6 %collective-permute-start.1 = (bf16[64,2048]{1,0:T(8,128)(2,1)}, bf16[64,2048]{1,0:T(8,128)(2,1)S(1)}, u32[]{:S(2)}, u32[]{:S(2)}) collective-permute-start(bf16[64,2048]{1,0:T(8,128)(2,1)} %get-tuple-element.61), channel_id=1, source_target_pairs={{0,2},{1,3},{2,0},{3,1},{4,6},{5,7},{6,4},{7,5},{8,10},{9,11},{10,... | collective-permute-start | bytes 786440 | tf_op jit(solution)/shard_map/ppermute | solution.py:465
  11.0 1.4 collective-permute-start.2
  13.4 4.3 %collective-permute-done.refs_1_ = bf16[64,2048]{1,0:T(8,128)(2,1)S(1)} collective-permute-done((bf16[64,2048]{1,0:T(8,128)(2,1)S(1)}, bf16[64,2048]{1,0:T(8,128)(2,1)S(1)}, u32[]{:S(2)}, u32[]{:S(2)}) %collective-permute-start) | collective-permute-done | bytes 262176 | tf_op jit(solution)/shard_map/ppermute | solution.py:465
  17.7 2.5 %collective-permute-start.8 = (bf16[64,2048]{1,0:T(8,128)(2,1)S(1)}, bf16[64,2048]{1,0:T(8,128)(2,1)S(1)}, u32[]{:S(2)}, u32[]{:S(2)}) collective-permute-start(bf16[64,2048]{1,0:T(8,128)(2,1)S(1)} %get-tuple-element.72), channel_id=1, source_target_pairs={{0,3},{1,0},{2,1},{3,2},{4,7},{5,4},{6,5},{7,6},{8,11},{9,8},{10,9... | collective-permute-start | bytes 786440 | tf_op jit(solution)/shard_map/ppermute | solution.py:465
  20.3 8.7 %collective-permute-done.1.refs_2_ = bf16[64,2048]{1,0:T(8,128)(2,1)S(1)} collective-permute-done((bf16[64,2048]{1,0:T(8,128)(2,1)}, bf16[64,2048]{1,0:T(8,128)(2,1)S(1)}, u32[]{:S(2)}, u32[]{:S(2)}) %collective-permute-start.1) | collective-permute-done | bytes 262176 | tf_op jit(solution)/shard_map/ppermute | solution.py:465
  29.0 7.4 %forward.1 = (f32[256,768]{1,0:T(8,128)S(1)}, f32[256,768]{1,0:T(8,128)S(1)}, bf16[256,768]{1,0:T(8,128)(2,1)S(1)}, bf16[64,2048]{1,0:T(8,128)(2,1)S(1)}, bf16[6...) custom-call(bf16[64,2048]{1,0:T(8,128)(2,1)S(1)} %get-tuple-element.59.refs_0_, ...), custom_call_target="tpu_custom_call" | custom-call | flops 2415919104 | bytes 13500416 | tf_op jit(solution)/shard_map/forward/pallas_call | solution.py:145
  37.1 13.5 %collective-permute-done.7.refs_2_ = bf16[64,2048]{1,0:T(8,128)(2,1)S(1)} collective-permute-done((bf16[64,2048]{1,0:T(8,128)(2,1)S(1)}, bf16[64,2048]{1,0:T(8,128)(2,1)S(1)}, u32[]{:S(2)}, u32[]{:S(2)}) %collective-permute-start.7) | collective-permute-done | bytes 262176 | tf_op jit(solution)/shard_map/ppermute | solution.py:465
  50.7 3.7 %down_part.1 = (bf16[4,96,2048]{2,1,0:T(8,128)(2,1)S(1)}, bf16[4,96,2048]{2,1,0:T(8,128)(2,1)}) custom-call(s32[8]{0:T(128)S(1)} %stack.35.me_ref, bf16[64,2048]{1,0:T(8,128)(2,1)S(1)} %get-tuple-element.69.refs_0_, bf16[64,2048]{1,0:T(8,128)(2,1)S(1)} %collective-permute-done.6.refs_1_, bf16[64,2048]{1,0:T(8,128)(2,1)S(1)} %collective-permute-done.7.refs_2_, ...), custom_call_target="tpu_custom_call" | custom-call | flops 805306368 | bytes 4587520 | tf_op jit(solution)/shard_map/down_part/pallas_call | solution.py:182
  54.4 3.5 %hidden_grad.1 = (bf16[256,768]{1,0:T(8,128)(2,1)S(1)}, bf16[256,768]{1,0:T(8,128)(2,1)S(1)}) custom-call(bf16[64,2048]{1,0:T(8,128)(2,1)S(1)} %get-tuple-element.69.refs_0_, bf16[64,2048]{1,0:T(8,128)(2,1)S(1)} %collective-permute-done.6.refs_1_, bf16[64,2048]{1,0:T(8,128)(2,1)S(1)} %collective-permute-done.7.refs_2_, ...), custom_call_target="tpu_custom_call" | custom-call | flops 805306368 | bytes 6553600 | tf_op jit(solution)/shard_map/hidden_grad/pallas_call | solution.py:215
  57.9 3.5 %weight_part.3 = (bf16[4,256,768]{2,1,0:T(8,128)(2,1)S(1)}, bf16[4,256,768]{2,1,0:T(8,128)(2,1)}) custom-call(s32[8]{0:T(128)S(1)} %stack.35.me_ref, bf16[64,2048]{1,0:T(8,128)(2,1)S(1)} %get-tuple-element.59.refs_0_, bf16[64,2048]{1,0:T(8,128)(2,1)S(1)} %collective-permute-done.refs_1_, bf16[64,2048]{1,0:T(8,128)(2,1)S(1)} %collective-permute-done.1.refs_2_, ...), custom_call_target="tpu_custom_call" | custom-call | flops 805306368 | bytes 4587520 | tf_op jit(solution)/shard_map/weight_part/pallas_call | solution.py:256
  61.9 3.4 %weight_part.2 = (bf16[4,256,768]{2,1,0:T(8,128)(2,1)S(1)}, bf16[4,256,768]{2,1,0:T(8,128)(2,1)}) custom-call(s32[8]{0:T(128)S(1)} %stack.35.me_ref, bf16[64,2048]{1,0:T(8,128)(2,1)S(1)} %get-tuple-element.59.refs_0_, bf16[64,2048]{1,0:T(8,128)(2,1)S(1)} %collective-permute-done.refs_1_, bf16[64,2048]{1,0:T(8,128)(2,1)S(1)} %collective-permute-done.1.refs_2_, ...), custom_call_target="tpu_custom_call" | custom-call | flops 805306368 | bytes 4587520 | tf_op jit(solution)/shard_map/weight_part/pallas_call | solution.py:256
  66.1 1.6 %collective-permute-start.23 = (bf16[2,48,2048]{2,1,0:T(8,128)(2,1)S(1)}, bf16[2,48,2048]{2,1,0:T(8,128)(2,1)S(1)}, u32[]{:S(2)}, u32[]{:S(2)}) collective-permute-start(bf16[2,48,2048]{2,1,0:T(8,128)(2,1)S(1)} %get-tuple-element.105), channel_id=1, source_target_pairs={{0,8},{4,12},{8,0},{12,4},{16,24},{20,28},{24,16},{28,20},{1,9},{5... | collective-permute-start | bytes 1179656 | tf_op jit(solution)/shard_map/ppermute | solution.py:360
  67.7 7.1 %collective-permute-start.3 = (bf16[64,2048]{1,0:T(8,128)(2,1)}, bf16[64,2048]{1,0:T(8,128)(2,1)S(1)}, u32[]{:S(2)}, u32[]{:S(2)}) collective-permute-start(bf16[64,2048]{1,0:T(8,128)(2,1)} %get-tuple-element.64), channel_id=1, source_target_pairs={{0,3},{1,0},{2,1},{3,2},{4,7},{5,4},{6,5},{7,6},{8,11},{9,8},{10,9... | collective-permute-start | bytes 786440 | tf_op jit(solution)/shard_map/ppermute | solution.py:465
  75.2 1.5 %collective-permute-start.24 = (bf16[2,48,2048]{2,1,0:T(8,128)(2,1)S(1)}, bf16[2,48,2048]{2,1,0:T(8,128)(2,1)S(1)}, u32[]{:S(2)}, u32[]{:S(2)}) collective-permute-start(bf16[2,48,2048]{2,1,0:T(8,128)(2,1)S(1)} %get-tuple-element.107), channel_id=1, source_target_pairs={{0,16},{4,20},{8,24},{12,28},{16,0},{20,4},{24,8},{28,12},{1,17},{... | collective-permute-start | bytes 1179656 | tf_op jit(solution)/shard_map/ppermute | solution.py:360
  78.9 3.0 %collective-permute-done.3.refs_1_ = bf16[64,2048]{1,0:T(8,128)(2,1)S(1)} collective-permute-done((bf16[64,2048]{1,0:T(8,128)(2,1)}, bf16[64,2048]{1,0:T(8,128)(2,1)S(1)}, u32[]{:S(2)}, u32[]{:S(2)}) %collective-permute-start.3) | collective-permute-done | bytes 262176 | tf_op jit(solution)/shard_map/ppermute | solution.py:465
  81.8 1.5 %collective-permute-start.19 = (bf16[2,128,768]{2,1,0:T(8,128)(2,1)S(1)}, bf16[2,128,768]{2,1,0:T(8,128)(2,1)S(1)}, u32[]{:S(2)}, u32[]{:S(2)}) collective-permute-start(bf16[2,128,768]{2,1,0:T(8,128)(2,1)S(1)} %get-tuple-element.96), channel_id=1, source_target_pairs={{0,16},{4,20},{8,24},{12,28},{16,0},{20,4},{24,8},{28,12},{1,17},{... | collective-permute-start | bytes 1179656 | tf_op jit(solution)/shard_map/ppermute | solution.py:360
  83.3 9.7 %collective-permute-done.4.refs_2_ = bf16[64,2048]{1,0:T(8,128)(2,1)S(1)} collective-permute-done((bf16[64,2048]{1,0:T(8,128)(2,1)S(1)}, bf16[64,2048]{1,0:T(8,128)(2,1)S(1)}, u32[]{:S(2)}, u32[]{:S(2)}) %collective-permute-start.4) | collective-permute-done | bytes 262176 | tf_op jit(solution)/shard_map/ppermute | solution.py:465
  93.6 1.5 %collective-permute-start.14 = (bf16[2,128,768]{2,1,0:T(8,128)(2,1)S(1)}, bf16[2,128,768]{2,1,0:T(8,128)(2,1)S(1)}, u32[]{:S(2)}, u32[]{:S(2)}) collective-permute-start(bf16[2,128,768]{2,1,0:T(8,128)(2,1)S(1)} %get-tuple-element.86), channel_id=1, source_target_pairs={{0,16},{4,20},{8,24},{12,28},{16,0},{20,4},{24,8},{28,12},{1,17},{... | collective-permute-start | bytes 1179656 | tf_op jit(solution)/shard_map/ppermute | solution.py:360
  95.1 4.2 %input_grad.1 = (bf16[64,2048]{1,0:T(8,128)(2,1)S(1)}, bf16[64,2048]{1,0:T(8,128)(2,1)S(1)}, bf16[64,2048]{1,0:T(8,128)(2,1)S(1)}, bf16[64,2048]{1,0:T(8,128)(2,1)S(1)}) custom-call(bf16[256,768]{1,0:T(8,128)(2,1)S(1)} %get-tuple-element.75.dgate_ref.refs_4_, bf16[256,768]{1,0:T(8,128)(2,1)S(1)} %get-tuple-element.76.dup_ref.refs_4_, ...), custom_call_target="tpu_custom_call" | custom-call | flops 1610612736 | bytes 8126464 | tf_op jit(solution)/shard_map/input_grad/pallas_call | solution.py:280
  99.5 3.8 %collective-permute-start.9 = (bf16[64,2048]{1,0:T(8,128)(2,1)S(1)}, bf16[64,2048]{1,0:T(8,128)(2,1)S(1)}, u32[]{:S(2)}, u32[]{:S(2)}) collective-permute-start(bf16[64,2048]{1,0:T(8,128)(2,1)S(1)} %get-tuple-element.78), channel_id=1, source_target_pairs={{0,3},{1,0},{2,1},{3,2},{4,7},{5,4},{6,5},{7,6},{8,11},{9,8},{10,9... | collective-permute-start | bytes 786440 | tf_op jit(solution)/shard_map/ppermute | solution.py:465
  105.7 5.0 %collective-permute-done.5.refs_3_ = bf16[64,2048]{1,0:T(8,128)(2,1)S(1)} collective-permute-done((bf16[64,2048]{1,0:T(8,128)(2,1)}, bf16[64,2048]{1,0:T(8,128)(2,1)S(1)}, u32[]{:S(2)}, u32[]{:S(2)}) %collective-permute-start.5) | collective-permute-done | bytes 262176 | tf_op jit(solution)/shard_map/ppermute | solution.py:465
  110.7 1.5 %collective-permute-start.26 = (bf16[48,2048]{1,0:T(8,128)(2,1)S(1)}, bf16[48,2048]{1,0:T(8,128)(2,1)S(1)}, u32[]{:S(2)}, u32[]{:S(2)}) collective-permute-start(bf16[48,2048]{1,0:T(8,128)(2,1)S(1)} %get-tuple-element.111), channel_id=1, source_target_pairs={{0,8},{4,12},{8,0},{12,4},{16,24},{20,28},{24,16},{28,20},{1,9},{5... | collective-permute-start | bytes 589832 | tf_op jit(solution)/shard_map/ppermute | solution.py:360
  113.0 16.8 %collective-permute-done.10.refs_2_ = bf16[64,2048]{1,0:T(8,128)(2,1)S(1)} collective-permute-done((bf16[64,2048]{1,0:T(8,128)(2,1)S(1)}, bf16[64,2048]{1,0:T(8,128)(2,1)S(1)}, u32[]{:S(2)}, u32[]{:S(2)}) %collective-permute-start.10) | collective-permute-done | bytes 262176 | tf_op jit(solution)/shard_map/ppermute | solution.py:465
  129.8 1.5 %collective-permute-start.21 = (bf16[128,768]{1,0:T(8,128)(2,1)S(1)}, bf16[128,768]{1,0:T(8,128)(2,1)S(1)}, u32[]{:S(2)}, u32[]{:S(2)}) collective-permute-start(bf16[128,768]{1,0:T(8,128)(2,1)S(1)} %get-tuple-element.100), channel_id=1, source_target_pairs={{0,8},{4,12},{8,0},{12,4},{16,24},{20,28},{24,16},{28,20},{1,9},{5... | collective-permute-start | bytes 589832 | tf_op jit(solution)/shard_map/ppermute | solution.py:360
  132.3 1.6 %combine_in.1 = bf16[128,2048]{1,0:T(8,128)(2,1)} custom-call(s32[1]{0:T(128)} %bitcast.z_ref, s32[2,128]{1,0:T(2,128)S(1)} %bitcast.13, bf16[64,2048]{1,0:T(8,128)(2,1)S(1)} %get-tuple-element.77.refs_0_, bf16[64,2048]{1,0:T(8,128)(2,1)S(1)} %collective-permute-done.9.refs_1_, bf16[64,2048]{1,0:T(8,128)(2,1)S(1)} %collective-permute-done.10.refs_2_, ...), custom_call_target="tpu_custom_call" | custom-call | flops 134217728 | bytes 1572864 | tf_op jit(solution)/shard_map/combine_in/pallas_call | solution.py:447
  134.0 3.1 %combine_out.1 = (bf16[128,2048]{1,0:T(8,128)(2,1)}, f32[2,128]{1,0:T(2,128)}) custom-call(s32[1]{0:T(128)} %bitcast.z_ref, s32[2,128]{1,0:T(2,128)S(1)} %bitcast.14, f32[2,128]{1,0:T(2,128)S(1)} %bitcast.16, bf16[128,2048]{1,0:T(8,128)(2,1)S(1)} %copy-done.2, bf16[64,2048]{1,0:T(8,128)(2,1)S(1)} %copy-done.5, ...), custom_call_target="tpu_custom_call" | custom-call | flops 268435456 | bytes 2097152 | tf_op jit(solution)/shard_map/combine_out/pallas_call | solution.py:414
  137.1 0.8 fold_last.5
  139.6 0.8 fold_last.3
  (61 shorter events, 13.5 us)
Async XLA Ops:
  5.4 12.3 %collective-permute-start = (bf16[64,2048]{1,0:T(8,128)(2,1)S(1)}, bf16[64,2048]{1,0:T(8,128)(2,1)S(1)}, u32[]{:S(2)}, u32[]{:S(2)}) collective-permute-start(bf16[64,2048]{1,0:T(8,128)(2,1)S(1)} %get-tuple-element.60), channel_id=1, source_target_pairs={{0,1},{1,2},{2,3},{3,0},{4,5},{5,6},{6,7},{7,4},{8,9},{9,10},{10,1... | collective-permute-start | bytes 786440 | tf_op jit(solution)/shard_map/ppermute | solution.py:465
  8.4 20.6 %collective-permute-start.1 = (bf16[64,2048]{1,0:T(8,128)(2,1)}, bf16[64,2048]{1,0:T(8,128)(2,1)S(1)}, u32[]{:S(2)}, u32[]{:S(2)}) collective-permute-start(bf16[64,2048]{1,0:T(8,128)(2,1)} %get-tuple-element.61), channel_id=1, source_target_pairs={{0,2},{1,3},{2,0},{3,1},{4,6},{5,7},{6,4},{7,5},{8,10},{9,11},{10,... | collective-permute-start | bytes 786440 | tf_op jit(solution)/shard_map/ppermute | solution.py:465
  11.0 18.0 %collective-permute-start.2 = (bf16[64,2048]{1,0:T(8,128)(2,1)S(1)}, bf16[64,2048]{1,0:T(8,128)(2,1)S(1)}, u32[]{:S(2)}, u32[]{:S(2)}) collective-permute-start(bf16[64,2048]{1,0:T(8,128)(2,1)S(1)} %get-tuple-element.62), channel_id=1, source_target_pairs={{0,3},{1,0},{2,1},{3,2},{4,7},{5,4},{6,5},{7,6},{8,11},{9,8},{10,9... | collective-permute-start | bytes 786440 | tf_op jit(solution)/shard_map/ppermute | solution.py:465
  12.4 24.8 %collective-permute-start.6 = (bf16[64,2048]{1,0:T(8,128)(2,1)S(1)}, bf16[64,2048]{1,0:T(8,128)(2,1)S(1)}, u32[]{:S(2)}, u32[]{:S(2)}) collective-permute-start(bf16[64,2048]{1,0:T(8,128)(2,1)S(1)} %get-tuple-element.70), channel_id=1, source_target_pairs={{0,1},{1,2},{2,3},{3,0},{4,5},{5,6},{6,7},{7,4},{8,9},{9,10},{10,1... | collective-permute-start | bytes 786440 | tf_op jit(solution)/shard_map/ppermute | solution.py:465
  13.0 37.6 %collective-permute-start.7 = (bf16[64,2048]{1,0:T(8,128)(2,1)S(1)}, bf16[64,2048]{1,0:T(8,128)(2,1)S(1)}, u32[]{:S(2)}, u32[]{:S(2)}) collective-permute-start(bf16[64,2048]{1,0:T(8,128)(2,1)S(1)} %get-tuple-element.71), channel_id=1, source_target_pairs={{0,2},{1,3},{2,0},{3,1},{4,6},{5,7},{6,4},{7,5},{8,10},{9,11},{10,... | collective-permute-start | bytes 786440 | tf_op jit(solution)/shard_map/ppermute | solution.py:465
  17.7 32.9 %collective-permute-start.8 = (bf16[64,2048]{1,0:T(8,128)(2,1)S(1)}, bf16[64,2048]{1,0:T(8,128)(2,1)S(1)}, u32[]{:S(2)}, u32[]{:S(2)}) collective-permute-start(bf16[64,2048]{1,0:T(8,128)(2,1)S(1)} %get-tuple-element.72), channel_id=1, source_target_pairs={{0,3},{1,0},{2,1},{3,2},{4,7},{5,4},{6,5},{7,6},{8,11},{9,8},{10,9... | collective-permute-start | bytes 786440 | tf_op jit(solution)/shard_map/ppermute | solution.py:465
  54.4 11.0 %collective-permute-start.22 = (bf16[4,96,2048]{2,1,0:T(8,128)(2,1)}, bf16[4,96,2048]{2,1,0:T(8,128)(2,1)S(1)}, u32[]{:S(2)}, u32[]{:S(2)}) collective-permute-start(bf16[4,96,2048]{2,1,0:T(8,128)(2,1)} %get-tuple-element.103), channel_id=1, source_target_pairs={{0,4},{4,0},{8,12},{12,8},{16,20},{20,16},{24,28},{28,24},{1,5},{5... | collective-permute-start | bytes 4718600 | tf_op jit(solution)/shard_map/ppermute | solution.py:360
  61.4 13.9 %collective-permute-start.17 = (bf16[4,256,768]{2,1,0:T(8,128)(2,1)}, bf16[4,256,768]{2,1,0:T(8,128)(2,1)S(1)}, u32[]{:S(2)}, u32[]{:S(2)}) collective-permute-start(bf16[4,256,768]{2,1,0:T(8,128)(2,1)} %get-tuple-element.92), channel_id=1, source_target_pairs={{0,4},{4,0},{8,12},{12,8},{16,20},{20,16},{24,28},{28,24},{1,5},{5... | collective-permute-start | bytes 4718600 | tf_op jit(solution)/shard_map/ppermute | solution.py:360
  65.3 12.2 %collective-permute-start.12 = (bf16[4,256,768]{2,1,0:T(8,128)(2,1)}, bf16[4,256,768]{2,1,0:T(8,128)(2,1)S(1)}, u32[]{:S(2)}, u32[]{:S(2)}) collective-permute-start(bf16[4,256,768]{2,1,0:T(8,128)(2,1)} %get-tuple-element.82), channel_id=1, source_target_pairs={{0,4},{4,0},{8,12},{12,8},{16,20},{20,16},{24,28},{28,24},{1,5},{5... | collective-permute-start | bytes 4718600 | tf_op jit(solution)/shard_map/ppermute | solution.py:360
  66.1 27.5 %collective-permute-start.23 = (bf16[2,48,2048]{2,1,0:T(8,128)(2,1)S(1)}, bf16[2,48,2048]{2,1,0:T(8,128)(2,1)S(1)}, u32[]{:S(2)}, u32[]{:S(2)}) collective-permute-start(bf16[2,48,2048]{2,1,0:T(8,128)(2,1)S(1)} %get-tuple-element.105), channel_id=1, source_target_pairs={{0,8},{4,12},{8,0},{12,4},{16,24},{20,28},{24,16},{28,20},{1,9},{5... | collective-permute-start | bytes 1179656 | tf_op jit(solution)/shard_map/ppermute | solution.py:360
  67.7 14.1 %collective-permute-start.3 = (bf16[64,2048]{1,0:T(8,128)(2,1)}, bf16[64,2048]{1,0:T(8,128)(2,1)S(1)}, u32[]{:S(2)}, u32[]{:S(2)}) collective-permute-start(bf16[64,2048]{1,0:T(8,128)(2,1)} %get-tuple-element.64), channel_id=1, source_target_pairs={{0,3},{1,0},{2,1},{3,2},{4,7},{5,4},{6,5},{7,6},{8,11},{9,8},{10,9... | collective-permute-start | bytes 786440 | tf_op jit(solution)/shard_map/ppermute | solution.py:465
  74.8 18.3 %collective-permute-start.4 = (bf16[64,2048]{1,0:T(8,128)(2,1)S(1)}, bf16[64,2048]{1,0:T(8,128)(2,1)S(1)}, u32[]{:S(2)}, u32[]{:S(2)}) collective-permute-start(bf16[64,2048]{1,0:T(8,128)(2,1)S(1)} %get-tuple-element.65), channel_id=1, source_target_pairs={{0,2},{1,3},{2,0},{3,1},{4,6},{5,7},{6,4},{7,5},{8,10},{9,11},{10,... | collective-permute-start | bytes 786440 | tf_op jit(solution)/shard_map/ppermute | solution.py:465
  75.2 24.1 %collective-permute-start.24 = (bf16[2,48,2048]{2,1,0:T(8,128)(2,1)S(1)}, bf16[2,48,2048]{2,1,0:T(8,128)(2,1)S(1)}, u32[]{:S(2)}, u32[]{:S(2)}) collective-permute-start(bf16[2,48,2048]{2,1,0:T(8,128)(2,1)S(1)} %get-tuple-element.107), channel_id=1, source_target_pairs={{0,16},{4,20},{8,24},{12,28},{16,0},{20,4},{24,8},{28,12},{1,17},{... | collective-permute-start | bytes 1179656 | tf_op jit(solution)/shard_map/ppermute | solution.py:360
  77.5 21.9 %collective-permute-start.18 = (bf16[2,128,768]{2,1,0:T(8,128)(2,1)S(1)}, bf16[2,128,768]{2,1,0:T(8,128)(2,1)S(1)}, u32[]{:S(2)}, u32[]{:S(2)}) collective-permute-start(bf16[2,128,768]{2,1,0:T(8,128)(2,1)S(1)} %get-tuple-element.94), channel_id=1, source_target_pairs={{0,8},{4,12},{8,0},{12,4},{16,24},{20,28},{24,16},{28,20},{1,9},{5... | collective-permute-start | bytes 1179656 | tf_op jit(solution)/shard_map/ppermute | solution.py:360
  78.1 17.0 %copy-start = (bf16[1,2048,768]{2,1,0:T(8,128)(2,1)S(1)}, bf16[1,2048,768]{2,1,0:T(8,128)(2,1)}, u32[]{:S(2)}) copy-start(bf16[1,2048,768]{2,1,0:T(8,128)(2,1)} %wg_ref.1) | copy-start | bytes 9437188
  81.8 21.4 %collective-permute-start.19 = (bf16[2,128,768]{2,1,0:T(8,128)(2,1)S(1)}, bf16[2,128,768]{2,1,0:T(8,128)(2,1)S(1)}, u32[]{:S(2)}, u32[]{:S(2)}) collective-permute-start(bf16[2,128,768]{2,1,0:T(8,128)(2,1)S(1)} %get-tuple-element.96), channel_id=1, source_target_pairs={{0,16},{4,20},{8,24},{12,28},{16,0},{20,4},{24,8},{28,12},{1,17},{... | collective-permute-start | bytes 1179656 | tf_op jit(solution)/shard_map/ppermute | solution.py:360
  93.1 10.4 %collective-permute-start.13 = (bf16[2,128,768]{2,1,0:T(8,128)(2,1)S(1)}, bf16[2,128,768]{2,1,0:T(8,128)(2,1)S(1)}, u32[]{:S(2)}, u32[]{:S(2)}) collective-permute-start(bf16[2,128,768]{2,1,0:T(8,128)(2,1)S(1)} %get-tuple-element.84), channel_id=1, source_target_pairs={{0,8},{4,12},{8,0},{12,4},{16,24},{20,28},{24,16},{28,20},{1,9},{5... | collective-permute-start | bytes 1179656 | tf_op jit(solution)/shard_map/ppermute | solution.py:360
  93.6 10.9 %collective-permute-start.14 = (bf16[2,128,768]{2,1,0:T(8,128)(2,1)S(1)}, bf16[2,128,768]{2,1,0:T(8,128)(2,1)S(1)}, u32[]{:S(2)}, u32[]{:S(2)}) collective-permute-start(bf16[2,128,768]{2,1,0:T(8,128)(2,1)S(1)} %get-tuple-element.86), channel_id=1, source_target_pairs={{0,16},{4,20},{8,24},{12,28},{16,0},{20,4},{24,8},{28,12},{1,17},{... | collective-permute-start | bytes 1179656 | tf_op jit(solution)/shard_map/ppermute | solution.py:360
  99.4 11.3 %collective-permute-start.5 = (bf16[64,2048]{1,0:T(8,128)(2,1)}, bf16[64,2048]{1,0:T(8,128)(2,1)S(1)}, u32[]{:S(2)}, u32[]{:S(2)}) collective-permute-start(bf16[64,2048]{1,0:T(8,128)(2,1)} %get-tuple-element.66), channel_id=1, source_target_pairs={{0,1},{1,2},{2,3},{3,0},{4,5},{5,6},{6,7},{7,4},{8,9},{9,10},{10,1... | collective-permute-start | bytes 786440 | tf_op jit(solution)/shard_map/ppermute | solution.py:465
  99.5 13.0 %collective-permute-start.9 = (bf16[64,2048]{1,0:T(8,128)(2,1)S(1)}, bf16[64,2048]{1,0:T(8,128)(2,1)S(1)}, u32[]{:S(2)}, u32[]{:S(2)}) collective-permute-start(bf16[64,2048]{1,0:T(8,128)(2,1)S(1)} %get-tuple-element.78), channel_id=1, source_target_pairs={{0,3},{1,0},{2,1},{3,2},{4,7},{5,4},{6,5},{7,6},{8,11},{9,8},{10,9... | collective-permute-start | bytes 786440 | tf_op jit(solution)/shard_map/ppermute | solution.py:465
  103.3 26.5 %collective-permute-start.10 = (bf16[64,2048]{1,0:T(8,128)(2,1)S(1)}, bf16[64,2048]{1,0:T(8,128)(2,1)S(1)}, u32[]{:S(2)}, u32[]{:S(2)}) collective-permute-start(bf16[64,2048]{1,0:T(8,128)(2,1)S(1)} %get-tuple-element.79), channel_id=1, source_target_pairs={{0,2},{1,3},{2,0},{3,1},{4,6},{5,7},{6,4},{7,5},{8,10},{9,11},{10,... | collective-permute-start | bytes 786440 | tf_op jit(solution)/shard_map/ppermute | solution.py:465
  103.5 27.8 %collective-permute-start.11 = (bf16[64,2048]{1,0:T(8,128)(2,1)S(1)}, bf16[64,2048]{1,0:T(8,128)(2,1)S(1)}, u32[]{:S(2)}, u32[]{:S(2)}) collective-permute-start(bf16[64,2048]{1,0:T(8,128)(2,1)S(1)} %get-tuple-element.80), channel_id=1, source_target_pairs={{0,1},{1,2},{2,3},{3,0},{4,5},{5,6},{6,7},{7,4},{8,9},{9,10},{10,1... | collective-permute-start | bytes 786440 | tf_op jit(solution)/shard_map/ppermute | solution.py:465
  104.5 27.3 %collective-permute-start.25 = (bf16[48,2048]{1,0:T(8,128)(2,1)S(1)}, bf16[48,2048]{1,0:T(8,128)(2,1)S(1)}, u32[]{:S(2)}, u32[]{:S(2)}) collective-permute-start(bf16[48,2048]{1,0:T(8,128)(2,1)S(1)} %get-tuple-element.109), channel_id=1, source_target_pairs={{0,16},{4,20},{8,24},{12,28},{16,0},{20,4},{24,8},{28,12},{1,17},{... | collective-permute-start | bytes 589832 | tf_op jit(solution)/shard_map/ppermute | solution.py:360
  105.3 27.0 %copy-start.7 = (s32[128,2]{0,1:T(2,128)S(1)}, s32[128,2]{0,1:T(2,128)}, u32[]{:S(2)}) copy-start(s32[128,2]{0,1:T(2,128)} %param.8) | copy-start | bytes 3076
  105.5 28.5 %copy-start.2 = (bf16[128,2048]{1,0:T(8,128)(2,1)S(1)}, bf16[128,2048]{1,0:T(8,128)(2,1)}, u32[]{:S(2)}) copy-start(bf16[128,2048]{1,0:T(8,128)(2,1)} %grad_ref.3) | copy-start | bytes 1572868
  105.5 28.5 %copy-start.5 = (bf16[64,2048]{1,0:T(8,128)(2,1)S(1)}, bf16[64,2048]{1,0:T(8,128)(2,1)}, u32[]{:S(2)}) copy-start(bf16[64,2048]{1,0:T(8,128)(2,1)} %copy-done.4) | copy-start | bytes 786436
  105.5 28.5 %copy-start.9 = (f32[128,2]{0,1:T(2,128)S(1)}, f32[128,2]{0,1:T(2,128)}, u32[]{:S(2)}) copy-start(f32[128,2]{0,1:T(2,128)} %param.9) | copy-start | bytes 3076
  110.7 26.4 %collective-permute-start.26 = (bf16[48,2048]{1,0:T(8,128)(2,1)S(1)}, bf16[48,2048]{1,0:T(8,128)(2,1)S(1)}, u32[]{:S(2)}, u32[]{:S(2)}) collective-permute-start(bf16[48,2048]{1,0:T(8,128)(2,1)S(1)} %get-tuple-element.111), channel_id=1, source_target_pairs={{0,8},{4,12},{8,0},{12,4},{16,24},{20,28},{24,16},{28,20},{1,9},{5... | collective-permute-start | bytes 589832 | tf_op jit(solution)/shard_map/ppermute | solution.py:360
  112.5 25.4 %collective-permute-start.20 = (bf16[128,768]{1,0:T(8,128)(2,1)S(1)}, bf16[128,768]{1,0:T(8,128)(2,1)S(1)}, u32[]{:S(2)}, u32[]{:S(2)}) collective-permute-start(bf16[128,768]{1,0:T(8,128)(2,1)S(1)} %get-tuple-element.98), channel_id=1, source_target_pairs={{0,16},{4,20},{8,24},{12,28},{16,0},{20,4},{24,8},{28,12},{1,17},{... | collective-permute-start | bytes 589832 | tf_op jit(solution)/shard_map/ppermute | solution.py:360
  129.8 8.2 %collective-permute-start.21 = (bf16[128,768]{1,0:T(8,128)(2,1)S(1)}, bf16[128,768]{1,0:T(8,128)(2,1)S(1)}, u32[]{:S(2)}, u32[]{:S(2)}) collective-permute-start(bf16[128,768]{1,0:T(8,128)(2,1)S(1)} %get-tuple-element.100), channel_id=1, source_target_pairs={{0,8},{4,12},{8,0},{12,4},{16,24},{20,28},{24,16},{28,20},{1,9},{5... | collective-permute-start | bytes 589832 | tf_op jit(solution)/shard_map/ppermute | solution.py:360
  131.3 7.5 %collective-permute-start.15 = (bf16[128,768]{1,0:T(8,128)(2,1)S(1)}, bf16[128,768]{1,0:T(8,128)(2,1)S(1)}, u32[]{:S(2)}, u32[]{:S(2)}) collective-permute-start(bf16[128,768]{1,0:T(8,128)(2,1)S(1)} %get-tuple-element.88), channel_id=1, source_target_pairs={{0,16},{4,20},{8,24},{12,28},{16,0},{20,4},{24,8},{28,12},{1,17},{... | collective-permute-start | bytes 589832 | tf_op jit(solution)/shard_map/ppermute | solution.py:360
  131.8 7.8 %collective-permute-start.16 = (bf16[128,768]{1,0:T(8,128)(2,1)S(1)}, bf16[128,768]{1,0:T(8,128)(2,1)S(1)}, u32[]{:S(2)}, u32[]{:S(2)}) collective-permute-start(bf16[128,768]{1,0:T(8,128)(2,1)S(1)} %get-tuple-element.90), channel_id=1, source_target_pairs={{0,8},{4,12},{8,0},{12,4},{16,24},{20,28},{24,16},{28,20},{1,9},{5... | collective-permute-start | bytes 589832 | tf_op jit(solution)/shard_map/ppermute | solution.py:360
  (5 other events, 4.1 us)

commit v2 on v1

v2 whole, which is shorter than its diff:
```python
import functools
import jax
import jax.numpy as jnp
from jax import lax
from jax.experimental import pallas as pl
from jax.experimental.pallas import tpu as pltpu
from jax.sharding import PartitionSpec as P

CAP = 64
BF = jnp.bfloat16
F32 = jnp.float32
MIB = 1 << 20


def mm(left, right):
    return jnp.dot(left, right, preferred_element_type=F32)


def mm_rows(left, right):
    return lax.dot_general(left, right, (((0,), (0,)), ((), ())), preferred_element_type=F32)


def mm_cols(left, right):
    return lax.dot_general(left, right, (((1,), (1,)), ((), ())), preferred_element_type=F32)


def shape_of(shape, dtype=BF):
    return jax.ShapeDtypeStruct(tuple(shape), dtype)


def whole(shape):
    return pl.BlockSpec(tuple(shape), lambda *_: (0,) * len(shape))


def in_smem():
    return pl.BlockSpec(memory_space=pltpu.SMEM)


def params(limit=28):
    return pltpu.CompilerParams(vmem_limit_bytes=limit * MIB)


def call(kernel, after, in_specs, args, **kwargs):
    count = len(args)

    def body(*refs):
        kernel(*refs[:count], *refs[count + len(after) :])

    specs = list(in_specs) + [pl.BlockSpec(memory_space=pl.ANY)] * len(after)
    return pl.pallas_call(body, in_specs=specs, **kwargs)(*args, *after)


def cost(flops, moved):
    return pl.CostEstimate(flops=int(flops), bytes_accessed=int(moved), transcendentals=0)


def chosen(ids, expert):
    first = ids[0:1, :] == expert
    second = ids[1:2, :] == expert
    return first, second


def ranks(ids, experts):
    tok_count = ids.shape[1]
    masks = [jnp.where(jnp.logical_or(*chosen(ids, e)), 1.0, 0.0) for e in experts]
    mask = jnp.concatenate(masks + [jnp.zeros((-len(masks) % 16, tok_count), F32)], axis=0)
    before = lax.broadcasted_iota(jnp.int32, (tok_count, tok_count), 0)
    after = lax.broadcasted_iota(jnp.int32, (tok_count, tok_count), 1)
    upper = jnp.where(before < after, 1.0, 0.0).astype(BF)
    return mm(mask.astype(BF), upper).astype(jnp.int32)


def places(rank_row):
    tok_count = rank_row.shape[1]
    return lax.broadcasted_iota(jnp.int32, (CAP, tok_count), 0) == rank_row


def pick_kernel(n, z_ref, ids_ref, prob_ref, tok_ref, grad_ref, *outs):
    ids = ids_ref[...]
    prob = prob_ref[...]
    tok, grad = tok_ref[...], grad_ref[...]
    experts = [jnp.bitwise_xor(z_ref[0], k) for k in range(n)]
    rank = ranks(ids, experts)
    for k in range(n):
        first, second = chosen(ids, experts[k])
        at = places(rank[k : k + 1, :])
        here = jnp.logical_and(at, jnp.logical_or(first, second))
        pick = jnp.where(here, 1.0, 0.0)
        weight = jnp.where(first, prob[0:1, :], prob[1:2, :])
        scale = jnp.sum(jnp.where(here, weight, 0.0), axis=1, keepdims=True)
        outs[k][...] = mm(pick.astype(BF), tok).astype(BF)
        outs[n + k][...] = (scale * mm(pick.astype(BF), grad)).astype(BF)


def pick_rows(n, z, ids_t, prob_t, tokens, out_grad):
    tok_count, width = tokens.shape
    return pl.pallas_call(
        functools.partial(pick_kernel, n),
        out_shape=[shape_of((CAP, width))] * (2 * n),
        in_specs=[in_smem(), whole(ids_t.shape), whole(prob_t.shape)] + [whole(tokens.shape)] * 2,
        out_specs=[whole((CAP, width))] * (2 * n),
        grid=(1,),
        compiler_params=params(60),
        cost_estimate=cost(4 * n * CAP * tok_count * width, 4 * tok_count * width * 3),
        name="pick_rows",
    )(z, ids_t, prob_t, tokens, out_grad)


def silu_parts(gate):
    sig = jax.nn.sigmoid(gate)
    return gate * sig, sig * (1.0 + gate * (1.0 - sig))


def forward_kernel(n, steps, tile, *refs):
    x_refs = refs[:n]
    weights = refs[n : n + 3]
    slope_ref, act_ref, hid_ref = refs[n + 3 : n + 6]
    out_refs = refs[n + 6 : 2 * n + 6]
    rows, total, wg_buf, wu_buf, wd_buf, sems = refs[2 * n + 6 :]
    step = pl.program_id(0)

    def loads(j):
        at = pl.ds(pl.multiple_of(j * tile, tile), tile)
        wg_ref, wu_ref, wd_ref = weights
        return (
            pltpu.make_async_copy(wg_ref.at[0, :, at], wg_buf.at[j], sems.at[0, j]),
            pltpu.make_async_copy(wu_ref.at[0, :, at], wu_buf.at[j], sems.at[1, j]),
            pltpu.make_async_copy(wd_ref.at[0, at, :], wd_buf.at[j], sems.at[2, j]),
        )

    @pl.when(step == 0)
    def _():
        for j in range(steps):
            for load in loads(j):
                load.start()
        for k in range(n):
            rows[k * CAP : (k + 1) * CAP, :] = x_refs[k][...]

    for load in loads(step):
        load.wait()
    gate = mm(rows[...], wg_buf[step])
    up = mm(rows[...], wu_buf[step])
    act, slope = silu_parts(gate)
    act_ref[...] = act
    slope_ref[...] = up * slope
    hidden = (act * up).astype(BF)
    hid_ref[...] = hidden
    part = mm(hidden, wd_buf[step])

    @pl.when(step == 0)
    def _():
        total[...] = part

    @pl.when(step > 0)
    def _():
        total[...] += part

    @pl.when(step == steps - 1)
    def _():
        for k in range(n):
            out_refs[k][...] = total[k * CAP : (k + 1) * CAP, :].astype(BF)


def weight_specs(width, tile):
    by_col = pl.BlockSpec((1, width, tile), lambda j: (0, 0, j))
    by_row = pl.BlockSpec((1, tile, width), lambda j: (0, j, 0))
    return [by_col, by_col, by_row]


def forward(xs, w_gate, w_up, w_down):
    n = len(xs)
    width, ff = w_gate.shape[1:]
    tile = 256
    steps = ff // tile
    rows = n * CAP
    part = pl.BlockSpec((rows, tile), lambda j: (0, j))
    return pl.pallas_call(
        functools.partial(forward_kernel, n, steps, tile),
        grid=(steps,),
        out_shape=[shape_of((rows, ff), F32)] * 2 + [shape_of((rows, ff))] + [shape_of((CAP, width))] * n,
        in_specs=[whole((CAP, width))] * n + [pl.BlockSpec(memory_space=pltpu.HBM)] * 3,
        out_specs=[part, part, part] + [whole((CAP, width))] * n,
        scratch_shapes=[
            pltpu.VMEM((rows, width), BF),
            pltpu.VMEM((rows, width), F32),
            pltpu.VMEM((steps, width, tile), BF),
            pltpu.VMEM((steps, width, tile), BF),
            pltpu.VMEM((steps, tile, width), BF),
            pltpu.SemaphoreType.DMA((3, steps)),
        ],
        compiler_params=params(),
        cost_estimate=cost(6 * rows * width * ff, 6 * width * ff + 4 * rows * width + 10 * rows * ff),
        name="forward",
    )(*xs, w_gate, w_up, w_down)


def turn_kernel(n, parts, me_ref, *refs):
    x_refs = refs[:n]
    hid_ref, keep_ref, send_ref, rows, turned = refs[n:]
    for k in range(n):
        rows[k * CAP : (k + 1) * CAP, :] = x_refs[k][...]
    turned[...] = hid_ref[...].T
    half = parts // 2
    x_size, h_size = rows.shape[1] // parts, turned.shape[0] // parts
    strip = h_size // 6
    for rel in range(parts):
        out_ref, i = (keep_ref, rel) if rel < half else (send_ref, rel - half)
        at = pl.multiple_of(me_ref[rel] * x_size, x_size)
        out_ref[i * x_size : (i + 1) * x_size, :] = rows[:, pl.ds(at, x_size)].T
        for j in range(6):
            at = pl.multiple_of(me_ref[rel] * h_size + j * strip, strip)
            base = half * x_size + ((j % 3) * 2 * half + 2 * i + j // 3) * strip
            out_ref[base : base + strip, :] = turned[pl.ds(at, strip), :]


def turn(parts, owners, xs, hidden):
    n = len(xs)
    width = xs[0].shape[1]
    rows, ff = hidden.shape
    high = (width + ff) // 2
    return pl.pallas_call(
        functools.partial(turn_kernel, n, parts),
        grid=(1,),
        out_shape=[shape_of((high, rows))] * 2,
        in_specs=[in_smem()] + [whole((CAP, width))] * n + [whole(hidden.shape)],
        out_specs=[whole((high, rows))] * 2,
        scratch_shapes=[pltpu.VMEM((rows, width), BF), pltpu.VMEM((ff, rows), BF)],
        compiler_params=params(),
        cost_estimate=cost(2 * rows * width, 6 * rows * (width + ff)),
        name="turn",
    )(owners, *xs, hidden)


def outer_kernel(keep_ref, recv_ref, own_ref, other_ref, own_g_ref, other_g_ref, x_send, x_keep, y_send, y_keep):
    step = pl.program_id(0)
    half, high = 4, own_ref.shape[0] // 2
    size = 256
    strip = 16
    for block in range(half):
        at = slice(block * size, (block + 1) * size)
        across, along = block & 1, block >> 1
        gate = mm(keep_ref[at, :], own_ref[:high, :]) + mm(recv_ref[at, :], other_ref[:high, :])
        (x_send if across else x_keep)[along, :size, :] = gate.astype(BF)
        up = mm(keep_ref[at, :], own_ref[high:, :]) + mm(recv_ref[at, :], other_ref[high:, :])
        (y_send if along else y_keep)[across, :size, :] = up.astype(BF)
    at = pl.ds(pl.multiple_of(half * size + step * 2 * half * strip, strip), 2 * half * strip)
    down = mm(keep_ref[at, :], own_g_ref[...]) + mm(recv_ref[at, :], other_g_ref[...])
    down = down.astype(BF)
    tile = x_send.shape[2]
    for block in range(half):
        across, along = block & 1, block >> 1
        for part, (out_ref, i) in enumerate(
            ((x_send if across else x_keep, along), (y_send if along else y_keep, across))
        ):
            base = (2 * block + part) * strip
            for c in range(down.shape[1] // tile):
                out_ref[i, size + c * strip : size + (c + 1) * strip, :] = down[
                    base : base + strip, c * tile : (c + 1) * tile
                ]


def outer(keep, recv, own, other, own_g, other_g):
    rows, width = own_g.shape
    ff = own.shape[1]
    tile = 256
    col = pl.BlockSpec((2 * rows, tile), lambda j: (0, j))
    high = 256 + 16 * (width // tile)
    part = pl.BlockSpec((2, high, tile), lambda j: (0, 0, j))
    return pl.pallas_call(
        outer_kernel,
        grid=(ff // tile,),
        out_shape=[shape_of((2, high, ff))] * 4,
        in_specs=[whole(keep.shape)] * 2 + [col] * 2 + [whole(own_g.shape)] * 2,
        out_specs=[part] * 4,
        compiler_params=params(),
        cost_estimate=cost(6 * rows * width * ff, 4 * keep.size + 16 * high * ff),
        name="outer",
    )(keep, recv, own, other, own_g, other_g)


def hidden_grad_kernel(n, *refs):
    g_refs = refs[:n]
    wd_ref, slope_ref, act_ref, grad_ref, rows = refs[n:]

    @pl.when(pl.program_id(0) == 0)
    def _():
        for k in range(n):
            rows[k * CAP : (k + 1) * CAP, :] = g_refs[k][...]

    grad = mm_cols(rows[...], wd_ref[0])
    grad_ref[: n * CAP, :] = (grad * slope_ref[...]).astype(BF)
    grad_ref[n * CAP :, :] = (grad * act_ref[...]).astype(BF)


def hidden_grad(gs, w_down, slope, act, after):
    n = len(gs)
    ff, width = w_down.shape[1:]
    rows = n * CAP
    tile = 256
    part = pl.BlockSpec((rows, tile), lambda j: (0, j))
    return call(
        functools.partial(hidden_grad_kernel, n),
        after,
        grid=(ff // tile,),
        out_shape=[shape_of((2 * rows, ff)), shape_of((rows, width))],
        in_specs=[whole((CAP, width))] * n + [weight_specs(width, tile)[2], part, part],
        args=(*gs, w_down, slope, act),
        out_specs=[pl.BlockSpec((2 * rows, tile), lambda j: (0, j)), whole((rows, width))],
        compiler_params=params(),
        cost_estimate=cost(2 * rows * width * ff, 2 * width * ff + 4 * rows * width + 12 * rows * ff),
        name="hidden_grad",
    )


def input_grad_kernel(n, grad_ref, wg_ref, wu_ref, *out_refs):
    rows = n * CAP
    total = mm_cols(grad_ref[:rows, :], wg_ref[0]) + mm_cols(grad_ref[rows:, :], wu_ref[0])
    for k in range(n):
        out_refs[k][...] = total[k * CAP : (k + 1) * CAP, :].astype(BF)


def input_grad(n, grad, w_gate, w_up, after):
    rows, ff = n * CAP, grad.shape[1]
    width = w_gate.shape[1]
    tile = 512
    by_row = pl.BlockSpec((1, tile, ff), lambda j: (0, j, 0))
    return call(
        functools.partial(input_grad_kernel, n),
        after,
        grid=(width // tile,),
        out_shape=[shape_of((CAP, width))] * n,
        in_specs=[whole((2 * rows, ff)), by_row, by_row],
        args=(grad, w_gate, w_up),
        out_specs=[pl.BlockSpec((CAP, tile), lambda j: (0, j))] * n,
        compiler_params=params(),
        cost_estimate=cost(4 * rows * width * ff, 4 * width * ff + 2 * rows * (width + 2 * ff)),
        name="input_grad",
    )


def fold_two_kernel(x_keep, x_recv, y_keep, y_recv, x_next, x_mine, y_next, y_mine):
    for keep, recv, away, mine in ((x_keep, x_recv, x_next, x_mine), (y_keep, y_recv, y_next, y_mine)):
        away[...] = (keep[1].astype(F32) + recv[1].astype(F32)).astype(BF)
        mine[...] = (keep[0].astype(F32) + recv[0].astype(F32)).astype(BF)


def fold_two(x_keep, x_recv, y_keep, y_recv, after):
    _, high, width = x_keep.shape
    return call(
        fold_two_kernel,
        after,
        grid=(1,),
        out_shape=[shape_of((high, width))] * 4,
        in_specs=[whole((2, high, width))] * 4,
        args=(x_keep, x_recv, y_keep, y_recv),
        out_specs=[whole((high, width))] * 4,
        compiler_params=params(),
        cost_estimate=cost(4 * high * width, 24 * high * width),
        name="fold_two",
    )


def fold_last_kernel(x_mine, x_recv, y_mine, y_recv, gate_ref, up_ref, down_ref):
    size, strip = gate_ref.shape[1], 16
    tile = 256
    for i, (mine, recv, out_ref) in enumerate(((x_mine, x_recv, gate_ref), (y_mine, y_recv, up_ref))):
        total = (mine[...].astype(F32) + recv[...].astype(F32)).astype(BF)
        out_ref[0] = total[:size]
        for c in range(down_ref.shape[2] // tile):
            for j in range(3):
                down_ref[0, (3 * i + j) * strip : (3 * i + j + 1) * strip, c * tile : (c + 1) * tile] = total[
                    size + c * strip : size + (c + 1) * strip, j * tile : (j + 1) * tile
                ]


def fold_last(x_mine, x_recv, y_mine, y_recv, shapes):
    high, width = x_mine.shape
    return pl.pallas_call(
        fold_last_kernel,
        grid=(1,),
        out_shape=[shape_of(s) for s in shapes],
        in_specs=[whole((high, width))] * 4,
        out_specs=[whole(s) for s in shapes],
        compiler_params=params(),
        cost_estimate=cost(2 * high * width, 12 * high * width),
        name="fold_last",
    )(x_mine, x_recv, y_mine, y_recv)


CORE, ALONG_X, ALONG_Y = 1, 2, 4


def swap(value, bit, count=8):
    return lax.ppermute(value, "dp", [(i, i ^ bit) for i in range(count)])


def combine_kernel(n, z_ref, ids_ref, prob_ref, grad_ref, *refs):
    out_back_refs, in_back_refs = refs[:n], refs[n : 2 * n]
    out_ref, in_ref, prob_grad_ref, out_rows, in_rows, sums, firsts, seconds = refs[2 * n :]
    tok_count = ids_ref.shape[1]
    step = pl.program_id(0)

    @pl.when(step == 0)
    def _():
        ids = ids_ref[...]
        experts = [jnp.bitwise_xor(z_ref[0], k) for k in range(n)]
        rank = ranks(ids, experts)
        for k in range(n):
            first, second = chosen(ids, experts[k])
            at = places(rank[k : k + 1, :])
            rows = slice(k * CAP, (k + 1) * CAP)
            firsts[rows, :] = jnp.where(jnp.logical_and(at, first), 1.0, 0.0)
            seconds[rows, :] = jnp.where(jnp.logical_and(at, second), 1.0, 0.0)
        sums[...] = jnp.zeros_like(sums)

    for k in range(n):
        out_rows[k * CAP : (k + 1) * CAP, :] = out_back_refs[k][...]
        in_rows[k * CAP : (k + 1) * CAP, :] = in_back_refs[k][...]
    prob = jnp.concatenate([prob_ref[...], jnp.zeros((6, tok_count), F32)], axis=0).T
    grad = grad_ref[...].astype(F32)
    one, two = firsts[...].astype(BF), seconds[...].astype(BF)
    total = 0.0
    part = []
    for choice, at in enumerate((one, two)):
        out = mm_rows(at, out_rows[...])
        total = total + prob[:, choice : choice + 1] * out
        part.append(jnp.sum(grad * out, axis=1, keepdims=True))
    out_ref[...] = total.astype(BF)
    in_ref[...] = mm_rows(one + two, in_rows[...]).astype(BF)
    sums[...] += jnp.concatenate(part + [jnp.zeros((tok_count, 6), F32)], axis=1)

    @pl.when(step == pl.num_programs(0) - 1)
    def _():
        prob_grad_ref[...] = sums[...].T[0:2, :]


def combine(z, ids_t, prob_t, out_grad, back_out, back_in):
    n = len(back_in)
    tok_count, width = out_grad.shape
    tile = 512
    by_tile = pl.BlockSpec((tok_count, tile), lambda j: (0, j))
    rows = n * CAP
    return pl.pallas_call(
        functools.partial(combine_kernel, n),
        grid=(width // tile,),
        out_shape=[shape_of((tok_count, width))] * 2 + [shape_of((2, tok_count), F32)],
        in_specs=[in_smem(), whole(ids_t.shape), whole(prob_t.shape), by_tile]
        + [pl.BlockSpec((CAP, tile), lambda j: (0, j))] * (2 * n),
        out_specs=[by_tile, by_tile, whole((2, tok_count))],
        scratch_shapes=[pltpu.VMEM((rows, tile), BF)] * 2
        + [pltpu.VMEM((tok_count, 8), F32)]
        + [pltpu.VMEM((rows, tok_count), F32)] * 2,
        compiler_params=params(),
        cost_estimate=cost(6 * rows * tok_count * width, 4 * width * (rows + 2 * tok_count)),
        name="combine",
    )(z, ids_t, prob_t, out_grad, *back_out, *back_in)


def exchange(values):
    n = len(values)
    moved = list(values)
    for k in range(n - 1, 0, -1):
        moved[k] = lax.ppermute(values[k], "expert", [(i, i ^ k) for i in range(n)])
    return moved


def local(tokens, expert_ids, gate_probs, w_gate, w_up, w_down, out_grad):
    n = lax.axis_size("expert")
    parts = lax.axis_size("dp")
    z = lax.axis_index("expert").astype(jnp.int32).reshape(1)
    ids_t, prob_t = expert_ids.T, gate_probs.T
    sent = pick_rows(n, z, ids_t, prob_t, tokens, out_grad)
    xs, gs = exchange(sent[:n]), exchange(sent[n:])
    made = forward(xs, w_gate, w_up, w_down)
    slope, act, hidden = made[:3]
    back_out = exchange(made[3:])
    if parts == 8:
        me = lax.axis_index("dp").astype(jnp.int32)
        flips = [(r >> 2 & 1) * CORE | (r & 1) * ALONG_X | (r >> 1 & 1) * ALONG_Y for r in range(8)]
        owners = jnp.stack([me ^ f for f in flips])
        keep_t, send_t = turn(parts, owners, xs, hidden)
        grad, g_rows = hidden_grad(gs, w_down, slope, act, [keep_t])
        x_send, x_keep, y_send, y_keep = outer(
            keep_t, swap(send_t, CORE), grad, swap(grad, CORE), g_rows, swap(g_rows, CORE)
        )
        back_in = exchange(input_grad(n, grad, w_gate, w_up, [x_send]))
        x_next, x_mine, y_next, y_mine = fold_two(
            x_keep, swap(x_send, ALONG_X), y_keep, swap(y_send, ALONG_Y), [back_in[0], *back_out[1:]]
        )
        shapes = [(1, d // parts, w) for d, w in (w_gate.shape[1:], w_up.shape[1:], w_down.shape[1:])]
        sum_gate, sum_up, sum_down = fold_last(x_mine, swap(x_next, ALONG_Y), y_mine, swap(y_next, ALONG_X), shapes)
    else:
        grad, d_rows = hidden_grad(gs, w_down, slope, act, [])
        back_in = exchange(input_grad(n, grad, w_gate, w_up, []))
        x_rows, count = jnp.concatenate(xs, 0), n * CAP
        sum_gate, sum_up, sum_down = (
            lax.psum_scatter(mm_rows(a, b).astype(BF), "dp", scatter_dimension=0, tiled=True)[None]
            for a, b in ((x_rows, grad[:count]), (x_rows, grad[count:]), (hidden, d_rows))
        )
    layer_out, token_grad, prob_grad_t = combine(z, ids_t, prob_t, out_grad, back_out, back_in)
    return layer_out, prob_grad_t.T, token_grad, sum_gate, sum_up, sum_down


def solution(mesh):
    rows = P(("dp", "expert"), None)
    weights = P("expert", None, None)
    summed = P("expert", "dp", None)
    return jax.shard_map(
        local,
        mesh=mesh,
        in_specs=(rows, rows, rows, weights, weights, weights, rows),
        out_specs=(rows, rows, rows, summed, summed, summed),
        check_vma=False,
    )
```

time: 141 us -> 127 us (0.901)
  Pallas kernels: 37.2 us -> 21.5 us
  waiting for transfers between devices: 62.4 us -> 59.4 us
  local copies, waits for them, and re-layouts: 4.25 us -> 6.74 us
  starting transfers between devices: 35.8 us -> 37.7 us
    pallas_call x17 -> x8, Pallas kernels: 35.9 us -> 18.4 us  [the longest x1 4.94 us: forward(): pl.pallas_call(functools.partial(forward_kernel, n, steps, tile), grid=(s...]
    ppermute x12, starting transfers between devices: 22.7 us -> 32.9 us  [exchange(): moved[k] = lax.ppermute(values[k], 'expert', [(i, i ^ k) for i in range(n)])]
    ppermute x15 -> x7, starting transfers between devices: 13.1 us -> 4.83 us  [swap(): return lax.ppermute(value, 'dp', [(i, i ^ bit) for i in range(count)])]
    ppermute x12, waiting for transfers between devices: 61.3 us -> 55.1 us  [exchange(): moved[k] = lax.ppermute(values[k], 'expert', [(i, i ^ k) for i in range(n)])]
    ppermute x15 -> x7, waiting for transfers between devices: 1.07 us -> 4.24 us  [swap(): return lax.ppermute(value, 'dp', [(i, i ^ bit) for i in range(count)])]
    unnamed x20 -> x22, local copies, waits for them, and re-layouts: 4.16 us -> 6.66 us
    pallas_call x1, Pallas kernels: 1.33 us -> 3.06 us  [pick_rows(): pl.pallas_call(functools.partial(pick_kernel, n), out_shape=[shape_of((CA...]
  transfers between devices with their start and end apart: 27 -> 19, of which waited for: 10 -> 8; matrix products, arithmetic and copies ran while one was open for 0% -> 0% of each run, Pallas kernels for 22% -> 9%
where the time goes in v2:
time: 127 us; the launch traced here: 126 us
  waiting for transfers between devices  59.4 us (47%)
  starting transfers between devices  37.7 us (30%)
  Pallas kernels  21.5 us (17%)
  local copies, waits for them, and re-layouts  6.74 us (5%)
    ppermute x12, waiting for transfers between devices, exchange(): moved[k] = lax.ppermute(values[k], 'expert', [(i, i ^ k) for i in range(n)])  55.1 us
    ppermute x12, starting transfers between devices, exchange(): moved[k] = lax.ppermute(values[k], 'expert', [(i, i ^ k) for i in range(n)])  32.9 us
    unnamed x22, local copies, waits for them, and re-layouts  6.66 us
    pallas_call x1, Pallas kernels, forward(): pl.pallas_call(functools.partial(forward_kernel, n, steps, tile), grid=(s...  4.94 us
    ppermute x7, starting transfers between devices, swap(): return lax.ppermute(value, 'dp', [(i, i ^ bit) for i in range(count)])  4.83 us
    pallas_call x3, Pallas kernels, call(): return pl.pallas_call(body, in_specs=specs, **kwargs)(*args, *after)  4.78 us
    ppermute x7, waiting for transfers between devices, swap(): return lax.ppermute(value, 'dp', [(i, i ^ bit) for i in range(count)])  4.24 us
    pallas_call x1, Pallas kernels, outer(): pl.pallas_call(outer_kernel, grid=(ff // tile,), out_shape=[shape_of((2,...  3.4 us
  transfers between devices with their start and end apart: 19, of which 8 were waited for; matrix products, arithmetic and copies ran while one was open for 0% of the time, Pallas kernels for 9%

profile of v2, /device:TPU:0, one launch (start us, length us, event | category | flops | bytes accessed | tf_op | source)
XLA Modules:
  0.0 126.1 jit_solution(7094345364220850429)
XLA Ops:
  0.6 3.1 %pick_rows.1 = (bf16[64,2048]{1,0:T(8,128)(2,1)}, bf16[64,2048]{1,0:T(8,128)(2,1)}, bf16[64,2048]{1,0:T(8,128)(2,1)}, bf16[64,2048]{1,0:T(8,128)(2,1)}, bf16[64,...) custom-call(s32[1]{0:T(128)} %bitcast.z_ref, ...), custom_call_target="tpu_custom_call" | custom-call | flops 268435456 | bytes 3145728 | tf_op jit(solution)/shard_map/pick_rows/pallas_call | solution.py:97
  3.7 3.0 %collective-permute-start = (bf16[64,2048]{1,0:T(8,128)(2,1)}, bf16[64,2048]{1,0:T(8,128)(2,1)S(1)}, u32[]{:S(2)}, u32[]{:S(2)}) collective-permute-start(bf16[64,2048]{1,0:T(8,128)(2,1)} %get-tuple-element.44), channel_id=1, source_target_pairs={{0,1},{1,0},{2,3},{3,2},{4,5},{5,4},{6,7},{7,6},{8,9},{9,8},{10,11... | collective-permute-start | bytes 786440 | tf_op jit(solution)/shard_map/ppermute | solution.py:463
  6.7 2.6 %collective-permute-start.1 = (bf16[64,2048]{1,0:T(8,128)(2,1)}, bf16[64,2048]{1,0:T(8,128)(2,1)S(1)}, u32[]{:S(2)}, u32[]{:S(2)}) collective-permute-start(bf16[64,2048]{1,0:T(8,128)(2,1)} %get-tuple-element.45), channel_id=1, source_target_pairs={{0,2},{1,3},{2,0},{3,1},{4,6},{5,7},{6,4},{7,5},{8,10},{9,11},{10,... | collective-permute-start | bytes 786440 | tf_op jit(solution)/shard_map/ppermute | solution.py:463
  10.2 3.5 %collective-permute-start.7 = (bf16[64,2048]{1,0:T(8,128)(2,1)}, bf16[64,2048]{1,0:T(8,128)(2,1)S(1)}, u32[]{:S(2)}, u32[]{:S(2)}) collective-permute-start(bf16[64,2048]{1,0:T(8,128)(2,1)} %get-tuple-element.53), channel_id=1, source_target_pairs={{0,2},{1,3},{2,0},{3,1},{4,6},{5,7},{6,4},{7,5},{8,10},{9,11},{10,... | collective-permute-start | bytes 786440 | tf_op jit(solution)/shard_map/ppermute | solution.py:463
  13.7 5.2 %collective-permute-done.refs_1_ = bf16[64,2048]{1,0:T(8,128)(2,1)S(1)} collective-permute-done((bf16[64,2048]{1,0:T(8,128)(2,1)}, bf16[64,2048]{1,0:T(8,128)(2,1)S(1)}, u32[]{:S(2)}, u32[]{:S(2)}) %collective-permute-start) | collective-permute-done | bytes 262176 | tf_op jit(solution)/shard_map/ppermute | solution.py:463
  18.9 4.6 %collective-permute-start.8 = (bf16[64,2048]{1,0:T(8,128)(2,1)}, bf16[64,2048]{1,0:T(8,128)(2,1)S(1)}, u32[]{:S(2)}, u32[]{:S(2)}) collective-permute-start(bf16[64,2048]{1,0:T(8,128)(2,1)} %get-tuple-element.54), channel_id=1, source_target_pairs={{0,3},{1,2},{2,1},{3,0},{4,7},{5,6},{6,5},{7,4},{8,11},{9,10},{10,... | collective-permute-start | bytes 786440 | tf_op jit(solution)/shard_map/ppermute | solution.py:463
  23.6 4.8 %collective-permute-done.1.refs_2_ = bf16[64,2048]{1,0:T(8,128)(2,1)S(1)} collective-permute-done((bf16[64,2048]{1,0:T(8,128)(2,1)}, bf16[64,2048]{1,0:T(8,128)(2,1)S(1)}, u32[]{:S(2)}, u32[]{:S(2)}) %collective-permute-start.1) | collective-permute-done | bytes 262176 | tf_op jit(solution)/shard_map/ppermute | solution.py:463
  28.3 1.9 %copy-done = bf16[1,768,2048]{2,1,0:T(8,128)(2,1)S(1)} copy-done((bf16[1,768,2048]{2,1,0:T(8,128)(2,1)S(1)}, bf16[1,768,2048]{2,1,0:T(8,128)(2,1)}, u32[]{:S(2)}) %copy-start) | copy-done | bytes 3145752
  30.2 1.9 %copy-done.2 = bf16[1,2048,768]{2,1,0:T(8,128)(2,1)S(1)} copy-done((bf16[1,2048,768]{2,1,0:T(8,128)(2,1)S(1)}, bf16[1,2048,768]{2,1,0:T(8,128)(2,1)}, u32[]{:S(2)}) %copy-start.2) | copy-done | bytes 3145752
  32.1 1.9 %copy-done.4 = bf16[1,2048,768]{2,1,0:T(8,128)(2,1)S(1)} copy-done((bf16[1,2048,768]{2,1,0:T(8,128)(2,1)S(1)}, bf16[1,2048,768]{2,1,0:T(8,128)(2,1)}, u32[]{:S(2)}) %copy-start.4) | copy-done | bytes 3145752
  34.0 0.9 copy-done.7
  35.0 4.9 %forward.1 = (f32[256,768]{1,0:T(8,128)S(1)}, f32[256,768]{1,0:T(8,128)S(1)}, bf16[256,768]{1,0:T(8,128)(2,1)S(1)}, bf16[64,2048]{1,0:T(8,128)(2,1)S(1)}, bf16[6...) custom-call(bf16[64,2048]{1,0:T(8,128)(2,1)S(1)} %copy-done.7, ...), custom_call_target="tpu_custom_call" | custom-call | flops 2415919104 | bytes 13500416 | tf_op jit(solution)/shard_map/forward/pallas_call | solution.py:177
  39.9 1.0 turn.1
  40.9 9.9 %collective-permute-done.7.refs_2_ = bf16[64,2048]{1,0:T(8,128)(2,1)S(1)} collective-permute-done((bf16[64,2048]{1,0:T(8,128)(2,1)}, bf16[64,2048]{1,0:T(8,128)(2,1)S(1)}, u32[]{:S(2)}, u32[]{:S(2)}) %collective-permute-start.7) | collective-permute-done | bytes 262176 | tf_op jit(solution)/shard_map/ppermute | solution.py:463
  50.8 1.7 %hidden_grad.1 = (bf16[512,768]{1,0:T(8,128)(2,1)S(1)}, bf16[256,2048]{1,0:T(8,128)(2,1)S(1)}) custom-call(bf16[64,2048]{1,0:T(8,128)(2,1)S(1)} %copy-done.8, bf16[64,2048]{1,0:T(8,128)(2,1)S(1)} %collective-permute-done.6.refs_1_, bf16[64,2048]{1,0:T(8,128)(2,1)S(1)} %collective-permute-done.7.refs_2_, bf16[64,2048]{1,0:T(8,128)(2,1)S(1)} %collective-permute-done.8.refs_3_, ...), custom_call_target="tpu_custom_call" | custom-call | flops 805306368 | bytes 7602176 | tf_op jit(solution)/shard_map/hidden_grad/pallas_call | solution.py:50
  53.2 4.2 %collective-permute-done.9.recv_ref = bf16[1408,256]{1,0:T(8,128)(2,1)S(1)} collective-permute-done((bf16[1408,256]{1,0:T(8,128)(2,1)S(1)}, bf16[1408,256]{1,0:T(8,128)(2,1)S(1)}, u32[]{:S(2)}, u32[]{:S(2)}) %collective-permute-start.9) | collective-permute-done | bytes 720928 | tf_op jit(solution)/shard_map/ppermute | solution.py:394
  57.4 3.4 %outer.1 = (bf16[2,384,768]{2,1,0:T(8,128)(2,1)S(1)}, bf16[2,384,768]{2,1,0:T(8,128)(2,1)S(1)}, bf16[2,384,768]{2,1,0:T(8,128)(2,1)S(1)}, bf16[2,384,768]{2,1,0:T(8,128)(2,1)S(1)}) custom-call(bf16[1408,256]{1,0:T(8,128)(2,1)S(1)} %get-tuple-element.58.refs_7_.keep_ref, bf16[1408,256]{1,0:T(8,128)(2,1)S(1)} %collective-permute-done.9.recv_ref, ...), custom_call_target="tpu_custom_call" | custom-call | flops 2415919104 | bytes 6160384 | tf_op jit(solution)/shard_map/outer/pallas_call | solution.py:269
  60.9 1.6 %collective-permute-start.16 = (bf16[2,384,768]{2,1,0:T(8,128)(2,1)S(1)}, bf16[2,384,768]{2,1,0:T(8,128)(2,1)S(1)}, u32[]{:S(2)}, u32[]{:S(2)}) collective-permute-start(bf16[2,384,768]{2,1,0:T(8,128)(2,1)S(1)} %get-tuple-element.72), channel_id=1, source_target_pairs={{0,16},{4,20},{8,24},{12,28},{16,0},{20,4},{24,8},{28,12},{1,17},{... | collective-permute-start | bytes 3538952 | tf_op jit(solution)/shard_map/ppermute | solution.py:394
  62.4 1.5 %collective-permute-start.15 = (bf16[2,384,768]{2,1,0:T(8,128)(2,1)S(1)}, bf16[2,384,768]{2,1,0:T(8,128)(2,1)S(1)}, u32[]{:S(2)}, u32[]{:S(2)}) collective-permute-start(bf16[2,384,768]{2,1,0:T(8,128)(2,1)S(1)} %get-tuple-element.62.refs_3_), channel_id=1, source_target_pairs={{0,8},{4,12},{8,0},{12,4},{16,24},{20,28},{24,16},{28,20},{1,9},{5... | collective-permute-start | bytes 3538952 | tf_op jit(solution)/shard_map/ppermute | solution.py:394
  63.9 7.6 %collective-permute-start.3 = (bf16[64,2048]{1,0:T(8,128)(2,1)S(1)}, bf16[64,2048]{1,0:T(8,128)(2,1)S(1)}, u32[]{:S(2)}, u32[]{:S(2)}) collective-permute-start(bf16[64,2048]{1,0:T(8,128)(2,1)S(1)} %get-tuple-element.48), channel_id=1, source_target_pairs={{0,1},{1,0},{2,3},{3,2},{4,5},{5,4},{6,7},{7,6},{8,9},{9,8},{10,11... | collective-permute-start | bytes 786440 | tf_op jit(solution)/shard_map/ppermute | solution.py:463
  71.5 1.0 collective-permute-start.4
  72.5 1.5 %collective-permute-start.5 = (bf16[64,2048]{1,0:T(8,128)(2,1)S(1)}, bf16[64,2048]{1,0:T(8,128)(2,1)S(1)}, u32[]{:S(2)}, u32[]{:S(2)}) collective-permute-start(bf16[64,2048]{1,0:T(8,128)(2,1)S(1)} %get-tuple-element.50), channel_id=1, source_target_pairs={{0,3},{1,2},{2,1},{3,0},{4,7},{5,6},{6,5},{7,4},{8,11},{9,10},{10,... | collective-permute-start | bytes 786440 | tf_op jit(solution)/shard_map/ppermute | solution.py:463
  74.0 2.5 %input_grad.1 = (bf16[64,2048]{1,0:T(8,128)(2,1)S(1)}, bf16[64,2048]{1,0:T(8,128)(2,1)S(1)}, bf16[64,2048]{1,0:T(8,128)(2,1)S(1)}, bf16[64,2048]{1,0:T(8,128)(2,1)S(1)}) custom-call(bf16[512,768]{1,0:T(8,128)(2,1)S(1)} %get-tuple-element.59.own_ref.refs_0_, bf16[1,2048,768]{2,1,0:T(8,128)(2,1)S(1)} %copy-done.3, bf16[1,2048,768]{2,1,0:T(8,128)(2,1)S(1)} %copy-done.5, ...), custom_call_target="tpu_custom_call" | custom-call | flops 1610612736 | bytes 8126464 | tf_op jit(solution)/shard_map/input_grad/pallas_call | solution.py:50
  76.5 5.7 %collective-permute-done.3.refs_1_.refs_5_ = bf16[64,2048]{1,0:T(8,128)(2,1)S(1)} collective-permute-done((bf16[64,2048]{1,0:T(8,128)(2,1)S(1)}, bf16[64,2048]{1,0:T(8,128)(2,1)S(1)}, u32[]{:S(2)}, u32[]{:S(2)}) %collective-permute-start.3) | collective-permute-done | bytes 262176 | tf_op jit(solution)/shard_map/ppermute | solution.py:463
  82.3 10.6 %collective-permute-done.4.refs_2_.refs_6_ = bf16[64,2048]{1,0:T(8,128)(2,1)S(1)} collective-permute-done((bf16[64,2048]{1,0:T(8,128)(2,1)S(1)}, bf16[64,2048]{1,0:T(8,128)(2,1)S(1)}, u32[]{:S(2)}, u32[]{:S(2)}) %collective-permute-start.4) | collective-permute-done | bytes 262176 | tf_op jit(solution)/shard_map/ppermute | solution.py:463
  94.6 5.8 %collective-permute-start.12 = (bf16[64,2048]{1,0:T(8,128)(2,1)S(1)}, bf16[64,2048]{1,0:T(8,128)(2,1)S(1)}, u32[]{:S(2)}, u32[]{:S(2)}) collective-permute-start(bf16[64,2048]{1,0:T(8,128)(2,1)S(1)} %get-tuple-element.64), channel_id=1, source_target_pairs={{0,1},{1,0},{2,3},{3,2},{4,5},{5,4},{6,7},{7,6},{8,9},{9,8},{10,11... | collective-permute-start | bytes 786440 | tf_op jit(solution)/shard_map/ppermute | solution.py:463
  100.4 1.0 collective-permute-start.13
  101.4 1.5 %collective-permute-start.14 = (bf16[64,2048]{1,0:T(8,128)(2,1)S(1)}, bf16[64,2048]{1,0:T(8,128)(2,1)S(1)}, u32[]{:S(2)}, u32[]{:S(2)}) collective-permute-start(bf16[64,2048]{1,0:T(8,128)(2,1)S(1)} %get-tuple-element.66), channel_id=1, source_target_pairs={{0,3},{1,2},{2,1},{3,0},{4,7},{5,6},{6,5},{7,4},{8,11},{9,10},{10,... | collective-permute-start | bytes 786440 | tf_op jit(solution)/shard_map/ppermute | solution.py:463
  102.8 6.5 %collective-permute-done.12.refs_5_ = bf16[64,2048]{1,0:T(8,128)(2,1)S(1)} collective-permute-done((bf16[64,2048]{1,0:T(8,128)(2,1)S(1)}, bf16[64,2048]{1,0:T(8,128)(2,1)S(1)}, u32[]{:S(2)}, u32[]{:S(2)}) %collective-permute-start.12) | collective-permute-done | bytes 262176 | tf_op jit(solution)/shard_map/ppermute | solution.py:463
  109.3 12.4 %collective-permute-done.13.refs_6_ = bf16[64,2048]{1,0:T(8,128)(2,1)S(1)} collective-permute-done((bf16[64,2048]{1,0:T(8,128)(2,1)S(1)}, bf16[64,2048]{1,0:T(8,128)(2,1)S(1)}, u32[]{:S(2)}, u32[]{:S(2)}) %collective-permute-start.13) | collective-permute-done | bytes 262176 | tf_op jit(solution)/shard_map/ppermute | solution.py:463
  121.8 3.1 %combine.1 = (bf16[128,2048]{1,0:T(8,128)(2,1)}, bf16[128,2048]{1,0:T(8,128)(2,1)}, f32[2,128]{1,0:T(2,128)}) custom-call(s32[1]{0:T(128)} %bitcast.z_ref, s32[2,128]{1,0:T(2,128)S(1)} %bitcast.13, f32[2,128]{1,0:T(2,128)S(1)} %bitcast.15, bf16[128,2048]{1,0:T(8,128)(2,1)S(1)} %copy-done.6, bf16[64,2048]{1,0:T(8,128)(2,1)S(1)} %get-tuple-element.47.refs_0_, ...), custom_call_target="tpu_custom_call" | custom-call | flops 402653184 | bytes 4194304 | tf_op jit(solution)/shard_map/combine/pallas_call | solution.py:443
  124.9 1.2 fold_last.1
  (38 shorter events, 3.3 us)
Async XLA Ops:
  3.7 15.2 %collective-permute-start = (bf16[64,2048]{1,0:T(8,128)(2,1)}, bf16[64,2048]{1,0:T(8,128)(2,1)S(1)}, u32[]{:S(2)}, u32[]{:S(2)}) collective-permute-start(bf16[64,2048]{1,0:T(8,128)(2,1)} %get-tuple-element.44), channel_id=1, source_target_pairs={{0,1},{1,0},{2,3},{3,2},{4,5},{5,4},{6,7},{7,6},{8,9},{9,8},{10,11... | collective-permute-start | bytes 786440 | tf_op jit(solution)/shard_map/ppermute | solution.py:463
  6.7 21.6 %collective-permute-start.1 = (bf16[64,2048]{1,0:T(8,128)(2,1)}, bf16[64,2048]{1,0:T(8,128)(2,1)S(1)}, u32[]{:S(2)}, u32[]{:S(2)}) collective-permute-start(bf16[64,2048]{1,0:T(8,128)(2,1)} %get-tuple-element.45), channel_id=1, source_target_pairs={{0,2},{1,3},{2,0},{3,1},{4,6},{5,7},{6,4},{7,5},{8,10},{9,11},{10,... | collective-permute-start | bytes 786440 | tf_op jit(solution)/shard_map/ppermute | solution.py:463
  9.3 19.0 %collective-permute-start.2 = (bf16[64,2048]{1,0:T(8,128)(2,1)}, bf16[64,2048]{1,0:T(8,128)(2,1)S(1)}, u32[]{:S(2)}, u32[]{:S(2)}) collective-permute-start(bf16[64,2048]{1,0:T(8,128)(2,1)} %get-tuple-element.46), channel_id=1, source_target_pairs={{0,3},{1,2},{2,1},{3,0},{4,7},{5,6},{6,5},{7,4},{8,11},{9,10},{10,... | collective-permute-start | bytes 786440 | tf_op jit(solution)/shard_map/ppermute | solution.py:463
  9.3 31.6 %collective-permute-start.6 = (bf16[64,2048]{1,0:T(8,128)(2,1)}, bf16[64,2048]{1,0:T(8,128)(2,1)S(1)}, u32[]{:S(2)}, u32[]{:S(2)}) collective-permute-start(bf16[64,2048]{1,0:T(8,128)(2,1)} %get-tuple-element.52), channel_id=1, source_target_pairs={{0,1},{1,0},{2,3},{3,2},{4,5},{5,4},{6,7},{7,6},{8,9},{9,8},{10,11... | collective-permute-start | bytes 786440 | tf_op jit(solution)/shard_map/ppermute | solution.py:463
  10.2 40.6 %collective-permute-start.7 = (bf16[64,2048]{1,0:T(8,128)(2,1)}, bf16[64,2048]{1,0:T(8,128)(2,1)S(1)}, u32[]{:S(2)}, u32[]{:S(2)}) collective-permute-start(bf16[64,2048]{1,0:T(8,128)(2,1)} %get-tuple-element.53), channel_id=1, source_target_pairs={{0,2},{1,3},{2,0},{3,1},{4,6},{5,7},{6,4},{7,5},{8,10},{9,11},{10,... | collective-permute-start | bytes 786440 | tf_op jit(solution)/shard_map/ppermute | solution.py:463
  18.9 31.9 %collective-permute-start.8 = (bf16[64,2048]{1,0:T(8,128)(2,1)}, bf16[64,2048]{1,0:T(8,128)(2,1)S(1)}, u32[]{:S(2)}, u32[]{:S(2)}) collective-permute-start(bf16[64,2048]{1,0:T(8,128)(2,1)} %get-tuple-element.54), channel_id=1, source_target_pairs={{0,3},{1,2},{2,1},{3,0},{4,7},{5,6},{6,5},{7,4},{8,11},{9,10},{10,... | collective-permute-start | bytes 786440 | tf_op jit(solution)/shard_map/ppermute | solution.py:463
  28.3 1.9 %copy-start = (bf16[1,768,2048]{2,1,0:T(8,128)(2,1)S(1)}, bf16[1,768,2048]{2,1,0:T(8,128)(2,1)}, u32[]{:S(2)}) copy-start(bf16[1,768,2048]{2,1,0:T(8,128)(2,1)} %refs_4_.3) | copy-start | bytes 9437188
  30.2 1.9 %copy-start.2 = (bf16[1,2048,768]{2,1,0:T(8,128)(2,1)S(1)}, bf16[1,2048,768]{2,1,0:T(8,128)(2,1)}, u32[]{:S(2)}) copy-start(bf16[1,2048,768]{2,1,0:T(8,128)(2,1)} %refs_1_.1) | copy-start | bytes 9437188
  32.1 1.9 %copy-start.4 = (bf16[1,2048,768]{2,1,0:T(8,128)(2,1)S(1)}, bf16[1,2048,768]{2,1,0:T(8,128)(2,1)}, u32[]{:S(2)}) copy-start(bf16[1,2048,768]{2,1,0:T(8,128)(2,1)} %refs_2_.1) | copy-start | bytes 9437188
  34.0 0.9 copy-start.7
  35.0 15.8 %copy-start.1 = (bf16[1,768,2048]{2,1,0:T(8,128)(2,1)S(1)}, bf16[1,768,2048]{2,1,0:T(8,128)(2,1)}, u32[]{:S(2)}) copy-start(bf16[1,768,2048]{2,1,0:T(8,128)(2,1)} %refs_4_.3) | copy-start | bytes 9437188
  39.9 10.9 %copy-start.8 = (bf16[64,2048]{1,0:T(8,128)(2,1)S(1)}, bf16[64,2048]{1,0:T(8,128)(2,1)}, u32[]{:S(2)}) copy-start(bf16[64,2048]{1,0:T(8,128)(2,1)} %get-tuple-element.51.refs_0_) | copy-start | bytes 786436
  52.5 4.9 %collective-permute-start.11 = (bf16[256,2048]{1,0:T(8,128)(2,1)S(1)}, bf16[256,2048]{1,0:T(8,128)(2,1)S(1)}, u32[]{:S(2)}, u32[]{:S(2)}) collective-permute-start(bf16[256,2048]{1,0:T(8,128)(2,1)S(1)} %get-tuple-element.61.own_g_ref), channel_id=1, source_target_pairs={{0,4},{4,0},{8,12},{12,8},{16,20},{20,16},{24,28},{28,24},{1,5},{5... | collective-permute-start | bytes 3145736 | tf_op jit(solution)/shard_map/ppermute | solution.py:394
  52.6 4.8 %collective-permute-start.10 = (bf16[512,768]{1,0:T(8,128)(2,1)S(1)}, bf16[512,768]{1,0:T(8,128)(2,1)S(1)}, u32[]{:S(2)}, u32[]{:S(2)}) collective-permute-start(bf16[512,768]{1,0:T(8,128)(2,1)S(1)} %get-tuple-element.59.own_ref.refs_0_), channel_id=1, source_target_pairs={{0,4},{4,0},{8,12},{12,8},{16,20},{20,16},{24,28},{28,24},{1,5},{5... | collective-permute-start | bytes 2359304 | tf_op jit(solution)/shard_map/ppermute | solution.py:394
  53.1 4.3 %collective-permute-start.9 = (bf16[1408,256]{1,0:T(8,128)(2,1)S(1)}, bf16[1408,256]{1,0:T(8,128)(2,1)S(1)}, u32[]{:S(2)}, u32[]{:S(2)}) collective-permute-start(bf16[1408,256]{1,0:T(8,128)(2,1)S(1)} %get-tuple-element.60), channel_id=1, source_target_pairs={{0,4},{4,0},{8,12},{12,8},{16,20},{20,16},{24,28},{28,24},{1,5},{5... | collective-permute-start | bytes 2162696 | tf_op jit(solution)/shard_map/ppermute | solution.py:394
  57.4 16.6 %copy-start.3 = (bf16[1,2048,768]{2,1,0:T(8,128)(2,1)S(1)}, bf16[1,2048,768]{2,1,0:T(8,128)(2,1)}, u32[]{:S(2)}) copy-start(bf16[1,2048,768]{2,1,0:T(8,128)(2,1)} %refs_1_.1) | copy-start | bytes 9437188
  57.4 16.6 %copy-start.5 = (bf16[1,2048,768]{2,1,0:T(8,128)(2,1)S(1)}, bf16[1,2048,768]{2,1,0:T(8,128)(2,1)}, u32[]{:S(2)}) copy-start(bf16[1,2048,768]{2,1,0:T(8,128)(2,1)} %refs_2_.1) | copy-start | bytes 9437188
  60.9 32.0 %collective-permute-start.16 = (bf16[2,384,768]{2,1,0:T(8,128)(2,1)S(1)}, bf16[2,384,768]{2,1,0:T(8,128)(2,1)S(1)}, u32[]{:S(2)}, u32[]{:S(2)}) collective-permute-start(bf16[2,384,768]{2,1,0:T(8,128)(2,1)S(1)} %get-tuple-element.72), channel_id=1, source_target_pairs={{0,16},{4,20},{8,24},{12,28},{16,0},{20,4},{24,8},{28,12},{1,17},{... | collective-permute-start | bytes 3538952 | tf_op jit(solution)/shard_map/ppermute | solution.py:394
  62.4 30.5 %collective-permute-start.15 = (bf16[2,384,768]{2,1,0:T(8,128)(2,1)S(1)}, bf16[2,384,768]{2,1,0:T(8,128)(2,1)S(1)}, u32[]{:S(2)}, u32[]{:S(2)}) collective-permute-start(bf16[2,384,768]{2,1,0:T(8,128)(2,1)S(1)} %get-tuple-element.62.refs_3_), channel_id=1, source_target_pairs={{0,8},{4,12},{8,0},{12,4},{16,24},{20,28},{24,16},{28,20},{1,9},{5... | collective-permute-start | bytes 3538952 | tf_op jit(solution)/shard_map/ppermute | solution.py:394
  63.9 18.3 %collective-permute-start.3 = (bf16[64,2048]{1,0:T(8,128)(2,1)S(1)}, bf16[64,2048]{1,0:T(8,128)(2,1)S(1)}, u32[]{:S(2)}, u32[]{:S(2)}) collective-permute-start(bf16[64,2048]{1,0:T(8,128)(2,1)S(1)} %get-tuple-element.48), channel_id=1, source_target_pairs={{0,1},{1,0},{2,3},{3,2},{4,5},{5,4},{6,7},{7,6},{8,9},{9,8},{10,11... | collective-permute-start | bytes 786440 | tf_op jit(solution)/shard_map/ppermute | solution.py:463
  71.5 21.4 %collective-permute-start.4 = (bf16[64,2048]{1,0:T(8,128)(2,1)S(1)}, bf16[64,2048]{1,0:T(8,128)(2,1)S(1)}, u32[]{:S(2)}, u32[]{:S(2)}) collective-permute-start(bf16[64,2048]{1,0:T(8,128)(2,1)S(1)} %get-tuple-element.49), channel_id=1, source_target_pairs={{0,2},{1,3},{2,0},{3,1},{4,6},{5,7},{6,4},{7,5},{8,10},{9,11},{10,... | collective-permute-start | bytes 786440 | tf_op jit(solution)/shard_map/ppermute | solution.py:463
  72.5 20.4 %collective-permute-start.5 = (bf16[64,2048]{1,0:T(8,128)(2,1)S(1)}, bf16[64,2048]{1,0:T(8,128)(2,1)S(1)}, u32[]{:S(2)}, u32[]{:S(2)}) collective-permute-start(bf16[64,2048]{1,0:T(8,128)(2,1)S(1)} %get-tuple-element.50), channel_id=1, source_target_pairs={{0,3},{1,2},{2,1},{3,0},{4,7},{5,6},{6,5},{7,4},{8,11},{9,10},{10,... | collective-permute-start | bytes 786440 | tf_op jit(solution)/shard_map/ppermute | solution.py:463
  92.9 28.8 %copy-start.6 = (bf16[128,2048]{1,0:T(8,128)(2,1)S(1)}, bf16[128,2048]{1,0:T(8,128)(2,1)}, u32[]{:S(2)}) copy-start(bf16[128,2048]{1,0:T(8,128)(2,1)} %grad_ref.3) | copy-start | bytes 1572868
  92.9 28.8 %copy-start.9 = (s32[128,2]{0,1:T(2,128)S(1)}, s32[128,2]{0,1:T(2,128)}, u32[]{:S(2)}) copy-start(s32[128,2]{0,1:T(2,128)} %param.8) | copy-start | bytes 3076
  92.9 28.8 %copy-start.10 = (f32[128,2]{0,1:T(2,128)S(1)}, f32[128,2]{0,1:T(2,128)}, u32[]{:S(2)}) copy-start(f32[128,2]{0,1:T(2,128)} %param.9) | copy-start | bytes 3076
  93.5 31.4 %collective-permute-start.17 = (bf16[384,768]{1,0:T(8,128)(2,1)S(1)}, bf16[384,768]{1,0:T(8,128)(2,1)S(1)}, u32[]{:S(2)}, u32[]{:S(2)}) collective-permute-start(bf16[384,768]{1,0:T(8,128)(2,1)S(1)} %get-tuple-element.74), channel_id=1, source_target_pairs={{0,16},{4,20},{8,24},{12,28},{16,0},{20,4},{24,8},{28,12},{1,17},{... | collective-permute-start | bytes 1769480 | tf_op jit(solution)/shard_map/ppermute | solution.py:394
  94.1 30.8 %collective-permute-start.18 = (bf16[384,768]{1,0:T(8,128)(2,1)S(1)}, bf16[384,768]{1,0:T(8,128)(2,1)S(1)}, u32[]{:S(2)}, u32[]{:S(2)}) collective-permute-start(bf16[384,768]{1,0:T(8,128)(2,1)S(1)} %get-tuple-element.76), channel_id=1, source_target_pairs={{0,8},{4,12},{8,0},{12,4},{16,24},{20,28},{24,16},{28,20},{1,9},{5... | collective-permute-start | bytes 1769480 | tf_op jit(solution)/shard_map/ppermute | solution.py:394
  94.6 14.7 %collective-permute-start.12 = (bf16[64,2048]{1,0:T(8,128)(2,1)S(1)}, bf16[64,2048]{1,0:T(8,128)(2,1)S(1)}, u32[]{:S(2)}, u32[]{:S(2)}) collective-permute-start(bf16[64,2048]{1,0:T(8,128)(2,1)S(1)} %get-tuple-element.64), channel_id=1, source_target_pairs={{0,1},{1,0},{2,3},{3,2},{4,5},{5,4},{6,7},{7,6},{8,9},{9,8},{10,11... | collective-permute-start | bytes 786440 | tf_op jit(solution)/shard_map/ppermute | solution.py:463
  100.4 21.4 %collective-permute-start.13 = (bf16[64,2048]{1,0:T(8,128)(2,1)S(1)}, bf16[64,2048]{1,0:T(8,128)(2,1)S(1)}, u32[]{:S(2)}, u32[]{:S(2)}) collective-permute-start(bf16[64,2048]{1,0:T(8,128)(2,1)S(1)} %get-tuple-element.65), channel_id=1, source_target_pairs={{0,2},{1,3},{2,0},{3,1},{4,6},{5,7},{6,4},{7,5},{8,10},{9,11},{10,... | collective-permute-start | bytes 786440 | tf_op jit(solution)/shard_map/ppermute | solution.py:463
  101.4 20.4 %collective-permute-start.14 = (bf16[64,2048]{1,0:T(8,128)(2,1)S(1)}, bf16[64,2048]{1,0:T(8,128)(2,1)S(1)}, u32[]{:S(2)}, u32[]{:S(2)}) collective-permute-start(bf16[64,2048]{1,0:T(8,128)(2,1)S(1)} %get-tuple-element.66), channel_id=1, source_target_pairs={{0,3},{1,2},{2,1},{3,0},{4,7},{5,6},{6,5},{7,4},{8,11},{9,10},{10,... | collective-permute-start | bytes 786440 | tf_op jit(solution)/shard_map/ppermute | solution.py:463

commit v3 on v2

--- a/solution.py
+++ b/solution.py
@@ -36,7 +36,7 @@
     return pl.BlockSpec(memory_space=pltpu.SMEM)
 
 
-def params(limit=28):
+def params(limit=16):
     return pltpu.CompilerParams(vmem_limit_bytes=limit * MIB)
 
 
@@ -188,7 +188,7 @@
             pltpu.VMEM((steps, tile, width), BF),
             pltpu.SemaphoreType.DMA((3, steps)),
         ],
-        compiler_params=params(),
+        compiler_params=params(50),
         cost_estimate=cost(6 * rows * width * ff, 6 * width * ff + 4 * rows * width + 10 * rows * ff),
         name="forward",
     )(*xs, w_gate, w_up, w_down)
@@ -196,7 +196,9 @@
 
 def turn_kernel(n, parts, me_ref, *refs):
     x_refs = refs[:n]
-    hid_ref, keep_ref, send_ref, rows, turned = refs[n:]
+    hid_ref, w_ref, keep_ref, send_ref, copy_ref, rows, turned, sem = refs[n:]
+    load = pltpu.make_async_copy(w_ref, copy_ref, sem)
+    load.start()
     for k in range(n):
         rows[k * CAP : (k + 1) * CAP, :] = x_refs[k][...]
     turned[...] = hid_ref[...].T
@@ -211,9 +213,10 @@
             at = pl.multiple_of(me_ref[rel] * h_size + j * strip, strip)
             base = half * x_size + ((j % 3) * 2 * half + 2 * i + j // 3) * strip
             out_ref[base : base + strip, :] = turned[pl.ds(at, strip), :]
-
-
-def turn(parts, owners, xs, hidden):
+    load.wait()
+
+
+def turn(parts, owners, xs, hidden, w_down):
     n = len(xs)
     width = xs[0].shape[1]
     rows, ff = hidden.shape
@@ -221,14 +224,14 @@
     return pl.pallas_call(
         functools.partial(turn_kernel, n, parts),
         grid=(1,),
-        out_shape=[shape_of((high, rows))] * 2,
-        in_specs=[in_smem()] + [whole((CAP, width))] * n + [whole(hidden.shape)],
-        out_specs=[whole((high, rows))] * 2,
-        scratch_shapes=[pltpu.VMEM((rows, width), BF), pltpu.VMEM((ff, rows), BF)],
+        out_shape=[shape_of((high, rows))] * 2 + [shape_of(w_down.shape)],
+        in_specs=[in_smem()] + [whole((CAP, width))] * n + [whole(hidden.shape), pl.BlockSpec(memory_space=pltpu.HBM)],
+        out_specs=[whole((high, rows))] * 2 + [whole(w_down.shape)],
+        scratch_shapes=[pltpu.VMEM((rows, width), BF), pltpu.VMEM((ff, rows), BF), pltpu.SemaphoreType.DMA],
         compiler_params=params(),
         cost_estimate=cost(2 * rows * width, 6 * rows * (width + ff)),
         name="turn",
-    )(owners, *xs, hidden)
+    )(owners, *xs, hidden, w_down)
 
 
 def outer_kernel(keep_ref, recv_ref, own_ref, other_ref, own_g_ref, other_g_ref, x_send, x_keep, y_send, y_keep):
@@ -259,23 +262,25 @@
                 ]
 
 
-def outer(keep, recv, own, other, own_g, other_g):
+def outer(keep, recv, own, other, own_g, other_g, after):
     rows, width = own_g.shape
     ff = own.shape[1]
     tile = 256
     col = pl.BlockSpec((2 * rows, tile), lambda j: (0, j))
     high = 256 + 16 * (width // tile)
     part = pl.BlockSpec((2, high, tile), lambda j: (0, 0, j))
-    return pl.pallas_call(
+    return call(
         outer_kernel,
+        after,
         grid=(ff // tile,),
         out_shape=[shape_of((2, high, ff))] * 4,
         in_specs=[whole(keep.shape)] * 2 + [col] * 2 + [whole(own_g.shape)] * 2,
+        args=(keep, recv, own, other, own_g, other_g),
         out_specs=[part] * 4,
         compiler_params=params(),
         cost_estimate=cost(6 * rows * width * ff, 4 * keep.size + 16 * high * ff),
         name="outer",
-    )(keep, recv, own, other, own_g, other_g)
+    )
 
 
 def hidden_grad_kernel(n, *refs):
@@ -312,29 +317,64 @@
     )
 
 
-def input_grad_kernel(n, grad_ref, wg_ref, wu_ref, *out_refs):
+def input_grad_kernel(n, steps, tile, z_ref, grad_ref, wg_ref, wu_ref, *refs):
+    out_ref, wg_buf, wu_buf, sems = refs
+    step = pl.program_id(0)
+
+    def loads(j):
+        at = pl.ds(pl.multiple_of(j * tile, tile), tile)
+        return (
+            pltpu.make_async_copy(wg_ref.at[0, at, :], wg_buf.at[j], sems.at[0, j]),
+            pltpu.make_async_copy(wu_ref.at[0, at, :], wu_buf.at[j], sems.at[1, j]),
+        )
+
+    @pl.when(step == 0)
+    def _():
+        for j in range(steps):
+            for load in loads(j):
+                load.start()
+
+    for load in loads(step):
+        load.wait()
     rows = n * CAP
-    total = mm_cols(grad_ref[:rows, :], wg_ref[0]) + mm_cols(grad_ref[rows:, :], wu_ref[0])
+    total = mm_cols(grad_ref[:rows, :], wg_buf[step]) + mm_cols(grad_ref[rows:, :], wu_buf[step])
     for k in range(n):
-        out_refs[k][...] = total[k * CAP : (k + 1) * CAP, :].astype(BF)
-
-
-def input_grad(n, grad, w_gate, w_up, after):
+        partner = jnp.bitwise_xor(z_ref[0], k)
+        out_ref[partner] = total[k * CAP : (k + 1) * CAP, :].astype(BF)
+
+
+def input_grad(z, n, grad, w_gate, w_up):
     rows, ff = n * CAP, grad.shape[1]
     width = w_gate.shape[1]
     tile = 512
-    by_row = pl.BlockSpec((1, tile, ff), lambda j: (0, j, 0))
-    return call(
-        functools.partial(input_grad_kernel, n),
-        after,
-        grid=(width // tile,),
-        out_shape=[shape_of((CAP, width))] * n,
-        in_specs=[whole((2 * rows, ff)), by_row, by_row],
-        args=(grad, w_gate, w_up),
-        out_specs=[pl.BlockSpec((CAP, tile), lambda j: (0, j))] * n,
+    steps = width // tile
+    return pl.pallas_call(
+        functools.partial(input_grad_kernel, n, steps, tile),
+        grid=(steps,),
+        out_shape=shape_of((n, CAP, width)),
+        in_specs=[in_smem(), whole((2 * rows, ff))] + [pl.BlockSpec(memory_space=pltpu.HBM)] * 2,
+        out_specs=pl.BlockSpec((n, CAP, tile), lambda j: (0, 0, j)),
+        scratch_shapes=[pltpu.VMEM((steps, tile, ff), BF)] * 2 + [pltpu.SemaphoreType.DMA((2, steps))],
         compiler_params=params(),
         cost_estimate=cost(4 * rows * width * ff, 4 * width * ff + 2 * rows * (width + 2 * ff)),
         name="input_grad",
+    )(z, grad, w_gate, w_up)
+
+
+def hold_kernel(_, __):
+    pass
+
+
+def hold(value, after):
+    return call(
+        hold_kernel,
+        after,
+        [pl.BlockSpec(memory_space=pl.ANY)],
+        [value],
+        out_shape=shape_of(value.shape),
+        out_specs=pl.BlockSpec(memory_space=pl.ANY),
+        input_output_aliases={0: 0},
+        name="hold",
     )
 
 
@@ -373,18 +413,20 @@
                 ]
 
 
-def fold_last(x_mine, x_recv, y_mine, y_recv, shapes):
+def fold_last(x_mine, x_recv, y_mine, y_recv, shapes, after):
     high, width = x_mine.shape
-    return pl.pallas_call(
+    return call(
         fold_last_kernel,
+        after,
         grid=(1,),
         out_shape=[shape_of(s) for s in shapes],
         in_specs=[whole((high, width))] * 4,
+        args=(x_mine, x_recv, y_mine, y_recv),
         out_specs=[whole(s) for s in shapes],
         compiler_params=params(),
         cost_estimate=cost(2 * high * width, 12 * high * width),
         name="fold_last",
-    )(x_mine, x_recv, y_mine, y_recv)
+    )
 
 
 CORE, ALONG_X, ALONG_Y = 1, 2, 4
@@ -395,8 +437,8 @@
 
 
 def combine_kernel(n, z_ref, ids_ref, prob_ref, grad_ref, *refs):
-    out_back_refs, in_back_refs = refs[:n], refs[n : 2 * n]
-    out_ref, in_ref, prob_grad_ref, out_rows, in_rows, sums, firsts, seconds = refs[2 * n :]
+    out_back_refs, in_back_ref = refs[:n], refs[n]
+    out_ref, in_ref, prob_grad_ref, out_rows, in_rows, sums, firsts, seconds = refs[n + 1 :]
     tok_count = ids_ref.shape[1]
     step = pl.program_id(0)
 
@@ -414,8 +456,9 @@
         sums[...] = jnp.zeros_like(sums)
 
     for k in range(n):
+        partner = jnp.bitwise_xor(z_ref[0], k)
         out_rows[k * CAP : (k + 1) * CAP, :] = out_back_refs[k][...]
-        in_rows[k * CAP : (k + 1) * CAP, :] = in_back_refs[k][...]
+        in_rows[k * CAP : (k + 1) * CAP, :] = in_back_ref[partner]
     prob = jnp.concatenate([prob_ref[...], jnp.zeros((6, tok_count), F32)], axis=0).T
     grad = grad_ref[...].astype(F32)
     one, two = firsts[...].astype(BF), seconds[...].astype(BF)
@@ -435,7 +478,7 @@
 
 
 def combine(z, ids_t, prob_t, out_grad, back_out, back_in):
-    n = len(back_in)
+    n = len(back_out)
     tok_count, width = out_grad.shape
     tile = 512
     by_tile = pl.BlockSpec((tok_count, tile), lambda j: (0, j))
@@ -445,7 +488,8 @@
         grid=(width // tile,),
         out_shape=[shape_of((tok_count, width))] * 2 + [shape_of((2, tok_count), F32)],
         in_specs=[in_smem(), whole(ids_t.shape), whole(prob_t.shape), by_tile]
-        + [pl.BlockSpec((CAP, tile), lambda j: (0, j))] * (2 * n),
+        + [pl.BlockSpec((CAP, tile), lambda j: (0, j))] * n
+        + [pl.BlockSpec((n, CAP, tile), lambda j: (0, 0, j))],
         out_specs=[by_tile, by_tile, whole((2, tok_count))],
         scratch_shapes=[pltpu.VMEM((rows, tile), BF)] * 2
         + [pltpu.VMEM((tok_count, 8), F32)]
@@ -453,7 +497,7 @@
         compiler_params=params(),
         cost_estimate=cost(6 * rows * tok_count * width, 4 * width * (rows + 2 * tok_count)),
         name="combine",
-    )(z, ids_t, prob_t, out_grad, *back_out, *back_in)
+    )(z, ids_t, prob_t, out_grad, *back_out, back_in)
 
 
 def exchange(values):
@@ -478,26 +522,32 @@
         me = lax.axis_index("dp").astype(jnp.int32)
         flips = [(r >> 2 & 1) * CORE | (r & 1) * ALONG_X | (r >> 1 & 1) * ALONG_Y for r in range(8)]
         owners = jnp.stack([me ^ f for f in flips])
-        keep_t, send_t = turn(parts, owners, xs, hidden)
-        grad, g_rows = hidden_grad(gs, w_down, slope, act, [keep_t])
+        keep_t, send_t, w_near = turn(parts, owners, xs, hidden, w_down)
+        grad, g_rows = hidden_grad(gs, w_near, slope, act, [])
+        din = input_grad(z, n, grad, w_gate, w_up)
         x_send, x_keep, y_send, y_keep = outer(
-            keep_t, swap(send_t, CORE), grad, swap(grad, CORE), g_rows, swap(g_rows, CORE)
+            keep_t, swap(send_t, CORE), grad, swap(grad, CORE), g_rows, swap(g_rows, CORE), []
         )
-        back_in = exchange(input_grad(n, grad, w_gate, w_up, [x_send]))
+        din = hold(din, back_out[1:])
+        back_in = lax.all_to_all(din, "expert", split_axis=0, concat_axis=0, tiled=True)
         x_next, x_mine, y_next, y_mine = fold_two(
-            x_keep, swap(x_send, ALONG_X), y_keep, swap(y_send, ALONG_Y), [back_in[0], *back_out[1:]]
+            x_keep, swap(x_send, ALONG_X), y_keep, swap(y_send, ALONG_Y), [din]
         )
+        layer_out, token_grad, prob_grad_t = combine(z, ids_t, prob_t, out_grad, back_out, back_in)
         shapes = [(1, d // parts, w) for d, w in (w_gate.shape[1:], w_up.shape[1:], w_down.shape[1:])]
-        sum_gate, sum_up, sum_down = fold_last(x_mine, swap(x_next, ALONG_Y), y_mine, swap(y_next, ALONG_X), shapes)
+        sum_gate, sum_up, sum_down = fold_last(
+            x_mine, swap(x_next, ALONG_Y), y_mine, swap(y_next, ALONG_X), shapes, [token_grad]
+        )
     else:
         grad, d_rows = hidden_grad(gs, w_down, slope, act, [])
-        back_in = exchange(input_grad(n, grad, w_gate, w_up, []))
+        din = input_grad(z, n, grad, w_gate, w_up)
+        back_in = lax.all_to_all(din, "expert", split_axis=0, concat_axis=0, tiled=True)
+        layer_out, token_grad, prob_grad_t = combine(z, ids_t, prob_t, out_grad, back_out, back_in)
         x_rows, count = jnp.concatenate(xs, 0), n * CAP
         sum_gate, sum_up, sum_down = (
             lax.psum_scatter(mm_rows(a, b).astype(BF), "dp", scatter_dimension=0, tiled=True)[None]
             for a, b in ((x_rows, grad[:count]), (x_rows, grad[count:]), (hidden, d_rows))
         )
-    layer_out, token_grad, prob_grad_t = combine(z, ids_t, prob_t, out_grad, back_out, back_in)
     return layer_out, prob_grad_t.T, token_grad, sum_gate, sum_up, sum_down
 
 

time: 127 us -> 122 us (0.961)
  waiting for transfers between devices: 59.4 us -> 44.7 us
  Pallas kernels: 21.5 us -> 28.1 us
  local copies, waits for them, and re-layouts: 6.74 us -> 12 us
  starting transfers between devices: 37.7 us -> 35.4 us
    ppermute x12 -> x9, waiting for transfers between devices: 55.1 us -> 30.8 us  [exchange(): moved[k] = lax.ppermute(values[k], 'expert', [(i, i ^ k) for i in range(n)])]
    ppermute x12 -> x9, starting transfers between devices: 32.9 us -> 21.8 us  [exchange(): moved[k] = lax.ppermute(values[k], 'expert', [(i, i ^ k) for i in range(n)])]
    all_to_all x0 -> x1, waiting for transfers between devices: none -> 8.34 us  [local(): lax.all_to_all(din, 'expert', split_axis=0, concat_axis=0, tiled=True)]
    all_to_all x0 -> x1, starting transfers between devices: none -> 7.13 us  [local(): lax.all_to_all(din, 'expert', split_axis=0, concat_axis=0, tiled=True)]
    pallas_call x3 -> x5, Pallas kernels: 4.78 us -> 10.8 us  [call(): return pl.pallas_call(body, in_specs=specs, **kwargs)(*args, *after)]
    unnamed x22 -> x58, local copies, waits for them, and re-layouts: 6.66 us -> 11.9 us
    pallas_call x1, Pallas kernels: 4.94 us -> 7 us  [forward(): pl.pallas_call(functools.partial(forward_kernel, n, steps, tile), grid=(s...]
    ppermute x7, starting transfers between devices: 4.83 us -> 6.42 us  [swap(): return lax.ppermute(value, 'dp', [(i, i ^ bit) for i in range(count)])]
  transfers between devices with their start and end apart: 19 -> 17, of which waited for: 8 -> 8; matrix products, arithmetic and copies ran while one was open for 0% -> 0% of each run, Pallas kernels for 9% -> 17%
where the time goes in v3:
time: 122 us; the launch traced here: 121 us
  waiting for transfers between devices  44.7 us (37%)
  starting transfers between devices  35.4 us (29%)
  Pallas kernels  28.1 us (23%)
  local copies, waits for them, and re-layouts  12 us (10%)
    ppermute x9, waiting for transfers between devices, exchange(): moved[k] = lax.ppermute(values[k], 'expert', [(i, i ^ k) for i in range(n)])  30.8 us
    ppermute x9, starting transfers between devices, exchange(): moved[k] = lax.ppermute(values[k], 'expert', [(i, i ^ k) for i in range(n)])  21.8 us
    unnamed x58, local copies, waits for them, and re-layouts  11.9 us
    pallas_call x5, Pallas kernels, call(): return pl.pallas_call(body, in_specs=specs, **kwargs)(*args, *after)  10.8 us
    all_to_all x1, waiting for transfers between devices, local(): lax.all_to_all(din, 'expert', split_axis=0, concat_axis=0, tiled=True)  8.34 us
    all_to_all x1, starting transfers between devices, local(): lax.all_to_all(din, 'expert', split_axis=0, concat_axis=0, tiled=True)  7.13 us
    pallas_call x1, Pallas kernels, forward(): pl.pallas_call(functools.partial(forward_kernel, n, steps, tile), grid=(s...  7 us
    ppermute x7, starting transfers between devices, swap(): return lax.ppermute(value, 'dp', [(i, i ^ bit) for i in range(count)])  6.42 us
  transfers between devices with their start and end apart: 17, of which 8 were waited for; matrix products, arithmetic and copies ran while one was open for 0% of the time, Pallas kernels for 17%

profile of v3, /device:TPU:0, one launch (start us, length us, event | category | flops | bytes accessed | tf_op | source)
XLA Modules:
  0.0 121.0 jit_solution(7743760689184586429)
XLA Ops:
  0.6 3.0 %pick_rows.1 = (bf16[64,2048]{1,0:T(8,128)(2,1)}, bf16[64,2048]{1,0:T(8,128)(2,1)}, bf16[64,2048]{1,0:T(8,128)(2,1)}, bf16[64,2048]{1,0:T(8,128)(2,1)}, bf16[64,...) custom-call(s32[1]{0:T(128)} %bitcast.z_ref, ...), custom_call_target="tpu_custom_call" | custom-call | flops 268435456 | bytes 3145728 | tf_op jit(solution)/shard_map/pick_rows/pallas_call | solution.py:97
  3.7 3.0 %collective-permute-start = (bf16[64,2048]{1,0:T(8,128)(2,1)}, bf16[64,2048]{1,0:T(8,128)(2,1)S(1)}, u32[]{:S(2)}, u32[]{:S(2)}) collective-permute-start(bf16[64,2048]{1,0:T(8,128)(2,1)} %get-tuple-element.41), channel_id=1, source_target_pairs={{0,1},{1,0},{2,3},{3,2},{4,5},{5,4},{6,7},{7,6},{8,9},{9,8},{10,11... | collective-permute-start | bytes 786440 | tf_op jit(solution)/shard_map/ppermute | solution.py:507
  6.7 2.6 %collective-permute-start.1 = (bf16[64,2048]{1,0:T(8,128)(2,1)}, bf16[64,2048]{1,0:T(8,128)(2,1)S(1)}, u32[]{:S(2)}, u32[]{:S(2)}) collective-permute-start(bf16[64,2048]{1,0:T(8,128)(2,1)} %get-tuple-element.42), channel_id=1, source_target_pairs={{0,2},{1,3},{2,0},{3,1},{4,6},{5,7},{6,4},{7,5},{8,10},{9,11},{10,... | collective-permute-start | bytes 786440 | tf_op jit(solution)/shard_map/ppermute | solution.py:507
  10.2 3.5 %collective-permute-start.7 = (bf16[64,2048]{1,0:T(8,128)(2,1)}, bf16[64,2048]{1,0:T(8,128)(2,1)S(1)}, u32[]{:S(2)}, u32[]{:S(2)}) collective-permute-start(bf16[64,2048]{1,0:T(8,128)(2,1)} %get-tuple-element.50), channel_id=1, source_target_pairs={{0,2},{1,3},{2,0},{3,1},{4,6},{5,7},{6,4},{7,5},{8,10},{9,11},{10,... | collective-permute-start | bytes 786440 | tf_op jit(solution)/shard_map/ppermute | solution.py:507
  13.7 5.2 %collective-permute-done.refs_1_ = bf16[64,2048]{1,0:T(8,128)(2,1)S(1)} collective-permute-done((bf16[64,2048]{1,0:T(8,128)(2,1)}, bf16[64,2048]{1,0:T(8,128)(2,1)S(1)}, u32[]{:S(2)}, u32[]{:S(2)}) %collective-permute-start) | collective-permute-done | bytes 262176 | tf_op jit(solution)/shard_map/ppermute | solution.py:507
  18.9 4.6 %collective-permute-start.8 = (bf16[64,2048]{1,0:T(8,128)(2,1)}, bf16[64,2048]{1,0:T(8,128)(2,1)S(1)}, u32[]{:S(2)}, u32[]{:S(2)}) collective-permute-start(bf16[64,2048]{1,0:T(8,128)(2,1)} %get-tuple-element.51), channel_id=1, source_target_pairs={{0,3},{1,2},{2,1},{3,0},{4,7},{5,6},{6,5},{7,4},{8,11},{9,10},{10,... | collective-permute-start | bytes 786440 | tf_op jit(solution)/shard_map/ppermute | solution.py:507
  23.6 4.8 %collective-permute-done.1.refs_2_ = bf16[64,2048]{1,0:T(8,128)(2,1)S(1)} collective-permute-done((bf16[64,2048]{1,0:T(8,128)(2,1)}, bf16[64,2048]{1,0:T(8,128)(2,1)S(1)}, u32[]{:S(2)}, u32[]{:S(2)}) %collective-permute-start.1) | collective-permute-done | bytes 262176 | tf_op jit(solution)/shard_map/ppermute | solution.py:507
  29.3 7.0 %forward.1 = (f32[256,768]{1,0:T(8,128)S(1)}, f32[256,768]{1,0:T(8,128)S(1)}, bf16[256,768]{1,0:T(8,128)(2,1)S(1)}, bf16[64,2048]{1,0:T(8,128)(2,1)S(1)}, bf16[6...) custom-call(bf16[64,2048]{1,0:T(8,128)(2,1)S(1)} %copy-done.12, ...), custom_call_target="tpu_custom_call" | custom-call | flops 2415919104 | bytes 13500416 | tf_op jit(solution)/shard_map/forward/pallas_call | solution.py:177
  36.3 1.2 turn.1
  37.6 13.2 %collective-permute-done.7.refs_2_ = bf16[64,2048]{1,0:T(8,128)(2,1)S(1)} collective-permute-done((bf16[64,2048]{1,0:T(8,128)(2,1)}, bf16[64,2048]{1,0:T(8,128)(2,1)S(1)}, u32[]{:S(2)}, u32[]{:S(2)}) %collective-permute-start.7) | collective-permute-done | bytes 262176 | tf_op jit(solution)/shard_map/ppermute | solution.py:507
  50.8 1.7 %hidden_grad.1 = (bf16[512,768]{1,0:T(8,128)(2,1)S(1)}, bf16[256,2048]{1,0:T(8,128)(2,1)S(1)}) custom-call(bf16[64,2048]{1,0:T(8,128)(2,1)S(1)} %copy-done.26, bf16[64,2048]{1,0:T(8,128)(2,1)S(1)} %collective-permute-done.6.refs_1_, bf16[64,2048]{1,0:T(8,128)(2,1)S(1)} %collective-permute-done.7.refs_2_, ...), custom_call_target="tpu_custom_call" | custom-call | flops 805306368 | bytes 7602176 | tf_op jit(solution)/shard_map/hidden_grad/pallas_call | solution.py:50
  53.2 4.7 %collective-permute-start.3 = (bf16[64,2048]{1,0:T(8,128)(2,1)S(1)}, bf16[64,2048]{1,0:T(8,128)(2,1)S(1)}, u32[]{:S(2)}, u32[]{:S(2)}) collective-permute-start(bf16[64,2048]{1,0:T(8,128)(2,1)S(1)} %get-tuple-element.45), channel_id=1, source_target_pairs={{0,1},{1,0},{2,3},{3,2},{4,5},{5,4},{6,7},{7,6},{8,9},{9,8},{10,11... | collective-permute-start | bytes 786440 | tf_op jit(solution)/shard_map/ppermute | solution.py:507
  57.9 1.0 collective-permute-start.4
  59.0 1.5 %collective-permute-start.5 = (bf16[64,2048]{1,0:T(8,128)(2,1)S(1)}, bf16[64,2048]{1,0:T(8,128)(2,1)S(1)}, u32[]{:S(2)}, u32[]{:S(2)}) collective-permute-start(bf16[64,2048]{1,0:T(8,128)(2,1)S(1)} %get-tuple-element.47), channel_id=1, source_target_pairs={{0,3},{1,2},{2,1},{3,0},{4,7},{5,6},{6,5},{7,4},{8,11},{9,10},{10,... | collective-permute-start | bytes 786440 | tf_op jit(solution)/shard_map/ppermute | solution.py:507
  60.4 4.2 %outer.1 = (bf16[2,384,768]{2,1,0:T(8,128)(2,1)}, bf16[2,384,768]{2,1,0:T(8,128)(2,1)S(1)}, bf16[2,384,768]{2,1,0:T(8,128)(2,1)}, bf16[2,384,768]{2,1,0:T(8,128)(2,1)S(1)}) custom-call(bf16[1408,256]{1,0:T(8,128)(2,1)S(1)} %get-tuple-element.60.refs_0_, bf16[1408,256]{1,0:T(8,128)(2,1)S(1)} %collective-permute-done.9.refs_1_, ...), custom_call_target="tpu_custom_call" | custom-call | flops 2415919104 | bytes 6160384 | tf_op jit(solution)/shard_map/outer/pallas_call | solution.py:50
  64.6 1.5 %collective-permute-start.12 = (bf16[2,384,768]{2,1,0:T(8,128)(2,1)}, bf16[2,384,768]{2,1,0:T(8,128)(2,1)S(1)}, u32[]{:S(2)}, u32[]{:S(2)}) collective-permute-start(bf16[2,384,768]{2,1,0:T(8,128)(2,1)} %get-tuple-element.64), channel_id=1, source_target_pairs={{0,8},{4,12},{8,0},{12,4},{16,24},{20,28},{24,16},{28,20},{1,9},{5... | collective-permute-start | bytes 3538952 | tf_op jit(solution)/shard_map/ppermute | solution.py:436
  66.1 1.5 %collective-permute-start.13 = (bf16[2,384,768]{2,1,0:T(8,128)(2,1)}, bf16[2,384,768]{2,1,0:T(8,128)(2,1)}, u32[]{:S(2)}, u32[]{:S(2)}) collective-permute-start(bf16[2,384,768]{2,1,0:T(8,128)(2,1)} %get-tuple-element.66), channel_id=1, source_target_pairs={{0,16},{4,20},{8,24},{12,28},{16,0},{20,4},{24,8},{28,12},{1,17},{... | collective-permute-start | bytes 3538952 | tf_op jit(solution)/shard_map/ppermute | solution.py:436
  67.7 3.0 %input_grad.1.refs_0_ = bf16[4,64,2048]{2,1,0:T(8,128)(2,1)S(1)} custom-call(s32[1]{0:T(128)} %bitcast.z_ref, bf16[512,768]{1,0:T(8,128)(2,1)S(1)} %get-tuple-element.56.grad_ref.refs_2_, bf16[1,2048,768]{2,1,0:T(8,128)(2,1)S(1)} %copy-done.3, bf16[1,2048,768]{2,1,0:T(8,128)(2,1)S(1)} %copy-done.4), custom_call_target="tpu_custom_call" | custom-call | flops 1610612736 | bytes 8126464 | tf_op jit(solution)/shard_map/input_grad/pallas_call | solution.py:351
  71.7 7.6 %collective-permute-done.4.refs_2_ = bf16[64,2048]{1,0:T(8,128)(2,1)S(1)} collective-permute-done((bf16[64,2048]{1,0:T(8,128)(2,1)S(1)}, bf16[64,2048]{1,0:T(8,128)(2,1)S(1)}, u32[]{:S(2)}, u32[]{:S(2)}) %collective-permute-start.4) | collective-permute-done | bytes 262176 | tf_op jit(solution)/shard_map/ppermute | solution.py:507
  80.7 7.1 %all-to-all-start = ((bf16[4,64,2048]{2,1,0:T(8,128)(2,1)}), bf16[4,64,2048]{2,1,0:T(8,128)(2,1)S(1)}, u32[]{:S(2)}, u32[]{:S(2)}) async-start(bf16[4,64,2048]{2,1,0:T(8,128)(2,1)} %hold.1.refs_4_), calls=%async_computation | async-start | bytes 2097152 | tf_op jit(solution)/shard_map/all_to_all | solution.py:532
  87.8 4.8 %collective-permute-done.12.refs_1_ = bf16[2,384,768]{2,1,0:T(8,128)(2,1)S(1)} collective-permute-done((bf16[2,384,768]{2,1,0:T(8,128)(2,1)}, bf16[2,384,768]{2,1,0:T(8,128)(2,1)S(1)}, u32[]{:S(2)}, u32[]{:S(2)}) %collective-permute-start.12) | collective-permute-done | bytes 1179680 | tf_op jit(solution)/shard_map/ppermute | solution.py:436
  92.6 1.0 copy-done.10
  93.9 1.3 %copy-done.7 = bf16[2,384,768]{2,1,0:T(8,128)(2,1)S(1)} copy-done((bf16[2,384,768]{2,1,0:T(8,128)(2,1)S(1)}, bf16[2,384,768]{2,1,0:T(8,128)(2,1)}, u32[]{:S(2)}) %copy-start.7) | copy-done | bytes 1179672
  95.2 1.3 %copy-done.9 = bf16[2,384,768]{2,1,0:T(8,128)(2,1)S(1)} copy-done((bf16[2,384,768]{2,1,0:T(8,128)(2,1)S(1)}, bf16[2,384,768]{2,1,0:T(8,128)(2,1)}, u32[]{:S(2)}) %copy-start.9) | copy-done | bytes 1179672
  96.5 1.3 %copy-done.11 = bf16[2,384,768]{2,1,0:T(8,128)(2,1)S(1)} copy-done((bf16[2,384,768]{2,1,0:T(8,128)(2,1)S(1)}, bf16[2,384,768]{2,1,0:T(8,128)(2,1)}, u32[]{:S(2)}) %copy-start.11) | copy-done | bytes 1179672
  97.8 2.6 %fold_two.1 = (bf16[384,768]{1,0:T(8,128)(2,1)}, bf16[384,768]{1,0:T(8,128)(2,1)S(1)}, bf16[384,768]{1,0:T(8,128)(2,1)}, bf16[384,768]{1,0:T(8,128)(2,1)S(1)}) custom-call(bf16[2,384,768]{2,1,0:T(8,128)(2,1)S(1)} %copy-done.7, bf16[2,384,768]{2,1,0:T(8,128)(2,1)S(1)} %copy-done.11, bf16[2,384,768]{2,1,0:T(8,128)(2,1)S(1)} %copy-done.9, ...), custom_call_target="tpu_custom_call" | custom-call | flops 1179648 | bytes 7077888 | tf_op jit(solution)/shard_map/fold_two/pallas_call | solution.py:50
  102.0 1.5 %collective-permute-start.14 = (bf16[384,768]{1,0:T(8,128)(2,1)}, bf16[384,768]{1,0:T(8,128)(2,1)S(1)}, u32[]{:S(2)}, u32[]{:S(2)}) collective-permute-start(bf16[384,768]{1,0:T(8,128)(2,1)} %get-tuple-element.68), channel_id=1, source_target_pairs={{0,16},{4,20},{8,24},{12,28},{16,0},{20,4},{24,8},{28,12},{1,17},{... | collective-permute-start | bytes 1769480 | tf_op jit(solution)/shard_map/ppermute | solution.py:436
  103.6 1.2 %collective-permute-start.15 = (bf16[384,768]{1,0:T(8,128)(2,1)}, bf16[384,768]{1,0:T(8,128)(2,1)}, u32[]{:S(2)}, u32[]{:S(2)}) collective-permute-start(bf16[384,768]{1,0:T(8,128)(2,1)} %get-tuple-element.70), channel_id=1, source_target_pairs={{0,8},{4,12},{8,0},{12,4},{16,24},{20,28},{24,16},{28,20},{1,9},{5... | collective-permute-start | bytes 1769480 | tf_op jit(solution)/shard_map/ppermute | solution.py:436
  104.8 8.3 %all-to-all-done.refs_4_ = bf16[4,64,2048]{2,1,0:T(8,128)(2,1)S(1)} async-done(((bf16[4,64,2048]{2,1,0:T(8,128)(2,1)}), bf16[4,64,2048]{2,1,0:T(8,128)(2,1)S(1)}, u32[]{:S(2)}, u32[]{:S(2)}) %all-to-all-start) | async-done | bytes 1048608 | tf_op jit(solution)/shard_map/all_to_all | solution.py:532
  114.1 3.0 %combine.1 = (bf16[128,2048]{1,0:T(8,128)(2,1)}, bf16[128,2048]{1,0:T(8,128)(2,1)}, f32[2,128]{1,0:T(2,128)}) custom-call(s32[1]{0:T(128)} %bitcast.z_ref, s32[2,128]{1,0:T(2,128)S(1)} %bitcast.13, f32[2,128]{1,0:T(2,128)S(1)} %bitcast.15, bf16[128,2048]{1,0:T(8,128)(2,1)S(1)} %copy-done.5, bf16[64,2048]{1,0:T(8,128)(2,1)S(1)} %copy-done.25, ...), custom_call_target="tpu_custom_call" | custom-call | flops 402653184 | bytes 4194304 | tf_op jit(solution)/shard_map/combine/pallas_call | solution.py:486
  117.7 1.0 copy-done.23
  118.7 2.3 %fold_last.1 = (bf16[1,256,768]{2,1,0:T(8,128)(2,1)}, bf16[1,256,768]{2,1,0:T(8,128)(2,1)}, bf16[1,96,2048]{2,1,0:T(8,128)(2,1)}) custom-call(bf16[384,768]{1,0:T(8,128)(2,1)S(1)} %copy-done.20, bf16[384,768]{1,0:T(8,128)(2,1)S(1)} %collective-permute-done.14.refs_1_, bf16[384,768]{1,0:T(8,128)(2,1)S(1)} %copy-done.22, ...), custom_call_target="tpu_custom_call" | custom-call | flops 589824 | bytes 3538944 | tf_op jit(solution)/shard_map/fold_last/pallas_call | solution.py:50
  (71 shorter events, 8.5 us)
Async XLA Ops:
  3.7 15.2 %collective-permute-start = (bf16[64,2048]{1,0:T(8,128)(2,1)}, bf16[64,2048]{1,0:T(8,128)(2,1)S(1)}, u32[]{:S(2)}, u32[]{:S(2)}) collective-permute-start(bf16[64,2048]{1,0:T(8,128)(2,1)} %get-tuple-element.41), channel_id=1, source_target_pairs={{0,1},{1,0},{2,3},{3,2},{4,5},{5,4},{6,7},{7,6},{8,9},{9,8},{10,11... | collective-permute-start | bytes 786440 | tf_op jit(solution)/shard_map/ppermute | solution.py:507
  6.7 21.6 %collective-permute-start.1 = (bf16[64,2048]{1,0:T(8,128)(2,1)}, bf16[64,2048]{1,0:T(8,128)(2,1)S(1)}, u32[]{:S(2)}, u32[]{:S(2)}) collective-permute-start(bf16[64,2048]{1,0:T(8,128)(2,1)} %get-tuple-element.42), channel_id=1, source_target_pairs={{0,2},{1,3},{2,0},{3,1},{4,6},{5,7},{6,4},{7,5},{8,10},{9,11},{10,... | collective-permute-start | bytes 786440 | tf_op jit(solution)/shard_map/ppermute | solution.py:507
  9.3 19.0 %collective-permute-start.2 = (bf16[64,2048]{1,0:T(8,128)(2,1)}, bf16[64,2048]{1,0:T(8,128)(2,1)S(1)}, u32[]{:S(2)}, u32[]{:S(2)}) collective-permute-start(bf16[64,2048]{1,0:T(8,128)(2,1)} %get-tuple-element.43), channel_id=1, source_target_pairs={{0,3},{1,2},{2,1},{3,0},{4,7},{5,6},{6,5},{7,4},{8,11},{9,10},{10,... | collective-permute-start | bytes 786440 | tf_op jit(solution)/shard_map/ppermute | solution.py:507
  9.3 28.3 %collective-permute-start.6 = (bf16[64,2048]{1,0:T(8,128)(2,1)}, bf16[64,2048]{1,0:T(8,128)(2,1)S(1)}, u32[]{:S(2)}, u32[]{:S(2)}) collective-permute-start(bf16[64,2048]{1,0:T(8,128)(2,1)} %get-tuple-element.49), channel_id=1, source_target_pairs={{0,1},{1,0},{2,3},{3,2},{4,5},{5,4},{6,7},{7,6},{8,9},{9,8},{10,11... | collective-permute-start | bytes 786440 | tf_op jit(solution)/shard_map/ppermute | solution.py:507
  10.2 40.6 %collective-permute-start.7 = (bf16[64,2048]{1,0:T(8,128)(2,1)}, bf16[64,2048]{1,0:T(8,128)(2,1)S(1)}, u32[]{:S(2)}, u32[]{:S(2)}) collective-permute-start(bf16[64,2048]{1,0:T(8,128)(2,1)} %get-tuple-element.50), channel_id=1, source_target_pairs={{0,2},{1,3},{2,0},{3,1},{4,6},{5,7},{6,4},{7,5},{8,10},{9,11},{10,... | collective-permute-start | bytes 786440 | tf_op jit(solution)/shard_map/ppermute | solution.py:507
  18.9 31.9 %collective-permute-start.8 = (bf16[64,2048]{1,0:T(8,128)(2,1)}, bf16[64,2048]{1,0:T(8,128)(2,1)S(1)}, u32[]{:S(2)}, u32[]{:S(2)}) collective-permute-start(bf16[64,2048]{1,0:T(8,128)(2,1)} %get-tuple-element.51), channel_id=1, source_target_pairs={{0,3},{1,2},{2,1},{3,0},{4,7},{5,6},{6,5},{7,4},{8,11},{9,10},{10,... | collective-permute-start | bytes 786440 | tf_op jit(solution)/shard_map/ppermute | solution.py:507
  29.3 7.0 %copy-start.2 = (bf16[1,768,2048]{2,1,0:T(8,128)(2,1)S(1)}, bf16[1,768,2048]{2,1,0:T(8,128)(2,1)}, u32[]{:S(2)}) copy-start(bf16[1,768,2048]{2,1,0:T(8,128)(2,1)} %refs_5_.3) | copy-start | bytes 9437188
  36.3 14.5 %copy-start.26 = (bf16[64,2048]{1,0:T(8,128)(2,1)S(1)}, bf16[64,2048]{1,0:T(8,128)(2,1)}, u32[]{:S(2)}) copy-start(bf16[64,2048]{1,0:T(8,128)(2,1)} %get-tuple-element.48.refs_0_) | copy-start | bytes 786436
  52.5 7.9 %collective-permute-start.11 = (bf16[256,2048]{1,0:T(8,128)(2,1)S(1)}, bf16[256,2048]{1,0:T(8,128)(2,1)S(1)}, u32[]{:S(2)}, u32[]{:S(2)}) collective-permute-start(bf16[256,2048]{1,0:T(8,128)(2,1)S(1)} %get-tuple-element.62.refs_4_), channel_id=1, source_target_pairs={{0,4},{4,0},{8,12},{12,8},{16,20},{20,16},{24,28},{28,24},{1,5},{5... | collective-permute-start | bytes 3145736 | tf_op jit(solution)/shard_map/ppermute | solution.py:436
  52.6 7.8 %collective-permute-start.10 = (bf16[512,768]{1,0:T(8,128)(2,1)S(1)}, bf16[512,768]{1,0:T(8,128)(2,1)S(1)}, u32[]{:S(2)}, u32[]{:S(2)}) collective-permute-start(bf16[512,768]{1,0:T(8,128)(2,1)S(1)} %get-tuple-element.56.grad_ref.refs_2_), channel_id=1, source_target_pairs={{0,4},{4,0},{8,12},{12,8},{16,20},{20,16},{24,28},{28,24},{1,5},{5... | collective-permute-start | bytes 2359304 | tf_op jit(solution)/shard_map/ppermute | solution.py:436
  53.1 5.8 %collective-permute-start.9 = (bf16[1408,256]{1,0:T(8,128)(2,1)S(1)}, bf16[1408,256]{1,0:T(8,128)(2,1)S(1)}, u32[]{:S(2)}, u32[]{:S(2)}) collective-permute-start(bf16[1408,256]{1,0:T(8,128)(2,1)S(1)} %get-tuple-element.61), channel_id=1, source_target_pairs={{0,4},{4,0},{8,12},{12,8},{16,20},{20,16},{24,28},{28,24},{1,5},{5... | collective-permute-start | bytes 2162696 | tf_op jit(solution)/shard_map/ppermute | solution.py:436
  53.2 18.5 %collective-permute-start.3 = (bf16[64,2048]{1,0:T(8,128)(2,1)S(1)}, bf16[64,2048]{1,0:T(8,128)(2,1)S(1)}, u32[]{:S(2)}, u32[]{:S(2)}) collective-permute-start(bf16[64,2048]{1,0:T(8,128)(2,1)S(1)} %get-tuple-element.45), channel_id=1, source_target_pairs={{0,1},{1,0},{2,3},{3,2},{4,5},{5,4},{6,7},{7,6},{8,9},{9,8},{10,11... | collective-permute-start | bytes 786440 | tf_op jit(solution)/shard_map/ppermute | solution.py:507
  57.9 21.3 %collective-permute-start.4 = (bf16[64,2048]{1,0:T(8,128)(2,1)S(1)}, bf16[64,2048]{1,0:T(8,128)(2,1)S(1)}, u32[]{:S(2)}, u32[]{:S(2)}) collective-permute-start(bf16[64,2048]{1,0:T(8,128)(2,1)S(1)} %get-tuple-element.46), channel_id=1, source_target_pairs={{0,2},{1,3},{2,0},{3,1},{4,6},{5,7},{6,4},{7,5},{8,10},{9,11},{10,... | collective-permute-start | bytes 786440 | tf_op jit(solution)/shard_map/ppermute | solution.py:507
  59.0 20.3 %collective-permute-start.5 = (bf16[64,2048]{1,0:T(8,128)(2,1)S(1)}, bf16[64,2048]{1,0:T(8,128)(2,1)S(1)}, u32[]{:S(2)}, u32[]{:S(2)}) collective-permute-start(bf16[64,2048]{1,0:T(8,128)(2,1)S(1)} %get-tuple-element.47), channel_id=1, source_target_pairs={{0,3},{1,2},{2,1},{3,0},{4,7},{5,6},{6,5},{7,4},{8,11},{9,10},{10,... | collective-permute-start | bytes 786440 | tf_op jit(solution)/shard_map/ppermute | solution.py:507
  60.4 7.2 %copy-start.3 = (bf16[1,2048,768]{2,1,0:T(8,128)(2,1)S(1)}, bf16[1,2048,768]{2,1,0:T(8,128)(2,1)}, u32[]{:S(2)}) copy-start(bf16[1,2048,768]{2,1,0:T(8,128)(2,1)} %wg_ref.1) | copy-start | bytes 9437188
  60.4 7.2 %copy-start.4 = (bf16[1,2048,768]{2,1,0:T(8,128)(2,1)S(1)}, bf16[1,2048,768]{2,1,0:T(8,128)(2,1)}, u32[]{:S(2)}) copy-start(bf16[1,2048,768]{2,1,0:T(8,128)(2,1)} %wu_ref.1) | copy-start | bytes 9437188
  64.6 6.1 %copy-start.6 = (bf16[2,384,768]{2,1,0:T(8,128)(2,1)}, bf16[2,384,768]{2,1,0:T(8,128)(2,1)S(1)}, u32[]{:S(2)}) copy-start(bf16[2,384,768]{2,1,0:T(8,128)(2,1)S(1)} %get-tuple-element.63.refs_0_) | copy-start | bytes 3538948
  64.6 6.1 %copy-start.8 = (bf16[2,384,768]{2,1,0:T(8,128)(2,1)}, bf16[2,384,768]{2,1,0:T(8,128)(2,1)S(1)}, u32[]{:S(2)}) copy-start(bf16[2,384,768]{2,1,0:T(8,128)(2,1)S(1)} %get-tuple-element.65.refs_2_) | copy-start | bytes 3538948
  64.6 28.0 %collective-permute-start.12 = (bf16[2,384,768]{2,1,0:T(8,128)(2,1)}, bf16[2,384,768]{2,1,0:T(8,128)(2,1)S(1)}, u32[]{:S(2)}, u32[]{:S(2)}) collective-permute-start(bf16[2,384,768]{2,1,0:T(8,128)(2,1)} %get-tuple-element.64), channel_id=1, source_target_pairs={{0,8},{4,12},{8,0},{12,4},{16,24},{20,28},{24,16},{28,20},{1,9},{5... | collective-permute-start | bytes 3538952 | tf_op jit(solution)/shard_map/ppermute | solution.py:436
  66.1 27.8 %collective-permute-start.13 = (bf16[2,384,768]{2,1,0:T(8,128)(2,1)}, bf16[2,384,768]{2,1,0:T(8,128)(2,1)}, u32[]{:S(2)}, u32[]{:S(2)}) collective-permute-start(bf16[2,384,768]{2,1,0:T(8,128)(2,1)} %get-tuple-element.66), channel_id=1, source_target_pairs={{0,16},{4,20},{8,24},{12,28},{16,0},{20,4},{24,8},{28,12},{1,17},{... | collective-permute-start | bytes 3538952 | tf_op jit(solution)/shard_map/ppermute | solution.py:436
  71.7 7.6 %copy-start.13 = (bf16[64,2048]{1,0:T(8,128)(2,1)}, bf16[64,2048]{1,0:T(8,128)(2,1)S(1)}, u32[]{:S(2)}) copy-start(bf16[64,2048]{1,0:T(8,128)(2,1)S(1)} %collective-permute-done.3.refs_1_) | copy-start | bytes 786436
  80.7 13.3 %copy-start.1 = (bf16[4,64,2048]{2,1,0:T(8,128)(2,1)S(1)}, bf16[4,64,2048]{2,1,0:T(8,128)(2,1)}, u32[]{:S(2)}) copy-start(bf16[4,64,2048]{2,1,0:T(8,128)(2,1)} %hold.1.refs_4_) | copy-start | bytes 3145732
  80.7 32.5 %all-to-all-start = ((bf16[4,64,2048]{2,1,0:T(8,128)(2,1)}), bf16[4,64,2048]{2,1,0:T(8,128)(2,1)S(1)}, u32[]{:S(2)}, u32[]{:S(2)}) async-start(bf16[4,64,2048]{2,1,0:T(8,128)(2,1)} %hold.1.refs_4_), calls=%async_computation | async-start | bytes 2097152 | tf_op jit(solution)/shard_map/all_to_all | solution.py:532
  97.7 15.4 %copy-start.5 = (bf16[128,2048]{1,0:T(8,128)(2,1)S(1)}, bf16[128,2048]{1,0:T(8,128)(2,1)}, u32[]{:S(2)}) copy-start(bf16[128,2048]{1,0:T(8,128)(2,1)} %grad_ref.3) | copy-start | bytes 1572868
  97.7 15.4 %copy-start.14 = (bf16[64,2048]{1,0:T(8,128)(2,1)S(1)}, bf16[64,2048]{1,0:T(8,128)(2,1)}, u32[]{:S(2)}) copy-start(bf16[64,2048]{1,0:T(8,128)(2,1)} %copy-done.13) | copy-start | bytes 786436
  97.7 15.4 %copy-start.16 = (bf16[64,2048]{1,0:T(8,128)(2,1)S(1)}, bf16[64,2048]{1,0:T(8,128)(2,1)}, u32[]{:S(2)}) copy-start(bf16[64,2048]{1,0:T(8,128)(2,1)} %copy-done.15) | copy-start | bytes 786436
  97.7 15.4 %copy-start.18 = (bf16[64,2048]{1,0:T(8,128)(2,1)S(1)}, bf16[64,2048]{1,0:T(8,128)(2,1)}, u32[]{:S(2)}) copy-start(bf16[64,2048]{1,0:T(8,128)(2,1)} %copy-done.17) | copy-start | bytes 786436
  97.7 15.4 %copy-start.27 = (s32[128,2]{0,1:T(2,128)S(1)}, s32[128,2]{0,1:T(2,128)}, u32[]{:S(2)}) copy-start(s32[128,2]{0,1:T(2,128)} %param.8) | copy-start | bytes 3076
  97.8 15.4 %copy-start.28 = (f32[128,2]{0,1:T(2,128)S(1)}, f32[128,2]{0,1:T(2,128)}, u32[]{:S(2)}) copy-start(f32[128,2]{0,1:T(2,128)} %param.9) | copy-start | bytes 3076
  102.0 15.1 %collective-permute-start.14 = (bf16[384,768]{1,0:T(8,128)(2,1)}, bf16[384,768]{1,0:T(8,128)(2,1)S(1)}, u32[]{:S(2)}, u32[]{:S(2)}) collective-permute-start(bf16[384,768]{1,0:T(8,128)(2,1)} %get-tuple-element.68), channel_id=1, source_target_pairs={{0,16},{4,20},{8,24},{12,28},{16,0},{20,4},{24,8},{28,12},{1,17},{... | collective-permute-start | bytes 1769480 | tf_op jit(solution)/shard_map/ppermute | solution.py:436
  103.6 14.1 %collective-permute-start.15 = (bf16[384,768]{1,0:T(8,128)(2,1)}, bf16[384,768]{1,0:T(8,128)(2,1)}, u32[]{:S(2)}, u32[]{:S(2)}) collective-permute-start(bf16[384,768]{1,0:T(8,128)(2,1)} %get-tuple-element.70), channel_id=1, source_target_pairs={{0,8},{4,12},{8,0},{12,4},{16,24},{20,28},{24,16},{28,20},{1,9},{5... | collective-permute-start | bytes 1769480 | tf_op jit(solution)/shard_map/ppermute | solution.py:436
  114.1 3.6 %copy-start.22 = (bf16[384,768]{1,0:T(8,128)(2,1)S(1)}, bf16[384,768]{1,0:T(8,128)(2,1)}, u32[]{:S(2)}) copy-start(bf16[384,768]{1,0:T(8,128)(2,1)} %copy-done.21) | copy-start | bytes 1769476
  (14 other events, 16.6 us)

commit v4 on v3

--- a/solution.py
+++ b/solution.py
@@ -75,35 +75,34 @@
     return lax.broadcasted_iota(jnp.int32, (CAP, tok_count), 0) == rank_row
 
 
-def pick_kernel(n, z_ref, ids_ref, prob_ref, tok_ref, grad_ref, *outs):
+def pick_kernel(n, scaled, z_ref, ids_ref, prob_ref, rows_ref, *outs):
     ids = ids_ref[...]
     prob = prob_ref[...]
-    tok, grad = tok_ref[...], grad_ref[...]
     experts = [jnp.bitwise_xor(z_ref[0], k) for k in range(n)]
     rank = ranks(ids, experts)
-    for k in range(n):
+    for k in range(n - 1, -1, -1):
         first, second = chosen(ids, experts[k])
         at = places(rank[k : k + 1, :])
         here = jnp.logical_and(at, jnp.logical_or(first, second))
-        pick = jnp.where(here, 1.0, 0.0)
-        weight = jnp.where(first, prob[0:1, :], prob[1:2, :])
-        scale = jnp.sum(jnp.where(here, weight, 0.0), axis=1, keepdims=True)
-        outs[k][...] = mm(pick.astype(BF), tok).astype(BF)
-        outs[n + k][...] = (scale * mm(pick.astype(BF), grad)).astype(BF)
-
-
-def pick_rows(n, z, ids_t, prob_t, tokens, out_grad):
-    tok_count, width = tokens.shape
+        picked = mm(jnp.where(here, 1.0, 0.0).astype(BF), rows_ref[...])
+        if scaled:
+            weight = jnp.where(first, prob[0:1, :], prob[1:2, :])
+            picked = jnp.sum(jnp.where(here, weight, 0.0), axis=1, keepdims=True) * picked
+        outs[k][...] = picked.astype(BF)
+
+
+def pick_rows(n, scaled, z, ids_t, prob_t, rows):
+    tok_count, width = rows.shape
     return pl.pallas_call(
-        functools.partial(pick_kernel, n),
-        out_shape=[shape_of((CAP, width))] * (2 * n),
-        in_specs=[in_smem(), whole(ids_t.shape), whole(prob_t.shape)] + [whole(tokens.shape)] * 2,
-        out_specs=[whole((CAP, width))] * (2 * n),
+        functools.partial(pick_kernel, n, scaled),
+        out_shape=[shape_of((CAP, width))] * n,
+        in_specs=[in_smem(), whole(ids_t.shape), whole(prob_t.shape), whole(rows.shape)],
+        out_specs=[whole((CAP, width))] * n,
         grid=(1,),
         compiler_params=params(60),
-        cost_estimate=cost(4 * n * CAP * tok_count * width, 4 * tok_count * width * 3),
+        cost_estimate=cost(2 * n * CAP * tok_count * width, 4 * tok_count * width * 2),
         name="pick_rows",
-    )(z, ids_t, prob_t, tokens, out_grad)
+    )(z, ids_t, prob_t, rows)
 
 
 def silu_parts(gate):
@@ -317,8 +316,9 @@
     )
 
 
-def input_grad_kernel(n, steps, tile, z_ref, grad_ref, wg_ref, wu_ref, *refs):
-    out_ref, wg_buf, wu_buf, sems = refs
+def input_grad_kernel(n, steps, tile, grad_ref, wg_ref, wu_ref, *refs):
+    out_refs = refs[:n]
+    wg_buf, wu_buf, sems = refs[n:]
     step = pl.program_id(0)
 
     def loads(j):
@@ -339,41 +339,44 @@
     rows = n * CAP
     total = mm_cols(grad_ref[:rows, :], wg_buf[step]) + mm_cols(grad_ref[rows:, :], wu_buf[step])
     for k in range(n):
-        partner = jnp.bitwise_xor(z_ref[0], k)
-        out_ref[partner] = total[k * CAP : (k + 1) * CAP, :].astype(BF)
-
-
-def input_grad(z, n, grad, w_gate, w_up):
+        out_refs[k][...] = total[k * CAP : (k + 1) * CAP, :].astype(BF)
+
+
+def input_grad(n, grad, w_gate, w_up, after):
     rows, ff = n * CAP, grad.shape[1]
     width = w_gate.shape[1]
     tile = 512
     steps = width // tile
-    return pl.pallas_call(
+    return call(
         functools.partial(input_grad_kernel, n, steps, tile),
+        after,
         grid=(steps,),
-        out_shape=shape_of((n, CAP, width)),
-        in_specs=[in_smem(), whole((2 * rows, ff))] + [pl.BlockSpec(memory_space=pltpu.HBM)] * 2,
-        out_specs=pl.BlockSpec((n, CAP, tile), lambda j: (0, 0, j)),
+        out_shape=[shape_of((CAP, width))] * n,
+        in_specs=[whole((2 * rows, ff))] + [pl.BlockSpec(memory_space=pltpu.HBM)] * 2,
+        args=(grad, w_gate, w_up),
+        out_specs=[pl.BlockSpec((CAP, tile), lambda j: (0, j))] * n,
         scratch_shapes=[pltpu.VMEM((steps, tile, ff), BF)] * 2 + [pltpu.SemaphoreType.DMA((2, steps))],
         compiler_params=params(),
         cost_estimate=cost(4 * rows * width * ff, 4 * width * ff + 2 * rows * (width + 2 * ff)),
         name="input_grad",
-    )(z, grad, w_gate, w_up)
-
-
-def hold_kernel(_, __):
+    )
+
+
+def hold_kernel(*_):
     pass
 
 
-def hold(value, after):
+def hold(values, after):
+    anywhere = pl.BlockSpec(memory_space=pl.ANY)
     return call(
         hold_kernel,
         after,
-        [pl.BlockSpec(memory_space=pl.ANY)],
-        [value],
-        out_shape=shape_of(value.shape),
-        out_specs=pl.BlockSpec(memory_space=pl.ANY),
-        input_output_aliases={0: 0},
+        [anywhere] * len(values),
+        values,
+        out_shape=[shape_of(v.shape) for v in values],
+        out_specs=[anywhere] * len(values),
+        input_output_aliases={i: i for i in range(len(values))},
+        cost_estimate=cost(10**11, 0),
         name="hold",
     )
 
@@ -437,8 +440,8 @@
 
 
 def combine_kernel(n, z_ref, ids_ref, prob_ref, grad_ref, *refs):
-    out_back_refs, in_back_ref = refs[:n], refs[n]
-    out_ref, in_ref, prob_grad_ref, out_rows, in_rows, sums, firsts, seconds = refs[n + 1 :]
+    out_back_refs, in_back_refs = refs[:n], refs[n : 2 * n]
+    out_ref, in_ref, prob_grad_ref, out_rows, in_rows, sums, firsts, seconds = refs[2 * n :]
     tok_count = ids_ref.shape[1]
     step = pl.program_id(0)
 
@@ -456,9 +459,8 @@
         sums[...] = jnp.zeros_like(sums)
 
     for k in range(n):
-        partner = jnp.bitwise_xor(z_ref[0], k)
         out_rows[k * CAP : (k + 1) * CAP, :] = out_back_refs[k][...]
-        in_rows[k * CAP : (k + 1) * CAP, :] = in_back_ref[partner]
+        in_rows[k * CAP : (k + 1) * CAP, :] = in_back_refs[k][...]
     prob = jnp.concatenate([prob_ref[...], jnp.zeros((6, tok_count), F32)], axis=0).T
     grad = grad_ref[...].astype(F32)
     one, two = firsts[...].astype(BF), seconds[...].astype(BF)
@@ -488,16 +490,15 @@
         grid=(width // tile,),
         out_shape=[shape_of((tok_count, width))] * 2 + [shape_of((2, tok_count), F32)],
         in_specs=[in_smem(), whole(ids_t.shape), whole(prob_t.shape), by_tile]
-        + [pl.BlockSpec((CAP, tile), lambda j: (0, j))] * n
-        + [pl.BlockSpec((n, CAP, tile), lambda j: (0, 0, j))],
+        + [pl.BlockSpec((CAP, tile), lambda j: (0, j))] * (2 * n),
         out_specs=[by_tile, by_tile, whole((2, tok_count))],
         scratch_shapes=[pltpu.VMEM((rows, tile), BF)] * 2
         + [pltpu.VMEM((tok_count, 8), F32)]
         + [pltpu.VMEM((rows, tok_count), F32)] * 2,
         compiler_params=params(),
-        cost_estimate=cost(6 * rows * tok_count * width, 4 * width * (rows + 2 * tok_count)),
+        cost_estimate=cost(600 * rows * tok_count * width, 4 * width * (rows + 2 * tok_count)),
         name="combine",
-    )(z, ids_t, prob_t, out_grad, *back_out, back_in)
+    )(z, ids_t, prob_t, out_grad, *back_out, *back_in)
 
 
 def exchange(values):
@@ -513,8 +514,8 @@
     parts = lax.axis_size("dp")
     z = lax.axis_index("expert").astype(jnp.int32).reshape(1)
     ids_t, prob_t = expert_ids.T, gate_probs.T
-    sent = pick_rows(n, z, ids_t, prob_t, tokens, out_grad)
-    xs, gs = exchange(sent[:n]), exchange(sent[n:])
+    xs = exchange(pick_rows(n, False, z, ids_t, prob_t, tokens))
+    gs = exchange(pick_rows(n, True, z, ids_t, prob_t, out_grad))
     made = forward(xs, w_gate, w_up, w_down)
     slope, act, hidden = made[:3]
     back_out = exchange(made[3:])
@@ -524,14 +525,13 @@
         owners = jnp.stack([me ^ f for f in flips])
         keep_t, send_t, w_near = turn(parts, owners, xs, hidden, w_down)
         grad, g_rows = hidden_grad(gs, w_near, slope, act, [])
-        din = input_grad(z, n, grad, w_gate, w_up)
         x_send, x_keep, y_send, y_keep = outer(
             keep_t, swap(send_t, CORE), grad, swap(grad, CORE), g_rows, swap(g_rows, CORE), []
         )
-        din = hold(din, back_out[1:])
-        back_in = lax.all_to_all(din, "expert", split_axis=0, concat_axis=0, tiled=True)
+        din = input_grad(n, grad, w_gate, w_up, [x_send])
+        back_in = exchange(din[:1] + hold(din[1:], back_out[1:]))
         x_next, x_mine, y_next, y_mine = fold_two(
-            x_keep, swap(x_send, ALONG_X), y_keep, swap(y_send, ALONG_Y), [din]
+            x_keep, swap(x_send, ALONG_X), y_keep, swap(y_send, ALONG_Y), din[:1]
         )
         layer_out, token_grad, prob_grad_t = combine(z, ids_t, prob_t, out_grad, back_out, back_in)
         shapes = [(1, d // parts, w) for d, w in (w_gate.shape[1:], w_up.shape[1:], w_down.shape[1:])]
@@ -540,8 +540,8 @@
         )
     else:
         grad, d_rows = hidden_grad(gs, w_down, slope, act, [])
-        din = input_grad(z, n, grad, w_gate, w_up)
-        back_in = lax.all_to_all(din, "expert", split_axis=0, concat_axis=0, tiled=True)
+        din = input_grad(n, grad, w_gate, w_up, [])
+        back_in = exchange(din)
         layer_out, token_grad, prob_grad_t = combine(z, ids_t, prob_t, out_grad, back_out, back_in)
         x_rows, count = jnp.concatenate(xs, 0), n * CAP
         sum_gate, sum_up, sum_down = (

time: 122 us -> 114 us (0.934)
  local copies, waits for them, and re-layouts: 12 us -> 3.78 us
    all_to_all x1 -> x0, waiting for transfers between devices: 8.34 us -> none  [local(): lax.all_to_all(din, 'expert', split_axis=0, concat_axis=0, tiled=True)]
    unnamed x58 -> x34, local copies, waits for them, and re-layouts: 11.9 us -> 3.7 us
    ppermute x9 -> x12, starting transfers between devices: 21.8 us -> 29.7 us  [exchange(): moved[k] = lax.ppermute(values[k], 'expert', [(i, i ^ k) for i in range(n)])]
    all_to_all x1 -> x0, starting transfers between devices: 7.13 us -> none  [local(): lax.all_to_all(din, 'expert', split_axis=0, concat_axis=0, tiled=True)]
    ppermute x9 -> x12, waiting for transfers between devices: 30.8 us -> 36.6 us  [exchange(): moved[k] = lax.ppermute(values[k], 'expert', [(i, i ^ k) for i in range(n)])]
    ppermute x7, waiting for transfers between devices: 5.6 us -> 6.91 us  [swap(): return lax.ppermute(value, 'dp', [(i, i ^ bit) for i in range(count)])]
    pallas_call x5 -> x6, Pallas kernels: 10.8 us -> 12 us  [call(): return pl.pallas_call(body, in_specs=specs, **kwargs)(*args, *after)]
    pallas_call x1, Pallas kernels: 3.03 us -> 4.29 us  [combine(): pl.pallas_call(functools.partial(combine_kernel, n), grid=(width // tile,...]
  transfers between devices with their start and end apart: 17 -> 19, of which waited for: 8 -> 8; matrix products, arithmetic and copies ran while one was open for 0% -> 0% of each run, Pallas kernels for 17% -> 21%
where the time goes in v4:
time: 114 us; the launch traced here: 113 us
  waiting for transfers between devices  43.5 us (38%)
  starting transfers between devices  35.5 us (31%)
  Pallas kernels  29.2 us (26%)
  local copies, waits for them, and re-layouts  3.78 us (3%)
    ppermute x12, waiting for transfers between devices, exchange(): moved[k] = lax.ppermute(values[k], 'expert', [(i, i ^ k) for i in range(n)])  36.6 us
    ppermute x12, starting transfers between devices, exchange(): moved[k] = lax.ppermute(values[k], 'expert', [(i, i ^ k) for i in range(n)])  29.7 us
    pallas_call x6, Pallas kernels, call(): return pl.pallas_call(body, in_specs=specs, **kwargs)(*args, *after)  12 us
    ppermute x7, waiting for transfers between devices, swap(): return lax.ppermute(value, 'dp', [(i, i ^ bit) for i in range(count)])  6.91 us
    pallas_call x1, Pallas kernels, forward(): pl.pallas_call(functools.partial(forward_kernel, n, steps, tile), grid=(s...  6.8 us
    ppermute x7, starting transfers between devices, swap(): return lax.ppermute(value, 'dp', [(i, i ^ bit) for i in range(count)])  5.73 us
    pallas_call x2, Pallas kernels, pick_rows(): pl.pallas_call(functools.partial(pick_kernel, n, scaled), out_shape=[shap...  4.88 us
    pallas_call x1, Pallas kernels, combine(): pl.pallas_call(functools.partial(combine_kernel, n), grid=(width // tile,...  4.29 us
  transfers between devices with their start and end apart: 19, of which 8 were waited for; matrix products, arithmetic and copies ran while one was open for 0% of the time, Pallas kernels for 21%

profile of v4, /device:TPU:0, one launch (start us, length us, event | category | flops | bytes accessed | tf_op | source)
XLA Modules:
  0.0 112.8 jit_solution(15074567332500855994)
XLA Ops:
  0.6 2.4 %pick_rows.2 = (bf16[64,2048]{1,0:T(8,128)(2,1)}, bf16[64,2048]{1,0:T(8,128)(2,1)}, bf16[64,2048]{1,0:T(8,128)(2,1)}, bf16[64,2048]{1,0:T(8,128)(2,1)}) custom-call(s32[1]{0:T(128)} %bitcast.z_ref, s32[2,128]{1,0:T(2,128)} %bitcast.12, f32[2,128]{1,0:T(2,128)} %bitcast.15, bf16[128,2048]{1,0:T(8,128)(2,1)} %rows_ref.2), custom_call_target="tpu_custom_call" | custom-call | flops 134217728 | bytes 2097152 | tf_op jit(solution)/shard_map/pick_rows/pallas_call | solution.py:96
  3.1 3.0 %collective-permute-start = (bf16[64,2048]{1,0:T(8,128)(2,1)}, bf16[64,2048]{1,0:T(8,128)(2,1)S(1)}, u32[]{:S(2)}, u32[]{:S(2)}) collective-permute-start(bf16[64,2048]{1,0:T(8,128)(2,1)} %get-tuple-element.48), channel_id=1, source_target_pairs={{0,1},{1,0},{2,3},{3,2},{4,5},{5,4},{6,7},{7,6},{8,9},{9,8},{10,11... | collective-permute-start | bytes 786440 | tf_op jit(solution)/shard_map/ppermute | solution.py:508
  6.1 2.6 %collective-permute-start.1 = (bf16[64,2048]{1,0:T(8,128)(2,1)}, bf16[64,2048]{1,0:T(8,128)(2,1)S(1)}, u32[]{:S(2)}, u32[]{:S(2)}) collective-permute-start(bf16[64,2048]{1,0:T(8,128)(2,1)} %get-tuple-element.49), channel_id=1, source_target_pairs={{0,2},{1,3},{2,0},{3,1},{4,6},{5,7},{6,4},{7,5},{8,10},{9,11},{10,... | collective-permute-start | bytes 786440 | tf_op jit(solution)/shard_map/ppermute | solution.py:508
  8.7 2.4 %pick_rows.3 = (bf16[64,2048]{1,0:T(8,128)(2,1)}, bf16[64,2048]{1,0:T(8,128)(2,1)}, bf16[64,2048]{1,0:T(8,128)(2,1)}, bf16[64,2048]{1,0:T(8,128)(2,1)}) custom-call(s32[1]{0:T(128)} %bitcast.z_ref, s32[2,128]{1,0:T(2,128)} %bitcast.13, f32[2,128]{1,0:T(2,128)} %bitcast.16, bf16[128,2048]{1,0:T(8,128)(2,1)} %grad_ref.1), custom_call_target="tpu_custom_call" | custom-call | flops 134217728 | bytes 2097152 | tf_op jit(solution)/shard_map/pick_rows/pallas_call | solution.py:96
  12.0 3.5 %collective-permute-start.7 = (bf16[64,2048]{1,0:T(8,128)(2,1)}, bf16[64,2048]{1,0:T(8,128)(2,1)S(1)}, u32[]{:S(2)}, u32[]{:S(2)}) collective-permute-start(bf16[64,2048]{1,0:T(8,128)(2,1)} %get-tuple-element.57), channel_id=1, source_target_pairs={{0,2},{1,3},{2,0},{3,1},{4,6},{5,7},{6,4},{7,5},{8,10},{9,11},{10,... | collective-permute-start | bytes 786440 | tf_op jit(solution)/shard_map/ppermute | solution.py:508
  15.5 2.8 %collective-permute-done.refs_1_ = bf16[64,2048]{1,0:T(8,128)(2,1)S(1)} collective-permute-done((bf16[64,2048]{1,0:T(8,128)(2,1)}, bf16[64,2048]{1,0:T(8,128)(2,1)S(1)}, u32[]{:S(2)}, u32[]{:S(2)}) %collective-permute-start) | collective-permute-done | bytes 262176 | tf_op jit(solution)/shard_map/ppermute | solution.py:508
  18.3 4.6 %collective-permute-start.8 = (bf16[64,2048]{1,0:T(8,128)(2,1)}, bf16[64,2048]{1,0:T(8,128)(2,1)S(1)}, u32[]{:S(2)}, u32[]{:S(2)}) collective-permute-start(bf16[64,2048]{1,0:T(8,128)(2,1)} %get-tuple-element.58), channel_id=1, source_target_pairs={{0,3},{1,2},{2,1},{3,0},{4,7},{5,6},{6,5},{7,4},{8,11},{9,10},{10,... | collective-permute-start | bytes 786440 | tf_op jit(solution)/shard_map/ppermute | solution.py:508
  23.0 4.8 %collective-permute-done.1.refs_2_ = bf16[64,2048]{1,0:T(8,128)(2,1)S(1)} collective-permute-done((bf16[64,2048]{1,0:T(8,128)(2,1)}, bf16[64,2048]{1,0:T(8,128)(2,1)S(1)}, u32[]{:S(2)}, u32[]{:S(2)}) %collective-permute-start.1) | collective-permute-done | bytes 262176 | tf_op jit(solution)/shard_map/ppermute | solution.py:508
  27.7 0.9 copy-done.3
  28.7 6.8 %forward.1 = (f32[256,768]{1,0:T(8,128)S(1)}, f32[256,768]{1,0:T(8,128)S(1)}, bf16[256,768]{1,0:T(8,128)(2,1)S(1)}, bf16[64,2048]{1,0:T(8,128)(2,1)S(1)}, bf16[6...) custom-call(bf16[64,2048]{1,0:T(8,128)(2,1)S(1)} %copy-done.3, ...), custom_call_target="tpu_custom_call" | custom-call | flops 2415919104 | bytes 13500416 | tf_op jit(solution)/shard_map/forward/pallas_call | solution.py:176
  35.5 1.2 %turn.1 = (bf16[1408,256]{1,0:T(8,128)(2,1)S(1)}, bf16[1408,256]{1,0:T(8,128)(2,1)S(1)}, bf16[1,768,2048]{2,1,0:T(8,128)(2,1)S(1)}) custom-call(s32[8]{0:T(128)S(1)} %stack.35.me_ref, bf16[64,2048]{1,0:T(8,128)(2,1)S(1)} %copy-done.3, bf16[64,2048]{1,0:T(8,128)(2,1)S(1)} %collective-permute-done.refs_1_, ...), custom_call_target="tpu_custom_call" | custom-call | flops 1048576 | bytes 4325376 | tf_op jit(solution)/shard_map/turn/pallas_call | solution.py:223
  36.8 13.4 %collective-permute-done.7.refs_2_ = bf16[64,2048]{1,0:T(8,128)(2,1)S(1)} collective-permute-done((bf16[64,2048]{1,0:T(8,128)(2,1)}, bf16[64,2048]{1,0:T(8,128)(2,1)S(1)}, u32[]{:S(2)}, u32[]{:S(2)}) %collective-permute-start.7) | collective-permute-done | bytes 262176 | tf_op jit(solution)/shard_map/ppermute | solution.py:508
  50.2 1.7 %hidden_grad.1 = (bf16[512,768]{1,0:T(8,128)(2,1)S(1)}, bf16[256,2048]{1,0:T(8,128)(2,1)S(1)}) custom-call(bf16[64,2048]{1,0:T(8,128)(2,1)S(1)} %copy-done.6, bf16[64,2048]{1,0:T(8,128)(2,1)S(1)} %collective-permute-done.6.refs_1_, bf16[64,2048]{1,0:T(8,128)(2,1)S(1)} %collective-permute-done.7.refs_2_, bf16[64,2048]{1,0:T(8,128)(2,1)S(1)} %collective-permute-done.8.refs_3_, ...), custom_call_target="tpu_custom_call" | custom-call | flops 805306368 | bytes 7602176 | tf_op jit(solution)/shard_map/hidden_grad/pallas_call | solution.py:50
  52.6 4.8 %collective-permute-start.3 = (bf16[64,2048]{1,0:T(8,128)(2,1)S(1)}, bf16[64,2048]{1,0:T(8,128)(2,1)}, u32[]{:S(2)}, u32[]{:S(2)}) collective-permute-start(bf16[64,2048]{1,0:T(8,128)(2,1)S(1)} %get-tuple-element.52), channel_id=1, source_target_pairs={{0,1},{1,0},{2,3},{3,2},{4,5},{5,4},{6,7},{7,6},{8,9},{9,8},{10,11... | collective-permute-start | bytes 786440 | tf_op jit(solution)/shard_map/ppermute | solution.py:508
  57.4 1.0 collective-permute-start.4
  58.4 1.5 %collective-permute-start.5 = (bf16[64,2048]{1,0:T(8,128)(2,1)S(1)}, bf16[64,2048]{1,0:T(8,128)(2,1)}, u32[]{:S(2)}, u32[]{:S(2)}) collective-permute-start(bf16[64,2048]{1,0:T(8,128)(2,1)S(1)} %get-tuple-element.54), channel_id=1, source_target_pairs={{0,3},{1,2},{2,1},{3,0},{4,7},{5,6},{6,5},{7,4},{8,11},{9,10},{10,... | collective-permute-start | bytes 786440 | tf_op jit(solution)/shard_map/ppermute | solution.py:508
  59.9 4.2 %outer.1 = (bf16[2,384,768]{2,1,0:T(8,128)(2,1)}, bf16[2,384,768]{2,1,0:T(8,128)(2,1)S(1)}, bf16[2,384,768]{2,1,0:T(8,128)(2,1)}, bf16[2,384,768]{2,1,0:T(8,128)(2,1)S(1)}) custom-call(bf16[1408,256]{1,0:T(8,128)(2,1)S(1)} %get-tuple-element.64.refs_0_, bf16[1408,256]{1,0:T(8,128)(2,1)S(1)} %collective-permute-done.9.refs_1_, ...), custom_call_target="tpu_custom_call" | custom-call | flops 2415919104 | bytes 6160384 | tf_op jit(solution)/shard_map/outer/pallas_call | solution.py:50
  64.0 1.5 %collective-permute-start.16 = (bf16[2,384,768]{2,1,0:T(8,128)(2,1)}, bf16[2,384,768]{2,1,0:T(8,128)(2,1)S(1)}, u32[]{:S(2)}, u32[]{:S(2)}) collective-permute-start(bf16[2,384,768]{2,1,0:T(8,128)(2,1)} %get-tuple-element.80), channel_id=1, source_target_pairs={{0,16},{4,20},{8,24},{12,28},{16,0},{20,4},{24,8},{28,12},{1,17},{... | collective-permute-start | bytes 3538952 | tf_op jit(solution)/shard_map/ppermute | solution.py:439
  65.6 1.5 %collective-permute-start.15 = (bf16[2,384,768]{2,1,0:T(8,128)(2,1)}, bf16[2,384,768]{2,1,0:T(8,128)(2,1)}, u32[]{:S(2)}, u32[]{:S(2)}) collective-permute-start(bf16[2,384,768]{2,1,0:T(8,128)(2,1)} %get-tuple-element.67.refs_3_), channel_id=1, source_target_pairs={{0,8},{4,12},{8,0},{12,4},{16,24},{20,28},{24,16},{28,20},{1,9},{5... | collective-permute-start | bytes 3538952 | tf_op jit(solution)/shard_map/ppermute | solution.py:439
  67.1 3.0 %input_grad.1 = (bf16[64,2048]{1,0:T(8,128)(2,1)S(1)}, bf16[64,2048]{1,0:T(8,128)(2,1)S(1)}, bf16[64,2048]{1,0:T(8,128)(2,1)S(1)}, bf16[64,2048]{1,0:T(8,128)(2,1)S(1)}) custom-call(bf16[512,768]{1,0:T(8,128)(2,1)S(1)} %get-tuple-element.63.refs_2_.refs_0_, bf16[1,2048,768]{2,1,0:T(8,128)(2,1)S(1)} %copy-done.1, bf16[1,2048,768]{2,1,0:T(8,128)(2,1)S(1)} %copy-done.2, ...), custom_call_target="tpu_custom_call" | custom-call | flops 1610612736 | bytes 8126464 | tf_op jit(solution)/shard_map/input_grad/pallas_call | solution.py:50
  70.8 8.0 %collective-permute-done.4.refs_4_.refs_2_ = bf16[64,2048]{1,0:T(8,128)(2,1)} collective-permute-done((bf16[64,2048]{1,0:T(8,128)(2,1)S(1)}, bf16[64,2048]{1,0:T(8,128)(2,1)}, u32[]{:S(2)}, u32[]{:S(2)}) %collective-permute-start.4) | collective-permute-done | bytes 262176 | tf_op jit(solution)/shard_map/ppermute | solution.py:508
  78.8 5.5 %collective-permute-start.12 = (bf16[64,2048]{1,0:T(8,128)(2,1)}, bf16[64,2048]{1,0:T(8,128)(2,1)S(1)}, u32[]{:S(2)}, u32[]{:S(2)}) collective-permute-start(bf16[64,2048]{1,0:T(8,128)(2,1)} %get-tuple-element.72), channel_id=1, source_target_pairs={{0,1},{1,0},{2,3},{3,2},{4,5},{5,4},{6,7},{7,6},{8,9},{9,8},{10,11... | collective-permute-start | bytes 786440 | tf_op jit(solution)/shard_map/ppermute | solution.py:508
  84.3 1.1 collective-permute-start.13
  85.4 1.4 %collective-permute-start.14 = (bf16[64,2048]{1,0:T(8,128)(2,1)}, bf16[64,2048]{1,0:T(8,128)(2,1)S(1)}, u32[]{:S(2)}, u32[]{:S(2)}) collective-permute-start(bf16[64,2048]{1,0:T(8,128)(2,1)} %get-tuple-element.74), channel_id=1, source_target_pairs={{0,3},{1,2},{2,1},{3,0},{4,7},{5,6},{6,5},{7,4},{8,11},{9,10},{10,... | collective-permute-start | bytes 786440 | tf_op jit(solution)/shard_map/ppermute | solution.py:508
  86.8 5.2 %collective-permute-done.16.refs_3_ = bf16[2,384,768]{2,1,0:T(8,128)(2,1)S(1)} collective-permute-done((bf16[2,384,768]{2,1,0:T(8,128)(2,1)}, bf16[2,384,768]{2,1,0:T(8,128)(2,1)S(1)}, u32[]{:S(2)}, u32[]{:S(2)}) %collective-permute-start.16) | collective-permute-done | bytes 1179680 | tf_op jit(solution)/shard_map/ppermute | solution.py:439
  92.0 1.4 %collective-permute-done.15.refs_1_ = bf16[2,384,768]{2,1,0:T(8,128)(2,1)} collective-permute-done((bf16[2,384,768]{2,1,0:T(8,128)(2,1)}, bf16[2,384,768]{2,1,0:T(8,128)(2,1)}, u32[]{:S(2)}, u32[]{:S(2)}) %collective-permute-start.15) | collective-permute-done | bytes 1179680 | tf_op jit(solution)/shard_map/ppermute | solution.py:439
  94.3 1.9 %fold_two.1 = (bf16[384,768]{1,0:T(8,128)(2,1)S(1)}, bf16[384,768]{1,0:T(8,128)(2,1)S(1)}, bf16[384,768]{1,0:T(8,128)(2,1)S(1)}, bf16[384,768]{1,0:T(8,128)(2,1)S(1)}) custom-call(bf16[2,384,768]{2,1,0:T(8,128)(2,1)S(1)} %get-tuple-element.78.refs_0_, bf16[2,384,768]{2,1,0:T(8,128)(2,1)} %collective-permute-done.15.refs_1_, ...), custom_call_target="tpu_custom_call" | custom-call | flops 1179648 | bytes 7077888 | tf_op jit(solution)/shard_map/fold_two/pallas_call | solution.py:50
  96.8 1.5 %collective-permute-start.18 = (bf16[384,768]{1,0:T(8,128)(2,1)S(1)}, bf16[384,768]{1,0:T(8,128)(2,1)S(1)}, u32[]{:S(2)}, u32[]{:S(2)}) collective-permute-start(bf16[384,768]{1,0:T(8,128)(2,1)S(1)} %get-tuple-element.84), channel_id=1, source_target_pairs={{0,8},{4,12},{8,0},{12,4},{16,24},{20,28},{24,16},{28,20},{1,9},{5... | collective-permute-start | bytes 1769480 | tf_op jit(solution)/shard_map/ppermute | solution.py:439
  98.3 7.6 %collective-permute-done.13.refs_6_ = bf16[64,2048]{1,0:T(8,128)(2,1)S(1)} collective-permute-done((bf16[64,2048]{1,0:T(8,128)(2,1)}, bf16[64,2048]{1,0:T(8,128)(2,1)S(1)}, u32[]{:S(2)}, u32[]{:S(2)}) %collective-permute-start.13) | collective-permute-done | bytes 262176 | tf_op jit(solution)/shard_map/ppermute | solution.py:508
  105.9 4.3 %combine.1 = (bf16[128,2048]{1,0:T(8,128)(2,1)}, bf16[128,2048]{1,0:T(8,128)(2,1)}, f32[2,128]{1,0:T(2,128)}) custom-call(s32[1]{0:T(128)} %bitcast.z_ref, s32[2,128]{1,0:T(2,128)S(1)} %bitcast.14, f32[2,128]{1,0:T(2,128)S(1)} %bitcast.17, bf16[128,2048]{1,0:T(8,128)(2,1)S(1)} %copy-done.4, bf16[64,2048]{1,0:T(8,128)(2,1)S(1)} %copy-done.13, ...), custom_call_target="tpu_custom_call" | custom-call | flops 40265318400 | bytes 4194304 | tf_op jit(solution)/shard_map/combine/pallas_call | solution.py:488
  110.5 1.0 copy-done.5
  111.6 1.2 %fold_last.1 = (bf16[1,256,768]{2,1,0:T(8,128)(2,1)}, bf16[1,256,768]{2,1,0:T(8,128)(2,1)}, bf16[1,96,2048]{2,1,0:T(8,128)(2,1)}) custom-call(bf16[384,768]{1,0:T(8,128)(2,1)S(1)} %get-tuple-element.81.refs_0_, bf16[384,768]{1,0:T(8,128)(2,1)S(1)} %collective-permute-done.17.refs_1_, bf16[384,768]{1,0:T(8,128)(2,1)S(1)} %get-tuple-element.83.refs_2_, ...), custom_call_target="tpu_custom_call" | custom-call | flops 589824 | bytes 3538944 | tf_op jit(solution)/shard_map/fold_last/pallas_call | solution.py:50
  (52 shorter events, 4.3 us)
Async XLA Ops:
  3.1 15.2 %collective-permute-start = (bf16[64,2048]{1,0:T(8,128)(2,1)}, bf16[64,2048]{1,0:T(8,128)(2,1)S(1)}, u32[]{:S(2)}, u32[]{:S(2)}) collective-permute-start(bf16[64,2048]{1,0:T(8,128)(2,1)} %get-tuple-element.48), channel_id=1, source_target_pairs={{0,1},{1,0},{2,3},{3,2},{4,5},{5,4},{6,7},{7,6},{8,9},{9,8},{10,11... | collective-permute-start | bytes 786440 | tf_op jit(solution)/shard_map/ppermute | solution.py:508
  6.1 21.6 %collective-permute-start.1 = (bf16[64,2048]{1,0:T(8,128)(2,1)}, bf16[64,2048]{1,0:T(8,128)(2,1)S(1)}, u32[]{:S(2)}, u32[]{:S(2)}) collective-permute-start(bf16[64,2048]{1,0:T(8,128)(2,1)} %get-tuple-element.49), channel_id=1, source_target_pairs={{0,2},{1,3},{2,0},{3,1},{4,6},{5,7},{6,4},{7,5},{8,10},{9,11},{10,... | collective-permute-start | bytes 786440 | tf_op jit(solution)/shard_map/ppermute | solution.py:508
  8.7 19.0 %collective-permute-start.2 = (bf16[64,2048]{1,0:T(8,128)(2,1)}, bf16[64,2048]{1,0:T(8,128)(2,1)S(1)}, u32[]{:S(2)}, u32[]{:S(2)}) collective-permute-start(bf16[64,2048]{1,0:T(8,128)(2,1)} %get-tuple-element.50), channel_id=1, source_target_pairs={{0,3},{1,2},{2,1},{3,0},{4,7},{5,6},{6,5},{7,4},{8,11},{9,10},{10,... | collective-permute-start | bytes 786440 | tf_op jit(solution)/shard_map/ppermute | solution.py:508
  11.1 25.6 %collective-permute-start.6 = (bf16[64,2048]{1,0:T(8,128)(2,1)}, bf16[64,2048]{1,0:T(8,128)(2,1)S(1)}, u32[]{:S(2)}, u32[]{:S(2)}) collective-permute-start(bf16[64,2048]{1,0:T(8,128)(2,1)} %get-tuple-element.56), channel_id=1, source_target_pairs={{0,1},{1,0},{2,3},{3,2},{4,5},{5,4},{6,7},{7,6},{8,9},{9,8},{10,11... | collective-permute-start | bytes 786440 | tf_op jit(solution)/shard_map/ppermute | solution.py:508
  12.0 38.2 %collective-permute-start.7 = (bf16[64,2048]{1,0:T(8,128)(2,1)}, bf16[64,2048]{1,0:T(8,128)(2,1)S(1)}, u32[]{:S(2)}, u32[]{:S(2)}) collective-permute-start(bf16[64,2048]{1,0:T(8,128)(2,1)} %get-tuple-element.57), channel_id=1, source_target_pairs={{0,2},{1,3},{2,0},{3,1},{4,6},{5,7},{6,4},{7,5},{8,10},{9,11},{10,... | collective-permute-start | bytes 786440 | tf_op jit(solution)/shard_map/ppermute | solution.py:508
  18.3 31.9 %collective-permute-start.8 = (bf16[64,2048]{1,0:T(8,128)(2,1)}, bf16[64,2048]{1,0:T(8,128)(2,1)S(1)}, u32[]{:S(2)}, u32[]{:S(2)}) collective-permute-start(bf16[64,2048]{1,0:T(8,128)(2,1)} %get-tuple-element.58), channel_id=1, source_target_pairs={{0,3},{1,2},{2,1},{3,0},{4,7},{5,6},{6,5},{7,4},{8,11},{9,10},{10,... | collective-permute-start | bytes 786440 | tf_op jit(solution)/shard_map/ppermute | solution.py:508
  28.7 6.8 %copy-start = (bf16[1,768,2048]{2,1,0:T(8,128)(2,1)S(1)}, bf16[1,768,2048]{2,1,0:T(8,128)(2,1)}, u32[]{:S(2)}) copy-start(bf16[1,768,2048]{2,1,0:T(8,128)(2,1)} %refs_5_.3) | copy-start | bytes 9437188
  35.5 1.2 %copy-start.12 = (bf16[64,2048]{1,0:T(8,128)(2,1)}, bf16[64,2048]{1,0:T(8,128)(2,1)S(1)}, u32[]{:S(2)}) copy-start(bf16[64,2048]{1,0:T(8,128)(2,1)S(1)} %get-tuple-element.51.refs_0_) | copy-start | bytes 786436
  35.5 14.7 %copy-start.6 = (bf16[64,2048]{1,0:T(8,128)(2,1)S(1)}, bf16[64,2048]{1,0:T(8,128)(2,1)}, u32[]{:S(2)}) copy-start(bf16[64,2048]{1,0:T(8,128)(2,1)} %get-tuple-element.55.refs_0_) | copy-start | bytes 786436
  52.0 7.9 %collective-permute-start.11 = (bf16[256,2048]{1,0:T(8,128)(2,1)S(1)}, bf16[256,2048]{1,0:T(8,128)(2,1)S(1)}, u32[]{:S(2)}, u32[]{:S(2)}) collective-permute-start(bf16[256,2048]{1,0:T(8,128)(2,1)S(1)} %get-tuple-element.66.refs_4_), channel_id=1, source_target_pairs={{0,4},{4,0},{8,12},{12,8},{16,20},{20,16},{24,28},{28,24},{1,5},{5... | collective-permute-start | bytes 3145736 | tf_op jit(solution)/shard_map/ppermute | solution.py:439
  52.0 7.8 %collective-permute-start.10 = (bf16[512,768]{1,0:T(8,128)(2,1)S(1)}, bf16[512,768]{1,0:T(8,128)(2,1)S(1)}, u32[]{:S(2)}, u32[]{:S(2)}) collective-permute-start(bf16[512,768]{1,0:T(8,128)(2,1)S(1)} %get-tuple-element.63.refs_2_.refs_0_), channel_id=1, source_target_pairs={{0,4},{4,0},{8,12},{12,8},{16,20},{20,16},{24,28},{28,24},{1,5},{5... | collective-permute-start | bytes 2359304 | tf_op jit(solution)/shard_map/ppermute | solution.py:439
  52.5 5.8 %collective-permute-start.9 = (bf16[1408,256]{1,0:T(8,128)(2,1)S(1)}, bf16[1408,256]{1,0:T(8,128)(2,1)S(1)}, u32[]{:S(2)}, u32[]{:S(2)}) collective-permute-start(bf16[1408,256]{1,0:T(8,128)(2,1)S(1)} %get-tuple-element.65), channel_id=1, source_target_pairs={{0,4},{4,0},{8,12},{12,8},{16,20},{20,16},{24,28},{28,24},{1,5},{5... | collective-permute-start | bytes 2162696 | tf_op jit(solution)/shard_map/ppermute | solution.py:439
  52.6 18.2 %collective-permute-start.3 = (bf16[64,2048]{1,0:T(8,128)(2,1)S(1)}, bf16[64,2048]{1,0:T(8,128)(2,1)}, u32[]{:S(2)}, u32[]{:S(2)}) collective-permute-start(bf16[64,2048]{1,0:T(8,128)(2,1)S(1)} %get-tuple-element.52), channel_id=1, source_target_pairs={{0,1},{1,0},{2,3},{3,2},{4,5},{5,4},{6,7},{7,6},{8,9},{9,8},{10,11... | collective-permute-start | bytes 786440 | tf_op jit(solution)/shard_map/ppermute | solution.py:508
  57.4 21.4 %collective-permute-start.4 = (bf16[64,2048]{1,0:T(8,128)(2,1)S(1)}, bf16[64,2048]{1,0:T(8,128)(2,1)}, u32[]{:S(2)}, u32[]{:S(2)}) collective-permute-start(bf16[64,2048]{1,0:T(8,128)(2,1)S(1)} %get-tuple-element.53), channel_id=1, source_target_pairs={{0,2},{1,3},{2,0},{3,1},{4,6},{5,7},{6,4},{7,5},{8,10},{9,11},{10,... | collective-permute-start | bytes 786440 | tf_op jit(solution)/shard_map/ppermute | solution.py:508
  58.4 20.4 %collective-permute-start.5 = (bf16[64,2048]{1,0:T(8,128)(2,1)S(1)}, bf16[64,2048]{1,0:T(8,128)(2,1)}, u32[]{:S(2)}, u32[]{:S(2)}) collective-permute-start(bf16[64,2048]{1,0:T(8,128)(2,1)S(1)} %get-tuple-element.54), channel_id=1, source_target_pairs={{0,3},{1,2},{2,1},{3,0},{4,7},{5,6},{6,5},{7,4},{8,11},{9,10},{10,... | collective-permute-start | bytes 786440 | tf_op jit(solution)/shard_map/ppermute | solution.py:508
  59.8 7.2 %copy-start.1 = (bf16[1,2048,768]{2,1,0:T(8,128)(2,1)S(1)}, bf16[1,2048,768]{2,1,0:T(8,128)(2,1)}, u32[]{:S(2)}) copy-start(bf16[1,2048,768]{2,1,0:T(8,128)(2,1)} %refs_1_.1) | copy-start | bytes 9437188
  59.8 7.2 %copy-start.2 = (bf16[1,2048,768]{2,1,0:T(8,128)(2,1)S(1)}, bf16[1,2048,768]{2,1,0:T(8,128)(2,1)}, u32[]{:S(2)}) copy-start(bf16[1,2048,768]{2,1,0:T(8,128)(2,1)} %refs_2_.1) | copy-start | bytes 9437188
  64.0 28.0 %collective-permute-start.16 = (bf16[2,384,768]{2,1,0:T(8,128)(2,1)}, bf16[2,384,768]{2,1,0:T(8,128)(2,1)S(1)}, u32[]{:S(2)}, u32[]{:S(2)}) collective-permute-start(bf16[2,384,768]{2,1,0:T(8,128)(2,1)} %get-tuple-element.80), channel_id=1, source_target_pairs={{0,16},{4,20},{8,24},{12,28},{16,0},{20,4},{24,8},{28,12},{1,17},{... | collective-permute-start | bytes 3538952 | tf_op jit(solution)/shard_map/ppermute | solution.py:439
  65.6 27.8 %collective-permute-start.15 = (bf16[2,384,768]{2,1,0:T(8,128)(2,1)}, bf16[2,384,768]{2,1,0:T(8,128)(2,1)}, u32[]{:S(2)}, u32[]{:S(2)}) collective-permute-start(bf16[2,384,768]{2,1,0:T(8,128)(2,1)} %get-tuple-element.67.refs_3_), channel_id=1, source_target_pairs={{0,8},{4,12},{8,0},{12,4},{16,24},{20,28},{24,16},{28,20},{1,9},{5... | collective-permute-start | bytes 3538952 | tf_op jit(solution)/shard_map/ppermute | solution.py:439
  70.8 8.0 %copy-start.14 = (bf16[64,2048]{1,0:T(8,128)(2,1)}, bf16[64,2048]{1,0:T(8,128)(2,1)S(1)}, u32[]{:S(2)}) copy-start(bf16[64,2048]{1,0:T(8,128)(2,1)S(1)} %get-tuple-element.69.refs_0_) | copy-start | bytes 786436
  70.8 8.0 %copy-start.15 = (bf16[64,2048]{1,0:T(8,128)(2,1)}, bf16[64,2048]{1,0:T(8,128)(2,1)S(1)}, u32[]{:S(2)}) copy-start(bf16[64,2048]{1,0:T(8,128)(2,1)S(1)} %get-tuple-element.70.refs_1_) | copy-start | bytes 786436
  70.8 8.0 %copy-start.16 = (bf16[64,2048]{1,0:T(8,128)(2,1)}, bf16[64,2048]{1,0:T(8,128)(2,1)S(1)}, u32[]{:S(2)}) copy-start(bf16[64,2048]{1,0:T(8,128)(2,1)S(1)} %get-tuple-element.71.refs_2_) | copy-start | bytes 786436
  78.8 19.5 %collective-permute-start.12 = (bf16[64,2048]{1,0:T(8,128)(2,1)}, bf16[64,2048]{1,0:T(8,128)(2,1)S(1)}, u32[]{:S(2)}, u32[]{:S(2)}) collective-permute-start(bf16[64,2048]{1,0:T(8,128)(2,1)} %get-tuple-element.72), channel_id=1, source_target_pairs={{0,1},{1,0},{2,3},{3,2},{4,5},{5,4},{6,7},{7,6},{8,9},{9,8},{10,11... | collective-permute-start | bytes 786440 | tf_op jit(solution)/shard_map/ppermute | solution.py:508
  84.3 21.6 %collective-permute-start.13 = (bf16[64,2048]{1,0:T(8,128)(2,1)}, bf16[64,2048]{1,0:T(8,128)(2,1)S(1)}, u32[]{:S(2)}, u32[]{:S(2)}) collective-permute-start(bf16[64,2048]{1,0:T(8,128)(2,1)} %get-tuple-element.73), channel_id=1, source_target_pairs={{0,2},{1,3},{2,0},{3,1},{4,6},{5,7},{6,4},{7,5},{8,10},{9,11},{10,... | collective-permute-start | bytes 786440 | tf_op jit(solution)/shard_map/ppermute | solution.py:508
  85.4 20.5 %collective-permute-start.14 = (bf16[64,2048]{1,0:T(8,128)(2,1)}, bf16[64,2048]{1,0:T(8,128)(2,1)S(1)}, u32[]{:S(2)}, u32[]{:S(2)}) collective-permute-start(bf16[64,2048]{1,0:T(8,128)(2,1)} %get-tuple-element.74), channel_id=1, source_target_pairs={{0,3},{1,2},{2,1},{3,0},{4,7},{5,6},{6,5},{7,4},{8,11},{9,10},{10,... | collective-permute-start | bytes 786440 | tf_op jit(solution)/shard_map/ppermute | solution.py:508
  94.3 11.6 %copy-start.4 = (bf16[128,2048]{1,0:T(8,128)(2,1)S(1)}, bf16[128,2048]{1,0:T(8,128)(2,1)}, u32[]{:S(2)}) copy-start(bf16[128,2048]{1,0:T(8,128)(2,1)} %grad_ref.1) | copy-start | bytes 1572868
  94.3 11.6 %copy-start.9 = (bf16[64,2048]{1,0:T(8,128)(2,1)S(1)}, bf16[64,2048]{1,0:T(8,128)(2,1)}, u32[]{:S(2)}) copy-start(bf16[64,2048]{1,0:T(8,128)(2,1)} %copy-done.7) | copy-start | bytes 786436
  94.3 11.6 %copy-start.10 = (s32[128,2]{0,1:T(2,128)S(1)}, s32[128,2]{0,1:T(2,128)}, u32[]{:S(2)}) copy-start(s32[128,2]{0,1:T(2,128)} %param.8) | copy-start | bytes 3076
  94.3 11.6 %copy-start.11 = (f32[128,2]{0,1:T(2,128)S(1)}, f32[128,2]{0,1:T(2,128)}, u32[]{:S(2)}) copy-start(f32[128,2]{0,1:T(2,128)} %param.9) | copy-start | bytes 3076
  94.3 11.6 %copy-start.13 = (bf16[64,2048]{1,0:T(8,128)(2,1)S(1)}, bf16[64,2048]{1,0:T(8,128)(2,1)}, u32[]{:S(2)}) copy-start(bf16[64,2048]{1,0:T(8,128)(2,1)} %copy-done.12) | copy-start | bytes 786436
  96.2 14.0 %collective-permute-start.17 = (bf16[384,768]{1,0:T(8,128)(2,1)S(1)}, bf16[384,768]{1,0:T(8,128)(2,1)S(1)}, u32[]{:S(2)}, u32[]{:S(2)}) collective-permute-start(bf16[384,768]{1,0:T(8,128)(2,1)S(1)} %get-tuple-element.82), channel_id=1, source_target_pairs={{0,16},{4,20},{8,24},{12,28},{16,0},{20,4},{24,8},{28,12},{1,17},{... | collective-permute-start | bytes 1769480 | tf_op jit(solution)/shard_map/ppermute | solution.py:439
  96.8 13.8 %collective-permute-start.18 = (bf16[384,768]{1,0:T(8,128)(2,1)S(1)}, bf16[384,768]{1,0:T(8,128)(2,1)S(1)}, u32[]{:S(2)}, u32[]{:S(2)}) collective-permute-start(bf16[384,768]{1,0:T(8,128)(2,1)S(1)} %get-tuple-element.84), channel_id=1, source_target_pairs={{0,8},{4,12},{8,0},{12,4},{16,24},{20,28},{24,16},{28,20},{1,9},{5... | collective-permute-start | bytes 1769480 | tf_op jit(solution)/shard_map/ppermute | solution.py:439
  (4 other events, 3.6 us)

commit v5 on v4

--- a/solution.py
+++ b/solution.py
@@ -210,7 +210,8 @@
         out_ref[i * x_size : (i + 1) * x_size, :] = rows[:, pl.ds(at, x_size)].T
         for j in range(6):
             at = pl.multiple_of(me_ref[rel] * h_size + j * strip, strip)
-            base = half * x_size + ((j % 3) * 2 * half + 2 * i + j // 3) * strip
+            leaves, spot = (i & 1, i >> 1) if j < 3 else (i >> 1, 2 + (i & 1))
+            base = half * x_size + ((j % 3) * 2 * half + leaves * half + spot) * strip
             out_ref[base : base + strip, :] = turned[pl.ds(at, strip), :]
     load.wait()
 
@@ -233,35 +234,33 @@
     )(owners, *xs, hidden, w_down)
 
 
-def outer_kernel(keep_ref, recv_ref, own_ref, other_ref, own_g_ref, other_g_ref, x_send, x_keep, y_send, y_keep):
+def outer_kernel(group, keep_ref, recv_ref, own_ref, other_ref, own_g_ref, x_ref, y_ref):
     step = pl.program_id(0)
     half, high = 4, own_ref.shape[0] // 2
     size = 256
     strip = 16
-    for block in range(half):
+    for i in range(2):
+        block = 2 * i + group
         at = slice(block * size, (block + 1) * size)
-        across, along = block & 1, block >> 1
         gate = mm(keep_ref[at, :], own_ref[:high, :]) + mm(recv_ref[at, :], other_ref[:high, :])
-        (x_send if across else x_keep)[along, :size, :] = gate.astype(BF)
+        x_ref[i, :size, :] = gate.astype(BF)
+        block = 2 * group + i
+        at = slice(block * size, (block + 1) * size)
         up = mm(keep_ref[at, :], own_ref[high:, :]) + mm(recv_ref[at, :], other_ref[high:, :])
-        (y_send if along else y_keep)[across, :size, :] = up.astype(BF)
-    at = pl.ds(pl.multiple_of(half * size + step * 2 * half * strip, strip), 2 * half * strip)
-    down = mm(keep_ref[at, :], own_g_ref[...]) + mm(recv_ref[at, :], other_g_ref[...])
-    down = down.astype(BF)
-    tile = x_send.shape[2]
-    for block in range(half):
-        across, along = block & 1, block >> 1
-        for part, (out_ref, i) in enumerate(
-            ((x_send if across else x_keep, along), (y_send if along else y_keep, across))
-        ):
-            base = (2 * block + part) * strip
-            for c in range(down.shape[1] // tile):
-                out_ref[i, size + c * strip : size + (c + 1) * strip, :] = down[
-                    base : base + strip, c * tile : (c + 1) * tile
-                ]
-
-
-def outer(keep, recv, own, other, own_g, other_g, after):
+        y_ref[i, :size, :] = up.astype(BF)
+    at = pl.ds(pl.multiple_of(half * size + (2 * step + group) * half * strip, strip), half * strip)
+    tile = x_ref.shape[2]
+    turned = keep_ref.shape[0]
+    for c in range(own_g_ref.shape[1] // tile):
+        theirs = recv_ref[turned + c * high : turned + (c + 1) * high, :]
+        down = mm(keep_ref[at, :], own_g_ref[:, c * tile : (c + 1) * tile]) + mm(recv_ref[at, :], theirs)
+        down = down.astype(BF)
+        for spot in range(half):
+            out_ref = x_ref if spot < 2 else y_ref
+            out_ref[spot % 2, size + c * strip : size + (c + 1) * strip, :] = down[spot * strip : (spot + 1) * strip]
+
+
+def outer(group, keep, recv, own, other, own_g, after):
     rows, width = own_g.shape
     ff = own.shape[1]
     tile = 256
@@ -269,51 +268,56 @@
     high = 256 + 16 * (width // tile)
     part = pl.BlockSpec((2, high, tile), lambda j: (0, 0, j))
     return call(
-        outer_kernel,
+        functools.partial(outer_kernel, group),
         after,
         grid=(ff // tile,),
-        out_shape=[shape_of((2, high, ff))] * 4,
-        in_specs=[whole(keep.shape)] * 2 + [col] * 2 + [whole(own_g.shape)] * 2,
-        args=(keep, recv, own, other, own_g, other_g),
-        out_specs=[part] * 4,
-        compiler_params=params(),
-        cost_estimate=cost(6 * rows * width * ff, 4 * keep.size + 16 * high * ff),
+        out_shape=[shape_of((2, high, ff))] * 2,
+        in_specs=[whole(keep.shape), whole(recv.shape)] + [col] * 2 + [whole(own_g.shape)],
+        args=(keep, recv, own, other, own_g),
+        out_specs=[part] * 2,
+        compiler_params=params(),
+        cost_estimate=cost(3 * rows * width * ff, 4 * keep.size + 8 * high * ff),
         name="outer",
     )
 
 
 def hidden_grad_kernel(n, *refs):
     g_refs = refs[:n]
-    wd_ref, slope_ref, act_ref, grad_ref, rows = refs[n:]
+    wd_ref, slope_ref, act_ref, turned_ref, grad_ref, rows, pack_ref = refs[n:]
 
     @pl.when(pl.program_id(0) == 0)
     def _():
         for k in range(n):
             rows[k * CAP : (k + 1) * CAP, :] = g_refs[k][...]
+        high = turned_ref.shape[0]
+        pack_ref[:high, :] = turned_ref[...]
+        tile = pack_ref.shape[1]
+        for c in range(rows.shape[1] // tile):
+            at = high + c * n * CAP
+            pack_ref[at : at + n * CAP, :] = rows[:, c * tile : (c + 1) * tile]
 
     grad = mm_cols(rows[...], wd_ref[0])
     grad_ref[: n * CAP, :] = (grad * slope_ref[...]).astype(BF)
     grad_ref[n * CAP :, :] = (grad * act_ref[...]).astype(BF)
 
 
-def hidden_grad(gs, w_down, slope, act, after):
+def hidden_grad(gs, w_down, slope, act, turned):
     n = len(gs)
     ff, width = w_down.shape[1:]
     rows = n * CAP
     tile = 256
     part = pl.BlockSpec((rows, tile), lambda j: (0, j))
-    return call(
+    tall = (turned.shape[0] + rows * (width // 256), 256)
+    return pl.pallas_call(
         functools.partial(hidden_grad_kernel, n),
-        after,
         grid=(ff // tile,),
-        out_shape=[shape_of((2 * rows, ff)), shape_of((rows, width))],
-        in_specs=[whole((CAP, width))] * n + [weight_specs(width, tile)[2], part, part],
-        args=(*gs, w_down, slope, act),
-        out_specs=[pl.BlockSpec((2 * rows, tile), lambda j: (0, j)), whole((rows, width))],
+        out_shape=[shape_of((2 * rows, ff)), shape_of((rows, width)), shape_of(tall)],
+        in_specs=[whole((CAP, width))] * n + [weight_specs(width, tile)[2], part, part, whole(turned.shape)],
+        out_specs=[pl.BlockSpec((2 * rows, tile), lambda j: (0, j)), whole((rows, width)), whole(tall)],
         compiler_params=params(),
         cost_estimate=cost(2 * rows * width * ff, 2 * width * ff + 4 * rows * width + 12 * rows * ff),
         name="hidden_grad",
-    )
+    )(*gs, w_down, slope, act, turned)
 
 
 def input_grad_kernel(n, steps, tile, grad_ref, wg_ref, wu_ref, *refs):
@@ -376,7 +380,7 @@
         out_shape=[shape_of(v.shape) for v in values],
         out_specs=[anywhere] * len(values),
         input_output_aliases={i: i for i in range(len(values))},
-        cost_estimate=cost(10**11, 0),
+        cost_estimate=cost(10 * 10**9, 0),
         name="hold",
     )
 
@@ -439,9 +443,9 @@
     return lax.ppermute(value, "dp", [(i, i ^ bit) for i in range(count)])
 
 
-def combine_kernel(n, z_ref, ids_ref, prob_ref, grad_ref, *refs):
-    out_back_refs, in_back_refs = refs[:n], refs[n : 2 * n]
-    out_ref, in_ref, prob_grad_ref, out_rows, in_rows, sums, firsts, seconds = refs[2 * n :]
+def combine_out_kernel(n, z_ref, ids_ref, prob_ref, grad_ref, *refs):
+    back_refs = refs[:n]
+    out_ref, prob_grad_ref, rows, sums, firsts, seconds = refs[n:]
     tok_count = ids_ref.shape[1]
     step = pl.program_id(0)
 
@@ -453,25 +457,22 @@
         for k in range(n):
             first, second = chosen(ids, experts[k])
             at = places(rank[k : k + 1, :])
-            rows = slice(k * CAP, (k + 1) * CAP)
-            firsts[rows, :] = jnp.where(jnp.logical_and(at, first), 1.0, 0.0)
-            seconds[rows, :] = jnp.where(jnp.logical_and(at, second), 1.0, 0.0)
+            here = slice(k * CAP, (k + 1) * CAP)
+            firsts[here, :] = jnp.where(jnp.logical_and(at, first), 1.0, 0.0)
+            seconds[here, :] = jnp.where(jnp.logical_and(at, second), 1.0, 0.0)
         sums[...] = jnp.zeros_like(sums)
 
     for k in range(n):
-        out_rows[k * CAP : (k + 1) * CAP, :] = out_back_refs[k][...]
-        in_rows[k * CAP : (k + 1) * CAP, :] = in_back_refs[k][...]
+        rows[k * CAP : (k + 1) * CAP, :] = back_refs[k][...]
     prob = jnp.concatenate([prob_ref[...], jnp.zeros((6, tok_count), F32)], axis=0).T
     grad = grad_ref[...].astype(F32)
-    one, two = firsts[...].astype(BF), seconds[...].astype(BF)
     total = 0.0
     part = []
-    for choice, at in enumerate((one, two)):
-        out = mm_rows(at, out_rows[...])
+    for choice, at in enumerate((firsts, seconds)):
+        out = mm_rows(at[...].astype(BF), rows[...])
         total = total + prob[:, choice : choice + 1] * out
         part.append(jnp.sum(grad * out, axis=1, keepdims=True))
     out_ref[...] = total.astype(BF)
-    in_ref[...] = mm_rows(one + two, in_rows[...]).astype(BF)
     sums[...] += jnp.concatenate(part + [jnp.zeros((tok_count, 6), F32)], axis=1)
 
     @pl.when(step == pl.num_programs(0) - 1)
@@ -479,26 +480,62 @@
         prob_grad_ref[...] = sums[...].T[0:2, :]
 
 
-def combine(z, ids_t, prob_t, out_grad, back_out, back_in):
-    n = len(back_out)
+def combine_out(z, ids_t, prob_t, out_grad, backs):
+    n = len(backs)
     tok_count, width = out_grad.shape
     tile = 512
     by_tile = pl.BlockSpec((tok_count, tile), lambda j: (0, j))
     rows = n * CAP
     return pl.pallas_call(
-        functools.partial(combine_kernel, n),
+        functools.partial(combine_out_kernel, n),
         grid=(width // tile,),
-        out_shape=[shape_of((tok_count, width))] * 2 + [shape_of((2, tok_count), F32)],
+        out_shape=[shape_of((tok_count, width)), shape_of((2, tok_count), F32)],
         in_specs=[in_smem(), whole(ids_t.shape), whole(prob_t.shape), by_tile]
-        + [pl.BlockSpec((CAP, tile), lambda j: (0, j))] * (2 * n),
-        out_specs=[by_tile, by_tile, whole((2, tok_count))],
-        scratch_shapes=[pltpu.VMEM((rows, tile), BF)] * 2
-        + [pltpu.VMEM((tok_count, 8), F32)]
+        + [pl.BlockSpec((CAP, tile), lambda j: (0, j))] * n,
+        out_specs=[by_tile, whole((2, tok_count))],
+        scratch_shapes=[pltpu.VMEM((rows, tile), BF), pltpu.VMEM((tok_count, 8), F32)]
         + [pltpu.VMEM((rows, tok_count), F32)] * 2,
         compiler_params=params(),
-        cost_estimate=cost(600 * rows * tok_count * width, 4 * width * (rows + 2 * tok_count)),
-        name="combine",
-    )(z, ids_t, prob_t, out_grad, *back_out, *back_in)
+        cost_estimate=cost(4 * rows * tok_count * width, 2 * width * (rows + 2 * tok_count)),
+        name="combine_out",
+    )(z, ids_t, prob_t, out_grad, *backs)
+
+
+def combine_in_kernel(n, z_ref, ids_ref, *refs):
+    back_refs = refs[:n]
+    out_ref, rows, picks = refs[n:]
+
+    @pl.when(pl.program_id(0) == 0)
+    def _():
+        ids = ids_ref[...]
+        experts = [jnp.bitwise_xor(z_ref[0], k) for k in range(n)]
+        rank = ranks(ids, experts)
+        for k in range(n):
+            here = jnp.logical_and(places(rank[k : k + 1, :]), jnp.logical_or(*chosen(ids, experts[k])))
+            picks[k * CAP : (k + 1) * CAP, :] = jnp.where(here, 1.0, 0.0)
+
+    for k in range(n):
+        rows[k * CAP : (k + 1) * CAP, :] = back_refs[k][...]
+    out_ref[...] = mm_rows(picks[...].astype(BF), rows[...]).astype(BF)
+
+
+def combine_in(z, ids_t, backs, hint):
+    n = len(backs)
+    width = backs[0].shape[1]
+    tok_count = ids_t.shape[1]
+    tile = 1024
+    rows = n * CAP
+    return pl.pallas_call(
+        functools.partial(combine_in_kernel, n),
+        grid=(width // tile,),
+        out_shape=shape_of((tok_count, width)),
+        in_specs=[in_smem(), whole(ids_t.shape)] + [pl.BlockSpec((CAP, tile), lambda j: (0, j))] * n,
+        out_specs=pl.BlockSpec((tok_count, tile), lambda j: (0, j)),
+        scratch_shapes=[pltpu.VMEM((rows, tile), BF), pltpu.VMEM((rows, tok_count), F32)],
+        compiler_params=params(),
+        cost_estimate=cost(hint, 2 * width * (rows + tok_count)),
+        name="combine_in",
+    )(z, ids_t, *backs)
 
 
 def exchange(values):
@@ -519,30 +556,31 @@
     made = forward(xs, w_gate, w_up, w_down)
     slope, act, hidden = made[:3]
     back_out = exchange(made[3:])
+    layer_out, prob_grad_t = combine_out(z, ids_t, prob_t, out_grad, back_out)
     if parts == 8:
         me = lax.axis_index("dp").astype(jnp.int32)
         flips = [(r >> 2 & 1) * CORE | (r & 1) * ALONG_X | (r >> 1 & 1) * ALONG_Y for r in range(8)]
         owners = jnp.stack([me ^ f for f in flips])
         keep_t, send_t, w_near = turn(parts, owners, xs, hidden, w_down)
-        grad, g_rows = hidden_grad(gs, w_near, slope, act, [])
-        x_send, x_keep, y_send, y_keep = outer(
-            keep_t, swap(send_t, CORE), grad, swap(grad, CORE), g_rows, swap(g_rows, CORE), []
+        grad, g_rows, pack = hidden_grad(gs, w_near, slope, act, send_t)
+        other, recv = swap(grad, CORE), swap(pack, CORE)
+        x_send, y_send = outer(1, keep_t, recv, grad, other, g_rows, [])
+        din = input_grad(n, grad, w_gate, w_up, [x_send])
+        x_keep, y_keep = outer(0, keep_t, recv, grad, other, g_rows, din[:1])
+        back_in = exchange(din[:1] + hold(din[1:], [*back_out[1:], x_keep]))
+        x_next, x_mine, y_next, y_mine = fold_two(
+            x_keep, swap(x_send, ALONG_X), y_keep, swap(y_send, ALONG_Y), [*din[:1], layer_out]
         )
-        din = input_grad(n, grad, w_gate, w_up, [x_send])
-        back_in = exchange(din[:1] + hold(din[1:], back_out[1:]))
-        x_next, x_mine, y_next, y_mine = fold_two(
-            x_keep, swap(x_send, ALONG_X), y_keep, swap(y_send, ALONG_Y), din[:1]
-        )
-        layer_out, token_grad, prob_grad_t = combine(z, ids_t, prob_t, out_grad, back_out, back_in)
+        token_grad = combine_in(z, ids_t, back_in, 10 * 10**9)
         shapes = [(1, d // parts, w) for d, w in (w_gate.shape[1:], w_up.shape[1:], w_down.shape[1:])]
         sum_gate, sum_up, sum_down = fold_last(
             x_mine, swap(x_next, ALONG_Y), y_mine, swap(y_next, ALONG_X), shapes, [token_grad]
         )
     else:
-        grad, d_rows = hidden_grad(gs, w_down, slope, act, [])
+        grad, d_rows, _ = hidden_grad(gs, w_down, slope, act, hidden[:16, :256])
         din = input_grad(n, grad, w_gate, w_up, [])
         back_in = exchange(din)
-        layer_out, token_grad, prob_grad_t = combine(z, ids_t, prob_t, out_grad, back_out, back_in)
+        token_grad = combine_in(z, ids_t, back_in, 10**8)
         x_rows, count = jnp.concatenate(xs, 0), n * CAP
         sum_gate, sum_up, sum_down = (
             lax.psum_scatter(mm_rows(a, b).astype(BF), "dp", scatter_dimension=0, tiled=True)[None]

time: 114 us -> 113 us (level)
  waiting for transfers between devices: 43.5 us -> 35.8 us
  local copies, waits for them, and re-layouts: 3.78 us -> 10.1 us
    unnamed x34 -> x46, local copies, waits for them, and re-layouts: 3.7 us -> 9.99 us
    ppermute x7 -> x6, waiting for transfers between devices: 6.91 us -> 2.89 us  [swap(): return lax.ppermute(value, 'dp', [(i, i ^ bit) for i in range(count)])]
    ppermute x12, waiting for transfers between devices: 36.6 us -> 32.9 us  [exchange(): moved[k] = lax.ppermute(values[k], 'expert', [(i, i ^ k) for i in range(n)])]
    pallas_call x1 -> x3, Pallas kernels: 4.29 us -> 6.16 us  [the longest x1 2.83 us: combine_out(): pl.pallas_call(functools.partial(combine_out_kernel, n), grid=(width // t...]
    pallas_call x6, Pallas kernels: 12 us -> 10.8 us  [call(): return pl.pallas_call(body, in_specs=specs, **kwargs)(*args, *after)]
    ppermute x7 -> x6, starting transfers between devices: 5.73 us -> 6.68 us  [swap(): return lax.ppermute(value, 'dp', [(i, i ^ bit) for i in range(count)])]
  transfers between devices with their start and end apart: 19 -> 18, of which waited for: 8 -> 7; matrix products, arithmetic and copies ran while one was open for 0% -> 0% of each run, Pallas kernels for 21% -> 22%
where the time goes in v5:
time: 113 us
  starting transfers between devices  36 us (32%)
  waiting for transfers between devices  35.8 us (32%)
  Pallas kernels  30.1 us (27%)
  local copies, waits for them, and re-layouts  10.1 us (9%)
    ppermute x12, waiting for transfers between devices, exchange(): moved[k] = lax.ppermute(values[k], 'expert', [(i, i ^ k) for i in range(n)])  32.9 us
    ppermute x12, starting transfers between devices, exchange(): moved[k] = lax.ppermute(values[k], 'expert', [(i, i ^ k) for i in range(n)])  29.3 us
    pallas_call x6, Pallas kernels, call(): return pl.pallas_call(body, in_specs=specs, **kwargs)(*args, *after)  10.8 us
    unnamed x46, local copies, waits for them, and re-layouts  9.99 us
    pallas_call x1, Pallas kernels, forward(): pl.pallas_call(functools.partial(forward_kernel, n, steps, tile), grid=(s...  6.99 us
    ppermute x6, starting transfers between devices, swap(): return lax.ppermute(value, 'dp', [(i, i ^ bit) for i in range(count)])  6.68 us
    pallas_call x2, Pallas kernels, pick_rows(): pl.pallas_call(functools.partial(pick_kernel, n, scaled), out_shape=[shap...  4.88 us
    ppermute x6, waiting for transfers between devices, swap(): return lax.ppermute(value, 'dp', [(i, i ^ bit) for i in range(count)])  2.89 us
  transfers between devices with their start and end apart: 18, of which 7 were waited for; matrix products, arithmetic and copies ran while one was open for 0% of the time, Pallas kernels for 22%

profile of v5, /device:TPU:0, one launch (start us, length us, event | category | flops | bytes accessed | tf_op | source)
XLA Modules:
  0.0 112.7 jit_solution(10367892330080196263)
XLA Ops:
  0.6 2.4 %pick_rows.2 = (bf16[64,2048]{1,0:T(8,128)(2,1)}, bf16[64,2048]{1,0:T(8,128)(2,1)}, bf16[64,2048]{1,0:T(8,128)(2,1)}, bf16[64,2048]{1,0:T(8,128)(2,1)}) custom-call(s32[1]{0:T(128)} %bitcast.z_ref, s32[2,128]{1,0:T(2,128)} %bitcast.15, f32[2,128]{1,0:T(2,128)} %bitcast.12, bf16[128,2048]{1,0:T(8,128)(2,1)} %rows_ref.2), custom_call_target="tpu_custom_call" | custom-call | flops 134217728 | bytes 2097152 | tf_op jit(solution)/shard_map/pick_rows/pallas_call | solution.py:96
  3.1 3.0 %collective-permute-start = (bf16[64,2048]{1,0:T(8,128)(2,1)}, bf16[64,2048]{1,0:T(8,128)(2,1)S(1)}, u32[]{:S(2)}, u32[]{:S(2)}) collective-permute-start(bf16[64,2048]{1,0:T(8,128)(2,1)} %get-tuple-element.48), channel_id=1, source_target_pairs={{0,1},{1,0},{2,3},{3,2},{4,5},{5,4},{6,7},{7,6},{8,9},{9,8},{10,11... | collective-permute-start | bytes 786440 | tf_op jit(solution)/shard_map/ppermute | solution.py:545
  6.1 2.6 %collective-permute-start.1 = (bf16[64,2048]{1,0:T(8,128)(2,1)}, bf16[64,2048]{1,0:T(8,128)(2,1)S(1)}, u32[]{:S(2)}, u32[]{:S(2)}) collective-permute-start(bf16[64,2048]{1,0:T(8,128)(2,1)} %get-tuple-element.49), channel_id=1, source_target_pairs={{0,2},{1,3},{2,0},{3,1},{4,6},{5,7},{6,4},{7,5},{8,10},{9,11},{10,... | collective-permute-start | bytes 786440 | tf_op jit(solution)/shard_map/ppermute | solution.py:545
  8.7 2.4 %pick_rows.3 = (bf16[64,2048]{1,0:T(8,128)(2,1)}, bf16[64,2048]{1,0:T(8,128)(2,1)}, bf16[64,2048]{1,0:T(8,128)(2,1)}, bf16[64,2048]{1,0:T(8,128)(2,1)}) custom-call(s32[1]{0:T(128)} %bitcast.z_ref, s32[2,128]{1,0:T(2,128)} %bitcast.16, f32[2,128]{1,0:T(2,128)} %bitcast.13, bf16[128,2048]{1,0:T(8,128)(2,1)} %rows_ref.3), custom_call_target="tpu_custom_call" | custom-call | flops 134217728 | bytes 2097152 | tf_op jit(solution)/shard_map/pick_rows/pallas_call | solution.py:96
  12.0 3.5 %collective-permute-start.7 = (bf16[64,2048]{1,0:T(8,128)(2,1)}, bf16[64,2048]{1,0:T(8,128)(2,1)S(1)}, u32[]{:S(2)}, u32[]{:S(2)}) collective-permute-start(bf16[64,2048]{1,0:T(8,128)(2,1)} %get-tuple-element.59), channel_id=1, source_target_pairs={{0,2},{1,3},{2,0},{3,1},{4,6},{5,7},{6,4},{7,5},{8,10},{9,11},{10,... | collective-permute-start | bytes 786440 | tf_op jit(solution)/shard_map/ppermute | solution.py:545
  15.5 2.8 %collective-permute-done.refs_1_ = bf16[64,2048]{1,0:T(8,128)(2,1)S(1)} collective-permute-done((bf16[64,2048]{1,0:T(8,128)(2,1)}, bf16[64,2048]{1,0:T(8,128)(2,1)S(1)}, u32[]{:S(2)}, u32[]{:S(2)}) %collective-permute-start) | collective-permute-done | bytes 262176 | tf_op jit(solution)/shard_map/ppermute | solution.py:545
  18.3 4.6 %collective-permute-start.8 = (bf16[64,2048]{1,0:T(8,128)(2,1)}, bf16[64,2048]{1,0:T(8,128)(2,1)S(1)}, u32[]{:S(2)}, u32[]{:S(2)}) collective-permute-start(bf16[64,2048]{1,0:T(8,128)(2,1)} %get-tuple-element.60), channel_id=1, source_target_pairs={{0,3},{1,2},{2,1},{3,0},{4,7},{5,6},{6,5},{7,4},{8,11},{9,10},{10,... | collective-permute-start | bytes 786440 | tf_op jit(solution)/shard_map/ppermute | solution.py:545
  23.0 4.8 %collective-permute-done.1.refs_2_ = bf16[64,2048]{1,0:T(8,128)(2,1)S(1)} collective-permute-done((bf16[64,2048]{1,0:T(8,128)(2,1)}, bf16[64,2048]{1,0:T(8,128)(2,1)S(1)}, u32[]{:S(2)}, u32[]{:S(2)}) %collective-permute-start.1) | collective-permute-done | bytes 262176 | tf_op jit(solution)/shard_map/ppermute | solution.py:545
  28.7 7.0 %forward.1 = (f32[256,768]{1,0:T(8,128)S(1)}, f32[256,768]{1,0:T(8,128)S(1)}, bf16[256,768]{1,0:T(8,128)(2,1)S(1)}, bf16[64,2048]{1,0:T(8,128)(2,1)S(1)}, bf16[6...) custom-call(bf16[64,2048]{1,0:T(8,128)(2,1)S(1)} %copy-done.8, ...), custom_call_target="tpu_custom_call" | custom-call | flops 2415919104 | bytes 13500416 | tf_op jit(solution)/shard_map/forward/pallas_call | solution.py:176
  35.7 1.2 %turn.1 = (bf16[1408,256]{1,0:T(8,128)(2,1)S(1)}, bf16[1408,256]{1,0:T(8,128)(2,1)S(1)}, bf16[1,768,2048]{2,1,0:T(8,128)(2,1)S(1)}) custom-call(s32[8]{0:T(128)S(1)} %stack.35.me_ref, bf16[64,2048]{1,0:T(8,128)(2,1)S(1)} %copy-done.8, bf16[64,2048]{1,0:T(8,128)(2,1)S(1)} %collective-permute-done.refs_1_, ...), custom_call_target="tpu_custom_call" | custom-call | flops 1048576 | bytes 4325376 | tf_op jit(solution)/shard_map/turn/pallas_call | solution.py:224
  36.9 13.3 %collective-permute-done.7.refs_2_ = bf16[64,2048]{1,0:T(8,128)(2,1)S(1)} collective-permute-done((bf16[64,2048]{1,0:T(8,128)(2,1)}, bf16[64,2048]{1,0:T(8,128)(2,1)S(1)}, u32[]{:S(2)}, u32[]{:S(2)}) %collective-permute-start.7) | collective-permute-done | bytes 262176 | tf_op jit(solution)/shard_map/ppermute | solution.py:545
  50.2 1.8 %hidden_grad.1 = (bf16[512,768]{1,0:T(8,128)(2,1)S(1)}, bf16[256,2048]{1,0:T(8,128)(2,1)S(1)}, bf16[3456,256]{1,0:T(8,128)(2,1)S(1)}) custom-call(bf16[64,2048]{1,0:T(8,128)(2,1)S(1)} %copy-done.11, bf16[64,2048]{1,0:T(8,128)(2,1)S(1)} %collective-permute-done.6.refs_1_, bf16[64,2048]{1,0:T(8,128)(2,1)S(1)} %collective-permute-done.7.refs_2_, ...), custom_call_target="tpu_custom_call" | custom-call | flops 805306368 | bytes 7602176 | tf_op jit(solution)/shard_map/hidden_grad/pallas_call | solution.py:311
  52.6 4.7 %collective-permute-start.3 = (bf16[64,2048]{1,0:T(8,128)(2,1)S(1)}, bf16[64,2048]{1,0:T(8,128)(2,1)S(1)}, u32[]{:S(2)}, u32[]{:S(2)}) collective-permute-start(bf16[64,2048]{1,0:T(8,128)(2,1)S(1)} %get-tuple-element.52), channel_id=1, source_target_pairs={{0,1},{1,0},{2,3},{3,2},{4,5},{5,4},{6,7},{7,6},{8,9},{9,8},{10,11... | collective-permute-start | bytes 786440 | tf_op jit(solution)/shard_map/ppermute | solution.py:545
  58.4 1.5 %collective-permute-start.5 = (bf16[64,2048]{1,0:T(8,128)(2,1)S(1)}, bf16[64,2048]{1,0:T(8,128)(2,1)S(1)}, u32[]{:S(2)}, u32[]{:S(2)}) collective-permute-start(bf16[64,2048]{1,0:T(8,128)(2,1)S(1)} %get-tuple-element.54), channel_id=1, source_target_pairs={{0,3},{1,2},{2,1},{3,0},{4,7},{5,6},{6,5},{7,4},{8,11},{9,10},{10,... | collective-permute-start | bytes 786440 | tf_op jit(solution)/shard_map/ppermute | solution.py:545
  59.9 3.5 %outer.2 = (bf16[2,384,768]{2,1,0:T(8,128)(2,1)}, bf16[2,384,768]{2,1,0:T(8,128)(2,1)}) custom-call(bf16[1408,256]{1,0:T(8,128)(2,1)S(1)} %get-tuple-element.67.refs_0_, bf16[3456,256]{1,0:T(8,128)(2,1)S(1)} %collective-permute-done.9.refs_1_, bf16[512,768]{1,0:T(8,128)(2,1)S(1)} %get-tuple-element.66.refs_2_.refs_0_, ...), custom_call_target="tpu_custom_call" | custom-call | flops 1207959552 | bytes 3801088 | tf_op jit(solution)/shard_map/outer/pallas_call | solution.py:50
  63.4 1.5 %collective-permute-start.14 = (bf16[2,384,768]{2,1,0:T(8,128)(2,1)}, bf16[2,384,768]{2,1,0:T(8,128)(2,1)S(1)}, u32[]{:S(2)}, u32[]{:S(2)}) collective-permute-start(bf16[2,384,768]{2,1,0:T(8,128)(2,1)} %get-tuple-element.70.refs_3_), channel_id=1, source_target_pairs={{0,8},{4,12},{8,0},{12,4},{16,24},{20,28},{24,16},{28,20},{1,9},{5... | collective-permute-start | bytes 3538952 | tf_op jit(solution)/shard_map/ppermute | solution.py:443
  64.9 1.5 %collective-permute-start.15 = (bf16[2,384,768]{2,1,0:T(8,128)(2,1)}, bf16[2,384,768]{2,1,0:T(8,128)(2,1)S(1)}, u32[]{:S(2)}, u32[]{:S(2)}) collective-permute-start(bf16[2,384,768]{2,1,0:T(8,128)(2,1)} %get-tuple-element.80), channel_id=1, source_target_pairs={{0,16},{4,20},{8,24},{12,28},{16,0},{20,4},{24,8},{28,12},{1,17},{... | collective-permute-start | bytes 3538952 | tf_op jit(solution)/shard_map/ppermute | solution.py:443
  66.4 3.0 %input_grad.1 = (bf16[64,2048]{1,0:T(8,128)(2,1)S(1)}, bf16[64,2048]{1,0:T(8,128)(2,1)S(1)}, bf16[64,2048]{1,0:T(8,128)(2,1)S(1)}, bf16[64,2048]{1,0:T(8,128)(2,1)S(1)}) custom-call(bf16[512,768]{1,0:T(8,128)(2,1)S(1)} %get-tuple-element.66.refs_2_.refs_0_, bf16[1,2048,768]{2,1,0:T(8,128)(2,1)S(1)} %copy-done.1, bf16[1,2048,768]{2,1,0:T(8,128)(2,1)S(1)} %copy-done.2, ...), custom_call_target="tpu_custom_call" | custom-call | flops 1610612736 | bytes 8126464 | tf_op jit(solution)/shard_map/input_grad/pallas_call | solution.py:50
  69.5 2.6 %outer.3 = (bf16[2,384,768]{2,1,0:T(8,128)(2,1)S(1)}, bf16[2,384,768]{2,1,0:T(8,128)(2,1)S(1)}) custom-call(bf16[1408,256]{1,0:T(8,128)(2,1)S(1)} %get-tuple-element.67.refs_0_, bf16[3456,256]{1,0:T(8,128)(2,1)S(1)} %collective-permute-done.9.refs_1_, bf16[512,768]{1,0:T(8,128)(2,1)S(1)} %get-tuple-element.66.refs_2_.refs_0_, ...), custom_call_target="tpu_custom_call" | custom-call | flops 1207959552 | bytes 3801088 | tf_op jit(solution)/shard_map/outer/pallas_call | solution.py:50
  74.1 4.6 %collective-permute-done.4.refs_2_.refs_4_ = bf16[64,2048]{1,0:T(8,128)(2,1)S(1)} collective-permute-done((bf16[64,2048]{1,0:T(8,128)(2,1)S(1)}, bf16[64,2048]{1,0:T(8,128)(2,1)S(1)}, u32[]{:S(2)}, u32[]{:S(2)}) %collective-permute-start.4) | collective-permute-done | bytes 262176 | tf_op jit(solution)/shard_map/ppermute | solution.py:545
  79.5 5.0 %collective-permute-start.11 = (bf16[64,2048]{1,0:T(8,128)(2,1)}, bf16[64,2048]{1,0:T(8,128)(2,1)S(1)}, u32[]{:S(2)}, u32[]{:S(2)}) collective-permute-start(bf16[64,2048]{1,0:T(8,128)(2,1)} %get-tuple-element.76), channel_id=1, source_target_pairs={{0,1},{1,0},{2,3},{3,2},{4,5},{5,4},{6,7},{7,6},{8,9},{9,8},{10,11... | collective-permute-start | bytes 786440 | tf_op jit(solution)/shard_map/ppermute | solution.py:545
  84.5 1.1 collective-permute-start.12
  85.6 1.4 %collective-permute-start.13 = (bf16[64,2048]{1,0:T(8,128)(2,1)}, bf16[64,2048]{1,0:T(8,128)(2,1)S(1)}, u32[]{:S(2)}, u32[]{:S(2)}) collective-permute-start(bf16[64,2048]{1,0:T(8,128)(2,1)} %get-tuple-element.78), channel_id=1, source_target_pairs={{0,3},{1,2},{2,1},{3,0},{4,7},{5,6},{6,5},{7,4},{8,11},{9,10},{10,... | collective-permute-start | bytes 786440 | tf_op jit(solution)/shard_map/ppermute | solution.py:545
  89.9 2.8 %combine_out.1 = (bf16[128,2048]{1,0:T(8,128)(2,1)}, f32[2,128]{1,0:T(2,128)}) custom-call(s32[1]{0:T(128)} %bitcast.z_ref, s32[2,128]{1,0:T(2,128)S(1)} %bitcast.17, f32[2,128]{1,0:T(2,128)S(1)} %bitcast.14, bf16[128,2048]{1,0:T(8,128)(2,1)S(1)} %copy-done.3, bf16[64,2048]{1,0:T(8,128)(2,1)S(1)} %get-tuple-element.51.refs_0_, ...), custom_call_target="tpu_custom_call" | custom-call | flops 268435456 | bytes 2097152 | tf_op jit(solution)/shard_map/combine_out/pallas_call | solution.py:489
  92.7 1.3 %copy-done.7 = bf16[2,384,768]{2,1,0:T(8,128)(2,1)S(1)} copy-done((bf16[2,384,768]{2,1,0:T(8,128)(2,1)S(1)}, bf16[2,384,768]{2,1,0:T(8,128)(2,1)}, u32[]{:S(2)}) %copy-start.7) | copy-done | bytes 1179672
  95.5 1.6 %collective-permute-start.16 = (bf16[384,768]{1,0:T(8,128)(2,1)S(1)}, bf16[384,768]{1,0:T(8,128)(2,1)S(1)}, u32[]{:S(2)}, u32[]{:S(2)}) collective-permute-start(bf16[384,768]{1,0:T(8,128)(2,1)S(1)} %get-tuple-element.82), channel_id=1, source_target_pairs={{0,16},{4,20},{8,24},{12,28},{16,0},{20,4},{24,8},{28,12},{1,17},{... | collective-permute-start | bytes 1769480 | tf_op jit(solution)/shard_map/ppermute | solution.py:443
  97.2 1.5 %collective-permute-start.17 = (bf16[384,768]{1,0:T(8,128)(2,1)S(1)}, bf16[384,768]{1,0:T(8,128)(2,1)S(1)}, u32[]{:S(2)}, u32[]{:S(2)}) collective-permute-start(bf16[384,768]{1,0:T(8,128)(2,1)S(1)} %get-tuple-element.84), channel_id=1, source_target_pairs={{0,8},{4,12},{8,0},{12,4},{16,24},{20,28},{24,16},{28,20},{1,9},{5... | collective-permute-start | bytes 1769480 | tf_op jit(solution)/shard_map/ppermute | solution.py:443
  98.6 7.5 %collective-permute-done.12.refs_2_ = bf16[64,2048]{1,0:T(8,128)(2,1)S(1)} collective-permute-done((bf16[64,2048]{1,0:T(8,128)(2,1)}, bf16[64,2048]{1,0:T(8,128)(2,1)S(1)}, u32[]{:S(2)}, u32[]{:S(2)}) %collective-permute-start.12) | collective-permute-done | bytes 262176 | tf_op jit(solution)/shard_map/ppermute | solution.py:545
  106.1 1.5 %combine_in.1.refs_4_ = bf16[128,2048]{1,0:T(8,128)(2,1)} custom-call(s32[1]{0:T(128)} %bitcast.z_ref, s32[2,128]{1,0:T(2,128)S(1)} %bitcast.18, bf16[64,2048]{1,0:T(8,128)(2,1)S(1)} %get-tuple-element.71.refs_5_.refs_0_.refs_4_, bf16[64,2048]{1,0:T(8,128)(2,1)S(1)} %collective-permute-done.11.refs_1_, bf16[64,2048]{1,0:T(8,128)(2,1)S(1)} %collective-permute-done.12.refs_2_, ...), custom_call_target="tpu_custom_call" | custom-call | flops 10000000000 | bytes 1572864 | tf_op jit(solution)/shard_map/combine_in/pallas_call | solution.py:528
  107.6 1.6 %collective-permute-done.16.refs_1_ = bf16[384,768]{1,0:T(8,128)(2,1)S(1)} collective-permute-done((bf16[384,768]{1,0:T(8,128)(2,1)S(1)}, bf16[384,768]{1,0:T(8,128)(2,1)S(1)}, u32[]{:S(2)}, u32[]{:S(2)}) %collective-permute-start.16) | collective-permute-done | bytes 589856 | tf_op jit(solution)/shard_map/ppermute | solution.py:443
  109.2 1.2 %collective-permute-done.17.refs_3_ = bf16[384,768]{1,0:T(8,128)(2,1)S(1)} collective-permute-done((bf16[384,768]{1,0:T(8,128)(2,1)S(1)}, bf16[384,768]{1,0:T(8,128)(2,1)S(1)}, u32[]{:S(2)}, u32[]{:S(2)}) %collective-permute-start.17) | collective-permute-done | bytes 589856 | tf_op jit(solution)/shard_map/ppermute | solution.py:443
  111.5 1.2 %fold_last.1 = (bf16[1,256,768]{2,1,0:T(8,128)(2,1)}, bf16[1,256,768]{2,1,0:T(8,128)(2,1)}, bf16[1,96,2048]{2,1,0:T(8,128)(2,1)}) custom-call(bf16[384,768]{1,0:T(8,128)(2,1)S(1)} %get-tuple-element.81.refs_0_, bf16[384,768]{1,0:T(8,128)(2,1)S(1)} %collective-permute-done.16.refs_1_, bf16[384,768]{1,0:T(8,128)(2,1)S(1)} %get-tuple-element.83.refs_2_, ...), custom_call_target="tpu_custom_call" | custom-call | flops 589824 | bytes 3538944 | tf_op jit(solution)/shard_map/fold_last/pallas_call | solution.py:50
  (64 shorter events, 11.8 us)
Async XLA Ops:
  3.1 15.2 %collective-permute-start = (bf16[64,2048]{1,0:T(8,128)(2,1)}, bf16[64,2048]{1,0:T(8,128)(2,1)S(1)}, u32[]{:S(2)}, u32[]{:S(2)}) collective-permute-start(bf16[64,2048]{1,0:T(8,128)(2,1)} %get-tuple-element.48), channel_id=1, source_target_pairs={{0,1},{1,0},{2,3},{3,2},{4,5},{5,4},{6,7},{7,6},{8,9},{9,8},{10,11... | collective-permute-start | bytes 786440 | tf_op jit(solution)/shard_map/ppermute | solution.py:545
  6.1 21.6 %collective-permute-start.1 = (bf16[64,2048]{1,0:T(8,128)(2,1)}, bf16[64,2048]{1,0:T(8,128)(2,1)S(1)}, u32[]{:S(2)}, u32[]{:S(2)}) collective-permute-start(bf16[64,2048]{1,0:T(8,128)(2,1)} %get-tuple-element.49), channel_id=1, source_target_pairs={{0,2},{1,3},{2,0},{3,1},{4,6},{5,7},{6,4},{7,5},{8,10},{9,11},{10,... | collective-permute-start | bytes 786440 | tf_op jit(solution)/shard_map/ppermute | solution.py:545
  8.7 19.0 %collective-permute-start.2 = (bf16[64,2048]{1,0:T(8,128)(2,1)}, bf16[64,2048]{1,0:T(8,128)(2,1)S(1)}, u32[]{:S(2)}, u32[]{:S(2)}) collective-permute-start(bf16[64,2048]{1,0:T(8,128)(2,1)} %get-tuple-element.50), channel_id=1, source_target_pairs={{0,3},{1,2},{2,1},{3,0},{4,7},{5,6},{6,5},{7,4},{8,11},{9,10},{10,... | collective-permute-start | bytes 786440 | tf_op jit(solution)/shard_map/ppermute | solution.py:545
  11.1 25.8 %collective-permute-start.6 = (bf16[64,2048]{1,0:T(8,128)(2,1)}, bf16[64,2048]{1,0:T(8,128)(2,1)S(1)}, u32[]{:S(2)}, u32[]{:S(2)}) collective-permute-start(bf16[64,2048]{1,0:T(8,128)(2,1)} %get-tuple-element.58), channel_id=1, source_target_pairs={{0,1},{1,0},{2,3},{3,2},{4,5},{5,4},{6,7},{7,6},{8,9},{9,8},{10,11... | collective-permute-start | bytes 786440 | tf_op jit(solution)/shard_map/ppermute | solution.py:545
  12.0 38.2 %collective-permute-start.7 = (bf16[64,2048]{1,0:T(8,128)(2,1)}, bf16[64,2048]{1,0:T(8,128)(2,1)S(1)}, u32[]{:S(2)}, u32[]{:S(2)}) collective-permute-start(bf16[64,2048]{1,0:T(8,128)(2,1)} %get-tuple-element.59), channel_id=1, source_target_pairs={{0,2},{1,3},{2,0},{3,1},{4,6},{5,7},{6,4},{7,5},{8,10},{9,11},{10,... | collective-permute-start | bytes 786440 | tf_op jit(solution)/shard_map/ppermute | solution.py:545
  18.3 31.9 %collective-permute-start.8 = (bf16[64,2048]{1,0:T(8,128)(2,1)}, bf16[64,2048]{1,0:T(8,128)(2,1)S(1)}, u32[]{:S(2)}, u32[]{:S(2)}) collective-permute-start(bf16[64,2048]{1,0:T(8,128)(2,1)} %get-tuple-element.60), channel_id=1, source_target_pairs={{0,3},{1,2},{2,1},{3,0},{4,7},{5,6},{6,5},{7,4},{8,11},{9,10},{10,... | collective-permute-start | bytes 786440 | tf_op jit(solution)/shard_map/ppermute | solution.py:545
  28.7 7.0 %copy-start = (bf16[1,768,2048]{2,1,0:T(8,128)(2,1)S(1)}, bf16[1,768,2048]{2,1,0:T(8,128)(2,1)}, u32[]{:S(2)}) copy-start(bf16[1,768,2048]{2,1,0:T(8,128)(2,1)} %refs_5_.3) | copy-start | bytes 9437188
  35.7 14.5 %copy-start.11 = (bf16[64,2048]{1,0:T(8,128)(2,1)S(1)}, bf16[64,2048]{1,0:T(8,128)(2,1)}, u32[]{:S(2)}) copy-start(bf16[64,2048]{1,0:T(8,128)(2,1)} %get-tuple-element.57.refs_0_) | copy-start | bytes 786436
  50.2 16.2 %copy-start.2 = (bf16[1,2048,768]{2,1,0:T(8,128)(2,1)S(1)}, bf16[1,2048,768]{2,1,0:T(8,128)(2,1)}, u32[]{:S(2)}) copy-start(bf16[1,2048,768]{2,1,0:T(8,128)(2,1)} %refs_2_.1) | copy-start | bytes 9437188
  52.1 7.8 %collective-permute-start.9 = (bf16[3456,256]{1,0:T(8,128)(2,1)S(1)}, bf16[3456,256]{1,0:T(8,128)(2,1)S(1)}, u32[]{:S(2)}, u32[]{:S(2)}) collective-permute-start(bf16[3456,256]{1,0:T(8,128)(2,1)S(1)} %get-tuple-element.68), channel_id=1, source_target_pairs={{0,4},{4,0},{8,12},{12,8},{16,20},{20,16},{24,28},{28,24},{1,5},{5... | collective-permute-start | bytes 5308424 | tf_op jit(solution)/shard_map/ppermute | solution.py:443
  52.1 7.7 %collective-permute-start.10 = (bf16[512,768]{1,0:T(8,128)(2,1)S(1)}, bf16[512,768]{1,0:T(8,128)(2,1)S(1)}, u32[]{:S(2)}, u32[]{:S(2)}) collective-permute-start(bf16[512,768]{1,0:T(8,128)(2,1)S(1)} %get-tuple-element.66.refs_2_.refs_0_), channel_id=1, source_target_pairs={{0,4},{4,0},{8,12},{12,8},{16,20},{20,16},{24,28},{28,24},{1,5},{5... | collective-permute-start | bytes 2359304 | tf_op jit(solution)/shard_map/ppermute | solution.py:443
  52.6 21.5 %collective-permute-start.3 = (bf16[64,2048]{1,0:T(8,128)(2,1)S(1)}, bf16[64,2048]{1,0:T(8,128)(2,1)S(1)}, u32[]{:S(2)}, u32[]{:S(2)}) collective-permute-start(bf16[64,2048]{1,0:T(8,128)(2,1)S(1)} %get-tuple-element.52), channel_id=1, source_target_pairs={{0,1},{1,0},{2,3},{3,2},{4,5},{5,4},{6,7},{7,6},{8,9},{9,8},{10,11... | collective-permute-start | bytes 786440 | tf_op jit(solution)/shard_map/ppermute | solution.py:545
  57.4 21.3 %collective-permute-start.4 = (bf16[64,2048]{1,0:T(8,128)(2,1)S(1)}, bf16[64,2048]{1,0:T(8,128)(2,1)S(1)}, u32[]{:S(2)}, u32[]{:S(2)}) collective-permute-start(bf16[64,2048]{1,0:T(8,128)(2,1)S(1)} %get-tuple-element.53), channel_id=1, source_target_pairs={{0,2},{1,3},{2,0},{3,1},{4,6},{5,7},{6,4},{7,5},{8,10},{9,11},{10,... | collective-permute-start | bytes 786440 | tf_op jit(solution)/shard_map/ppermute | solution.py:545
  58.4 20.3 %collective-permute-start.5 = (bf16[64,2048]{1,0:T(8,128)(2,1)S(1)}, bf16[64,2048]{1,0:T(8,128)(2,1)S(1)}, u32[]{:S(2)}, u32[]{:S(2)}) collective-permute-start(bf16[64,2048]{1,0:T(8,128)(2,1)S(1)} %get-tuple-element.54), channel_id=1, source_target_pairs={{0,3},{1,2},{2,1},{3,0},{4,7},{5,6},{6,5},{7,4},{8,11},{9,10},{10,... | collective-permute-start | bytes 786440 | tf_op jit(solution)/shard_map/ppermute | solution.py:545
  59.9 6.5 %copy-start.1 = (bf16[1,2048,768]{2,1,0:T(8,128)(2,1)S(1)}, bf16[1,2048,768]{2,1,0:T(8,128)(2,1)}, u32[]{:S(2)}) copy-start(bf16[1,2048,768]{2,1,0:T(8,128)(2,1)} %refs_1_.1) | copy-start | bytes 9437188
  63.4 29.3 %collective-permute-start.14 = (bf16[2,384,768]{2,1,0:T(8,128)(2,1)}, bf16[2,384,768]{2,1,0:T(8,128)(2,1)S(1)}, u32[]{:S(2)}, u32[]{:S(2)}) collective-permute-start(bf16[2,384,768]{2,1,0:T(8,128)(2,1)} %get-tuple-element.70.refs_3_), channel_id=1, source_target_pairs={{0,8},{4,12},{8,0},{12,4},{16,24},{20,28},{24,16},{28,20},{1,9},{5... | collective-permute-start | bytes 3538952 | tf_op jit(solution)/shard_map/ppermute | solution.py:443
  64.9 27.8 %collective-permute-start.15 = (bf16[2,384,768]{2,1,0:T(8,128)(2,1)}, bf16[2,384,768]{2,1,0:T(8,128)(2,1)S(1)}, u32[]{:S(2)}, u32[]{:S(2)}) collective-permute-start(bf16[2,384,768]{2,1,0:T(8,128)(2,1)} %get-tuple-element.80), channel_id=1, source_target_pairs={{0,16},{4,20},{8,24},{12,28},{16,0},{20,4},{24,8},{28,12},{1,17},{... | collective-permute-start | bytes 3538952 | tf_op jit(solution)/shard_map/ppermute | solution.py:443
  69.4 9.3 %copy-start.20 = (bf16[64,2048]{1,0:T(8,128)(2,1)}, bf16[64,2048]{1,0:T(8,128)(2,1)S(1)}, u32[]{:S(2)}) copy-start(bf16[64,2048]{1,0:T(8,128)(2,1)S(1)} %get-tuple-element.72.refs_0_) | copy-start | bytes 786436
  69.4 9.3 %copy-start.21 = (bf16[64,2048]{1,0:T(8,128)(2,1)}, bf16[64,2048]{1,0:T(8,128)(2,1)S(1)}, u32[]{:S(2)}) copy-start(bf16[64,2048]{1,0:T(8,128)(2,1)S(1)} %get-tuple-element.73.refs_1_) | copy-start | bytes 786436
  69.5 9.3 %copy-start.22 = (bf16[64,2048]{1,0:T(8,128)(2,1)}, bf16[64,2048]{1,0:T(8,128)(2,1)S(1)}, u32[]{:S(2)}) copy-start(bf16[64,2048]{1,0:T(8,128)(2,1)S(1)} %get-tuple-element.74.refs_2_) | copy-start | bytes 786436
  74.1 4.6 %copy-start.12 = (bf16[64,2048]{1,0:T(8,128)(2,1)}, bf16[64,2048]{1,0:T(8,128)(2,1)S(1)}, u32[]{:S(2)}) copy-start(bf16[64,2048]{1,0:T(8,128)(2,1)S(1)} %collective-permute-done.3.refs_1_.refs_3_) | copy-start | bytes 786436
  79.5 7.5 %copy-start.3 = (bf16[128,2048]{1,0:T(8,128)(2,1)S(1)}, bf16[128,2048]{1,0:T(8,128)(2,1)}, u32[]{:S(2)}) copy-start(bf16[128,2048]{1,0:T(8,128)(2,1)} %rows_ref.3) | copy-start | bytes 1572868
  79.5 7.5 %copy-start.18 = (f32[128,2]{0,1:T(2,128)S(1)}, f32[128,2]{0,1:T(2,128)}, u32[]{:S(2)}) copy-start(f32[128,2]{0,1:T(2,128)} %param.9) | copy-start | bytes 3076
  79.5 7.5 %copy-start.19 = (s32[128,2]{0,1:T(2,128)S(1)}, s32[128,2]{0,1:T(2,128)}, u32[]{:S(2)}) copy-start(s32[128,2]{0,1:T(2,128)} %param.8) | copy-start | bytes 3076
  79.5 13.2 %copy-start.5 = (bf16[2,384,768]{2,1,0:T(8,128)(2,1)S(1)}, bf16[2,384,768]{2,1,0:T(8,128)(2,1)}, u32[]{:S(2)}) copy-start(bf16[2,384,768]{2,1,0:T(8,128)(2,1)} %copy-done.4) | copy-start | bytes 3538948
  79.5 19.1 %collective-permute-start.11 = (bf16[64,2048]{1,0:T(8,128)(2,1)}, bf16[64,2048]{1,0:T(8,128)(2,1)S(1)}, u32[]{:S(2)}, u32[]{:S(2)}) collective-permute-start(bf16[64,2048]{1,0:T(8,128)(2,1)} %get-tuple-element.76), channel_id=1, source_target_pairs={{0,1},{1,0},{2,3},{3,2},{4,5},{5,4},{6,7},{7,6},{8,9},{9,8},{10,11... | collective-permute-start | bytes 786440 | tf_op jit(solution)/shard_map/ppermute | solution.py:545
  84.5 21.6 %collective-permute-start.12 = (bf16[64,2048]{1,0:T(8,128)(2,1)}, bf16[64,2048]{1,0:T(8,128)(2,1)S(1)}, u32[]{:S(2)}, u32[]{:S(2)}) collective-permute-start(bf16[64,2048]{1,0:T(8,128)(2,1)} %get-tuple-element.77), channel_id=1, source_target_pairs={{0,2},{1,3},{2,0},{3,1},{4,6},{5,7},{6,4},{7,5},{8,10},{9,11},{10,... | collective-permute-start | bytes 786440 | tf_op jit(solution)/shard_map/ppermute | solution.py:545
  85.6 20.5 %collective-permute-start.13 = (bf16[64,2048]{1,0:T(8,128)(2,1)}, bf16[64,2048]{1,0:T(8,128)(2,1)S(1)}, u32[]{:S(2)}, u32[]{:S(2)}) collective-permute-start(bf16[64,2048]{1,0:T(8,128)(2,1)} %get-tuple-element.78), channel_id=1, source_target_pairs={{0,3},{1,2},{2,1},{3,0},{4,7},{5,6},{6,5},{7,4},{8,11},{9,10},{10,... | collective-permute-start | bytes 786440 | tf_op jit(solution)/shard_map/ppermute | solution.py:545
  92.7 1.3 %copy-start.7 = (bf16[2,384,768]{2,1,0:T(8,128)(2,1)S(1)}, bf16[2,384,768]{2,1,0:T(8,128)(2,1)}, u32[]{:S(2)}) copy-start(bf16[2,384,768]{2,1,0:T(8,128)(2,1)} %copy-done.6) | copy-start | bytes 3538948
  95.5 13.7 %collective-permute-start.16 = (bf16[384,768]{1,0:T(8,128)(2,1)S(1)}, bf16[384,768]{1,0:T(8,128)(2,1)S(1)}, u32[]{:S(2)}, u32[]{:S(2)}) collective-permute-start(bf16[384,768]{1,0:T(8,128)(2,1)S(1)} %get-tuple-element.82), channel_id=1, source_target_pairs={{0,16},{4,20},{8,24},{12,28},{16,0},{20,4},{24,8},{28,12},{1,17},{... | collective-permute-start | bytes 1769480 | tf_op jit(solution)/shard_map/ppermute | solution.py:443
  97.2 13.3 %collective-permute-start.17 = (bf16[384,768]{1,0:T(8,128)(2,1)S(1)}, bf16[384,768]{1,0:T(8,128)(2,1)S(1)}, u32[]{:S(2)}, u32[]{:S(2)}) collective-permute-start(bf16[384,768]{1,0:T(8,128)(2,1)S(1)} %get-tuple-element.84), channel_id=1, source_target_pairs={{0,8},{4,12},{8,0},{12,4},{16,24},{20,28},{24,16},{28,20},{1,9},{5... | collective-permute-start | bytes 1769480 | tf_op jit(solution)/shard_map/ppermute | solution.py:443
  110.5 1.0 copy-start.9
  (9 other events, 8.4 us)

commit v6 on v5

--- a/solution.py
+++ b/solution.py
@@ -48,6 +48,13 @@
 
     specs = list(in_specs) + [pl.BlockSpec(memory_space=pl.ANY)] * len(after)
     return pl.pallas_call(body, in_specs=specs, **kwargs)(*args, *after)
+
+
+TOKEN = (8, 128)
+
+
+def mark(ref):
+    ref[...] = jnp.zeros(TOKEN, F32)
 
 
 def cost(flops, moved):
@@ -234,7 +241,8 @@
     )(owners, *xs, hidden, w_down)
 
 
-def outer_kernel(group, keep_ref, recv_ref, own_ref, other_ref, own_g_ref, x_ref, y_ref):
+def outer_kernel(group, keep_ref, recv_ref, own_ref, other_ref, own_g_ref, x_ref, y_ref, token_ref):
+    mark(token_ref)
     step = pl.program_id(0)
     half, high = 4, own_ref.shape[0] // 2
     size = 256
@@ -271,10 +279,10 @@
         functools.partial(outer_kernel, group),
         after,
         grid=(ff // tile,),
-        out_shape=[shape_of((2, high, ff))] * 2,
+        out_shape=[shape_of((2, high, ff))] * 2 + [shape_of(TOKEN, F32)],
         in_specs=[whole(keep.shape), whole(recv.shape)] + [col] * 2 + [whole(own_g.shape)],
         args=(keep, recv, own, other, own_g),
-        out_specs=[part] * 2,
+        out_specs=[part] * 2 + [whole(TOKEN)],
         compiler_params=params(),
         cost_estimate=cost(3 * rows * width * ff, 4 * keep.size + 8 * high * ff),
         name="outer",
@@ -322,7 +330,8 @@
 
 def input_grad_kernel(n, steps, tile, grad_ref, wg_ref, wu_ref, *refs):
     out_refs = refs[:n]
-    wg_buf, wu_buf, sems = refs[n:]
+    token_ref, wg_buf, wu_buf, sems = refs[n:]
+    mark(token_ref)
     step = pl.program_id(0)
 
     def loads(j):
@@ -355,10 +364,10 @@
         functools.partial(input_grad_kernel, n, steps, tile),
         after,
         grid=(steps,),
-        out_shape=[shape_of((CAP, width))] * n,
+        out_shape=[shape_of((CAP, width))] * n + [shape_of(TOKEN, F32)],
         in_specs=[whole((2 * rows, ff))] + [pl.BlockSpec(memory_space=pltpu.HBM)] * 2,
         args=(grad, w_gate, w_up),
-        out_specs=[pl.BlockSpec((CAP, tile), lambda j: (0, j))] * n,
+        out_specs=[pl.BlockSpec((CAP, tile), lambda j: (0, j))] * n + [whole(TOKEN)],
         scratch_shapes=[pltpu.VMEM((steps, tile, ff), BF)] * 2 + [pltpu.SemaphoreType.DMA((2, steps))],
         compiler_params=params(),
         cost_estimate=cost(4 * rows * width * ff, 4 * width * ff + 2 * rows * (width + 2 * ff)),
@@ -385,24 +394,24 @@
     )
 
 
-def fold_two_kernel(x_keep, x_recv, y_keep, y_recv, x_next, x_mine, y_next, y_mine):
-    for keep, recv, away, mine in ((x_keep, x_recv, x_next, x_mine), (y_keep, y_recv, y_next, y_mine)):
-        away[...] = (keep[1].astype(F32) + recv[1].astype(F32)).astype(BF)
-        mine[...] = (keep[0].astype(F32) + recv[0].astype(F32)).astype(BF)
-
-
-def fold_two(x_keep, x_recv, y_keep, y_recv, after):
-    _, high, width = x_keep.shape
+def fold_two_kernel(keep, recv, away, mine, token_ref):
+    mark(token_ref)
+    away[...] = (keep[1].astype(F32) + recv[1].astype(F32)).astype(BF)
+    mine[...] = (keep[0].astype(F32) + recv[0].astype(F32)).astype(BF)
+
+
+def fold_two(keep, recv, after):
+    _, high, width = keep.shape
     return call(
         fold_two_kernel,
         after,
         grid=(1,),
-        out_shape=[shape_of((high, width))] * 4,
-        in_specs=[whole((2, high, width))] * 4,
-        args=(x_keep, x_recv, y_keep, y_recv),
-        out_specs=[whole((high, width))] * 4,
-        compiler_params=params(),
-        cost_estimate=cost(4 * high * width, 24 * high * width),
+        out_shape=[shape_of((high, width))] * 2 + [shape_of(TOKEN, F32)],
+        in_specs=[whole((2, high, width))] * 2,
+        args=(keep, recv),
+        out_specs=[whole((high, width))] * 2 + [whole(TOKEN)],
+        compiler_params=params(),
+        cost_estimate=cost(2 * high * width, 12 * high * width),
         name="fold_two",
     )
 
@@ -445,7 +454,8 @@
 
 def combine_out_kernel(n, z_ref, ids_ref, prob_ref, grad_ref, *refs):
     back_refs = refs[:n]
-    out_ref, prob_grad_ref, rows, sums, firsts, seconds = refs[n:]
+    out_ref, prob_grad_ref, token_ref, rows, sums, firsts, seconds = refs[n:]
+    mark(token_ref)
     tok_count = ids_ref.shape[1]
     step = pl.program_id(0)
 
@@ -489,10 +499,10 @@
     return pl.pallas_call(
         functools.partial(combine_out_kernel, n),
         grid=(width // tile,),
-        out_shape=[shape_of((tok_count, width)), shape_of((2, tok_count), F32)],
+        out_shape=[shape_of((tok_count, width)), shape_of((2, tok_count), F32), shape_of(TOKEN, F32)],
         in_specs=[in_smem(), whole(ids_t.shape), whole(prob_t.shape), by_tile]
         + [pl.BlockSpec((CAP, tile), lambda j: (0, j))] * n,
-        out_specs=[by_tile, whole((2, tok_count))],
+        out_specs=[by_tile, whole((2, tok_count)), whole(TOKEN)],
         scratch_shapes=[pltpu.VMEM((rows, tile), BF), pltpu.VMEM((tok_count, 8), F32)]
         + [pltpu.VMEM((rows, tok_count), F32)] * 2,
         compiler_params=params(),
@@ -503,7 +513,8 @@
 
 def combine_in_kernel(n, z_ref, ids_ref, *refs):
     back_refs = refs[:n]
-    out_ref, rows, picks = refs[n:]
+    out_ref, token_ref, rows, picks = refs[n:]
+    mark(token_ref)
 
     @pl.when(pl.program_id(0) == 0)
     def _():
@@ -528,9 +539,9 @@
     return pl.pallas_call(
         functools.partial(combine_in_kernel, n),
         grid=(width // tile,),
-        out_shape=shape_of((tok_count, width)),
+        out_shape=[shape_of((tok_count, width)), shape_of(TOKEN, F32)],
         in_specs=[in_smem(), whole(ids_t.shape)] + [pl.BlockSpec((CAP, tile), lambda j: (0, j))] * n,
-        out_specs=pl.BlockSpec((tok_count, tile), lambda j: (0, j)),
+        out_specs=[pl.BlockSpec((tok_count, tile), lambda j: (0, j)), whole(TOKEN)],
         scratch_shapes=[pltpu.VMEM((rows, tile), BF), pltpu.VMEM((rows, tok_count), F32)],
         compiler_params=params(),
         cost_estimate=cost(hint, 2 * width * (rows + tok_count)),
@@ -556,7 +567,7 @@
     made = forward(xs, w_gate, w_up, w_down)
     slope, act, hidden = made[:3]
     back_out = exchange(made[3:])
-    layer_out, prob_grad_t = combine_out(z, ids_t, prob_t, out_grad, back_out)
+    layer_out, prob_grad_t, shown = combine_out(z, ids_t, prob_t, out_grad, back_out)
     if parts == 8:
         me = lax.axis_index("dp").astype(jnp.int32)
         flips = [(r >> 2 & 1) * CORE | (r & 1) * ALONG_X | (r >> 1 & 1) * ALONG_Y for r in range(8)]
@@ -564,23 +575,22 @@
         keep_t, send_t, w_near = turn(parts, owners, xs, hidden, w_down)
         grad, g_rows, pack = hidden_grad(gs, w_near, slope, act, send_t)
         other, recv = swap(grad, CORE), swap(pack, CORE)
-        x_send, y_send = outer(1, keep_t, recv, grad, other, g_rows, [])
-        din = input_grad(n, grad, w_gate, w_up, [x_send])
-        x_keep, y_keep = outer(0, keep_t, recv, grad, other, g_rows, din[:1])
-        back_in = exchange(din[:1] + hold(din[1:], [*back_out[1:], x_keep]))
-        x_next, x_mine, y_next, y_mine = fold_two(
-            x_keep, swap(x_send, ALONG_X), y_keep, swap(y_send, ALONG_Y), [*din[:1], layer_out]
-        )
-        token_grad = combine_in(z, ids_t, back_in, 10 * 10**9)
+        x_send, y_send, token = outer(1, keep_t, recv, grad, other, g_rows, [])
+        *din, token = input_grad(n, grad, w_gate, w_up, [token])
+        x_keep, y_keep, token = outer(0, keep_t, recv, grad, other, g_rows, [token])
+        back_in = exchange([din[0], *hold(din[1:], [*back_out[1:], token])])
+        x_next, x_mine, token = fold_two(x_keep, swap(x_send, ALONG_X), [shown])
+        y_next, y_mine, _ = fold_two(y_keep, swap(y_send, ALONG_Y), [token])
+        token_grad, token = combine_in(z, ids_t, back_in, 10 * 10**9)
         shapes = [(1, d // parts, w) for d, w in (w_gate.shape[1:], w_up.shape[1:], w_down.shape[1:])]
         sum_gate, sum_up, sum_down = fold_last(
-            x_mine, swap(x_next, ALONG_Y), y_mine, swap(y_next, ALONG_X), shapes, [token_grad]
+            x_mine, swap(x_next, ALONG_Y), y_mine, swap(y_next, ALONG_X), shapes, [token]
         )
     else:
         grad, d_rows, _ = hidden_grad(gs, w_down, slope, act, hidden[:16, :256])
-        din = input_grad(n, grad, w_gate, w_up, [])
+        *din, _ = input_grad(n, grad, w_gate, w_up, [])
         back_in = exchange(din)
-        token_grad = combine_in(z, ids_t, back_in, 10**8)
+        token_grad, _ = combine_in(z, ids_t, back_in, 10**8)
         x_rows, count = jnp.concatenate(xs, 0), n * CAP
         sum_gate, sum_up, sum_down = (
             lax.psum_scatter(mm_rows(a, b).astype(BF), "dp", scatter_dimension=0, tiled=True)[None]

time: 113 us -> 110 us (0.973)
  waiting for transfers between devices: 35.8 us -> 33.7 us
  local copies, waits for them, and re-layouts: 10.1 us -> 8.84 us
    ppermute x6, waiting for transfers between devices: 2.89 us -> 0.9 us  [swap(): return lax.ppermute(value, 'dp', [(i, i ^ bit) for i in range(count)])]
    unnamed x46 -> x48, local copies, waits for them, and re-layouts: 9.99 us -> 8.76 us
    pallas_call x6 -> x7, Pallas kernels: 10.8 us -> 11.2 us  [call(): return pl.pallas_call(body, in_specs=specs, **kwargs)(*args, *after)]
  transfers between devices with their start and end apart: 18 -> 18, of which waited for: 7 -> 6; matrix products, arithmetic and copies ran while one was open for 0% -> 0% of each run, Pallas kernels for 22% -> 23%
where the time goes in v6:
time: 110 us
  starting transfers between devices  35.9 us (33%)
  waiting for transfers between devices  33.7 us (31%)
  Pallas kernels  30.5 us (28%)
  local copies, waits for them, and re-layouts  8.84 us (8%)
    ppermute x12, waiting for transfers between devices, exchange(): moved[k] = lax.ppermute(values[k], 'expert', [(i, i ^ k) for i in range(n)])  32.8 us
    ppermute x12, starting transfers between devices, exchange(): moved[k] = lax.ppermute(values[k], 'expert', [(i, i ^ k) for i in range(n)])  29.3 us
    pallas_call x7, Pallas kernels, call(): return pl.pallas_call(body, in_specs=specs, **kwargs)(*args, *after)  11.2 us
    unnamed x48, local copies, waits for them, and re-layouts  8.76 us
    pallas_call x1, Pallas kernels, forward(): pl.pallas_call(functools.partial(forward_kernel, n, steps, tile), grid=(s...  6.99 us
    ppermute x6, starting transfers between devices, swap(): return lax.ppermute(value, 'dp', [(i, i ^ bit) for i in range(count)])  6.58 us
    pallas_call x2, Pallas kernels, pick_rows(): pl.pallas_call(functools.partial(pick_kernel, n, scaled), out_shape=[shap...  4.88 us
    pallas_call x1, Pallas kernels, combine_out(): pl.pallas_call(functools.partial(combine_out_kernel, n), grid=(width // t...  2.85 us
  transfers between devices with their start and end apart: 18, of which 6 were waited for; matrix products, arithmetic and copies ran while one was open for 0% of the time, Pallas kernels for 23%

profile of v6, /device:TPU:0, one launch (start us, length us, event | category | flops | bytes accessed | tf_op | source)
XLA Modules:
  0.0 109.7 jit_solution(11687027549119097839)
XLA Ops:
  0.6 2.4 %pick_rows.2 = (bf16[64,2048]{1,0:T(8,128)(2,1)}, bf16[64,2048]{1,0:T(8,128)(2,1)}, bf16[64,2048]{1,0:T(8,128)(2,1)}, bf16[64,2048]{1,0:T(8,128)(2,1)}) custom-call(s32[1]{0:T(128)} %bitcast.z_ref, s32[2,128]{1,0:T(2,128)} %bitcast.15, f32[2,128]{1,0:T(2,128)} %bitcast.12, bf16[128,2048]{1,0:T(8,128)(2,1)} %rows_ref.2), custom_call_target="tpu_custom_call" | custom-call | flops 134217728 | bytes 2097152 | tf_op jit(solution)/shard_map/pick_rows/pallas_call | solution.py:103
  3.1 3.0 %collective-permute-start = (bf16[64,2048]{1,0:T(8,128)(2,1)}, bf16[64,2048]{1,0:T(8,128)(2,1)S(1)}, u32[]{:S(2)}, u32[]{:S(2)}) collective-permute-start(bf16[64,2048]{1,0:T(8,128)(2,1)} %get-tuple-element.55), channel_id=1, source_target_pairs={{0,1},{1,0},{2,3},{3,2},{4,5},{5,4},{6,7},{7,6},{8,9},{9,8},{10,11... | collective-permute-start | bytes 786440 | tf_op jit(solution)/shard_map/ppermute | solution.py:556
  6.1 2.6 %collective-permute-start.1 = (bf16[64,2048]{1,0:T(8,128)(2,1)}, bf16[64,2048]{1,0:T(8,128)(2,1)S(1)}, u32[]{:S(2)}, u32[]{:S(2)}) collective-permute-start(bf16[64,2048]{1,0:T(8,128)(2,1)} %get-tuple-element.56), channel_id=1, source_target_pairs={{0,2},{1,3},{2,0},{3,1},{4,6},{5,7},{6,4},{7,5},{8,10},{9,11},{10,... | collective-permute-start | bytes 786440 | tf_op jit(solution)/shard_map/ppermute | solution.py:556
  8.7 2.4 %pick_rows.3 = (bf16[64,2048]{1,0:T(8,128)(2,1)}, bf16[64,2048]{1,0:T(8,128)(2,1)}, bf16[64,2048]{1,0:T(8,128)(2,1)}, bf16[64,2048]{1,0:T(8,128)(2,1)}) custom-call(s32[1]{0:T(128)} %bitcast.z_ref, s32[2,128]{1,0:T(2,128)} %bitcast.16, f32[2,128]{1,0:T(2,128)} %bitcast.13, bf16[128,2048]{1,0:T(8,128)(2,1)} %rows_ref.3), custom_call_target="tpu_custom_call" | custom-call | flops 134217728 | bytes 2097152 | tf_op jit(solution)/shard_map/pick_rows/pallas_call | solution.py:103
  12.0 3.5 %collective-permute-start.7 = (bf16[64,2048]{1,0:T(8,128)(2,1)}, bf16[64,2048]{1,0:T(8,128)(2,1)S(1)}, u32[]{:S(2)}, u32[]{:S(2)}) collective-permute-start(bf16[64,2048]{1,0:T(8,128)(2,1)} %get-tuple-element.66), channel_id=1, source_target_pairs={{0,2},{1,3},{2,0},{3,1},{4,6},{5,7},{6,4},{7,5},{8,10},{9,11},{10,... | collective-permute-start | bytes 786440 | tf_op jit(solution)/shard_map/ppermute | solution.py:556
  15.5 2.8 %collective-permute-done.refs_1_ = bf16[64,2048]{1,0:T(8,128)(2,1)S(1)} collective-permute-done((bf16[64,2048]{1,0:T(8,128)(2,1)}, bf16[64,2048]{1,0:T(8,128)(2,1)S(1)}, u32[]{:S(2)}, u32[]{:S(2)}) %collective-permute-start) | collective-permute-done | bytes 262176 | tf_op jit(solution)/shard_map/ppermute | solution.py:556
  18.3 4.6 %collective-permute-start.8 = (bf16[64,2048]{1,0:T(8,128)(2,1)}, bf16[64,2048]{1,0:T(8,128)(2,1)S(1)}, u32[]{:S(2)}, u32[]{:S(2)}) collective-permute-start(bf16[64,2048]{1,0:T(8,128)(2,1)} %get-tuple-element.67), channel_id=1, source_target_pairs={{0,3},{1,2},{2,1},{3,0},{4,7},{5,6},{6,5},{7,4},{8,11},{9,10},{10,... | collective-permute-start | bytes 786440 | tf_op jit(solution)/shard_map/ppermute | solution.py:556
  23.0 4.8 %collective-permute-done.1.refs_2_ = bf16[64,2048]{1,0:T(8,128)(2,1)S(1)} collective-permute-done((bf16[64,2048]{1,0:T(8,128)(2,1)}, bf16[64,2048]{1,0:T(8,128)(2,1)S(1)}, u32[]{:S(2)}, u32[]{:S(2)}) %collective-permute-start.1) | collective-permute-done | bytes 262176 | tf_op jit(solution)/shard_map/ppermute | solution.py:556
  28.7 7.0 %forward.1 = (f32[256,768]{1,0:T(8,128)S(1)}, f32[256,768]{1,0:T(8,128)S(1)}, bf16[256,768]{1,0:T(8,128)(2,1)S(1)}, bf16[64,2048]{1,0:T(8,128)(2,1)S(1)}, bf16[6...) custom-call(bf16[64,2048]{1,0:T(8,128)(2,1)S(1)} %copy-done.8, ...), custom_call_target="tpu_custom_call" | custom-call | flops 2415919104 | bytes 13500416 | tf_op jit(solution)/shard_map/forward/pallas_call | solution.py:183
  35.7 1.2 %turn.1 = (bf16[1408,256]{1,0:T(8,128)(2,1)S(1)}, bf16[1408,256]{1,0:T(8,128)(2,1)S(1)}, bf16[1,768,2048]{2,1,0:T(8,128)(2,1)S(1)}) custom-call(s32[8]{0:T(128)S(1)} %stack.35.me_ref, bf16[64,2048]{1,0:T(8,128)(2,1)S(1)} %copy-done.8, bf16[64,2048]{1,0:T(8,128)(2,1)S(1)} %collective-permute-done.refs_1_, ...), custom_call_target="tpu_custom_call" | custom-call | flops 1048576 | bytes 4325376 | tf_op jit(solution)/shard_map/turn/pallas_call | solution.py:231
  36.9 13.3 %collective-permute-done.7.refs_2_ = bf16[64,2048]{1,0:T(8,128)(2,1)S(1)} collective-permute-done((bf16[64,2048]{1,0:T(8,128)(2,1)}, bf16[64,2048]{1,0:T(8,128)(2,1)S(1)}, u32[]{:S(2)}, u32[]{:S(2)}) %collective-permute-start.7) | collective-permute-done | bytes 262176 | tf_op jit(solution)/shard_map/ppermute | solution.py:556
  50.2 1.8 %hidden_grad.1 = (bf16[512,768]{1,0:T(8,128)(2,1)S(1)}, bf16[256,2048]{1,0:T(8,128)(2,1)S(1)}, bf16[3456,256]{1,0:T(8,128)(2,1)S(1)}) custom-call(bf16[64,2048]{1,0:T(8,128)(2,1)S(1)} %copy-done.9, bf16[64,2048]{1,0:T(8,128)(2,1)S(1)} %collective-permute-done.6.refs_1_, bf16[64,2048]{1,0:T(8,128)(2,1)S(1)} %collective-permute-done.7.refs_2_, ...), custom_call_target="tpu_custom_call" | custom-call | flops 805306368 | bytes 7602176 | tf_op jit(solution)/shard_map/hidden_grad/pallas_call | solution.py:319
  52.6 4.7 %collective-permute-start.3 = (bf16[64,2048]{1,0:T(8,128)(2,1)S(1)}, bf16[64,2048]{1,0:T(8,128)(2,1)S(1)}, u32[]{:S(2)}, u32[]{:S(2)}) collective-permute-start(bf16[64,2048]{1,0:T(8,128)(2,1)S(1)} %get-tuple-element.59), channel_id=1, source_target_pairs={{0,1},{1,0},{2,3},{3,2},{4,5},{5,4},{6,7},{7,6},{8,9},{9,8},{10,11... | collective-permute-start | bytes 786440 | tf_op jit(solution)/shard_map/ppermute | solution.py:556
  57.4 1.0 collective-permute-start.4
  58.4 1.5 %collective-permute-start.5 = (bf16[64,2048]{1,0:T(8,128)(2,1)S(1)}, bf16[64,2048]{1,0:T(8,128)(2,1)S(1)}, u32[]{:S(2)}, u32[]{:S(2)}) collective-permute-start(bf16[64,2048]{1,0:T(8,128)(2,1)S(1)} %get-tuple-element.61), channel_id=1, source_target_pairs={{0,3},{1,2},{2,1},{3,0},{4,7},{5,6},{6,5},{7,4},{8,11},{9,10},{10,... | collective-permute-start | bytes 786440 | tf_op jit(solution)/shard_map/ppermute | solution.py:556
  59.9 3.5 %outer.2 = (bf16[2,384,768]{2,1,0:T(8,128)(2,1)}, bf16[2,384,768]{2,1,0:T(8,128)(2,1)}, f32[8,128]{1,0:T(8,128)S(1)}) custom-call(bf16[1408,256]{1,0:T(8,128)(2,1)S(1)} %get-tuple-element.74.refs_0_, bf16[3456,256]{1,0:T(8,128)(2,1)S(1)} %collective-permute-done.9.refs_1_, bf16[512,768]{1,0:T(8,128)(2,1)S(1)} %get-tuple-element.73.refs_2_.refs_0_, ...), custom_call_target="tpu_custom_call" | custom-call | flops 1207959552 | bytes 3801088 | tf_op jit(solution)/shard_map/outer/pallas_call | solution.py:50
  63.4 1.5 %collective-permute-start.14 = (bf16[2,384,768]{2,1,0:T(8,128)(2,1)}, bf16[2,384,768]{2,1,0:T(8,128)(2,1)S(1)}, u32[]{:S(2)}, u32[]{:S(2)}) collective-permute-start(bf16[2,384,768]{2,1,0:T(8,128)(2,1)} %get-tuple-element.89), channel_id=1, source_target_pairs={{0,8},{4,12},{8,0},{12,4},{16,24},{20,28},{24,16},{28,20},{1,9},{5... | collective-permute-start | bytes 3538952 | tf_op jit(solution)/shard_map/ppermute | solution.py:452
  64.9 1.5 %collective-permute-start.16 = (bf16[2,384,768]{2,1,0:T(8,128)(2,1)}, bf16[2,384,768]{2,1,0:T(8,128)(2,1)S(1)}, u32[]{:S(2)}, u32[]{:S(2)}) collective-permute-start(bf16[2,384,768]{2,1,0:T(8,128)(2,1)} %get-tuple-element.94), channel_id=1, source_target_pairs={{0,16},{4,20},{8,24},{12,28},{16,0},{20,4},{24,8},{28,12},{1,17},{... | collective-permute-start | bytes 3538952 | tf_op jit(solution)/shard_map/ppermute | solution.py:452
  66.4 3.0 %input_grad.1 = (bf16[64,2048]{1,0:T(8,128)(2,1)S(1)}, bf16[64,2048]{1,0:T(8,128)(2,1)S(1)}, bf16[64,2048]{1,0:T(8,128)(2,1)S(1)}, bf16[64,2048]{1,0:T(8,128)(2,1)S(1)}, f32[8,128]{1,0:T(8,128)S(1)}) custom-call(bf16[512,768]{1,0:T(8,128)(2,1)S(1)} %get-tuple-element.73.refs_2_.refs_0_, bf16[1,2048,768]{2,1,0:T(8,128)(2,1)S(1)} %copy-done.1, ...), custom_call_target="tpu_custom_call" | custom-call | flops 1610612736 | bytes 8126464 | tf_op jit(solution)/shard_map/input_grad/pallas_call | solution.py:50
  71.6 2.6 %outer.3 = (bf16[2,384,768]{2,1,0:T(8,128)(2,1)S(1)}, bf16[2,384,768]{2,1,0:T(8,128)(2,1)S(1)}, f32[8,128]{1,0:T(8,128)S(1)}) custom-call(bf16[1408,256]{1,0:T(8,128)(2,1)S(1)} %get-tuple-element.74.refs_0_, bf16[3456,256]{1,0:T(8,128)(2,1)S(1)} %collective-permute-done.9.refs_1_, bf16[512,768]{1,0:T(8,128)(2,1)S(1)} %get-tuple-element.73.refs_2_.refs_0_, ...), custom_call_target="tpu_custom_call" | custom-call | flops 1207959552 | bytes 3801088 | tf_op jit(solution)/shard_map/outer/pallas_call | solution.py:50
  74.1 1.0 copy-done.4
  75.2 1.0 copy-done.6
  76.2 2.5 %collective-permute-done.4.refs_2_.refs_4_ = bf16[64,2048]{1,0:T(8,128)(2,1)S(1)} collective-permute-done((bf16[64,2048]{1,0:T(8,128)(2,1)S(1)}, bf16[64,2048]{1,0:T(8,128)(2,1)S(1)}, u32[]{:S(2)}, u32[]{:S(2)}) %collective-permute-start.4) | collective-permute-done | bytes 262176 | tf_op jit(solution)/shard_map/ppermute | solution.py:556
  79.5 5.0 %collective-permute-start.11 = (bf16[64,2048]{1,0:T(8,128)(2,1)}, bf16[64,2048]{1,0:T(8,128)(2,1)S(1)}, u32[]{:S(2)}, u32[]{:S(2)}) collective-permute-start(bf16[64,2048]{1,0:T(8,128)(2,1)} %get-tuple-element.84), channel_id=1, source_target_pairs={{0,1},{1,0},{2,3},{3,2},{4,5},{5,4},{6,7},{7,6},{8,9},{9,8},{10,11... | collective-permute-start | bytes 786440 | tf_op jit(solution)/shard_map/ppermute | solution.py:556
  84.6 1.1 collective-permute-start.12
  85.6 1.4 %collective-permute-start.13 = (bf16[64,2048]{1,0:T(8,128)(2,1)}, bf16[64,2048]{1,0:T(8,128)(2,1)S(1)}, u32[]{:S(2)}, u32[]{:S(2)}) collective-permute-start(bf16[64,2048]{1,0:T(8,128)(2,1)} %get-tuple-element.86), channel_id=1, source_target_pairs={{0,3},{1,2},{2,1},{3,0},{4,7},{5,6},{6,5},{7,4},{8,11},{9,10},{10,... | collective-permute-start | bytes 786440 | tf_op jit(solution)/shard_map/ppermute | solution.py:556
  89.9 2.8 %combine_out.1 = (bf16[128,2048]{1,0:T(8,128)(2,1)}, f32[2,128]{1,0:T(2,128)}, f32[8,128]{1,0:T(8,128)S(1)}) custom-call(s32[1]{0:T(128)} %bitcast.z_ref, s32[2,128]{1,0:T(2,128)S(1)} %bitcast.17, f32[2,128]{1,0:T(2,128)S(1)} %bitcast.14, bf16[128,2048]{1,0:T(8,128)(2,1)S(1)} %copy-done.3, bf16[64,2048]{1,0:T(8,128)(2,1)S(1)} %get-tuple-element.58.refs_0_, ...), custom_call_target="tpu_custom_call" | custom-call | flops 268435456 | bytes 2097152 | tf_op jit(solution)/shard_map/combine_out/pallas_call | solution.py:499
  93.7 1.5 %collective-permute-start.17 = (bf16[384,768]{1,0:T(8,128)(2,1)S(1)}, bf16[384,768]{1,0:T(8,128)(2,1)S(1)}, u32[]{:S(2)}, u32[]{:S(2)}) collective-permute-start(bf16[384,768]{1,0:T(8,128)(2,1)S(1)} %get-tuple-element.97), channel_id=1, source_target_pairs={{0,8},{4,12},{8,0},{12,4},{16,24},{20,28},{24,16},{28,20},{1,9},{5... | collective-permute-start | bytes 1769480 | tf_op jit(solution)/shard_map/ppermute | solution.py:452
  95.2 1.5 %collective-permute-start.15 = (bf16[384,768]{1,0:T(8,128)(2,1)S(1)}, bf16[384,768]{1,0:T(8,128)(2,1)S(1)}, u32[]{:S(2)}, u32[]{:S(2)}) collective-permute-start(bf16[384,768]{1,0:T(8,128)(2,1)S(1)} %get-tuple-element.92), channel_id=1, source_target_pairs={{0,16},{4,20},{8,24},{12,28},{16,0},{20,4},{24,8},{28,12},{1,17},{... | collective-permute-start | bytes 1769480 | tf_op jit(solution)/shard_map/ppermute | solution.py:452
  96.7 9.5 %collective-permute-done.12.refs_2_ = bf16[64,2048]{1,0:T(8,128)(2,1)S(1)} collective-permute-done((bf16[64,2048]{1,0:T(8,128)(2,1)}, bf16[64,2048]{1,0:T(8,128)(2,1)S(1)}, u32[]{:S(2)}, u32[]{:S(2)}) %collective-permute-start.12) | collective-permute-done | bytes 262176 | tf_op jit(solution)/shard_map/ppermute | solution.py:556
  106.1 1.5 %combine_in.1 = (bf16[128,2048]{1,0:T(8,128)(2,1)}, f32[8,128]{1,0:T(8,128)S(1)}) custom-call(s32[1]{0:T(128)} %bitcast.z_ref, s32[2,128]{1,0:T(2,128)S(1)} %bitcast.18, bf16[64,2048]{1,0:T(8,128)(2,1)S(1)} %copy-done.19, bf16[64,2048]{1,0:T(8,128)(2,1)S(1)} %collective-permute-done.11.refs_1_, bf16[64,2048]{1,0:T(8,128)(2,1)S(1)} %collective-permute-done.12.refs_2_, ...), custom_call_target="tpu_custom_call" | custom-call | flops 10000000000 | bytes 1572864 | tf_op jit(solution)/shard_map/combine_in/pallas_call | solution.py:539
  108.5 1.2 %fold_last.1 = (bf16[1,256,768]{2,1,0:T(8,128)(2,1)}, bf16[1,256,768]{2,1,0:T(8,128)(2,1)}, bf16[1,96,2048]{2,1,0:T(8,128)(2,1)}) custom-call(bf16[384,768]{1,0:T(8,128)(2,1)S(1)} %get-tuple-element.91.refs_0_, bf16[384,768]{1,0:T(8,128)(2,1)S(1)} %collective-permute-done.15.refs_1_, bf16[384,768]{1,0:T(8,128)(2,1)S(1)} %get-tuple-element.96.refs_2_, ...), custom_call_target="tpu_custom_call" | custom-call | flops 589824 | bytes 3538944 | tf_op jit(solution)/shard_map/fold_last/pallas_call | solution.py:50
  (67 shorter events, 10.1 us)
Async XLA Ops:
  3.1 15.2 %collective-permute-start = (bf16[64,2048]{1,0:T(8,128)(2,1)}, bf16[64,2048]{1,0:T(8,128)(2,1)S(1)}, u32[]{:S(2)}, u32[]{:S(2)}) collective-permute-start(bf16[64,2048]{1,0:T(8,128)(2,1)} %get-tuple-element.55), channel_id=1, source_target_pairs={{0,1},{1,0},{2,3},{3,2},{4,5},{5,4},{6,7},{7,6},{8,9},{9,8},{10,11... | collective-permute-start | bytes 786440 | tf_op jit(solution)/shard_map/ppermute | solution.py:556
  6.1 21.6 %collective-permute-start.1 = (bf16[64,2048]{1,0:T(8,128)(2,1)}, bf16[64,2048]{1,0:T(8,128)(2,1)S(1)}, u32[]{:S(2)}, u32[]{:S(2)}) collective-permute-start(bf16[64,2048]{1,0:T(8,128)(2,1)} %get-tuple-element.56), channel_id=1, source_target_pairs={{0,2},{1,3},{2,0},{3,1},{4,6},{5,7},{6,4},{7,5},{8,10},{9,11},{10,... | collective-permute-start | bytes 786440 | tf_op jit(solution)/shard_map/ppermute | solution.py:556
  8.7 19.0 %collective-permute-start.2 = (bf16[64,2048]{1,0:T(8,128)(2,1)}, bf16[64,2048]{1,0:T(8,128)(2,1)S(1)}, u32[]{:S(2)}, u32[]{:S(2)}) collective-permute-start(bf16[64,2048]{1,0:T(8,128)(2,1)} %get-tuple-element.57), channel_id=1, source_target_pairs={{0,3},{1,2},{2,1},{3,0},{4,7},{5,6},{6,5},{7,4},{8,11},{9,10},{10,... | collective-permute-start | bytes 786440 | tf_op jit(solution)/shard_map/ppermute | solution.py:556
  11.1 25.8 %collective-permute-start.6 = (bf16[64,2048]{1,0:T(8,128)(2,1)}, bf16[64,2048]{1,0:T(8,128)(2,1)S(1)}, u32[]{:S(2)}, u32[]{:S(2)}) collective-permute-start(bf16[64,2048]{1,0:T(8,128)(2,1)} %get-tuple-element.65), channel_id=1, source_target_pairs={{0,1},{1,0},{2,3},{3,2},{4,5},{5,4},{6,7},{7,6},{8,9},{9,8},{10,11... | collective-permute-start | bytes 786440 | tf_op jit(solution)/shard_map/ppermute | solution.py:556
  12.0 38.2 %collective-permute-start.7 = (bf16[64,2048]{1,0:T(8,128)(2,1)}, bf16[64,2048]{1,0:T(8,128)(2,1)S(1)}, u32[]{:S(2)}, u32[]{:S(2)}) collective-permute-start(bf16[64,2048]{1,0:T(8,128)(2,1)} %get-tuple-element.66), channel_id=1, source_target_pairs={{0,2},{1,3},{2,0},{3,1},{4,6},{5,7},{6,4},{7,5},{8,10},{9,11},{10,... | collective-permute-start | bytes 786440 | tf_op jit(solution)/shard_map/ppermute | solution.py:556
  18.3 31.9 %collective-permute-start.8 = (bf16[64,2048]{1,0:T(8,128)(2,1)}, bf16[64,2048]{1,0:T(8,128)(2,1)S(1)}, u32[]{:S(2)}, u32[]{:S(2)}) collective-permute-start(bf16[64,2048]{1,0:T(8,128)(2,1)} %get-tuple-element.67), channel_id=1, source_target_pairs={{0,3},{1,2},{2,1},{3,0},{4,7},{5,6},{6,5},{7,4},{8,11},{9,10},{10,... | collective-permute-start | bytes 786440 | tf_op jit(solution)/shard_map/ppermute | solution.py:556
  28.7 7.0 %copy-start = (bf16[1,768,2048]{2,1,0:T(8,128)(2,1)S(1)}, bf16[1,768,2048]{2,1,0:T(8,128)(2,1)}, u32[]{:S(2)}) copy-start(bf16[1,768,2048]{2,1,0:T(8,128)(2,1)} %refs_5_.3) | copy-start | bytes 9437188
  35.7 14.5 %copy-start.9 = (bf16[64,2048]{1,0:T(8,128)(2,1)S(1)}, bf16[64,2048]{1,0:T(8,128)(2,1)}, u32[]{:S(2)}) copy-start(bf16[64,2048]{1,0:T(8,128)(2,1)} %get-tuple-element.64.refs_0_) | copy-start | bytes 786436
  50.2 16.2 %copy-start.2 = (bf16[1,2048,768]{2,1,0:T(8,128)(2,1)S(1)}, bf16[1,2048,768]{2,1,0:T(8,128)(2,1)}, u32[]{:S(2)}) copy-start(bf16[1,2048,768]{2,1,0:T(8,128)(2,1)} %refs_2_.1) | copy-start | bytes 9437188
  52.1 7.8 %collective-permute-start.9 = (bf16[3456,256]{1,0:T(8,128)(2,1)S(1)}, bf16[3456,256]{1,0:T(8,128)(2,1)S(1)}, u32[]{:S(2)}, u32[]{:S(2)}) collective-permute-start(bf16[3456,256]{1,0:T(8,128)(2,1)S(1)} %get-tuple-element.75), channel_id=1, source_target_pairs={{0,4},{4,0},{8,12},{12,8},{16,20},{20,16},{24,28},{28,24},{1,5},{5... | collective-permute-start | bytes 5308424 | tf_op jit(solution)/shard_map/ppermute | solution.py:452
  52.1 7.7 %collective-permute-start.10 = (bf16[512,768]{1,0:T(8,128)(2,1)S(1)}, bf16[512,768]{1,0:T(8,128)(2,1)S(1)}, u32[]{:S(2)}, u32[]{:S(2)}) collective-permute-start(bf16[512,768]{1,0:T(8,128)(2,1)S(1)} %get-tuple-element.73.refs_2_.refs_0_), channel_id=1, source_target_pairs={{0,4},{4,0},{8,12},{12,8},{16,20},{20,16},{24,28},{28,24},{1,5},{5... | collective-permute-start | bytes 2359304 | tf_op jit(solution)/shard_map/ppermute | solution.py:452
  52.6 23.6 %collective-permute-start.3 = (bf16[64,2048]{1,0:T(8,128)(2,1)S(1)}, bf16[64,2048]{1,0:T(8,128)(2,1)S(1)}, u32[]{:S(2)}, u32[]{:S(2)}) collective-permute-start(bf16[64,2048]{1,0:T(8,128)(2,1)S(1)} %get-tuple-element.59), channel_id=1, source_target_pairs={{0,1},{1,0},{2,3},{3,2},{4,5},{5,4},{6,7},{7,6},{8,9},{9,8},{10,11... | collective-permute-start | bytes 786440 | tf_op jit(solution)/shard_map/ppermute | solution.py:556
  57.4 21.3 %collective-permute-start.4 = (bf16[64,2048]{1,0:T(8,128)(2,1)S(1)}, bf16[64,2048]{1,0:T(8,128)(2,1)S(1)}, u32[]{:S(2)}, u32[]{:S(2)}) collective-permute-start(bf16[64,2048]{1,0:T(8,128)(2,1)S(1)} %get-tuple-element.60), channel_id=1, source_target_pairs={{0,2},{1,3},{2,0},{3,1},{4,6},{5,7},{6,4},{7,5},{8,10},{9,11},{10,... | collective-permute-start | bytes 786440 | tf_op jit(solution)/shard_map/ppermute | solution.py:556
  58.4 20.3 %collective-permute-start.5 = (bf16[64,2048]{1,0:T(8,128)(2,1)S(1)}, bf16[64,2048]{1,0:T(8,128)(2,1)S(1)}, u32[]{:S(2)}, u32[]{:S(2)}) collective-permute-start(bf16[64,2048]{1,0:T(8,128)(2,1)S(1)} %get-tuple-element.61), channel_id=1, source_target_pairs={{0,3},{1,2},{2,1},{3,0},{4,7},{5,6},{6,5},{7,4},{8,11},{9,10},{10,... | collective-permute-start | bytes 786440 | tf_op jit(solution)/shard_map/ppermute | solution.py:556
  59.9 6.6 %copy-start.1 = (bf16[1,2048,768]{2,1,0:T(8,128)(2,1)S(1)}, bf16[1,2048,768]{2,1,0:T(8,128)(2,1)}, u32[]{:S(2)}) copy-start(bf16[1,2048,768]{2,1,0:T(8,128)(2,1)} %refs_1_.1) | copy-start | bytes 9437188
  63.4 29.3 %collective-permute-start.14 = (bf16[2,384,768]{2,1,0:T(8,128)(2,1)}, bf16[2,384,768]{2,1,0:T(8,128)(2,1)S(1)}, u32[]{:S(2)}, u32[]{:S(2)}) collective-permute-start(bf16[2,384,768]{2,1,0:T(8,128)(2,1)} %get-tuple-element.89), channel_id=1, source_target_pairs={{0,8},{4,12},{8,0},{12,4},{16,24},{20,28},{24,16},{28,20},{1,9},{5... | collective-permute-start | bytes 3538952 | tf_op jit(solution)/shard_map/ppermute | solution.py:452
  64.9 28.1 %collective-permute-start.16 = (bf16[2,384,768]{2,1,0:T(8,128)(2,1)}, bf16[2,384,768]{2,1,0:T(8,128)(2,1)S(1)}, u32[]{:S(2)}, u32[]{:S(2)}) collective-permute-start(bf16[2,384,768]{2,1,0:T(8,128)(2,1)} %get-tuple-element.94), channel_id=1, source_target_pairs={{0,16},{4,20},{8,24},{12,28},{16,0},{20,4},{24,8},{28,12},{1,17},{... | collective-permute-start | bytes 3538952 | tf_op jit(solution)/shard_map/ppermute | solution.py:452
  71.6 2.6 %copy-start.18 = (bf16[64,2048]{1,0:T(8,128)(2,1)}, bf16[64,2048]{1,0:T(8,128)(2,1)S(1)}, u32[]{:S(2)}) copy-start(bf16[64,2048]{1,0:T(8,128)(2,1)S(1)} %get-tuple-element.78.refs_0_) | copy-start | bytes 786436
  74.1 1.0 copy-start.4
  76.2 2.5 %copy-start.23 = (f32[8,128]{1,0:T(8,128)}, f32[8,128]{1,0:T(8,128)S(1)}, u32[]{:S(2)}) copy-start(f32[8,128]{1,0:T(8,128)S(1)} %get-tuple-element.83.refs_6_) | copy-start | bytes 12292
  76.2 3.3 %copy-start.10 = (bf16[64,2048]{1,0:T(8,128)(2,1)}, bf16[64,2048]{1,0:T(8,128)(2,1)S(1)}, u32[]{:S(2)}) copy-start(bf16[64,2048]{1,0:T(8,128)(2,1)S(1)} %collective-permute-done.3.refs_1_.refs_3_) | copy-start | bytes 786436
  79.5 7.5 %copy-start.3 = (bf16[128,2048]{1,0:T(8,128)(2,1)S(1)}, bf16[128,2048]{1,0:T(8,128)(2,1)}, u32[]{:S(2)}) copy-start(bf16[128,2048]{1,0:T(8,128)(2,1)} %rows_ref.3) | copy-start | bytes 1572868
  79.5 7.5 %copy-start.16 = (f32[128,2]{0,1:T(2,128)S(1)}, f32[128,2]{0,1:T(2,128)}, u32[]{:S(2)}) copy-start(f32[128,2]{0,1:T(2,128)} %param.9) | copy-start | bytes 3076
  79.5 7.5 %copy-start.17 = (s32[128,2]{0,1:T(2,128)S(1)}, s32[128,2]{0,1:T(2,128)}, u32[]{:S(2)}) copy-start(s32[128,2]{0,1:T(2,128)} %param.8) | copy-start | bytes 3076
  79.5 13.2 %copy-start.7 = (bf16[2,384,768]{2,1,0:T(8,128)(2,1)S(1)}, bf16[2,384,768]{2,1,0:T(8,128)(2,1)}, u32[]{:S(2)}) copy-start(bf16[2,384,768]{2,1,0:T(8,128)(2,1)} %copy-done.6) | copy-start | bytes 3538948
  79.5 17.1 %collective-permute-start.11 = (bf16[64,2048]{1,0:T(8,128)(2,1)}, bf16[64,2048]{1,0:T(8,128)(2,1)S(1)}, u32[]{:S(2)}, u32[]{:S(2)}) collective-permute-start(bf16[64,2048]{1,0:T(8,128)(2,1)} %get-tuple-element.84), channel_id=1, source_target_pairs={{0,1},{1,0},{2,3},{3,2},{4,5},{5,4},{6,7},{7,6},{8,9},{9,8},{10,11... | collective-permute-start | bytes 786440 | tf_op jit(solution)/shard_map/ppermute | solution.py:556
  84.6 21.6 %collective-permute-start.12 = (bf16[64,2048]{1,0:T(8,128)(2,1)}, bf16[64,2048]{1,0:T(8,128)(2,1)S(1)}, u32[]{:S(2)}, u32[]{:S(2)}) collective-permute-start(bf16[64,2048]{1,0:T(8,128)(2,1)} %get-tuple-element.85), channel_id=1, source_target_pairs={{0,2},{1,3},{2,0},{3,1},{4,6},{5,7},{6,4},{7,5},{8,10},{9,11},{10,... | collective-permute-start | bytes 786440 | tf_op jit(solution)/shard_map/ppermute | solution.py:556
  85.6 20.5 %collective-permute-start.13 = (bf16[64,2048]{1,0:T(8,128)(2,1)}, bf16[64,2048]{1,0:T(8,128)(2,1)S(1)}, u32[]{:S(2)}, u32[]{:S(2)}) collective-permute-start(bf16[64,2048]{1,0:T(8,128)(2,1)} %get-tuple-element.86), channel_id=1, source_target_pairs={{0,3},{1,2},{2,1},{3,0},{4,7},{5,6},{6,5},{7,4},{8,11},{9,10},{10,... | collective-permute-start | bytes 786440 | tf_op jit(solution)/shard_map/ppermute | solution.py:556
  89.9 3.2 %copy-start.5 = (bf16[2,384,768]{2,1,0:T(8,128)(2,1)S(1)}, bf16[2,384,768]{2,1,0:T(8,128)(2,1)}, u32[]{:S(2)}) copy-start(bf16[2,384,768]{2,1,0:T(8,128)(2,1)} %copy-done.4) | copy-start | bytes 3538948
  93.0 13.1 %copy-start.19 = (bf16[64,2048]{1,0:T(8,128)(2,1)S(1)}, bf16[64,2048]{1,0:T(8,128)(2,1)}, u32[]{:S(2)}) copy-start(bf16[64,2048]{1,0:T(8,128)(2,1)} %copy-done.18) | copy-start | bytes 786436
  93.7 14.0 %collective-permute-start.17 = (bf16[384,768]{1,0:T(8,128)(2,1)S(1)}, bf16[384,768]{1,0:T(8,128)(2,1)S(1)}, u32[]{:S(2)}, u32[]{:S(2)}) collective-permute-start(bf16[384,768]{1,0:T(8,128)(2,1)S(1)} %get-tuple-element.97), channel_id=1, source_target_pairs={{0,8},{4,12},{8,0},{12,4},{16,24},{20,28},{24,16},{28,20},{1,9},{5... | collective-permute-start | bytes 1769480 | tf_op jit(solution)/shard_map/ppermute | solution.py:452
  95.2 13.3 %collective-permute-start.15 = (bf16[384,768]{1,0:T(8,128)(2,1)S(1)}, bf16[384,768]{1,0:T(8,128)(2,1)S(1)}, u32[]{:S(2)}, u32[]{:S(2)}) collective-permute-start(bf16[384,768]{1,0:T(8,128)(2,1)S(1)} %get-tuple-element.92), channel_id=1, source_target_pairs={{0,16},{4,20},{8,24},{12,28},{16,0},{20,4},{24,8},{28,12},{1,17},{... | collective-permute-start | bytes 1769480 | tf_op jit(solution)/shard_map/ppermute | solution.py:452
  (10 other events, 8.4 us)

commit v7 on v6

--- a/solution.py
+++ b/solution.py
@@ -59,6 +59,10 @@
 
 def cost(flops, moved):
     return pl.CostEstimate(flops=int(flops), bytes_accessed=int(moved), transcendentals=0)
+
+
+def partners(n):
+    return [0] + list(range(n - 1, 0, -1))
 
 
 def chosen(ids, expert):
@@ -85,7 +89,7 @@
 def pick_kernel(n, scaled, z_ref, ids_ref, prob_ref, rows_ref, *outs):
     ids = ids_ref[...]
     prob = prob_ref[...]
-    experts = [jnp.bitwise_xor(z_ref[0], k) for k in range(n)]
+    experts = [jnp.bitwise_xor(z_ref[0], k) for k in partners(n)]
     rank = ranks(ids, experts)
     for k in range(n - 1, -1, -1):
         first, second = chosen(ids, experts[k])
@@ -296,7 +300,7 @@
     @pl.when(pl.program_id(0) == 0)
     def _():
         for k in range(n):
-            rows[k * CAP : (k + 1) * CAP, :] = g_refs[k][...]
+            rows[k * CAP : (k + 1) * CAP, :] = g_refs[-k][...]
         high = turned_ref.shape[0]
         pack_ref[:high, :] = turned_ref[...]
         tile = pack_ref.shape[1]
@@ -325,7 +329,7 @@
         compiler_params=params(),
         cost_estimate=cost(2 * rows * width * ff, 2 * width * ff + 4 * rows * width + 12 * rows * ff),
         name="hidden_grad",
-    )(*gs, w_down, slope, act, turned)
+    )(gs[0], *gs[:0:-1], w_down, slope, act, turned)
 
 
 def input_grad_kernel(n, steps, tile, grad_ref, wg_ref, wu_ref, *refs):
@@ -462,7 +466,7 @@
     @pl.when(step == 0)
     def _():
         ids = ids_ref[...]
-        experts = [jnp.bitwise_xor(z_ref[0], k) for k in range(n)]
+        experts = [jnp.bitwise_xor(z_ref[0], k) for k in partners(n)]
         rank = ranks(ids, experts)
         for k in range(n):
             first, second = chosen(ids, experts[k])
@@ -519,7 +523,7 @@
     @pl.when(pl.program_id(0) == 0)
     def _():
         ids = ids_ref[...]
-        experts = [jnp.bitwise_xor(z_ref[0], k) for k in range(n)]
+        experts = [jnp.bitwise_xor(z_ref[0], k) for k in partners(n)]
         rank = ranks(ids, experts)
         for k in range(n):
             here = jnp.logical_and(places(rank[k : k + 1, :]), jnp.logical_or(*chosen(ids, experts[k])))
@@ -552,8 +556,9 @@
 def exchange(values):
     n = len(values)
     moved = list(values)
-    for k in range(n - 1, 0, -1):
-        moved[k] = lax.ppermute(values[k], "expert", [(i, i ^ k) for i in range(n)])
+    for i, k in enumerate(partners(n)):
+        if k:
+            moved[i] = lax.ppermute(values[i], "expert", [(d, d ^ k) for d in range(n)])
     return moved
 
 

time: 110 us -> 107 us (0.973)
  starting transfers between devices: 35.9 us -> 30.7 us
  waiting for transfers between devices: 33.7 us -> 35.8 us
    ppermute x12, starting transfers between devices: 29.3 us -> 25 us  [exchange(): moved[i] = lax.ppermute(values[i], 'expert', [(d, d ^ k) for d in range(n)])]
    ppermute x12, waiting for transfers between devices: 32.8 us -> 34.2 us  [exchange(): moved[i] = lax.ppermute(values[i], 'expert', [(d, d ^ k) for d in range(n)])]
  transfers between devices with their start and end apart: 18 -> 18, of which waited for: 6 -> 7; matrix products, arithmetic and copies ran while one was open for 0% -> 0% of each run, Pallas kernels for 23% -> 23%
where the time goes in v7:
time: 107 us
  waiting for transfers between devices  35.8 us (33%)
  starting transfers between devices  30.7 us (29%)
  Pallas kernels  30.5 us (29%)
  local copies, waits for them, and re-layouts  8.84 us (8%)
    ppermute x12, waiting for transfers between devices, exchange(): moved[i] = lax.ppermute(values[i], 'expert', [(d, d ^ k) for d in range(n)])  34.2 us
    ppermute x12, starting transfers between devices, exchange(): moved[i] = lax.ppermute(values[i], 'expert', [(d, d ^ k) for d in range(n)])  25 us
    pallas_call x7, Pallas kernels, call(): return pl.pallas_call(body, in_specs=specs, **kwargs)(*args, *after)  11.2 us
    unnamed x48, local copies, waits for them, and re-layouts  8.76 us
    pallas_call x1, Pallas kernels, forward(): pl.pallas_call(functools.partial(forward_kernel, n, steps, tile), grid=(s...  7 us
    ppermute x6, starting transfers between devices, swap(): return lax.ppermute(value, 'dp', [(i, i ^ bit) for i in range(count)])  5.69 us
    pallas_call x2, Pallas kernels, pick_rows(): pl.pallas_call(functools.partial(pick_kernel, n, scaled), out_shape=[shap...  4.88 us
    pallas_call x1, Pallas kernels, combine_out(): pl.pallas_call(functools.partial(combine_out_kernel, n), grid=(width // t...  2.82 us
  transfers between devices with their start and end apart: 18, of which 7 were waited for; matrix products, arithmetic and copies ran while one was open for 0% of the time, Pallas kernels for 23%

profile of v7, /device:TPU:0, one launch (start us, length us, event | category | flops | bytes accessed | tf_op | source)
XLA Modules:
  0.0 106.6 jit_solution(17662816556935719502)
XLA Ops:
  0.6 2.4 %pick_rows.2 = (bf16[64,2048]{1,0:T(8,128)(2,1)}, bf16[64,2048]{1,0:T(8,128)(2,1)}, bf16[64,2048]{1,0:T(8,128)(2,1)}, bf16[64,2048]{1,0:T(8,128)(2,1)}) custom-call(s32[1]{0:T(128)} %bitcast.z_ref, s32[2,128]{1,0:T(2,128)} %bitcast.15, f32[2,128]{1,0:T(2,128)} %bitcast.12, bf16[128,2048]{1,0:T(8,128)(2,1)} %rows_ref.2), custom_call_target="tpu_custom_call" | custom-call | flops 134217728 | bytes 2097152 | tf_op jit(solution)/shard_map/pick_rows/pallas_call | solution.py:107
  3.1 5.0 %collective-permute-start = (bf16[64,2048]{1,0:T(8,128)(2,1)}, bf16[64,2048]{1,0:T(8,128)(2,1)S(1)}, u32[]{:S(2)}, u32[]{:S(2)}) collective-permute-start(bf16[64,2048]{1,0:T(8,128)(2,1)} %get-tuple-element.55), channel_id=1, source_target_pairs={{0,3},{1,2},{2,1},{3,0},{4,7},{5,6},{6,5},{7,4},{8,11},{9,10},{10,... | collective-permute-start | bytes 786440 | tf_op jit(solution)/shard_map/ppermute | solution.py:561
  8.7 2.4 %pick_rows.3 = (bf16[64,2048]{1,0:T(8,128)(2,1)}, bf16[64,2048]{1,0:T(8,128)(2,1)}, bf16[64,2048]{1,0:T(8,128)(2,1)}, bf16[64,2048]{1,0:T(8,128)(2,1)}) custom-call(s32[1]{0:T(128)} %bitcast.z_ref, s32[2,128]{1,0:T(2,128)} %bitcast.16, f32[2,128]{1,0:T(2,128)} %bitcast.13, bf16[128,2048]{1,0:T(8,128)(2,1)} %rows_ref.3), custom_call_target="tpu_custom_call" | custom-call | flops 134217728 | bytes 2097152 | tf_op jit(solution)/shard_map/pick_rows/pallas_call | solution.py:107
  11.1 1.5 %collective-permute-start.6 = (bf16[64,2048]{1,0:T(8,128)(2,1)}, bf16[64,2048]{1,0:T(8,128)(2,1)S(1)}, u32[]{:S(2)}, u32[]{:S(2)}) collective-permute-start(bf16[64,2048]{1,0:T(8,128)(2,1)} %get-tuple-element.65), channel_id=1, source_target_pairs={{0,1},{1,0},{2,3},{3,2},{4,5},{5,4},{6,7},{7,6},{8,9},{9,8},{10,11... | collective-permute-start | bytes 786440 | tf_op jit(solution)/shard_map/ppermute | solution.py:561
  12.6 2.9 %collective-permute-start.7 = (bf16[64,2048]{1,0:T(8,128)(2,1)}, bf16[64,2048]{1,0:T(8,128)(2,1)S(1)}, u32[]{:S(2)}, u32[]{:S(2)}) collective-permute-start(bf16[64,2048]{1,0:T(8,128)(2,1)} %get-tuple-element.66), channel_id=1, source_target_pairs={{0,2},{1,3},{2,0},{3,1},{4,6},{5,7},{6,4},{7,5},{8,10},{9,11},{10,... | collective-permute-start | bytes 786440 | tf_op jit(solution)/shard_map/ppermute | solution.py:561
  15.6 3.8 %collective-permute-start.8 = (bf16[64,2048]{1,0:T(8,128)(2,1)}, bf16[64,2048]{1,0:T(8,128)(2,1)S(1)}, u32[]{:S(2)}, u32[]{:S(2)}) collective-permute-start(bf16[64,2048]{1,0:T(8,128)(2,1)} %get-tuple-element.67), channel_id=1, source_target_pairs={{0,3},{1,2},{2,1},{3,0},{4,7},{5,6},{6,5},{7,4},{8,11},{9,10},{10,... | collective-permute-start | bytes 786440 | tf_op jit(solution)/shard_map/ppermute | solution.py:561
  19.5 13.0 %collective-permute-done.1.refs_2_ = bf16[64,2048]{1,0:T(8,128)(2,1)S(1)} collective-permute-done((bf16[64,2048]{1,0:T(8,128)(2,1)}, bf16[64,2048]{1,0:T(8,128)(2,1)S(1)}, u32[]{:S(2)}, u32[]{:S(2)}) %collective-permute-start.1) | collective-permute-done | bytes 262176 | tf_op jit(solution)/shard_map/ppermute | solution.py:561
  32.5 0.9 copy-done.8
  33.5 7.0 %forward.1 = (f32[256,768]{1,0:T(8,128)S(1)}, f32[256,768]{1,0:T(8,128)S(1)}, bf16[256,768]{1,0:T(8,128)(2,1)S(1)}, bf16[64,2048]{1,0:T(8,128)(2,1)S(1)}, bf16[6...) custom-call(bf16[64,2048]{1,0:T(8,128)(2,1)S(1)} %copy-done.8, ...), custom_call_target="tpu_custom_call" | custom-call | flops 2415919104 | bytes 13500416 | tf_op jit(solution)/shard_map/forward/pallas_call | solution.py:187
  40.5 1.2 %turn.1 = (bf16[1408,256]{1,0:T(8,128)(2,1)S(1)}, bf16[1408,256]{1,0:T(8,128)(2,1)S(1)}, bf16[1,768,2048]{2,1,0:T(8,128)(2,1)S(1)}) custom-call(s32[8]{0:T(128)S(1)} %stack.35.me_ref, bf16[64,2048]{1,0:T(8,128)(2,1)S(1)} %copy-done.8, bf16[64,2048]{1,0:T(8,128)(2,1)S(1)} %collective-permute-done.refs_1_, ...), custom_call_target="tpu_custom_call" | custom-call | flops 1048576 | bytes 4325376 | tf_op jit(solution)/shard_map/turn/pallas_call | solution.py:235
  41.7 6.8 %collective-permute-done.7.refs_2_ = bf16[64,2048]{1,0:T(8,128)(2,1)S(1)} collective-permute-done((bf16[64,2048]{1,0:T(8,128)(2,1)}, bf16[64,2048]{1,0:T(8,128)(2,1)S(1)}, u32[]{:S(2)}, u32[]{:S(2)}) %collective-permute-start.7) | collective-permute-done | bytes 262176 | tf_op jit(solution)/shard_map/ppermute | solution.py:561
  48.5 1.9 %hidden_grad.1 = (bf16[512,768]{1,0:T(8,128)(2,1)S(1)}, bf16[256,2048]{1,0:T(8,128)(2,1)S(1)}, bf16[3456,256]{1,0:T(8,128)(2,1)S(1)}) custom-call(bf16[64,2048]{1,0:T(8,128)(2,1)S(1)} %copy-done.9, bf16[64,2048]{1,0:T(8,128)(2,1)S(1)} %collective-permute-done.6.refs_1_, bf16[64,2048]{1,0:T(8,128)(2,1)S(1)} %collective-permute-done.7.refs_2_, ...), custom_call_target="tpu_custom_call" | custom-call | flops 805306368 | bytes 7602176 | tf_op jit(solution)/shard_map/hidden_grad/pallas_call | solution.py:323
  50.9 2.7 %collective-permute-start.3 = (bf16[64,2048]{1,0:T(8,128)(2,1)S(1)}, bf16[64,2048]{1,0:T(8,128)(2,1)S(1)}, u32[]{:S(2)}, u32[]{:S(2)}) collective-permute-start(bf16[64,2048]{1,0:T(8,128)(2,1)S(1)} %get-tuple-element.59), channel_id=1, source_target_pairs={{0,3},{1,2},{2,1},{3,0},{4,7},{5,6},{6,5},{7,4},{8,11},{9,10},{10,... | collective-permute-start | bytes 786440 | tf_op jit(solution)/shard_map/ppermute | solution.py:561
  53.6 4.0 %collective-permute-start.4 = (bf16[64,2048]{1,0:T(8,128)(2,1)S(1)}, bf16[64,2048]{1,0:T(8,128)(2,1)S(1)}, u32[]{:S(2)}, u32[]{:S(2)}) collective-permute-start(bf16[64,2048]{1,0:T(8,128)(2,1)S(1)} %get-tuple-element.60), channel_id=1, source_target_pairs={{0,2},{1,3},{2,0},{3,1},{4,6},{5,7},{6,4},{7,5},{8,10},{9,11},{10,... | collective-permute-start | bytes 786440 | tf_op jit(solution)/shard_map/ppermute | solution.py:561
  57.7 3.5 %outer.2 = (bf16[2,384,768]{2,1,0:T(8,128)(2,1)}, bf16[2,384,768]{2,1,0:T(8,128)(2,1)}, f32[8,128]{1,0:T(8,128)S(1)}) custom-call(bf16[1408,256]{1,0:T(8,128)(2,1)S(1)} %get-tuple-element.74.refs_0_, bf16[3456,256]{1,0:T(8,128)(2,1)S(1)} %collective-permute-done.9.refs_1_, bf16[512,768]{1,0:T(8,128)(2,1)S(1)} %get-tuple-element.73.refs_2_.refs_0_, ...), custom_call_target="tpu_custom_call" | custom-call | flops 1207959552 | bytes 3801088 | tf_op jit(solution)/shard_map/outer/pallas_call | solution.py:50
  61.3 1.5 %collective-permute-start.14 = (bf16[2,384,768]{2,1,0:T(8,128)(2,1)}, bf16[2,384,768]{2,1,0:T(8,128)(2,1)S(1)}, u32[]{:S(2)}, u32[]{:S(2)}) collective-permute-start(bf16[2,384,768]{2,1,0:T(8,128)(2,1)} %get-tuple-element.89), channel_id=1, source_target_pairs={{0,8},{4,12},{8,0},{12,4},{16,24},{20,28},{24,16},{28,20},{1,9},{5... | collective-permute-start | bytes 3538952 | tf_op jit(solution)/shard_map/ppermute | solution.py:456
  62.8 1.5 %collective-permute-start.16 = (bf16[2,384,768]{2,1,0:T(8,128)(2,1)}, bf16[2,384,768]{2,1,0:T(8,128)(2,1)S(1)}, u32[]{:S(2)}, u32[]{:S(2)}) collective-permute-start(bf16[2,384,768]{2,1,0:T(8,128)(2,1)} %get-tuple-element.94), channel_id=1, source_target_pairs={{0,16},{4,20},{8,24},{12,28},{16,0},{20,4},{24,8},{28,12},{1,17},{... | collective-permute-start | bytes 3538952 | tf_op jit(solution)/shard_map/ppermute | solution.py:456
  64.3 3.0 %input_grad.1 = (bf16[64,2048]{1,0:T(8,128)(2,1)S(1)}, bf16[64,2048]{1,0:T(8,128)(2,1)S(1)}, bf16[64,2048]{1,0:T(8,128)(2,1)S(1)}, bf16[64,2048]{1,0:T(8,128)(2,1)S(1)}, f32[8,128]{1,0:T(8,128)S(1)}) custom-call(bf16[512,768]{1,0:T(8,128)(2,1)S(1)} %get-tuple-element.73.refs_2_.refs_0_, bf16[1,2048,768]{2,1,0:T(8,128)(2,1)S(1)} %copy-done.1, ...), custom_call_target="tpu_custom_call" | custom-call | flops 1610612736 | bytes 8126464 | tf_op jit(solution)/shard_map/input_grad/pallas_call | solution.py:50
  69.4 2.6 %outer.3 = (bf16[2,384,768]{2,1,0:T(8,128)(2,1)S(1)}, bf16[2,384,768]{2,1,0:T(8,128)(2,1)S(1)}, f32[8,128]{1,0:T(8,128)S(1)}) custom-call(bf16[1408,256]{1,0:T(8,128)(2,1)S(1)} %get-tuple-element.74.refs_0_, bf16[3456,256]{1,0:T(8,128)(2,1)S(1)} %collective-permute-done.9.refs_1_, bf16[512,768]{1,0:T(8,128)(2,1)S(1)} %get-tuple-element.73.refs_2_.refs_0_, ...), custom_call_target="tpu_custom_call" | custom-call | flops 1207959552 | bytes 3801088 | tf_op jit(solution)/shard_map/outer/pallas_call | solution.py:50
  72.0 1.0 copy-done.4
  73.0 1.0 copy-done.6
  74.1 3.8 %collective-permute-done.4.refs_2_.refs_4_ = bf16[64,2048]{1,0:T(8,128)(2,1)S(1)} collective-permute-done((bf16[64,2048]{1,0:T(8,128)(2,1)S(1)}, bf16[64,2048]{1,0:T(8,128)(2,1)S(1)}, u32[]{:S(2)}, u32[]{:S(2)}) %collective-permute-start.4) | collective-permute-done | bytes 262176 | tf_op jit(solution)/shard_map/ppermute | solution.py:561
  78.7 2.7 %collective-permute-start.11 = (bf16[64,2048]{1,0:T(8,128)(2,1)}, bf16[64,2048]{1,0:T(8,128)(2,1)S(1)}, u32[]{:S(2)}, u32[]{:S(2)}) collective-permute-start(bf16[64,2048]{1,0:T(8,128)(2,1)} %get-tuple-element.84), channel_id=1, source_target_pairs={{0,3},{1,2},{2,1},{3,0},{4,7},{5,6},{6,5},{7,4},{8,11},{9,10},{10,... | collective-permute-start | bytes 786440 | tf_op jit(solution)/shard_map/ppermute | solution.py:561
  81.4 1.7 %collective-permute-start.13 = (bf16[64,2048]{1,0:T(8,128)(2,1)}, bf16[64,2048]{1,0:T(8,128)(2,1)S(1)}, u32[]{:S(2)}, u32[]{:S(2)}) collective-permute-start(bf16[64,2048]{1,0:T(8,128)(2,1)} %get-tuple-element.86), channel_id=1, source_target_pairs={{0,1},{1,0},{2,3},{3,2},{4,5},{5,4},{6,7},{7,6},{8,9},{9,8},{10,11... | collective-permute-start | bytes 786440 | tf_op jit(solution)/shard_map/ppermute | solution.py:561
  83.2 0.9 copy-done.11
  84.1 0.9 copy-done.13
  85.1 0.9 copy-done.15
  86.0 2.8 %combine_out.1 = (bf16[128,2048]{1,0:T(8,128)(2,1)}, f32[2,128]{1,0:T(2,128)}, f32[8,128]{1,0:T(8,128)S(1)}) custom-call(s32[1]{0:T(128)} %bitcast.z_ref, s32[2,128]{1,0:T(2,128)S(1)} %bitcast.17, f32[2,128]{1,0:T(2,128)S(1)} %bitcast.14, bf16[128,2048]{1,0:T(8,128)(2,1)S(1)} %copy-done.3, bf16[64,2048]{1,0:T(8,128)(2,1)S(1)} %get-tuple-element.58.refs_0_, ...), custom_call_target="tpu_custom_call" | custom-call | flops 268435456 | bytes 2097152 | tf_op jit(solution)/shard_map/combine_out/pallas_call | solution.py:503
  91.3 1.5 %collective-permute-start.15 = (bf16[384,768]{1,0:T(8,128)(2,1)S(1)}, bf16[384,768]{1,0:T(8,128)(2,1)S(1)}, u32[]{:S(2)}, u32[]{:S(2)}) collective-permute-start(bf16[384,768]{1,0:T(8,128)(2,1)S(1)} %get-tuple-element.92), channel_id=1, source_target_pairs={{0,16},{4,20},{8,24},{12,28},{16,0},{20,4},{24,8},{28,12},{1,17},{... | collective-permute-start | bytes 1769480 | tf_op jit(solution)/shard_map/ppermute | solution.py:456
  92.9 10.5 %collective-permute-done.12.refs_2_ = bf16[64,2048]{1,0:T(8,128)(2,1)S(1)} collective-permute-done((bf16[64,2048]{1,0:T(8,128)(2,1)}, bf16[64,2048]{1,0:T(8,128)(2,1)S(1)}, u32[]{:S(2)}, u32[]{:S(2)}) %collective-permute-start.12) | collective-permute-done | bytes 262176 | tf_op jit(solution)/shard_map/ppermute | solution.py:561
  103.4 1.5 %combine_in.1 = (bf16[128,2048]{1,0:T(8,128)(2,1)}, f32[8,128]{1,0:T(8,128)S(1)}) custom-call(s32[1]{0:T(128)} %bitcast.z_ref, s32[2,128]{1,0:T(2,128)S(1)} %bitcast.18, bf16[64,2048]{1,0:T(8,128)(2,1)S(1)} %copy-done.19, bf16[64,2048]{1,0:T(8,128)(2,1)S(1)} %collective-permute-done.11.refs_1_, bf16[64,2048]{1,0:T(8,128)(2,1)S(1)} %collective-permute-done.12.refs_2_, ...), custom_call_target="tpu_custom_call" | custom-call | flops 10000000000 | bytes 1572864 | tf_op jit(solution)/shard_map/combine_in/pallas_call | solution.py:543
  105.4 1.2 %fold_last.1 = (bf16[1,256,768]{2,1,0:T(8,128)(2,1)}, bf16[1,256,768]{2,1,0:T(8,128)(2,1)}, bf16[1,96,2048]{2,1,0:T(8,128)(2,1)}) custom-call(bf16[384,768]{1,0:T(8,128)(2,1)S(1)} %get-tuple-element.91.refs_0_, bf16[384,768]{1,0:T(8,128)(2,1)S(1)} %collective-permute-done.15.refs_1_, bf16[384,768]{1,0:T(8,128)(2,1)S(1)} %get-tuple-element.96.refs_2_, ...), custom_call_target="tpu_custom_call" | custom-call | flops 589824 | bytes 3538944 | tf_op jit(solution)/shard_map/fold_last/pallas_call | solution.py:50
  (67 shorter events, 7.4 us)
Async XLA Ops:
  3.1 12.5 %collective-permute-start = (bf16[64,2048]{1,0:T(8,128)(2,1)}, bf16[64,2048]{1,0:T(8,128)(2,1)S(1)}, u32[]{:S(2)}, u32[]{:S(2)}) collective-permute-start(bf16[64,2048]{1,0:T(8,128)(2,1)} %get-tuple-element.55), channel_id=1, source_target_pairs={{0,3},{1,2},{2,1},{3,0},{4,7},{5,6},{6,5},{7,4},{8,11},{9,10},{10,... | collective-permute-start | bytes 786440 | tf_op jit(solution)/shard_map/ppermute | solution.py:561
  8.1 24.4 %collective-permute-start.1 = (bf16[64,2048]{1,0:T(8,128)(2,1)}, bf16[64,2048]{1,0:T(8,128)(2,1)S(1)}, u32[]{:S(2)}, u32[]{:S(2)}) collective-permute-start(bf16[64,2048]{1,0:T(8,128)(2,1)} %get-tuple-element.56), channel_id=1, source_target_pairs={{0,2},{1,3},{2,0},{3,1},{4,6},{5,7},{6,4},{7,5},{8,10},{9,11},{10,... | collective-permute-start | bytes 786440 | tf_op jit(solution)/shard_map/ppermute | solution.py:561
  8.1 24.4 %collective-permute-start.2 = (bf16[64,2048]{1,0:T(8,128)(2,1)}, bf16[64,2048]{1,0:T(8,128)(2,1)S(1)}, u32[]{:S(2)}, u32[]{:S(2)}) collective-permute-start(bf16[64,2048]{1,0:T(8,128)(2,1)} %get-tuple-element.57), channel_id=1, source_target_pairs={{0,1},{1,0},{2,3},{3,2},{4,5},{5,4},{6,7},{7,6},{8,9},{9,8},{10,11... | collective-permute-start | bytes 786440 | tf_op jit(solution)/shard_map/ppermute | solution.py:561
  11.1 30.6 %collective-permute-start.6 = (bf16[64,2048]{1,0:T(8,128)(2,1)}, bf16[64,2048]{1,0:T(8,128)(2,1)S(1)}, u32[]{:S(2)}, u32[]{:S(2)}) collective-permute-start(bf16[64,2048]{1,0:T(8,128)(2,1)} %get-tuple-element.65), channel_id=1, source_target_pairs={{0,1},{1,0},{2,3},{3,2},{4,5},{5,4},{6,7},{7,6},{8,9},{9,8},{10,11... | collective-permute-start | bytes 786440 | tf_op jit(solution)/shard_map/ppermute | solution.py:561
  12.6 35.9 %collective-permute-start.7 = (bf16[64,2048]{1,0:T(8,128)(2,1)}, bf16[64,2048]{1,0:T(8,128)(2,1)S(1)}, u32[]{:S(2)}, u32[]{:S(2)}) collective-permute-start(bf16[64,2048]{1,0:T(8,128)(2,1)} %get-tuple-element.66), channel_id=1, source_target_pairs={{0,2},{1,3},{2,0},{3,1},{4,6},{5,7},{6,4},{7,5},{8,10},{9,11},{10,... | collective-permute-start | bytes 786440 | tf_op jit(solution)/shard_map/ppermute | solution.py:561
  15.6 32.9 %collective-permute-start.8 = (bf16[64,2048]{1,0:T(8,128)(2,1)}, bf16[64,2048]{1,0:T(8,128)(2,1)S(1)}, u32[]{:S(2)}, u32[]{:S(2)}) collective-permute-start(bf16[64,2048]{1,0:T(8,128)(2,1)} %get-tuple-element.67), channel_id=1, source_target_pairs={{0,3},{1,2},{2,1},{3,0},{4,7},{5,6},{6,5},{7,4},{8,11},{9,10},{10,... | collective-permute-start | bytes 786440 | tf_op jit(solution)/shard_map/ppermute | solution.py:561
  33.5 7.0 %copy-start = (bf16[1,768,2048]{2,1,0:T(8,128)(2,1)S(1)}, bf16[1,768,2048]{2,1,0:T(8,128)(2,1)}, u32[]{:S(2)}) copy-start(bf16[1,768,2048]{2,1,0:T(8,128)(2,1)} %refs_5_.3) | copy-start | bytes 9437188
  40.5 8.0 %copy-start.9 = (bf16[64,2048]{1,0:T(8,128)(2,1)S(1)}, bf16[64,2048]{1,0:T(8,128)(2,1)}, u32[]{:S(2)}) copy-start(bf16[64,2048]{1,0:T(8,128)(2,1)} %get-tuple-element.64.refs_0_) | copy-start | bytes 786436
  48.5 15.8 %copy-start.2 = (bf16[1,2048,768]{2,1,0:T(8,128)(2,1)S(1)}, bf16[1,2048,768]{2,1,0:T(8,128)(2,1)}, u32[]{:S(2)}) copy-start(bf16[1,2048,768]{2,1,0:T(8,128)(2,1)} %refs_2_.1) | copy-start | bytes 9437188
  50.4 7.4 %collective-permute-start.9 = (bf16[3456,256]{1,0:T(8,128)(2,1)S(1)}, bf16[3456,256]{1,0:T(8,128)(2,1)S(1)}, u32[]{:S(2)}, u32[]{:S(2)}) collective-permute-start(bf16[3456,256]{1,0:T(8,128)(2,1)S(1)} %get-tuple-element.75), channel_id=1, source_target_pairs={{0,4},{4,0},{8,12},{12,8},{16,20},{20,16},{24,28},{28,24},{1,5},{5... | collective-permute-start | bytes 5308424 | tf_op jit(solution)/shard_map/ppermute | solution.py:456
  50.4 7.3 %collective-permute-start.10 = (bf16[512,768]{1,0:T(8,128)(2,1)S(1)}, bf16[512,768]{1,0:T(8,128)(2,1)S(1)}, u32[]{:S(2)}, u32[]{:S(2)}) collective-permute-start(bf16[512,768]{1,0:T(8,128)(2,1)S(1)} %get-tuple-element.73.refs_2_.refs_0_), channel_id=1, source_target_pairs={{0,4},{4,0},{8,12},{12,8},{16,20},{20,16},{24,28},{28,24},{1,5},{5... | collective-permute-start | bytes 2359304 | tf_op jit(solution)/shard_map/ppermute | solution.py:456
  50.9 23.1 %collective-permute-start.3 = (bf16[64,2048]{1,0:T(8,128)(2,1)S(1)}, bf16[64,2048]{1,0:T(8,128)(2,1)S(1)}, u32[]{:S(2)}, u32[]{:S(2)}) collective-permute-start(bf16[64,2048]{1,0:T(8,128)(2,1)S(1)} %get-tuple-element.59), channel_id=1, source_target_pairs={{0,3},{1,2},{2,1},{3,0},{4,7},{5,6},{6,5},{7,4},{8,11},{9,10},{10,... | collective-permute-start | bytes 786440 | tf_op jit(solution)/shard_map/ppermute | solution.py:561
  53.6 24.3 %collective-permute-start.4 = (bf16[64,2048]{1,0:T(8,128)(2,1)S(1)}, bf16[64,2048]{1,0:T(8,128)(2,1)S(1)}, u32[]{:S(2)}, u32[]{:S(2)}) collective-permute-start(bf16[64,2048]{1,0:T(8,128)(2,1)S(1)} %get-tuple-element.60), channel_id=1, source_target_pairs={{0,2},{1,3},{2,0},{3,1},{4,6},{5,7},{6,4},{7,5},{8,10},{9,11},{10,... | collective-permute-start | bytes 786440 | tf_op jit(solution)/shard_map/ppermute | solution.py:561
  57.6 20.3 %collective-permute-start.5 = (bf16[64,2048]{1,0:T(8,128)(2,1)S(1)}, bf16[64,2048]{1,0:T(8,128)(2,1)S(1)}, u32[]{:S(2)}, u32[]{:S(2)}) collective-permute-start(bf16[64,2048]{1,0:T(8,128)(2,1)S(1)} %get-tuple-element.61), channel_id=1, source_target_pairs={{0,1},{1,0},{2,3},{3,2},{4,5},{5,4},{6,7},{7,6},{8,9},{9,8},{10,11... | collective-permute-start | bytes 786440 | tf_op jit(solution)/shard_map/ppermute | solution.py:561
  57.7 6.6 %copy-start.1 = (bf16[1,2048,768]{2,1,0:T(8,128)(2,1)S(1)}, bf16[1,2048,768]{2,1,0:T(8,128)(2,1)}, u32[]{:S(2)}) copy-start(bf16[1,2048,768]{2,1,0:T(8,128)(2,1)} %refs_1_.1) | copy-start | bytes 9437188
  61.3 27.6 %collective-permute-start.14 = (bf16[2,384,768]{2,1,0:T(8,128)(2,1)}, bf16[2,384,768]{2,1,0:T(8,128)(2,1)S(1)}, u32[]{:S(2)}, u32[]{:S(2)}) collective-permute-start(bf16[2,384,768]{2,1,0:T(8,128)(2,1)} %get-tuple-element.89), channel_id=1, source_target_pairs={{0,8},{4,12},{8,0},{12,4},{16,24},{20,28},{24,16},{28,20},{1,9},{5... | collective-permute-start | bytes 3538952 | tf_op jit(solution)/shard_map/ppermute | solution.py:456
  62.8 27.3 %collective-permute-start.16 = (bf16[2,384,768]{2,1,0:T(8,128)(2,1)}, bf16[2,384,768]{2,1,0:T(8,128)(2,1)S(1)}, u32[]{:S(2)}, u32[]{:S(2)}) collective-permute-start(bf16[2,384,768]{2,1,0:T(8,128)(2,1)} %get-tuple-element.94), channel_id=1, source_target_pairs={{0,16},{4,20},{8,24},{12,28},{16,0},{20,4},{24,8},{28,12},{1,17},{... | collective-permute-start | bytes 3538952 | tf_op jit(solution)/shard_map/ppermute | solution.py:456
  69.4 2.6 %copy-start.18 = (bf16[64,2048]{1,0:T(8,128)(2,1)}, bf16[64,2048]{1,0:T(8,128)(2,1)S(1)}, u32[]{:S(2)}) copy-start(bf16[64,2048]{1,0:T(8,128)(2,1)S(1)} %get-tuple-element.78.refs_0_) | copy-start | bytes 786436
  72.0 1.0 copy-start.4
  74.1 3.8 %copy-start.23 = (f32[8,128]{1,0:T(8,128)}, f32[8,128]{1,0:T(8,128)S(1)}, u32[]{:S(2)}) copy-start(f32[8,128]{1,0:T(8,128)S(1)} %get-tuple-element.83.refs_6_) | copy-start | bytes 12292
  74.1 4.6 %copy-start.10 = (bf16[64,2048]{1,0:T(8,128)(2,1)}, bf16[64,2048]{1,0:T(8,128)(2,1)S(1)}, u32[]{:S(2)}) copy-start(bf16[64,2048]{1,0:T(8,128)(2,1)S(1)} %collective-permute-done.3.refs_1_.refs_3_) | copy-start | bytes 786436
  78.7 4.5 %copy-start.3 = (bf16[128,2048]{1,0:T(8,128)(2,1)S(1)}, bf16[128,2048]{1,0:T(8,128)(2,1)}, u32[]{:S(2)}) copy-start(bf16[128,2048]{1,0:T(8,128)(2,1)} %rows_ref.3) | copy-start | bytes 1572868
  78.7 4.5 %copy-start.16 = (f32[128,2]{0,1:T(2,128)S(1)}, f32[128,2]{0,1:T(2,128)}, u32[]{:S(2)}) copy-start(f32[128,2]{0,1:T(2,128)} %param.9) | copy-start | bytes 3076
  78.7 4.5 %copy-start.17 = (s32[128,2]{0,1:T(2,128)S(1)}, s32[128,2]{0,1:T(2,128)}, u32[]{:S(2)}) copy-start(s32[128,2]{0,1:T(2,128)} %param.8) | copy-start | bytes 3076
  78.7 10.2 %copy-start.7 = (bf16[2,384,768]{2,1,0:T(8,128)(2,1)S(1)}, bf16[2,384,768]{2,1,0:T(8,128)(2,1)}, u32[]{:S(2)}) copy-start(bf16[2,384,768]{2,1,0:T(8,128)(2,1)} %copy-done.6) | copy-start | bytes 3538948
  78.7 14.1 %collective-permute-start.11 = (bf16[64,2048]{1,0:T(8,128)(2,1)}, bf16[64,2048]{1,0:T(8,128)(2,1)S(1)}, u32[]{:S(2)}, u32[]{:S(2)}) collective-permute-start(bf16[64,2048]{1,0:T(8,128)(2,1)} %get-tuple-element.84), channel_id=1, source_target_pairs={{0,3},{1,2},{2,1},{3,0},{4,7},{5,6},{6,5},{7,4},{8,11},{9,10},{10,... | collective-permute-start | bytes 786440 | tf_op jit(solution)/shard_map/ppermute | solution.py:561
  81.4 21.9 %collective-permute-start.12 = (bf16[64,2048]{1,0:T(8,128)(2,1)}, bf16[64,2048]{1,0:T(8,128)(2,1)S(1)}, u32[]{:S(2)}, u32[]{:S(2)}) collective-permute-start(bf16[64,2048]{1,0:T(8,128)(2,1)} %get-tuple-element.85), channel_id=1, source_target_pairs={{0,2},{1,3},{2,0},{3,1},{4,6},{5,7},{6,4},{7,5},{8,10},{9,11},{10,... | collective-permute-start | bytes 786440 | tf_op jit(solution)/shard_map/ppermute | solution.py:561
  81.4 21.9 %collective-permute-start.13 = (bf16[64,2048]{1,0:T(8,128)(2,1)}, bf16[64,2048]{1,0:T(8,128)(2,1)S(1)}, u32[]{:S(2)}, u32[]{:S(2)}) collective-permute-start(bf16[64,2048]{1,0:T(8,128)(2,1)} %get-tuple-element.86), channel_id=1, source_target_pairs={{0,1},{1,0},{2,3},{3,2},{4,5},{5,4},{6,7},{7,6},{8,9},{9,8},{10,11... | collective-permute-start | bytes 786440 | tf_op jit(solution)/shard_map/ppermute | solution.py:561
  86.0 4.1 %copy-start.5 = (bf16[2,384,768]{2,1,0:T(8,128)(2,1)S(1)}, bf16[2,384,768]{2,1,0:T(8,128)(2,1)}, u32[]{:S(2)}) copy-start(bf16[2,384,768]{2,1,0:T(8,128)(2,1)} %copy-done.4) | copy-start | bytes 3538948
  89.2 14.2 %copy-start.19 = (bf16[64,2048]{1,0:T(8,128)(2,1)S(1)}, bf16[64,2048]{1,0:T(8,128)(2,1)}, u32[]{:S(2)}) copy-start(bf16[64,2048]{1,0:T(8,128)(2,1)} %copy-done.18) | copy-start | bytes 786436
  90.7 14.1 %collective-permute-start.17 = (bf16[384,768]{1,0:T(8,128)(2,1)S(1)}, bf16[384,768]{1,0:T(8,128)(2,1)S(1)}, u32[]{:S(2)}, u32[]{:S(2)}) collective-permute-start(bf16[384,768]{1,0:T(8,128)(2,1)S(1)} %get-tuple-element.97), channel_id=1, source_target_pairs={{0,8},{4,12},{8,0},{12,4},{16,24},{20,28},{24,16},{28,20},{1,9},{5... | collective-permute-start | bytes 1769480 | tf_op jit(solution)/shard_map/ppermute | solution.py:456
  91.3 14.1 %collective-permute-start.15 = (bf16[384,768]{1,0:T(8,128)(2,1)S(1)}, bf16[384,768]{1,0:T(8,128)(2,1)S(1)}, u32[]{:S(2)}, u32[]{:S(2)}) collective-permute-start(bf16[384,768]{1,0:T(8,128)(2,1)S(1)} %get-tuple-element.92), channel_id=1, source_target_pairs={{0,16},{4,20},{8,24},{12,28},{16,0},{20,4},{24,8},{28,12},{1,17},{... | collective-permute-start | bytes 1769480 | tf_op jit(solution)/shard_map/ppermute | solution.py:456
  (10 other events, 8.4 us)

commit v8 on v7

--- a/solution.py
+++ b/solution.py
@@ -584,8 +584,8 @@
         *din, token = input_grad(n, grad, w_gate, w_up, [token])
         x_keep, y_keep, token = outer(0, keep_t, recv, grad, other, g_rows, [token])
         back_in = exchange([din[0], *hold(din[1:], [*back_out[1:], token])])
-        x_next, x_mine, token = fold_two(x_keep, swap(x_send, ALONG_X), [shown])
-        y_next, y_mine, _ = fold_two(y_keep, swap(y_send, ALONG_Y), [token])
+        x_next, x_mine, _ = fold_two(x_keep, swap(x_send, ALONG_X), [shown])
+        y_next, y_mine, _ = fold_two(y_keep, swap(y_send, ALONG_Y), [shown])
         token_grad, token = combine_in(z, ids_t, back_in, 10 * 10**9)
         shapes = [(1, d // parts, w) for d, w in (w_gate.shape[1:], w_up.shape[1:], w_down.shape[1:])]
         sum_gate, sum_up, sum_down = fold_last(

time: 107 us -> 109 us (1.019)
  Pallas kernels: 30.5 us -> 32.1 us
    pallas_call x7, Pallas kernels: 11.2 us -> 12.9 us  [call(): return pl.pallas_call(body, in_specs=specs, **kwargs)(*args, *after)]
    unnamed x48 -> x44, local copies, waits for them, and re-layouts: 8.76 us -> 7.71 us
  transfers between devices with their start and end apart: 18 -> 18, of which waited for: 7 -> 8; matrix products, arithmetic and copies ran while one was open for 0% -> 0% of each run, Pallas kernels for 23% -> 25%
where the time goes in v8:
time: 109 us; the launch traced here: 108 us
  waiting for transfers between devices  35.9 us (33%)
  Pallas kernels  32.1 us (29%)
  starting transfers between devices  31.6 us (29%)
  local copies, waits for them, and re-layouts  7.8 us (7%)
    ppermute x12, waiting for transfers between devices, exchange(): moved[i] = lax.ppermute(values[i], 'expert', [(d, d ^ k) for d in range(n)])  33.5 us
    ppermute x12, starting transfers between devices, exchange(): moved[i] = lax.ppermute(values[i], 'expert', [(d, d ^ k) for d in range(n)])  25 us
    pallas_call x7, Pallas kernels, call(): return pl.pallas_call(body, in_specs=specs, **kwargs)(*args, *after)  12.9 us
    unnamed x44, local copies, waits for them, and re-layouts  7.71 us
    pallas_call x1, Pallas kernels, forward(): pl.pallas_call(functools.partial(forward_kernel, n, steps, tile), grid=(s...  7 us
    ppermute x6, starting transfers between devices, swap(): return lax.ppermute(value, 'dp', [(i, i ^ bit) for i in range(count)])  6.6 us
    pallas_call x2, Pallas kernels, pick_rows(): pl.pallas_call(functools.partial(pick_kernel, n, scaled), out_shape=[shap...  4.88 us
    pallas_call x1, Pallas kernels, combine_out(): pl.pallas_call(functools.partial(combine_out_kernel, n), grid=(width // t...  2.83 us
  transfers between devices with their start and end apart: 18, of which 8 were waited for; matrix products, arithmetic and copies ran while one was open for 0% of the time, Pallas kernels for 25%

profile of v8, /device:TPU:0, one launch (start us, length us, event | category | flops | bytes accessed | tf_op | source)
XLA Modules:
  0.0 108.2 jit_solution(10914572655152704205)
XLA Ops:
  0.6 2.4 %pick_rows.2 = (bf16[64,2048]{1,0:T(8,128)(2,1)}, bf16[64,2048]{1,0:T(8,128)(2,1)}, bf16[64,2048]{1,0:T(8,128)(2,1)}, bf16[64,2048]{1,0:T(8,128)(2,1)}) custom-call(s32[1]{0:T(128)} %bitcast.z_ref, s32[2,128]{1,0:T(2,128)} %bitcast.15, f32[2,128]{1,0:T(2,128)} %bitcast.12, bf16[128,2048]{1,0:T(8,128)(2,1)} %rows_ref.2), custom_call_target="tpu_custom_call" | custom-call | flops 134217728 | bytes 2097152 | tf_op jit(solution)/shard_map/pick_rows/pallas_call | solution.py:107
  3.1 5.0 %collective-permute-start = (bf16[64,2048]{1,0:T(8,128)(2,1)}, bf16[64,2048]{1,0:T(8,128)(2,1)S(1)}, u32[]{:S(2)}, u32[]{:S(2)}) collective-permute-start(bf16[64,2048]{1,0:T(8,128)(2,1)} %get-tuple-element.54), channel_id=1, source_target_pairs={{0,3},{1,2},{2,1},{3,0},{4,7},{5,6},{6,5},{7,4},{8,11},{9,10},{10,... | collective-permute-start | bytes 786440 | tf_op jit(solution)/shard_map/ppermute | solution.py:561
  8.7 2.4 %pick_rows.3 = (bf16[64,2048]{1,0:T(8,128)(2,1)}, bf16[64,2048]{1,0:T(8,128)(2,1)}, bf16[64,2048]{1,0:T(8,128)(2,1)}, bf16[64,2048]{1,0:T(8,128)(2,1)}) custom-call(s32[1]{0:T(128)} %bitcast.z_ref, s32[2,128]{1,0:T(2,128)} %bitcast.16, f32[2,128]{1,0:T(2,128)} %bitcast.13, bf16[128,2048]{1,0:T(8,128)(2,1)} %rows_ref.3), custom_call_target="tpu_custom_call" | custom-call | flops 134217728 | bytes 2097152 | tf_op jit(solution)/shard_map/pick_rows/pallas_call | solution.py:107
  11.1 1.5 %collective-permute-start.6 = (bf16[64,2048]{1,0:T(8,128)(2,1)}, bf16[64,2048]{1,0:T(8,128)(2,1)S(1)}, u32[]{:S(2)}, u32[]{:S(2)}) collective-permute-start(bf16[64,2048]{1,0:T(8,128)(2,1)} %get-tuple-element.64), channel_id=1, source_target_pairs={{0,1},{1,0},{2,3},{3,2},{4,5},{5,4},{6,7},{7,6},{8,9},{9,8},{10,11... | collective-permute-start | bytes 786440 | tf_op jit(solution)/shard_map/ppermute | solution.py:561
  12.6 2.9 %collective-permute-start.7 = (bf16[64,2048]{1,0:T(8,128)(2,1)}, bf16[64,2048]{1,0:T(8,128)(2,1)S(1)}, u32[]{:S(2)}, u32[]{:S(2)}) collective-permute-start(bf16[64,2048]{1,0:T(8,128)(2,1)} %get-tuple-element.65), channel_id=1, source_target_pairs={{0,2},{1,3},{2,0},{3,1},{4,6},{5,7},{6,4},{7,5},{8,10},{9,11},{10,... | collective-permute-start | bytes 786440 | tf_op jit(solution)/shard_map/ppermute | solution.py:561
  15.6 3.8 %collective-permute-start.8 = (bf16[64,2048]{1,0:T(8,128)(2,1)}, bf16[64,2048]{1,0:T(8,128)(2,1)S(1)}, u32[]{:S(2)}, u32[]{:S(2)}) collective-permute-start(bf16[64,2048]{1,0:T(8,128)(2,1)} %get-tuple-element.66), channel_id=1, source_target_pairs={{0,3},{1,2},{2,1},{3,0},{4,7},{5,6},{6,5},{7,4},{8,11},{9,10},{10,... | collective-permute-start | bytes 786440 | tf_op jit(solution)/shard_map/ppermute | solution.py:561
  19.5 13.0 %collective-permute-done.1.refs_2_ = bf16[64,2048]{1,0:T(8,128)(2,1)S(1)} collective-permute-done((bf16[64,2048]{1,0:T(8,128)(2,1)}, bf16[64,2048]{1,0:T(8,128)(2,1)S(1)}, u32[]{:S(2)}, u32[]{:S(2)}) %collective-permute-start.1) | collective-permute-done | bytes 262176 | tf_op jit(solution)/shard_map/ppermute | solution.py:561
  32.5 0.9 copy-done.6
  33.5 7.0 %forward.1 = (f32[256,768]{1,0:T(8,128)S(1)}, f32[256,768]{1,0:T(8,128)S(1)}, bf16[256,768]{1,0:T(8,128)(2,1)S(1)}, bf16[64,2048]{1,0:T(8,128)(2,1)S(1)}, bf16[6...) custom-call(bf16[64,2048]{1,0:T(8,128)(2,1)S(1)} %copy-done.6, ...), custom_call_target="tpu_custom_call" | custom-call | flops 2415919104 | bytes 13500416 | tf_op jit(solution)/shard_map/forward/pallas_call | solution.py:187
  40.5 1.2 %turn.1 = (bf16[1408,256]{1,0:T(8,128)(2,1)S(1)}, bf16[1408,256]{1,0:T(8,128)(2,1)S(1)}, bf16[1,768,2048]{2,1,0:T(8,128)(2,1)S(1)}) custom-call(s32[8]{0:T(128)S(1)} %stack.35.me_ref, bf16[64,2048]{1,0:T(8,128)(2,1)S(1)} %copy-done.6, bf16[64,2048]{1,0:T(8,128)(2,1)S(1)} %collective-permute-done.refs_1_, ...), custom_call_target="tpu_custom_call" | custom-call | flops 1048576 | bytes 4325376 | tf_op jit(solution)/shard_map/turn/pallas_call | solution.py:235
  41.7 6.8 %collective-permute-done.7.refs_2_ = bf16[64,2048]{1,0:T(8,128)(2,1)S(1)} collective-permute-done((bf16[64,2048]{1,0:T(8,128)(2,1)}, bf16[64,2048]{1,0:T(8,128)(2,1)S(1)}, u32[]{:S(2)}, u32[]{:S(2)}) %collective-permute-start.7) | collective-permute-done | bytes 262176 | tf_op jit(solution)/shard_map/ppermute | solution.py:561
  48.5 1.9 %hidden_grad.1 = (bf16[512,768]{1,0:T(8,128)(2,1)S(1)}, bf16[256,2048]{1,0:T(8,128)(2,1)S(1)}, bf16[3456,256]{1,0:T(8,128)(2,1)S(1)}) custom-call(bf16[64,2048]{1,0:T(8,128)(2,1)S(1)} %copy-done.7, bf16[64,2048]{1,0:T(8,128)(2,1)S(1)} %collective-permute-done.6.refs_1_, bf16[64,2048]{1,0:T(8,128)(2,1)S(1)} %collective-permute-done.7.refs_2_, ...), custom_call_target="tpu_custom_call" | custom-call | flops 805306368 | bytes 7602176 | tf_op jit(solution)/shard_map/hidden_grad/pallas_call | solution.py:323
  50.9 2.7 %collective-permute-start.3 = (bf16[64,2048]{1,0:T(8,128)(2,1)S(1)}, bf16[64,2048]{1,0:T(8,128)(2,1)S(1)}, u32[]{:S(2)}, u32[]{:S(2)}) collective-permute-start(bf16[64,2048]{1,0:T(8,128)(2,1)S(1)} %get-tuple-element.58), channel_id=1, source_target_pairs={{0,3},{1,2},{2,1},{3,0},{4,7},{5,6},{6,5},{7,4},{8,11},{9,10},{10,... | collective-permute-start | bytes 786440 | tf_op jit(solution)/shard_map/ppermute | solution.py:561
  53.6 4.0 %collective-permute-start.4 = (bf16[64,2048]{1,0:T(8,128)(2,1)S(1)}, bf16[64,2048]{1,0:T(8,128)(2,1)S(1)}, u32[]{:S(2)}, u32[]{:S(2)}) collective-permute-start(bf16[64,2048]{1,0:T(8,128)(2,1)S(1)} %get-tuple-element.59), channel_id=1, source_target_pairs={{0,2},{1,3},{2,0},{3,1},{4,6},{5,7},{6,4},{7,5},{8,10},{9,11},{10,... | collective-permute-start | bytes 786440 | tf_op jit(solution)/shard_map/ppermute | solution.py:561
  57.7 3.6 %outer.2 = (bf16[2,384,768]{2,1,0:T(8,128)(2,1)}, bf16[2,384,768]{2,1,0:T(8,128)(2,1)}, f32[8,128]{1,0:T(8,128)S(1)}) custom-call(bf16[1408,256]{1,0:T(8,128)(2,1)S(1)} %get-tuple-element.73.refs_0_, bf16[3456,256]{1,0:T(8,128)(2,1)S(1)} %collective-permute-done.9.refs_1_, bf16[512,768]{1,0:T(8,128)(2,1)S(1)} %get-tuple-element.72.refs_2_.refs_0_, ...), custom_call_target="tpu_custom_call" | custom-call | flops 1207959552 | bytes 3801088 | tf_op jit(solution)/shard_map/outer/pallas_call | solution.py:50
  61.3 1.5 %collective-permute-start.16 = (bf16[2,384,768]{2,1,0:T(8,128)(2,1)}, bf16[2,384,768]{2,1,0:T(8,128)(2,1)}, u32[]{:S(2)}, u32[]{:S(2)}) collective-permute-start(bf16[2,384,768]{2,1,0:T(8,128)(2,1)} %get-tuple-element.93), channel_id=1, source_target_pairs={{0,16},{4,20},{8,24},{12,28},{16,0},{20,4},{24,8},{28,12},{1,17},{... | collective-permute-start | bytes 3538952 | tf_op jit(solution)/shard_map/ppermute | solution.py:456
  62.8 1.5 %collective-permute-start.14 = (bf16[2,384,768]{2,1,0:T(8,128)(2,1)}, bf16[2,384,768]{2,1,0:T(8,128)(2,1)S(1)}, u32[]{:S(2)}, u32[]{:S(2)}) collective-permute-start(bf16[2,384,768]{2,1,0:T(8,128)(2,1)} %get-tuple-element.88), channel_id=1, source_target_pairs={{0,8},{4,12},{8,0},{12,4},{16,24},{20,28},{24,16},{28,20},{1,9},{5... | collective-permute-start | bytes 3538952 | tf_op jit(solution)/shard_map/ppermute | solution.py:456
  64.3 3.0 %input_grad.1 = (bf16[64,2048]{1,0:T(8,128)(2,1)S(1)}, bf16[64,2048]{1,0:T(8,128)(2,1)S(1)}, bf16[64,2048]{1,0:T(8,128)(2,1)S(1)}, bf16[64,2048]{1,0:T(8,128)(2,1)S(1)}, f32[8,128]{1,0:T(8,128)S(1)}) custom-call(bf16[512,768]{1,0:T(8,128)(2,1)S(1)} %get-tuple-element.72.refs_2_.refs_0_, bf16[1,2048,768]{2,1,0:T(8,128)(2,1)S(1)} %copy-done.1, ...), custom_call_target="tpu_custom_call" | custom-call | flops 1610612736 | bytes 8126464 | tf_op jit(solution)/shard_map/input_grad/pallas_call | solution.py:50
  69.5 2.6 %outer.3 = (bf16[2,384,768]{2,1,0:T(8,128)(2,1)S(1)}, bf16[2,384,768]{2,1,0:T(8,128)(2,1)S(1)}, f32[8,128]{1,0:T(8,128)S(1)}) custom-call(bf16[1408,256]{1,0:T(8,128)(2,1)S(1)} %get-tuple-element.73.refs_0_, bf16[3456,256]{1,0:T(8,128)(2,1)S(1)} %collective-permute-done.9.refs_1_, bf16[512,768]{1,0:T(8,128)(2,1)S(1)} %get-tuple-element.72.refs_2_.refs_0_, ...), custom_call_target="tpu_custom_call" | custom-call | flops 1207959552 | bytes 3801088 | tf_op jit(solution)/shard_map/outer/pallas_call | solution.py:50
  72.1 1.0 copy-done.4
  73.1 4.8 %collective-permute-done.4.refs_2_.refs_4_ = bf16[64,2048]{1,0:T(8,128)(2,1)S(1)} collective-permute-done((bf16[64,2048]{1,0:T(8,128)(2,1)S(1)}, bf16[64,2048]{1,0:T(8,128)(2,1)S(1)}, u32[]{:S(2)}, u32[]{:S(2)}) %collective-permute-start.4) | collective-permute-done | bytes 262176 | tf_op jit(solution)/shard_map/ppermute | solution.py:561
  78.7 2.7 %collective-permute-start.11 = (bf16[64,2048]{1,0:T(8,128)(2,1)}, bf16[64,2048]{1,0:T(8,128)(2,1)S(1)}, u32[]{:S(2)}, u32[]{:S(2)}) collective-permute-start(bf16[64,2048]{1,0:T(8,128)(2,1)} %get-tuple-element.83), channel_id=1, source_target_pairs={{0,3},{1,2},{2,1},{3,0},{4,7},{5,6},{6,5},{7,4},{8,11},{9,10},{10,... | collective-permute-start | bytes 786440 | tf_op jit(solution)/shard_map/ppermute | solution.py:561
  81.4 1.7 %collective-permute-start.13 = (bf16[64,2048]{1,0:T(8,128)(2,1)}, bf16[64,2048]{1,0:T(8,128)(2,1)S(1)}, u32[]{:S(2)}, u32[]{:S(2)}) collective-permute-start(bf16[64,2048]{1,0:T(8,128)(2,1)} %get-tuple-element.85), channel_id=1, source_target_pairs={{0,1},{1,0},{2,3},{3,2},{4,5},{5,4},{6,7},{7,6},{8,9},{9,8},{10,11... | collective-permute-start | bytes 786440 | tf_op jit(solution)/shard_map/ppermute | solution.py:561
  84.1 0.9 copy-done.11
  86.0 2.8 %combine_out.1 = (bf16[128,2048]{1,0:T(8,128)(2,1)}, f32[2,128]{1,0:T(2,128)}, f32[8,128]{1,0:T(8,128)S(1)}) custom-call(s32[1]{0:T(128)} %bitcast.z_ref, s32[2,128]{1,0:T(2,128)S(1)} %bitcast.17, f32[2,128]{1,0:T(2,128)S(1)} %bitcast.14, bf16[128,2048]{1,0:T(8,128)(2,1)S(1)} %copy-done.3, bf16[64,2048]{1,0:T(8,128)(2,1)S(1)} %get-tuple-element.57.refs_0_, ...), custom_call_target="tpu_custom_call" | custom-call | flops 268435456 | bytes 2097152 | tf_op jit(solution)/shard_map/combine_out/pallas_call | solution.py:503
  89.0 1.9 %fold_two.3 = (bf16[384,768]{1,0:T(8,128)(2,1)S(1)}, bf16[384,768]{1,0:T(8,128)(2,1)S(1)}, f32[8,128]{1,0:T(8,128)}) custom-call(bf16[2,384,768]{2,1,0:T(8,128)(2,1)S(1)} %copy-done.5, bf16[2,384,768]{2,1,0:T(8,128)(2,1)} %collective-permute-done.16.refs_1_, f32[8,128]{1,0:T(8,128)S(1)} %get-tuple-element.89.refs_2_), custom_call_target="tpu_custom_call" | custom-call | flops 589824 | bytes 3538944 | tf_op jit(solution)/shard_map/fold_two/pallas_call | solution.py:50
  90.9 1.5 %collective-permute-start.17 = (bf16[384,768]{1,0:T(8,128)(2,1)S(1)}, bf16[384,768]{1,0:T(8,128)(2,1)S(1)}, u32[]{:S(2)}, u32[]{:S(2)}) collective-permute-start(bf16[384,768]{1,0:T(8,128)(2,1)S(1)} %get-tuple-element.95), channel_id=1, source_target_pairs={{0,8},{4,12},{8,0},{12,4},{16,24},{20,28},{24,16},{28,20},{1,9},{5... | collective-permute-start | bytes 1769480 | tf_op jit(solution)/shard_map/ppermute | solution.py:456
  93.0 1.5 %collective-permute-start.15 = (bf16[384,768]{1,0:T(8,128)(2,1)S(1)}, bf16[384,768]{1,0:T(8,128)(2,1)S(1)}, u32[]{:S(2)}, u32[]{:S(2)}) collective-permute-start(bf16[384,768]{1,0:T(8,128)(2,1)S(1)} %get-tuple-element.91), channel_id=1, source_target_pairs={{0,16},{4,20},{8,24},{12,28},{16,0},{20,4},{24,8},{28,12},{1,17},{... | collective-permute-start | bytes 1769480 | tf_op jit(solution)/shard_map/ppermute | solution.py:456
  94.5 8.8 %collective-permute-done.12.refs_2_ = bf16[64,2048]{1,0:T(8,128)(2,1)S(1)} collective-permute-done((bf16[64,2048]{1,0:T(8,128)(2,1)}, bf16[64,2048]{1,0:T(8,128)(2,1)S(1)}, u32[]{:S(2)}, u32[]{:S(2)}) %collective-permute-start.12) | collective-permute-done | bytes 262176 | tf_op jit(solution)/shard_map/ppermute | solution.py:561
  103.4 1.5 %combine_in.1 = (bf16[128,2048]{1,0:T(8,128)(2,1)}, f32[8,128]{1,0:T(8,128)S(1)}) custom-call(s32[1]{0:T(128)} %bitcast.z_ref, s32[2,128]{1,0:T(2,128)S(1)} %bitcast.18, bf16[64,2048]{1,0:T(8,128)(2,1)S(1)} %copy-done.17, bf16[64,2048]{1,0:T(8,128)(2,1)S(1)} %collective-permute-done.11.refs_1_, bf16[64,2048]{1,0:T(8,128)(2,1)S(1)} %collective-permute-done.12.refs_2_, ...), custom_call_target="tpu_custom_call" | custom-call | flops 10000000000 | bytes 1572864 | tf_op jit(solution)/shard_map/combine_in/pallas_call | solution.py:543
  105.1 1.9 %collective-permute-done.15.refs_1_ = bf16[384,768]{1,0:T(8,128)(2,1)S(1)} collective-permute-done((bf16[384,768]{1,0:T(8,128)(2,1)S(1)}, bf16[384,768]{1,0:T(8,128)(2,1)S(1)}, u32[]{:S(2)}, u32[]{:S(2)}) %collective-permute-start.15) | collective-permute-done | bytes 589856 | tf_op jit(solution)/shard_map/ppermute | solution.py:456
  107.0 1.2 %fold_last.1 = (bf16[1,256,768]{2,1,0:T(8,128)(2,1)}, bf16[1,256,768]{2,1,0:T(8,128)(2,1)}, bf16[1,96,2048]{2,1,0:T(8,128)(2,1)}) custom-call(bf16[384,768]{1,0:T(8,128)(2,1)S(1)} %get-tuple-element.90.refs_0_, bf16[384,768]{1,0:T(8,128)(2,1)S(1)} %collective-permute-done.15.refs_1_, bf16[384,768]{1,0:T(8,128)(2,1)S(1)} %get-tuple-element.94.refs_2_, ...), custom_call_target="tpu_custom_call" | custom-call | flops 589824 | bytes 3538944 | tf_op jit(solution)/shard_map/fold_last/pallas_call | solution.py:50
  (63 shorter events, 7.4 us)
Async XLA Ops:
  3.1 12.5 %collective-permute-start = (bf16[64,2048]{1,0:T(8,128)(2,1)}, bf16[64,2048]{1,0:T(8,128)(2,1)S(1)}, u32[]{:S(2)}, u32[]{:S(2)}) collective-permute-start(bf16[64,2048]{1,0:T(8,128)(2,1)} %get-tuple-element.54), channel_id=1, source_target_pairs={{0,3},{1,2},{2,1},{3,0},{4,7},{5,6},{6,5},{7,4},{8,11},{9,10},{10,... | collective-permute-start | bytes 786440 | tf_op jit(solution)/shard_map/ppermute | solution.py:561
  8.1 24.4 %collective-permute-start.1 = (bf16[64,2048]{1,0:T(8,128)(2,1)}, bf16[64,2048]{1,0:T(8,128)(2,1)S(1)}, u32[]{:S(2)}, u32[]{:S(2)}) collective-permute-start(bf16[64,2048]{1,0:T(8,128)(2,1)} %get-tuple-element.55), channel_id=1, source_target_pairs={{0,2},{1,3},{2,0},{3,1},{4,6},{5,7},{6,4},{7,5},{8,10},{9,11},{10,... | collective-permute-start | bytes 786440 | tf_op jit(solution)/shard_map/ppermute | solution.py:561
  8.1 24.4 %collective-permute-start.2 = (bf16[64,2048]{1,0:T(8,128)(2,1)}, bf16[64,2048]{1,0:T(8,128)(2,1)S(1)}, u32[]{:S(2)}, u32[]{:S(2)}) collective-permute-start(bf16[64,2048]{1,0:T(8,128)(2,1)} %get-tuple-element.56), channel_id=1, source_target_pairs={{0,1},{1,0},{2,3},{3,2},{4,5},{5,4},{6,7},{7,6},{8,9},{9,8},{10,11... | collective-permute-start | bytes 786440 | tf_op jit(solution)/shard_map/ppermute | solution.py:561
  11.1 30.6 %collective-permute-start.6 = (bf16[64,2048]{1,0:T(8,128)(2,1)}, bf16[64,2048]{1,0:T(8,128)(2,1)S(1)}, u32[]{:S(2)}, u32[]{:S(2)}) collective-permute-start(bf16[64,2048]{1,0:T(8,128)(2,1)} %get-tuple-element.64), channel_id=1, source_target_pairs={{0,1},{1,0},{2,3},{3,2},{4,5},{5,4},{6,7},{7,6},{8,9},{9,8},{10,11... | collective-permute-start | bytes 786440 | tf_op jit(solution)/shard_map/ppermute | solution.py:561
  12.6 35.9 %collective-permute-start.7 = (bf16[64,2048]{1,0:T(8,128)(2,1)}, bf16[64,2048]{1,0:T(8,128)(2,1)S(1)}, u32[]{:S(2)}, u32[]{:S(2)}) collective-permute-start(bf16[64,2048]{1,0:T(8,128)(2,1)} %get-tuple-element.65), channel_id=1, source_target_pairs={{0,2},{1,3},{2,0},{3,1},{4,6},{5,7},{6,4},{7,5},{8,10},{9,11},{10,... | collective-permute-start | bytes 786440 | tf_op jit(solution)/shard_map/ppermute | solution.py:561
  15.6 32.9 %collective-permute-start.8 = (bf16[64,2048]{1,0:T(8,128)(2,1)}, bf16[64,2048]{1,0:T(8,128)(2,1)S(1)}, u32[]{:S(2)}, u32[]{:S(2)}) collective-permute-start(bf16[64,2048]{1,0:T(8,128)(2,1)} %get-tuple-element.66), channel_id=1, source_target_pairs={{0,3},{1,2},{2,1},{3,0},{4,7},{5,6},{6,5},{7,4},{8,11},{9,10},{10,... | collective-permute-start | bytes 786440 | tf_op jit(solution)/shard_map/ppermute | solution.py:561
  32.5 1.0 copy-start.6
  33.5 7.0 %copy-start = (bf16[1,768,2048]{2,1,0:T(8,128)(2,1)S(1)}, bf16[1,768,2048]{2,1,0:T(8,128)(2,1)}, u32[]{:S(2)}) copy-start(bf16[1,768,2048]{2,1,0:T(8,128)(2,1)} %refs_5_.3) | copy-start | bytes 9437188
  40.5 8.0 %copy-start.7 = (bf16[64,2048]{1,0:T(8,128)(2,1)S(1)}, bf16[64,2048]{1,0:T(8,128)(2,1)}, u32[]{:S(2)}) copy-start(bf16[64,2048]{1,0:T(8,128)(2,1)} %get-tuple-element.63.refs_0_) | copy-start | bytes 786436
  48.5 15.8 %copy-start.2 = (bf16[1,2048,768]{2,1,0:T(8,128)(2,1)S(1)}, bf16[1,2048,768]{2,1,0:T(8,128)(2,1)}, u32[]{:S(2)}) copy-start(bf16[1,2048,768]{2,1,0:T(8,128)(2,1)} %refs_2_.1) | copy-start | bytes 9437188
  50.4 7.4 %collective-permute-start.9 = (bf16[3456,256]{1,0:T(8,128)(2,1)S(1)}, bf16[3456,256]{1,0:T(8,128)(2,1)S(1)}, u32[]{:S(2)}, u32[]{:S(2)}) collective-permute-start(bf16[3456,256]{1,0:T(8,128)(2,1)S(1)} %get-tuple-element.74), channel_id=1, source_target_pairs={{0,4},{4,0},{8,12},{12,8},{16,20},{20,16},{24,28},{28,24},{1,5},{5... | collective-permute-start | bytes 5308424 | tf_op jit(solution)/shard_map/ppermute | solution.py:456
  50.4 7.3 %collective-permute-start.10 = (bf16[512,768]{1,0:T(8,128)(2,1)S(1)}, bf16[512,768]{1,0:T(8,128)(2,1)S(1)}, u32[]{:S(2)}, u32[]{:S(2)}) collective-permute-start(bf16[512,768]{1,0:T(8,128)(2,1)S(1)} %get-tuple-element.72.refs_2_.refs_0_), channel_id=1, source_target_pairs={{0,4},{4,0},{8,12},{12,8},{16,20},{20,16},{24,28},{28,24},{1,5},{5... | collective-permute-start | bytes 2359304 | tf_op jit(solution)/shard_map/ppermute | solution.py:456
  50.9 22.1 %collective-permute-start.3 = (bf16[64,2048]{1,0:T(8,128)(2,1)S(1)}, bf16[64,2048]{1,0:T(8,128)(2,1)S(1)}, u32[]{:S(2)}, u32[]{:S(2)}) collective-permute-start(bf16[64,2048]{1,0:T(8,128)(2,1)S(1)} %get-tuple-element.58), channel_id=1, source_target_pairs={{0,3},{1,2},{2,1},{3,0},{4,7},{5,6},{6,5},{7,4},{8,11},{9,10},{10,... | collective-permute-start | bytes 786440 | tf_op jit(solution)/shard_map/ppermute | solution.py:561
  53.6 24.3 %collective-permute-start.4 = (bf16[64,2048]{1,0:T(8,128)(2,1)S(1)}, bf16[64,2048]{1,0:T(8,128)(2,1)S(1)}, u32[]{:S(2)}, u32[]{:S(2)}) collective-permute-start(bf16[64,2048]{1,0:T(8,128)(2,1)S(1)} %get-tuple-element.59), channel_id=1, source_target_pairs={{0,2},{1,3},{2,0},{3,1},{4,6},{5,7},{6,4},{7,5},{8,10},{9,11},{10,... | collective-permute-start | bytes 786440 | tf_op jit(solution)/shard_map/ppermute | solution.py:561
  57.6 20.3 %collective-permute-start.5 = (bf16[64,2048]{1,0:T(8,128)(2,1)S(1)}, bf16[64,2048]{1,0:T(8,128)(2,1)S(1)}, u32[]{:S(2)}, u32[]{:S(2)}) collective-permute-start(bf16[64,2048]{1,0:T(8,128)(2,1)S(1)} %get-tuple-element.60), channel_id=1, source_target_pairs={{0,1},{1,0},{2,3},{3,2},{4,5},{5,4},{6,7},{7,6},{8,9},{9,8},{10,11... | collective-permute-start | bytes 786440 | tf_op jit(solution)/shard_map/ppermute | solution.py:561
  57.7 6.6 %copy-start.1 = (bf16[1,2048,768]{2,1,0:T(8,128)(2,1)S(1)}, bf16[1,2048,768]{2,1,0:T(8,128)(2,1)}, u32[]{:S(2)}) copy-start(bf16[1,2048,768]{2,1,0:T(8,128)(2,1)} %refs_1_.1) | copy-start | bytes 9437188
  61.3 27.7 %collective-permute-start.16 = (bf16[2,384,768]{2,1,0:T(8,128)(2,1)}, bf16[2,384,768]{2,1,0:T(8,128)(2,1)}, u32[]{:S(2)}, u32[]{:S(2)}) collective-permute-start(bf16[2,384,768]{2,1,0:T(8,128)(2,1)} %get-tuple-element.93), channel_id=1, source_target_pairs={{0,16},{4,20},{8,24},{12,28},{16,0},{20,4},{24,8},{28,12},{1,17},{... | collective-permute-start | bytes 3538952 | tf_op jit(solution)/shard_map/ppermute | solution.py:456
  62.8 29.6 %collective-permute-start.14 = (bf16[2,384,768]{2,1,0:T(8,128)(2,1)}, bf16[2,384,768]{2,1,0:T(8,128)(2,1)S(1)}, u32[]{:S(2)}, u32[]{:S(2)}) collective-permute-start(bf16[2,384,768]{2,1,0:T(8,128)(2,1)} %get-tuple-element.88), channel_id=1, source_target_pairs={{0,8},{4,12},{8,0},{12,4},{16,24},{20,28},{24,16},{28,20},{1,9},{5... | collective-permute-start | bytes 3538952 | tf_op jit(solution)/shard_map/ppermute | solution.py:456
  69.5 2.6 %copy-start.16 = (bf16[64,2048]{1,0:T(8,128)(2,1)}, bf16[64,2048]{1,0:T(8,128)(2,1)S(1)}, u32[]{:S(2)}) copy-start(bf16[64,2048]{1,0:T(8,128)(2,1)S(1)} %get-tuple-element.77.refs_0_) | copy-start | bytes 786436
  72.0 1.0 copy-start.4
  73.1 4.8 %copy-start.21 = (f32[8,128]{1,0:T(8,128)}, f32[8,128]{1,0:T(8,128)S(1)}, u32[]{:S(2)}) copy-start(f32[8,128]{1,0:T(8,128)S(1)} %get-tuple-element.82.refs_6_) | copy-start | bytes 12292
  73.1 5.6 %copy-start.8 = (bf16[64,2048]{1,0:T(8,128)(2,1)}, bf16[64,2048]{1,0:T(8,128)(2,1)S(1)}, u32[]{:S(2)}) copy-start(bf16[64,2048]{1,0:T(8,128)(2,1)S(1)} %collective-permute-done.3.refs_1_.refs_3_) | copy-start | bytes 786436
  78.7 4.5 %copy-start.3 = (bf16[128,2048]{1,0:T(8,128)(2,1)S(1)}, bf16[128,2048]{1,0:T(8,128)(2,1)}, u32[]{:S(2)}) copy-start(bf16[128,2048]{1,0:T(8,128)(2,1)} %rows_ref.3) | copy-start | bytes 1572868
  78.7 4.5 %copy-start.14 = (f32[128,2]{0,1:T(2,128)S(1)}, f32[128,2]{0,1:T(2,128)}, u32[]{:S(2)}) copy-start(f32[128,2]{0,1:T(2,128)} %param.9) | copy-start | bytes 3076
  78.7 4.5 %copy-start.15 = (s32[128,2]{0,1:T(2,128)S(1)}, s32[128,2]{0,1:T(2,128)}, u32[]{:S(2)}) copy-start(s32[128,2]{0,1:T(2,128)} %param.8) | copy-start | bytes 3076
  78.7 10.3 %copy-start.5 = (bf16[2,384,768]{2,1,0:T(8,128)(2,1)S(1)}, bf16[2,384,768]{2,1,0:T(8,128)(2,1)}, u32[]{:S(2)}) copy-start(bf16[2,384,768]{2,1,0:T(8,128)(2,1)} %copy-done.4) | copy-start | bytes 3538948
  78.7 15.8 %collective-permute-start.11 = (bf16[64,2048]{1,0:T(8,128)(2,1)}, bf16[64,2048]{1,0:T(8,128)(2,1)S(1)}, u32[]{:S(2)}, u32[]{:S(2)}) collective-permute-start(bf16[64,2048]{1,0:T(8,128)(2,1)} %get-tuple-element.83), channel_id=1, source_target_pairs={{0,3},{1,2},{2,1},{3,0},{4,7},{5,6},{6,5},{7,4},{8,11},{9,10},{10,... | collective-permute-start | bytes 786440 | tf_op jit(solution)/shard_map/ppermute | solution.py:561
  81.4 21.9 %collective-permute-start.12 = (bf16[64,2048]{1,0:T(8,128)(2,1)}, bf16[64,2048]{1,0:T(8,128)(2,1)S(1)}, u32[]{:S(2)}, u32[]{:S(2)}) collective-permute-start(bf16[64,2048]{1,0:T(8,128)(2,1)} %get-tuple-element.84), channel_id=1, source_target_pairs={{0,2},{1,3},{2,0},{3,1},{4,6},{5,7},{6,4},{7,5},{8,10},{9,11},{10,... | collective-permute-start | bytes 786440 | tf_op jit(solution)/shard_map/ppermute | solution.py:561
  81.4 21.9 %collective-permute-start.13 = (bf16[64,2048]{1,0:T(8,128)(2,1)}, bf16[64,2048]{1,0:T(8,128)(2,1)S(1)}, u32[]{:S(2)}, u32[]{:S(2)}) collective-permute-start(bf16[64,2048]{1,0:T(8,128)(2,1)} %get-tuple-element.85), channel_id=1, source_target_pairs={{0,1},{1,0},{2,3},{3,2},{4,5},{5,4},{6,7},{7,6},{8,9},{9,8},{10,11... | collective-permute-start | bytes 786440 | tf_op jit(solution)/shard_map/ppermute | solution.py:561
  90.9 12.5 %copy-start.17 = (bf16[64,2048]{1,0:T(8,128)(2,1)S(1)}, bf16[64,2048]{1,0:T(8,128)(2,1)}, u32[]{:S(2)}) copy-start(bf16[64,2048]{1,0:T(8,128)(2,1)} %copy-done.16) | copy-start | bytes 786436
  90.9 14.3 %collective-permute-start.17 = (bf16[384,768]{1,0:T(8,128)(2,1)S(1)}, bf16[384,768]{1,0:T(8,128)(2,1)S(1)}, u32[]{:S(2)}, u32[]{:S(2)}) collective-permute-start(bf16[384,768]{1,0:T(8,128)(2,1)S(1)} %get-tuple-element.95), channel_id=1, source_target_pairs={{0,8},{4,12},{8,0},{12,4},{16,24},{20,28},{24,16},{28,20},{1,9},{5... | collective-permute-start | bytes 1769480 | tf_op jit(solution)/shard_map/ppermute | solution.py:456
  93.0 14.0 %collective-permute-start.15 = (bf16[384,768]{1,0:T(8,128)(2,1)S(1)}, bf16[384,768]{1,0:T(8,128)(2,1)S(1)}, u32[]{:S(2)}, u32[]{:S(2)}) collective-permute-start(bf16[384,768]{1,0:T(8,128)(2,1)S(1)} %get-tuple-element.91), channel_id=1, source_target_pairs={{0,16},{4,20},{8,24},{12,28},{16,0},{20,4},{24,8},{28,12},{1,17},{... | collective-permute-start | bytes 1769480 | tf_op jit(solution)/shard_map/ppermute | solution.py:456
  (8 other events, 6.4 us)
